TPU v7x, 512 devices: a whole 4x8x8 slice. The times are simulated.
512 devices in a mesh: gx: 8 (over z_lo, core), gy: 16 (over z_hi, y), orb: 4 (over x).
Axes of the slice: x: 4, y: 8, z: 8 (z_hi: 2, z_lo: 4; z = z_hi * 4 + z_lo), core: 2. Of those that a mesh axis runs over, the one named last changes fastest.
Arguments:
- orbitals: float32 [16, 96, 256, 128], P('orb', 'gx', 'gy'), may hold values from -1800 to 1800
- potential: float32 [96, 256, 128], P('gx', 'gy'), may hold values from -2 to 0
- kinetic_mu: float32 [96, 256, 128], P('gx', 'gy'), may hold values from 0.2 to 1
- projectors: float32 [1024, 8, 512], P(('gx', 'gy')), may hold values from -4 to 4
- strengths: float32 [1024, 8], P(('gx', 'gy')), may hold values from -4 to 8
- box_offsets: int32 [1024, 3], P(('gx', 'gy')), may hold values from 0 to 120, as said below
- block_counts: int32 [128], P(('gx', 'gy')), may hold values from 1 to 8, as said below
Outputs:
- orthonormal: float32 [16, 96, 256, 128], P('orb', 'gx', 'gy')
Inputs may be any that keep to these rules, and one draw needn't show every extreme that they name: `box_offsets`: column 0 lies in 2 to 14, column 1 in 2 to 18, column 2 in 0 to 120. `block_counts`: some tile has all 8 slots live, and some tile only one.
All inputs are finite; a program needn't handle non-finite values.
Results may differ from a plain program's by a relative error of at most 0.0003.
Values sent between devices are 32-bit elements; how exact they have to be, the bound alone decides.
No kernel may reach another device: no remote copies, remote signals or barrier semaphores. Data moves between devices by JAX's collectives and lax.ppermute only.
A program may use at most 64 MiB of HBM per device.

v0:
```python
import jax
import jax.numpy as jnp
from jax import lax
from jax.sharding import PartitionSpec as P

STEPS = 3
BOX_EDGE = 8
HALO = 6


first_coefs = (6.0 / 7.0, -15.0 / 56.0, 5.0 / 63.0, -1.0 / 56.0, 2.0 / 825.0, -1.0 / 5544.0)
second_coefs = (12.0 / 7.0, -15.0 / 56.0, 10.0 / 189.0, -1.0 / 112.0, 2.0 / 1925.0, -1.0 / 16632.0)
center_coef = -5369.0 / 1800.0
filter_center = 13.5
filter_half = 10.5


def extended_2(block, sides, width):
    for axis, dim in sides:
        count = lax.axis_size(axis)
        forward = [(i, i + 1) for i in range(count - 1)]
        backward = [(target, source) for source, target in forward]
        low = lax.ppermute(
            lax.slice_in_dim(block, block.shape[dim] - width, None, axis=dim), axis, forward
        )
        high = lax.ppermute(lax.slice_in_dim(block, 0, width, axis=dim), axis, backward)
        block = jnp.concatenate([low, block, high], axis=dim)
    return block


def neighbour(extended, direction, offset):
    leading = extended.ndim - 3
    starts = [0] * extended.ndim
    limits = list(extended.shape)
    for dim_index in range(3):
        starts[leading + dim_index] = HALO
        limits[leading + dim_index] = extended.shape[leading + dim_index] - HALO
    starts[leading + direction] += offset
    limits[leading + direction] += offset
    return lax.slice(extended, starts, limits)


def pad_depth(padded):
    return jnp.pad(padded, [(0, 0)] * (padded.ndim - 1) + [(HALO, HALO)])


def gradient(extended):
    result = []
    for direction in range(3):
        summed = first_coefs[0] * (
            neighbour(extended, direction, 1) - neighbour(extended, direction, -1)
        )
        for offset in range(2, HALO + 1):
            summed = summed + first_coefs[offset - 1] * (
                neighbour(extended, direction, offset) - neighbour(extended, direction, -offset)
            )
        result.append(summed)
    return result


def laplacian(extended):
    summed = 3.0 * center_coef * neighbour(extended, 0, 0)
    for direction in range(3):
        for offset in range(1, HALO + 1):
            summed = summed + second_coefs[offset - 1] * (
                neighbour(extended, direction, offset) + neighbour(extended, direction, -offset)
            )
    return summed


def local_terms(padded, grad_mu, kinetic_mu, potential):
    extended = pad_depth(padded)
    laplace = laplacian(extended)
    slopes = gradient(extended)
    cross_term = grad_mu[0] * slopes[0] + grad_mu[1] * slopes[1] + grad_mu[2] * slopes[2]
    return (
        -0.5 * (1.0 + kinetic_mu) * laplace
        - 0.5 * cross_term
        + potential * neighbour(extended, 0, 0)
    )


def chebyshev(start, hamiltonian):
    previous = start
    current = (hamiltonian(start) - filter_center * start) / filter_half
    for repeat in range(STEPS - 1):
        following = 2.0 * (hamiltonian(current) - filter_center * current) / filter_half - previous
        previous, current = (current, following)
    return current


def nonlocal_terms(padded, projectors, strengths, box_offsets, live_count):
    orb_count = padded.shape[0]
    norm_scale = BOX_EDGE ** (-1.5)
    extent = (orb_count, BOX_EDGE, BOX_EDGE, BOX_EDGE)

    def add_atom(slot_index, accumulated):
        is_live = (slot_index < live_count).astype(jnp.float32)
        anchor = jnp.zeros((), jnp.int32)
        starts = (
            anchor,
            box_offsets[slot_index, 0],
            box_offsets[slot_index, 1],
            box_offsets[slot_index, 2],
        )
        support = lax.dynamic_slice(padded, starts, extent).reshape(orb_count, -1)
        table = projectors[slot_index]
        coeffs = jnp.dot(support, table.T, precision=lax.Precision.HIGHEST) * norm_scale
        weights = coeffs * strengths[slot_index] * is_live
        addition = (jnp.dot(weights, table, precision=lax.Precision.HIGHEST) * norm_scale).reshape(
            extent
        )
        current = lax.dynamic_slice(accumulated, starts, extent)
        return lax.dynamic_update_slice(accumulated, current + addition, starts)

    return lax.fori_loop(0, projectors.shape[0], add_atom, jnp.zeros_like(padded))


def fold_rims(accumulated, received):
    rows_x = accumulated.shape[-3] - 2 * HALO
    rows_y = accumulated.shape[-2] - 2 * HALO
    edge = 2 * HALO
    interior = accumulated[..., HALO : HALO + rows_x, HALO : HALO + rows_y, :]
    interior = interior.at[..., :HALO, :, :].add(received[..., :HALO, edge : edge + rows_y, :])
    interior = interior.at[..., rows_x - HALO :, :, :].add(
        received[..., -HALO:, edge : edge + rows_y, :]
    )
    interior = interior.at[..., :, :HALO, :].add(received[..., edge : edge + rows_x, :HALO, :])
    interior = interior.at[..., :, rows_y - HALO :, :].add(
        received[..., edge : edge + rows_x, -HALO:, :]
    )
    interior = interior.at[..., :HALO, :HALO, :].add(received[..., :HALO, :HALO, :])
    interior = interior.at[..., :HALO, rows_y - HALO :, :].add(received[..., :HALO, -HALO:, :])
    interior = interior.at[..., rows_x - HALO :, :HALO, :].add(received[..., -HALO:, :HALO, :])
    interior = interior.at[..., rows_x - HALO :, rows_y - HALO :, :].add(
        received[..., -HALO:, -HALO:, :]
    )
    return interior


def shards(orbitals, potential, kinetic_mu, projectors, strengths, box_offsets, block_counts):
    mu_padded = extended_2(kinetic_mu, (("gx", 0), ("gy", 1)), HALO)
    grad_mu = gradient(pad_depth(mu_padded))
    live_count = block_counts[0]

    def hamiltonian(field):
        padded = extended_2(field, (("gx", 1), ("gy", 2)), HALO)
        local = local_terms(padded, grad_mu, kinetic_mu, potential)
        accumulated = nonlocal_terms(padded, projectors, strengths, box_offsets, live_count)
        received = extended_2(accumulated, (("gx", 1), ("gy", 2)), HALO)
        return local + fold_rims(accumulated, received)

    filtered = chebyshev(orbitals, hamiltonian)
    orb_count = filtered.shape[0]
    cell_count = (
        filtered.shape[1]
        * filtered.shape[2]
        * filtered.shape[3]
        * lax.axis_size("gx")
        * lax.axis_size("gy")
    )
    everything = lax.all_gather(filtered, "orb", axis=0, tiled=True)
    flattened = everything.reshape(everything.shape[0], -1)
    partial_correlation = jnp.dot(flattened, flattened.T, precision=lax.Precision.HIGHEST)
    correlation = lax.psum(partial_correlation, ("gx", "gy")) / cell_count
    cholesky_factor = jnp.linalg.cholesky(correlation)
    identity = jnp.eye(correlation.shape[0], dtype=jnp.float32)
    inverse = jax.scipy.linalg.solve_triangular(cholesky_factor, identity, lower=True)
    own_rows = lax.dynamic_slice_in_dim(inverse, lax.axis_index("orb") * orb_count, orb_count, 0)
    result = jnp.dot(own_rows, flattened, precision=lax.Precision.HIGHEST).reshape(filtered.shape)
    return result


def solution(mesh):
    in_specs = (
        P("orb", "gx", "gy", None),
        P("gx", "gy", None),
        P("gx", "gy", None),
        P(("gx", "gy"), None, None),
        P(("gx", "gy"), None),
        P(("gx", "gy"), None),
        P(("gx", "gy")),
    )
    out_specs = P("orb", "gx", "gy", None)
    return jax.shard_map(shards, mesh=mesh, in_specs=in_specs, out_specs=out_specs, check_vma=False)
```

profile of v0, /device:TPU:448, one launch (start us, length us, event | category | flops | bytes accessed | tf_op | source)
XLA Modules:
  0.0 1183.6 jit_solution(14866823250108960389)
XLA Ops:
  21.9 4.4 collective-permute-start.2
  29.0 9.9 collective-permute-start.6
  41.5 5.3 collective-permute-done.3
  48.9 166.8 %while.63 = (s32[]{:T(128)}, f32[4,24,28,128]{3,0,2,1:T(4,128)S(1)}, s32[8,3]{0,1:T(4,128)S(1)}, f32[4,24,28,128]{3,0,2,1:T(4,128)}, f32[8,8,512]{2,1,0:T(8,128)...) while((s32[]{:T(128)}, ...), condition=%wide.region_1.2_spmd, body=%wide.region_0.1_spmd.sunk | while | flops 397397 | bytes 189069 | solution.py:116
  60.2 9.6 dynamic_update_slice.24
  81.0 9.6 dynamic_update_slice.24
  101.9 9.6 dynamic_update_slice.24
  122.8 9.6 dynamic_update_slice.24
  143.6 9.6 dynamic_update_slice.24
  164.5 9.6 dynamic_update_slice.24
  185.3 9.6 dynamic_update_slice.24
  206.2 9.6 dynamic_update_slice.24
  229.9 10.2 collective-permute-start.11
  240.3 10.3 collective-permute-done.10
  253.0 5.6 broadcast_multiply_fusion
  258.6 6.8 collective-permute-start.12
  268.6 3.8 collective-permute-done.13
  272.6 10.2 collective-permute-start.14
  287.0 14.1 %collective-permute-done.15 = f32[4,24,6,128]{3,0,2,1:T(4,128)S(1)} collective-permute-done((f32[4,24,6,128]{3,0,2,1:T(4,128)S(1)}, f32[4,24,6,128]{3,0,2,1:T(4,128)S(1)}, u32[]{:S(2)}, u32[]{:S(2)}) %collective-permute-start.15) | collective-permute-done | bytes 294944 | tf_op jit(solution)/shard_map/ppermute | solution.py:23
  302.6 165.4 %while.64 = (s32[]{:T(128)}, f32[4,24,28,128]{3,0,2,1:T(4,128)S(1)}, s32[8,3]{0,1:T(4,128)S(1)}, f32[4,24,28,128]{3,0,2,1:T(4,128)}, f32[8,8,512]{2,1,0:T(8,128)...) while((s32[]{:T(128)}, ...), condition=%wide.region_4.5_spmd, body=%wide.region_3.4_spmd.sunk | while | flops 397397 | bytes 189069 | solution.py:116
  313.7 9.6 dynamic_update_slice.25
  334.4 9.6 dynamic_update_slice.25
  355.1 9.6 dynamic_update_slice.25
  375.8 9.6 dynamic_update_slice.25
  396.4 9.6 dynamic_update_slice.25
  417.1 9.6 dynamic_update_slice.25
  437.8 9.6 dynamic_update_slice.25
  458.5 9.6 dynamic_update_slice.25
  480.6 10.3 collective-permute-start.19
  491.0 8.5 collective-permute-done.18
  501.8 4.5 multiply_subtract_fusion.1
  506.4 11.8 collective-permute-start.20
  525.3 10.5 collective-permute-start.22
  540.1 14.6 %collective-permute-done.23 = f32[4,24,6,128]{3,0,2,1:T(4,128)S(1)} collective-permute-done((f32[4,24,6,128]{3,0,2,1:T(4,128)S(1)}, f32[4,24,6,128]{3,0,2,1:T(4,128)S(1)}, u32[]{:S(2)}, u32[]{:S(2)}) %collective-permute-start.23) | collective-permute-done | bytes 294944 | tf_op jit(solution)/shard_map/ppermute | solution.py:23
  555.9 158.2 %while.65 = (s32[]{:T(128)}, f32[4,24,28,128]{3,0,2,1:T(4,128)S(1)}, s32[8,3]{0,1:T(4,128)S(1)}, f32[4,24,28,128]{3,0,2,1:T(4,128)S(1)}, f32[8,8,512]{2,1,0:T(8,...) while((s32[]{:T(128)}, ...), condition=%wide.region_6.7_spmd, body=%wide.region_5.6_spmd.sunk | while | flops 397397 | bytes 189069 | solution.py:116
  566.1 9.6 dynamic_update_slice.26
  585.8 9.6 dynamic_update_slice.26
  605.6 9.6 dynamic_update_slice.26
  625.4 9.6 dynamic_update_slice.26
  645.2 9.6 dynamic_update_slice.26
  664.9 9.6 dynamic_update_slice.26
  684.7 9.6 dynamic_update_slice.26
  704.5 9.6 dynamic_update_slice.26
  726.8 10.1 collective-permute-start.27
  737.0 8.7 collective-permute-done.26
  748.0 4.3 multiply_subtract_fusion
  753.1 40.4 %all-gather.2.cloned.1.call-done = f32[16,12,16,128]{3,2,1,0:T(8,128)} async-done(((f32[4,12,16,128]{3,2,1,0:T(8,128)}), f32[16,12,16,128]{3,2,1,0:T(8,128)}) %all-gather.2.cloned.1.call-update) | async-done | bytes 1572880 | tf_op jit(solution)/shard_map/all_gather | solution.py:162
  800.0 370.0 %psum.7 = f32[16,16]{0,1:T(8,128)S(1)} all-reduce(f32[16,16]{0,1:T(8,128)S(1)} %fusion.31), channel_id=1, replica_groups=mesh['gx'=8,'gy'=16,'orb'=4] {'gx','gy'}, use_global_device_ids=true, to_apply=%region_7.8 | all-reduce | flops 256 | bytes 2048 | tf_op jit(solution)/shard_map/psum | solution.py:165
  (451 shorter events, 206.1 us)
Async XLA Ops:
  6.5 787.0 %all-gather.2.cloned.1.call-start = ((), (), s32[]{:S(2)}) async-start(), calls=%async_computation | async-start | bytes 1966080 | tf_op jit(solution)/shard_map/all_gather | solution.py:162
  7.8 13.4 %collective-permute-start.1 = (f32[4,6,16,128]{3,0,2,1:T(4,128)S(1)}, f32[4,6,16,128]{3,0,2,1:T(4,128)S(1)}, u32[]{:S(2)}, u32[]{:S(2)}) collective-permute-start(f32[4,6,16,128]{3,0,2,1:T(4,128)S(1)} %copy.147), channel_id=1, source_target_pairs={{0,64},{64,128},{128,192},{192,256},{256,320},{320,384},{384,448},... | collective-permute-start | bytes 589832 | tf_op jit(solution)/shard_map/ppermute | solution.py:23
  9.8 11.9 %collective-permute-start = (f32[4,6,16,128]{3,0,2,1:T(4,128)S(1)}, f32[4,6,16,128]{3,0,2,1:T(4,128)S(1)}, u32[]{:S(2)}, u32[]{:S(2)}) collective-permute-start(f32[4,6,16,128]{3,0,2,1:T(4,128)S(1)} %copy.148), channel_id=1, source_target_pairs={{64,0},{128,64},{192,128},{256,192},{320,256},{384,320},{448,384},... | collective-permute-start | bytes 589832 | tf_op jit(solution)/shard_map/ppermute | solution.py:26
  13.5 7.0 collective-permute-start.5
  15.4 5.7 collective-permute-start.4
  21.8 25.0 %copy-start.2 = (f32[4,24,16,128]{3,0,2,1:T(4,128)}, f32[4,24,16,128]{3,0,2,1:T(4,128)S(1)}, u32[]{:S(2)}) copy-start(f32[4,24,16,128]{3,0,2,1:T(4,128)S(1)} %get-tuple-element.822) | copy-start | bytes 2359300
  21.9 19.6 %collective-permute-start.2 = (f32[4,24,6,128]{3,0,2,1:T(4,128)S(1)}, f32[4,24,6,128]{3,0,2,1:T(4,128)S(1)}, u32[]{:S(2)}, u32[]{:S(2)}) collective-permute-start(f32[4,24,6,128]{3,0,2,1:T(4,128)S(1)} %get-tuple-element.811), channel_id=1, source_target_pairs={{4,0},{8,4},{12,8},{16,12},{20,16},{24,20},{28,24},{32,28},{36,32}... | collective-permute-start | bytes 884744 | tf_op jit(solution)/shard_map/ppermute | solution.py:26
  26.3 20.5 %collective-permute-start.3 = (f32[4,24,6,128]{3,0,2,1:T(4,128)S(1)}, f32[4,24,6,128]{3,0,2,1:T(4,128)S(1)}, u32[]{:S(2)}, u32[]{:S(2)}) collective-permute-start(f32[4,24,6,128]{3,0,2,1:T(4,128)S(1)} %get-tuple-element.810), channel_id=1, source_target_pairs={{0,4},{4,8},{8,12},{12,16},{16,20},{20,24},{24,28},{28,32},{32,36}... | collective-permute-start | bytes 884744 | tf_op jit(solution)/shard_map/ppermute | solution.py:23
  29.0 188.8 %collective-permute-start.6 = (f32[24,6,128]{2,1,0:T(8,128)}, f32[24,6,128]{2,1,0:T(8,128)S(1)}, u32[]{:S(2)}, u32[]{:S(2)}) collective-permute-start(f32[24,6,128]{2,1,0:T(8,128)} %get-tuple-element.826), channel_id=1, source_target_pairs={{4,0},{8,4},{12,8},{16,12},{20,16},{24,20},{28,24},{32,28},{36,32}... | collective-permute-start | bytes 221192 | tf_op jit(solution)/shard_map/ppermute | solution.py:26
  38.9 178.9 %collective-permute-start.7 = (f32[24,6,128]{2,1,0:T(8,128)}, f32[24,6,128]{2,1,0:T(8,128)}, u32[]{:S(2)}, u32[]{:S(2)}) collective-permute-start(f32[24,6,128]{2,1,0:T(8,128)} %get-tuple-element.825), channel_id=1, source_target_pairs={{0,4},{4,8},{8,12},{12,16},{16,20},{20,24},{24,28},{28,32},{32,36}... | collective-permute-start | bytes 221192 | tf_op jit(solution)/shard_map/ppermute | solution.py:23
  215.8 8.6 collective-permute-start.8
  219.4 33.5 %copy-start.17 = (f32[12,16,128]{2,1,0:T(8,128)}, f32[12,16,128]{2,1,0:T(8,128)S(1)}, u32[]{:S(2)}) copy-start(f32[12,16,128]{2,1,0:T(8,128)S(1)} %fusion.103) | copy-start | bytes 294916
  219.4 8.4 collective-permute-start.9
  224.4 28.5 %copy-start.23 = (f32[12,16,128]{2,1,0:T(8,128)}, f32[12,16,128]{2,1,0:T(8,128)S(1)}, u32[]{:S(2)}) copy-start(f32[12,16,128]{2,1,0:T(8,128)S(1)} %fusion.81) | copy-start | bytes 294916
  227.9 25.0 %copy-start.34 = (f32[12,16,128]{2,1,0:T(8,128)S(1)}, f32[12,16,128]{2,1,0:T(8,128)}, u32[]{:S(2)}) copy-start(f32[12,16,128]{2,1,0:T(8,128)} %param.62) | copy-start | bytes 294916
  228.0 22.7 %collective-permute-start.10 = (f32[4,36,6,128]{3,0,2,1:T(4,128)S(1)}, f32[4,36,6,128]{3,0,2,1:T(4,128)S(1)}, u32[]{:S(2)}, u32[]{:S(2)}) collective-permute-start(f32[4,36,6,128]{3,0,2,1:T(4,128)S(1)} %get-tuple-element.795), channel_id=1, source_target_pairs={{0,4},{4,8},{8,12},{12,16},{16,20},{20,24},{24,28},{28,32},{32,36}... | collective-permute-start | bytes 1327112 | tf_op jit(solution)/shard_map/ppermute | solution.py:23
  229.9 23.0 %copy-start = (f32[4,24,28,128]{3,0,2,1:T(4,128)S(1)}, f32[4,24,28,128]{3,0,2,1:T(4,128)}, u32[]{:S(2)}) copy-start(f32[4,24,28,128]{3,0,2,1:T(4,128)} %get-tuple-element.1107) | copy-start | bytes 4128772
  229.9 23.0 %copy-start.3 = (f32[4,24,16,128]{3,0,2,1:T(4,128)S(1)}, f32[4,24,16,128]{3,0,2,1:T(4,128)}, u32[]{:S(2)}) copy-start(f32[4,24,16,128]{3,0,2,1:T(4,128)} %copy-done.2) | copy-start | bytes 2359300
  229.9 23.0 %copy-start.14 = (f32[12,16,128]{2,1,0:T(8,128)S(1)}, f32[12,16,128]{2,1,0:T(8,128)}, u32[]{:S(2)}) copy-start(f32[12,16,128]{2,1,0:T(8,128)} %fusion.116) | copy-start | bytes 294916
  229.9 23.0 %copy-start.20 = (f32[12,16,128]{2,1,0:T(8,128)S(1)}, f32[12,16,128]{2,1,0:T(8,128)}, u32[]{:S(2)}) copy-start(f32[12,16,128]{2,1,0:T(8,128)} %get-tuple-element.827) | copy-start | bytes 294916
  229.9 23.0 %copy-start.27 = (f32[4,24,6,128]{3,0,2,1:T(4,128)S(1)}, f32[4,24,6,128]{3,0,2,1:T(4,128)}, u32[]{:S(2)}) copy-start(f32[4,24,6,128]{3,0,2,1:T(4,128)} %copy-done.26) | copy-start | bytes 884740
  229.9 23.0 %copy-start.29 = (f32[4,24,6,128]{3,0,2,1:T(4,128)S(1)}, f32[4,24,6,128]{3,0,2,1:T(4,128)}, u32[]{:S(2)}) copy-start(f32[4,24,6,128]{3,0,2,1:T(4,128)} %copy-done.28) | copy-start | bytes 884740
  229.9 20.8 %collective-permute-start.11 = (f32[4,36,6,128]{3,0,2,1:T(4,128)S(1)}, f32[4,36,6,128]{3,0,2,1:T(4,128)S(1)}, u32[]{:S(2)}, u32[]{:S(2)}) collective-permute-start(f32[4,36,6,128]{3,0,2,1:T(4,128)S(1)} %get-tuple-element.794), channel_id=1, source_target_pairs={{4,0},{8,4},{12,8},{16,12},{20,16},{24,20},{28,24},{32,28},{36,32}... | collective-permute-start | bytes 1327112 | tf_op jit(solution)/shard_map/ppermute | solution.py:26
  258.6 9.9 collective-permute-start.12
  265.4 7.0 collective-permute-start.13
  272.4 201.3 %copy-start.12 = (f32[4,6,16,128]{3,0,2,1:T(4,128)}, f32[4,6,16,128]{3,0,2,1:T(4,128)S(1)}, u32[]{:S(2)}) copy-start(f32[4,6,16,128]{3,0,2,1:T(4,128)S(1)} %collective-permute-done.13) | copy-start | bytes 589828
  272.6 14.4 %collective-permute-start.14 = (f32[4,24,6,128]{3,0,2,1:T(4,128)S(1)}, f32[4,24,6,128]{3,0,2,1:T(4,128)S(1)}, u32[]{:S(2)}, u32[]{:S(2)}) collective-permute-start(f32[4,24,6,128]{3,0,2,1:T(4,128)S(1)} %get-tuple-element.809), channel_id=1, source_target_pairs={{4,0},{8,4},{12,8},{16,12},{20,16},{24,20},{28,24},{32,28},{36,32}... | collective-permute-start | bytes 884744 | tf_op jit(solution)/shard_map/ppermute | solution.py:26
  282.7 18.3 %collective-permute-start.15 = (f32[4,24,6,128]{3,0,2,1:T(4,128)S(1)}, f32[4,24,6,128]{3,0,2,1:T(4,128)S(1)}, u32[]{:S(2)}, u32[]{:S(2)}) collective-permute-start(f32[4,24,6,128]{3,0,2,1:T(4,128)S(1)} %get-tuple-element.808), channel_id=1, source_target_pairs={{0,4},{4,8},{8,12},{12,16},{16,20},{20,24},{24,28},{28,32},{32,36}... | collective-permute-start | bytes 884744 | tf_op jit(solution)/shard_map/ppermute | solution.py:23
  468.1 8.6 collective-permute-start.16
  470.1 8.4 collective-permute-start.17
  478.6 20.9 %collective-permute-start.18 = (f32[4,36,6,128]{3,0,2,1:T(4,128)S(1)}, f32[4,36,6,128]{3,0,2,1:T(4,128)S(1)}, u32[]{:S(2)}, u32[]{:S(2)}) collective-permute-start(f32[4,36,6,128]{3,0,2,1:T(4,128)S(1)} %get-tuple-element.793), channel_id=1, source_target_pairs={{0,4},{4,8},{8,12},{12,16},{16,20},{20,24},{24,28},{28,32},{32,36}... | collective-permute-start | bytes 1327112 | tf_op jit(solution)/shard_map/ppermute | solution.py:23
  480.6 19.0 %collective-permute-start.19 = (f32[4,36,6,128]{3,0,2,1:T(4,128)S(1)}, f32[4,36,6,128]{3,0,2,1:T(4,128)S(1)}, u32[]{:S(2)}, u32[]{:S(2)}) collective-permute-start(f32[4,36,6,128]{3,0,2,1:T(4,128)S(1)} %get-tuple-element.792), channel_id=1, source_target_pairs={{4,0},{8,4},{12,8},{16,12},{20,16},{24,20},{28,24},{32,28},{36,32}... | collective-permute-start | bytes 1327112 | tf_op jit(solution)/shard_map/ppermute | solution.py:26
  506.4 14.9 %collective-permute-start.20 = (f32[4,6,16,128]{3,0,2,1:T(4,128)S(1)}, f32[4,6,16,128]{3,0,2,1:T(4,128)S(1)}, u32[]{:S(2)}, u32[]{:S(2)}) collective-permute-start(f32[4,6,16,128]{3,0,2,1:T(4,128)S(1)} %get-tuple-element.813), channel_id=1, source_target_pairs={{64,0},{128,64},{192,128},{256,192},{320,256},{384,320},{448,384},... | collective-permute-start | bytes 589832 | tf_op jit(solution)/shard_map/ppermute | solution.py:26
  518.2 7.0 collective-permute-start.21
  521.3 33.3 %copy-start.8 = (f32[4,6,16,128]{3,0,2,1:T(4,128)}, f32[4,6,16,128]{3,0,2,1:T(4,128)S(1)}, u32[]{:S(2)}) copy-start(f32[4,6,16,128]{3,0,2,1:T(4,128)S(1)} %collective-permute-done.20) | copy-start | bytes 589828
  525.2 29.5 %copy-start.10 = (f32[4,6,16,128]{3,0,2,1:T(4,128)}, f32[4,6,16,128]{3,0,2,1:T(4,128)S(1)}, u32[]{:S(2)}) copy-start(f32[4,6,16,128]{3,0,2,1:T(4,128)S(1)} %collective-permute-done.21) | copy-start | bytes 589828
  525.3 14.8 %collective-permute-start.22 = (f32[4,24,6,128]{3,0,2,1:T(4,128)S(1)}, f32[4,24,6,128]{3,0,2,1:T(4,128)S(1)}, u32[]{:S(2)}, u32[]{:S(2)}) collective-permute-start(f32[4,24,6,128]{3,0,2,1:T(4,128)S(1)} %get-tuple-element.805), channel_id=1, source_target_pairs={{4,0},{8,4},{12,8},{16,12},{20,16},{24,20},{28,24},{32,28},{36,32}... | collective-permute-start | bytes 884744 | tf_op jit(solution)/shard_map/ppermute | solution.py:26
  535.9 18.8 %collective-permute-start.23 = (f32[4,24,6,128]{3,0,2,1:T(4,128)S(1)}, f32[4,24,6,128]{3,0,2,1:T(4,128)S(1)}, u32[]{:S(2)}, u32[]{:S(2)}) collective-permute-start(f32[4,24,6,128]{3,0,2,1:T(4,128)S(1)} %get-tuple-element.804), channel_id=1, source_target_pairs={{0,4},{4,8},{8,12},{12,16},{16,20},{20,24},{24,28},{28,32},{32,36}... | collective-permute-start | bytes 884744 | tf_op jit(solution)/shard_map/ppermute | solution.py:23
  714.2 8.7 collective-permute-start.24
  716.2 8.4 collective-permute-start.25
  724.8 20.9 %collective-permute-start.26 = (f32[4,36,6,128]{3,0,2,1:T(4,128)S(1)}, f32[4,36,6,128]{3,0,2,1:T(4,128)S(1)}, u32[]{:S(2)}, u32[]{:S(2)}) collective-permute-start(f32[4,36,6,128]{3,0,2,1:T(4,128)S(1)} %get-tuple-element.791), channel_id=1, source_target_pairs={{0,4},{4,8},{8,12},{12,16},{16,20},{20,24},{24,28},{28,32},{32,36}... | collective-permute-start | bytes 1327112 | tf_op jit(solution)/shard_map/ppermute | solution.py:23
  726.7 21.2 %copy-start.7 = (f32[4,12,16,128]{3,0,2,1:T(4,128)S(1)}, f32[4,12,16,128]{3,0,2,1:T(4,128)}, u32[]{:S(2)}) copy-start(f32[4,12,16,128]{3,0,2,1:T(4,128)} %get-tuple-element.774) | copy-start | bytes 1179652
  726.7 21.2 %copy-start.16 = (f32[12,16,128]{2,1,0:T(8,128)S(1)}, f32[12,16,128]{2,1,0:T(8,128)}, u32[]{:S(2)}) copy-start(f32[12,16,128]{2,1,0:T(8,128)} %fusion.116) | copy-start | bytes 294916
  726.7 21.2 %copy-start.19 = (f32[12,16,128]{2,1,0:T(8,128)S(1)}, f32[12,16,128]{2,1,0:T(8,128)}, u32[]{:S(2)}) copy-start(f32[12,16,128]{2,1,0:T(8,128)} %copy-done.17) | copy-start | bytes 294916
  726.7 21.2 %copy-start.22 = (f32[12,16,128]{2,1,0:T(8,128)S(1)}, f32[12,16,128]{2,1,0:T(8,128)}, u32[]{:S(2)}) copy-start(f32[12,16,128]{2,1,0:T(8,128)} %get-tuple-element.827) | copy-start | bytes 294916
  726.7 21.2 %copy-start.25 = (f32[12,16,128]{2,1,0:T(8,128)S(1)}, f32[12,16,128]{2,1,0:T(8,128)}, u32[]{:S(2)}) copy-start(f32[12,16,128]{2,1,0:T(8,128)} %copy-done.23) | copy-start | bytes 294916
  726.7 21.2 %copy-start.36 = (f32[12,16,128]{2,1,0:T(8,128)S(1)}, f32[12,16,128]{2,1,0:T(8,128)}, u32[]{:S(2)}) copy-start(f32[12,16,128]{2,1,0:T(8,128)} %param.62) | copy-start | bytes 294916
  726.8 19.0 %collective-permute-start.27 = (f32[4,36,6,128]{3,0,2,1:T(4,128)S(1)}, f32[4,36,6,128]{3,0,2,1:T(4,128)S(1)}, u32[]{:S(2)}, u32[]{:S(2)}) collective-permute-start(f32[4,36,6,128]{3,0,2,1:T(4,128)S(1)} %get-tuple-element.790), channel_id=1, source_target_pairs={{4,0},{8,4},{12,8},{16,12},{20,16},{24,20},{28,24},{32,28},{36,32}... | collective-permute-start | bytes 1327112 | tf_op jit(solution)/shard_map/ppermute | solution.py:26
  (21 other events, 232.4 us)
Sparse Core Ops, SparseCore 0:
  753.2 40.2 all-gather.1
where the time goes:
time: 1190 us; the launch traced here: 1180 us
  blocking collectives  370 us (31%)
  local copies, waits for them, and re-layouts  286 us (24%)
  loops' own time  158 us (13%)
  starting transfers between devices  129 us (11%)
  waiting for transfers between devices  128 us (11%)
  other arithmetic  52.2 us (4%)
  matrix products  45.8 us (4%)
  between operations  14.7 us (1%)
    psum x1, blocking collectives, shards(): correlation = lax.psum(partial_correlation, ('gx', 'gy')) / cell_count  370 us
    dynamic_update_slice x48, local copies, waits for them, and re-layouts, add_atom(): return lax.dynamic_update_slice(accumulated, current + addition, starts)  232 us
    another operation x3, loops' own time, nonlocal_terms(): lax.fori_loop(0, projectors.shape[0], add_atom, jnp.zeros_like(padded))  158 us
    ppermute x14, starting transfers between devices, extended_2(): lax.ppermute(lax.slice_in_dim(block, 0, width, axis=dim), axis, backward)  102 us
    ppermute x14, waiting for transfers between devices, extended_2(): lax.ppermute(lax.slice_in_dim(block, block.shape[dim] - width, None, axis...  73.9 us
    all_gather x1, waiting for transfers between devices, shards(): everything = lax.all_gather(filtered, 'orb', axis=0, tiled=True)  40.4 us
    ppermute x14, starting transfers between devices, extended_2(): lax.ppermute(lax.slice_in_dim(block, block.shape[dim] - width, None, axis...  27 us
  transfers between devices with their start and end apart: 29, of which 18 were waited for; matrix products, arithmetic and copies ran while one was open for 10% of the time, Pallas kernels for 0%

commit v1 on v0

v1 whole, which is shorter than its diff:
```python
import functools

import jax
import jax.numpy as jnp
import ml_dtypes
import numpy as np
from jax import lax
from jax.experimental import pallas as pl
from jax.experimental.pallas import tpu as pltpu
from jax.sharding import PartitionSpec as P

CX, CY, NZ, ORB = 12, 16, 128, 4
HALO = 6
TILES = 96
XH = HALO * 8
YH = CX * 3
STEPS = 3

first_coefs = (6.0 / 7.0, -15.0 / 56.0, 5.0 / 63.0, -1.0 / 56.0, 2.0 / 825.0, -1.0 / 5544.0)
second_coefs = (12.0 / 7.0, -15.0 / 56.0, 10.0 / 189.0, -1.0 / 112.0, 2.0 / 1925.0, -1.0 / 16632.0)
center_coef = -5369.0 / 1800.0
filter_center = 13.5
filter_half = 10.5

F32, BF16 = jnp.float32, jnp.bfloat16
VMEM = pl.BlockSpec(memory_space=pltpu.VMEM)
SMEM = pl.BlockSpec(memory_space=pltpu.SMEM)
ANY = pl.BlockSpec(memory_space=pl.ANY)
LIMIT = 50 * 1024 * 1024


def derivative_table():
    table = np.zeros((NZ, 2 * NZ), np.float64)
    for z in range(NZ):
        table[z, NZ + z] = 3.0 * center_coef
        for k in range(1, HALO + 1):
            if z + k < NZ:
                table[z + k, z] = first_coefs[k - 1]
                table[z + k, NZ + z] = second_coefs[k - 1]
            if z - k >= 0:
                table[z - k, z] = -first_coefs[k - 1]
                table[z - k, NZ + z] = second_coefs[k - 1]
    high = table.astype(ml_dtypes.bfloat16)
    low = (table - high.astype(np.float64)).astype(ml_dtypes.bfloat16)
    return np.concatenate([high, low], axis=0)


def group_table():
    table = np.zeros((8 * 128, 128), np.float32)
    for p in range(8):
        for slot in range(16):
            for k in range(8):
                table[p * 128 + slot * 8 + k, slot * 8 + p] = 1.0
    return table.astype(ml_dtypes.bfloat16)


def split(a):
    high = a.astype(BF16)
    return high, (a - high.astype(F32)).astype(BF16)


def mm(a, b):
    return jnp.dot(a, b, preferred_element_type=F32)


def mm_t(a, b):
    return lax.dot_general(a, b, (((1,), (1,)), ((), ())), preferred_element_type=F32)


def pick(a, table):
    high, low = split(a)
    return mm(high, table) + mm(low, table)


def pick_t(a, table):
    high, low = split(a)
    return mm_t(high, table) + mm_t(low, table)


def get(ref, tile):
    return ref[pl.ds(tile * 8, 8), :]


def put(ref, tile, value):
    ref[pl.ds(tile * 8, 8), :] = value


def get_at(ref, tile):
    return ref[pl.ds(pl.multiple_of(tile * 8, 8), 8), :]


def iotas():
    return (
        lax.broadcasted_iota(jnp.int32, (8, 128), 0),
        lax.broadcasted_iota(jnp.int32, (8, 128), 1),
    )


def row(value, index):
    return jnp.broadcast_to(value[index : index + 1, :], (8, 128))


def pack_rims(y_ref, hi_ref, lo_ref, low):
    for x in range(CX):
        for m in range(3):
            put(hi_ref, x * 3 + m, jnp.where(low, pltpu.roll(get(y_ref, x * 8 + 2 + m), 4, 0), get(y_ref, x * 8 + 5 + m)))
            put(lo_ref, x * 3 + m, jnp.where(low, get(y_ref, x * 8 + m), pltpu.roll(get(y_ref, x * 8 + 3 + m), 4, 0)))


def prep_kernel(offs, strg, cnt, orb, mu, proj, y_ref, t_ref, meta_ref, xr_ref, xl_ref, yh_ref, yl_ref):
    sub, lane = iotas()
    low = sub < 4
    left_half = lane < 64
    for x in range(CX):
        for o in range(ORB):
            for h in range(2):
                y_ref[pl.ds(x * 64 + 4 * h + o, 8, stride=8), :] = orb[o, x, 8 * h : 8 * h + 8, :]
    group = lane // 8
    place = lane % 8
    meta = jnp.zeros((8, 128), F32)
    for s in range(8):
        for column in range(3):
            value = offs[s, column].astype(F32)
            meta = jnp.where((group == s) & (sub == column), value, meta)
        alive = jnp.where(s < cnt[0], 1.0, 0.0).astype(F32)
        for p in range(8):
            weight = strg[s, p] * alive * (1.0 / (512.0 * filter_half))
            meta = jnp.where((lane == s * 8 + p) & (sub == 3), weight, meta)
    del place
    meta_ref[...] = meta
    for i in range(8):
        for j in range(8):
            start = (i % 2) * 64 + j * 8
            total = jnp.zeros((8, 128), F32)
            for s in range(8):
                source = proj[s, :, 128 * (i // 2) : 128 * (i // 2) + 128]
                shift = (s * 8 - start) % 128
                moved = pltpu.roll(source, shift, 1) if shift else source
                total = jnp.where(group == s, moved, total)
            put(t_ref, i * 8 + j, total)
    for q in range(XH):
        put(xr_ref, q, get(y_ref, XH + q))
        put(xl_ref, q, get(y_ref, q))
    for x in range(HALO):
        for h in range(2):
            put(xr_ref, XH + 2 * x + h, mu[CX - HALO + x, 8 * h : 8 * h + 8, :])
            put(xl_ref, XH + 2 * x + h, mu[x, 8 * h : 8 * h + 8, :])
    base = XH + 2 * HALO
    for i in range(2):
        for j in range(8):
            for ref, first in ((xr_ref, 4), (xl_ref, 0)):
                one = get(t_ref, (first + i) * 8 + j)
                two = pltpu.roll(get(t_ref, (first + 2 + i) * 8 + j), 64, 1)
                put(ref, base + i * 8 + j, jnp.where(left_half, one, two))
    put(xr_ref, base + 16, meta)
    put(xl_ref, base + 16, meta)
    pack_rims(y_ref, yh_ref, yl_ref, low)
    for x in range(CX):
        put(yh_ref, YH + x, mu[x, 8:16, :])
        put(yl_ref, YH + x, mu[x, 0:8, :])


FIRST_X = XH + 2 * HALO + 17
FIRST_Y = YH + CX


def widen_kernel(t_ref, meta_ref, fl_ref, fr_ref, t2_ref, m_ref, hi_ref, lo_ref):
    _, lane = iotas()
    left_half = lane < 64
    base = XH + 2 * HALO
    for i in range(8):
        for j in range(8):
            if i >= 4:
                other = get(fl_ref, base + (i % 2) * 8 + j)
                other = other if i >= 6 else pltpu.roll(other, 64, 1)
            else:
                other = get(fr_ref, base + (i % 2) * 8 + j)
                other = other if i >= 2 else pltpu.roll(other, 64, 1)
            both = jnp.where(left_half, get(t_ref, i * 8 + j), other)
            put(t2_ref, i * 8 + j, both)
            if j >= 4:
                put(hi_ref, i * 4 + j - 4, both)
            else:
                put(lo_ref, i * 4 + j, both)
    meta = meta_ref[...]
    for side, ref in enumerate((fl_ref, fr_ref)):
        both = jnp.where(left_half, meta, pltpu.roll(get(ref, base + 16), 64, 1))
        put(m_ref, side, both)
        put(hi_ref, 32 + side, both)
        put(lo_ref, 32 + side, both)


def coef_kernel(mu, pot, fl_ref, fr_ref, flo_ref, fhi_ref, dz_ref, out_ref, ex, ey):
    sub, _ = iotas()
    low = sub < 4

    def two(a, ia, b, ib):
        return jnp.where(low, row(a, ia), row(b, ib))

    for x in range(CX + 2 * HALO):
        if x < HALO:
            a, b = get(fl_ref, XH + 2 * x), get(fl_ref, XH + 2 * x + 1)
        elif x < HALO + CX:
            a, b = mu[x - HALO, 0:8, :], mu[x - HALO, 8:16, :]
        else:
            a, b = get(fr_ref, XH + 2 * (x - HALO - CX)), get(fr_ref, XH + 2 * (x - HALO - CX) + 1)
        for yl in range(8):
            put(ex, x * 8 + yl, two(a, yl, b, yl))
    for x in range(CX):
        parts = [get(flo_ref, YH + x), mu[x, 0:8, :], mu[x, 8:16, :], get(fhi_ref, YH + x)]
        for n in range(20):
            y = n - HALO
            put(ey, x * 20 + n, two(parts[(y + 8) // 8], y % 8, parts[(y + 16) // 8], y % 8))
    field = ex[XH * 8 : (XH + TILES) * 8, :]
    high, rest = split(field)
    zd = mm(high, dz_ref[0:NZ, 0:NZ]) + mm(rest, dz_ref[0:NZ, 0:NZ]) + mm(high, dz_ref[NZ : 2 * NZ, 0:NZ])
    out_ref[3 * 768 : 4 * 768, :] = zd * (-0.5 / filter_half)

    def body(x, carry):
        va, vb = pot[x, 0:8, :], pot[x, 8:16, :]
        for yl in range(8):
            gx = jnp.zeros((8, 128), F32)
            gy = jnp.zeros((8, 128), F32)
            for k in range(1, HALO + 1):
                gx += first_coefs[k - 1] * (get_at(ex, (x + HALO + k) * 8 + yl) - get_at(ex, (x + HALO - k) * 8 + yl))
                gy += first_coefs[k - 1] * (
                    get_at(ey, x * 20 + HALO + yl + k) - get_at(ey, x * 20 + HALO + yl - k)
                )
            r = x * 8 + yl
            center = get_at(ex, (x + HALO) * 8 + yl)

            def store(which, value):
                out_ref[pl.ds(pl.multiple_of((which * TILES + r) * 8, 8), 8), :] = value

            store(0, (1.0 + center) * (-0.5 / filter_half))
            store(1, gx * (-0.5 / filter_half))
            store(2, gy * (-0.5 / filter_half))
            store(4, (two(va, yl, vb, yl) - filter_center) * (1.0 / filter_half))
        return carry

    lax.fori_loop(0, CX, body, 0)


def block_tiles(xt, yq):
    return [(4 * xt + a) * 8 + 4 * yq for a in range(4)]


def side_of(xt):
    return 1 if xt == 2 else 0


def partial_coeffs(y_ref, q_ref, s_ref, g_ref, z_ref, acc):
    left_half = lax.broadcasted_iota(jnp.int32, (8, 1024), 1) % 128 < 64
    own = None
    ends = {}
    rims = [None, None]
    corners = {}
    for xt in range(3):
        for yq in range(2):
            b = xt * 2 + yq
            field = jnp.concatenate([y_ref[t * 8 : t * 8 + 32, :] for t in block_tiles(xt, yq)], axis=0)
            table = s_ref[(side_of(xt) * 2 + yq) * 128 : (side_of(xt) * 2 + yq) * 128 + 128, :]
            seen = pick(field, table).reshape(16, 8, 256)
            sums = []
            for p in range(8):
                base = (b * 8 + p) * 128
                product = seen * q_ref[base : base + 128, :].reshape(16, 8, 256)
                total = jnp.sum(product, axis=0)
                sums.append(total + pltpu.roll(total, 4, 0))
            col_a = jnp.concatenate([t[:, :128] for t in sums], axis=1)
            col_b = jnp.concatenate([t[:, 128:] for t in sums], axis=1)
            own = col_a if own is None else own + col_a
            rims[yq] = col_b if rims[yq] is None else rims[yq] + col_b
            if xt != 1:
                ends[xt] = ends[xt] + col_a if xt in ends else col_a
                corners[(xt, yq)] = col_b
    for side, xt in enumerate((0, 2)):
        acc[side * 24 : side * 24 + 8, :] = jnp.where(left_half, own, ends[xt])
        for yq in range(2):
            at = side * 24 + 8 + yq * 8
            acc[at : at + 8, :] = jnp.where(left_half, rims[yq], corners[(xt, yq)])
    z_ref[...] = pick(acc[...], g_ref[...])


def send_coeffs(z_ref, xr_ref, xl_ref, base):
    for t in range(3):
        put(xr_ref, base + t, pltpu.roll(get(z_ref, 3 + t), 64, 1))
        put(xl_ref, base + t, pltpu.roll(get(z_ref, t), 64, 1))


def build_kernel(t2_ref, m_ref, lo_ref, hi_ref, y_ref, g_ref, q_ref, s_ref, w_ref, z_ref, xr_ref, xl_ref, tx, acc):
    sub, lane = iotas()
    low = sub < 4
    right_half = lane >= 64
    metas = [get(m_ref, 0), get(lo_ref, 32), get(hi_ref, 32), get(m_ref, 1), get(lo_ref, 33), get(hi_ref, 33)]
    for t in range(6):
        put(w_ref, t, row(metas[t], 3))
    zi = lax.broadcasted_iota(jnp.int32, (128, 128), 0)
    for side in range(2):
        for yq in range(2):
            for col, t in enumerate((side * 3, side * 3 + 1 + yq)):
                place = metas[t][2:3, :].astype(jnp.int32) + lane[0:1, :] % 8
                base = (side * 2 + yq) * 128
                hot = jnp.where(zi == jnp.broadcast_to(place, (128, 128)), 1.0, 0.0).astype(BF16)
                s_ref[base : base + 128, col * 128 : col * 128 + 128] = hot

    def table(col, i, j):
        if col == 0:
            return get(t2_ref, i * 8 + j)
        return get(lo_ref, i * 4 + j - 4) if j >= 4 else get(hi_ref, i * 4 + j)

    zero = jnp.zeros((8, 128), F32)
    for xt in range(3):
        shift = (-12.0, 1000.0, 12.0)[xt]
        for col in range(2):
            for yq in range(2):
                b = xt * 2 + yq
                t = side_of(xt) * 3 + (0 if col == 0 else 1 + yq)
                x0 = row(metas[t], 0) - 6.0 + jnp.where(right_half, shift, 0.0)
                y0 = row(metas[t], 1) - 6.0
                if col == 1:
                    y0 = y0 + (16.0 if yq == 1 else -16.0)
                js = range(8) if col == 0 else (range(0, 4) if yq == 1 else range(4, 8))
                if col == 1 or yq == 0:
                    for a in range(4):
                        for j in js:
                            moved = zero
                            for i in range(8):
                                moved = jnp.where(x0 == float(4 * xt + a - i), table(col, i, j), moved)
                            put(tx, a * 8 + j, moved)
                for a in range(4):
                    for c in range(4):
                        rows = []
                        for h in range(2):
                            y = 8 * h + 4 * yq + c
                            moved = zero
                            if col == 0 or h == yq:
                                for j in js:
                                    moved = jnp.where(y0 == float(y - j), get(tx, a * 8 + j), moved)
                            rows.append(moved)
                        for p in range(8):
                            base = ((b * 8 + p) * 16 + a * 4 + c) * 8
                            value = jnp.where(low, row(rows[0], p), row(rows[1], p))
                            q_ref[base : base + 8, col * 128 : col * 128 + 128] = value
    partial_coeffs(y_ref, q_ref, s_ref, g_ref, z_ref, acc)
    send_coeffs(z_ref, xr_ref, xl_ref, 0)


def fold_kernel(z_ref, fl_ref, fr_ref, out_ref, hi_ref, lo_ref):
    _, lane = iotas()
    left_half = lane < 64
    tiles = []
    for side in range(2):
        near, far = (fl_ref, fr_ref) if side == 0 else (fr_ref, fl_ref)
        for t in range(3):
            tiles.append(get(z_ref, side * 3 + t) + get(near, t) + jnp.where(left_half, get(far, t), 0.0))
    for t in range(6):
        put(out_ref, t, tiles[t])
    for side in range(2):
        put(hi_ref, side * 2, tiles[side * 3 + 2])
        put(hi_ref, side * 2 + 1, tiles[side * 3])
        put(lo_ref, side * 2, tiles[side * 3 + 1])
        put(lo_ref, side * 2 + 1, tiles[side * 3])


def step_kernel(
    step, y_ref, prev_ref, fl_ref, fr_ref, plo_ref, phi_ref, coef_ref, q_hbm, s_ref, w_ref, z_ref, clo_ref, chi_ref,
    dz_ref, g_ref, *rest
):
    last = step == STEPS
    if last:
        new_ref, q_ref, ex, ey, zd, acc, wp, sem = rest
    else:
        new_ref, xr_ref, xl_ref, yh_ref, yl_ref, zn_ref, q_ref, ex, ey, zd, acc, wp, sem = rest
    copy = pltpu.make_async_copy(q_hbm, q_ref, sem)
    copy.start()
    sub, _ = iotas()
    low = sub < 4
    scale = 1.0 if step == 1 else 2.0

    high, rest_part = split(y_ref[...])
    zd[...] = mm(high, dz_ref[0:NZ, :]) + mm(rest_part, dz_ref[0:NZ, :]) + mm(high, dz_ref[NZ : 2 * NZ, :])

    ex[0 : XH * 8, :] = fl_ref[0 : XH * 8, :]
    ex[XH * 8 : (XH + TILES) * 8, :] = y_ref[...]
    ex[(XH + TILES) * 8 : (2 * XH + TILES) * 8, :] = fr_ref[0 : XH * 8, :]
    for x in range(CX):
        for yl in range(8):
            put(ey, x * 20 + HALO + yl, get(y_ref, x * 8 + yl))
        for m in range(HALO):
            rim = get(plo_ref, x * 3 + m) if m < 3 else pltpu.roll(get(plo_ref, x * 3 + m - 3), 4, 0)
            put(ey, x * 20 + m, jnp.where(low, rim, pltpu.roll(get(y_ref, x * 8 + 2 + m), 4, 0)))
            rim = pltpu.roll(get(phi_ref, x * 3 + m), 4, 0) if m < 3 else get(phi_ref, x * 3 + m - 3)
            put(ey, x * 20 + HALO + 8 + m, jnp.where(low, pltpu.roll(get(y_ref, x * 8 + m), 4, 0), rim))

    def body(x, carry):
        for yl in range(8):
            r = x * 8 + yl
            center = get_at(y_ref, r)
            gx = gy = lap = None
            for k in range(1, HALO + 1):
                xp, xm = get_at(ex, (x + HALO + k) * 8 + yl), get_at(ex, (x + HALO - k) * 8 + yl)
                yp, ym = get_at(ey, x * 20 + HALO + yl + k), get_at(ey, x * 20 + HALO + yl - k)
                tx = first_coefs[k - 1] * (xp - xm)
                ty = first_coefs[k - 1] * (yp - ym)
                tl = second_coefs[k - 1] * ((xp + xm) + (yp + ym))
                gx, gy, lap = (tx, ty, tl) if k == 1 else (gx + tx, gy + ty, lap + tl)
            at = pl.ds(pl.multiple_of(r * 8, 8), 8)
            total = get_at(coef_ref, r) * (lap + zd[at, NZ:])
            total += get_at(coef_ref, TILES + r) * gx
            total += get_at(coef_ref, 2 * TILES + r) * gy
            total += get_at(coef_ref, 3 * TILES + r) * zd[at, :NZ]
            total += get_at(coef_ref, 4 * TILES + r) * center
            new_ref[at, :] = total if step == 1 else 2.0 * total - get_at(prev_ref, r)
        return carry

    lax.fori_loop(0, CX, body, 0)

    tiles = []
    for side in range(2):
        own, lo, hi = (get(z_ref, side * 3 + t) for t in range(3))
        tiles.append(own + get(clo_ref, side * 2) + get(chi_ref, side * 2))
        tiles.append(lo + get(clo_ref, side * 2 + 1))
        tiles.append(hi + get(chi_ref, side * 2 + 1))
    weights = jnp.concatenate(tiles, axis=0) * w_ref[...] * scale
    wp[...] = pick_t(weights, g_ref[...])

    copy.wait()
    for xt in range(3):
        for yq in range(2):
            b = xt * 2 + yq
            ta, tb = side_of(xt) * 3, side_of(xt) * 3 + 1 + yq
            total = None
            for p in range(8):
                weight = jnp.concatenate(
                    [wp[t * 8 : t * 8 + 8, p * 128 : p * 128 + 128] for t in (ta, tb)], axis=1
                )
                base = (b * 8 + p) * 128
                term = weight[None] * q_ref[base : base + 128, :].reshape(16, 8, 256)
                total = term if total is None else total + term
            table = s_ref[(side_of(xt) * 2 + yq) * 128 : (side_of(xt) * 2 + yq) * 128 + 128, :]
            spread = pick_t(total.reshape(128, 256), table)
            for a, t in enumerate(block_tiles(xt, yq)):
                new_ref[t * 8 : t * 8 + 32, :] += spread[a * 32 : a * 32 + 32, :]

    if not last:
        for q in range(XH):
            put(xr_ref, q, get(new_ref, XH + q))
            put(xl_ref, q, get(new_ref, q))
        pack_rims(new_ref, yh_ref, yl_ref, low)
        partial_coeffs(new_ref, q_ref, s_ref, g_ref, zn_ref, acc)
        send_coeffs(zn_ref, xr_ref, xl_ref, XH)


def gram_kernel(order, a0, a1, a2, a3, out_ref, held):
    for n, ref in enumerate((a0, a1, a2, a3)):
        held[order[n]] = ref[...]

    def body(x, total):
        at = pl.ds(pl.multiple_of(x * 64, 64), 64)
        field = jnp.concatenate([held[d, at, :] for d in range(4)], axis=0)
        high, low = split(field)
        return total + (mm_t(high, high) + mm_t(high, low) + mm_t(low, high))

    total = lax.fori_loop(0, CX, body, jnp.zeros((256, 256), F32))
    rows = lax.broadcasted_iota(jnp.int32, (256, 256), 0)
    columns = lax.broadcasted_iota(jnp.int32, (256, 256), 1)
    total = jnp.where((rows % 64) // 4 == (columns % 64) // 4, total, 0.0)
    orbital = lax.broadcasted_iota(jnp.int32, (16, 256), 0)
    held_at = lax.broadcasted_iota(jnp.int32, (16, 256), 1)
    hot = jnp.where(orbital == held_at // 64 * 4 + held_at % 4, 1.0, 0.0).astype(F32)
    first = jnp.dot(hot, total, precision=lax.Precision.HIGHEST, preferred_element_type=F32)
    small = lax.dot_general(
        first, hot, (((1,), (1,)), ((), ())), precision=lax.Precision.HIGHEST, preferred_element_type=F32
    )
    out_ref[...] = jnp.zeros((16, 128), F32)
    out_ref[:, 0:16] = small


def rotate_kernel(cells, order, corr_ref, a0, a1, a2, a3, out_ref, flat):
    lane = lax.broadcasted_iota(jnp.int32, (16, 128), 1)
    rows = lax.broadcasted_iota(jnp.int32, (16, 128), 0)
    work = jnp.where(lane < 16, corr_ref[...] * (1.0 / cells), jnp.where(lane == rows + 16, 1.0, 0.0))
    pivots = jnp.ones((16, 128), F32)
    for k in range(16):
        pivot_row = jnp.broadcast_to(work[k : k + 1, :], (16, 128))
        pivot = jnp.broadcast_to(pivot_row[:, k : k + 1], (16, 128))
        column = jnp.broadcast_to(work[:, k : k + 1], (16, 128))
        pivots = jnp.where(rows == k, pivot, pivots)
        work = jnp.where(rows > k, work - column / pivot * pivot_row, work)
    inverse = (work / jnp.sqrt(pivots))[:, 16:32]
    me = order[0]
    own_row = lax.broadcasted_iota(jnp.int32, (64, 16), 0)
    orbital = lax.broadcasted_iota(jnp.int32, (64, 16), 1)
    left = jnp.where(orbital == me * 4 + own_row % 4, 1.0, 0.0).astype(F32)
    orbital = lax.broadcasted_iota(jnp.int32, (16, 256), 0)
    held_at = lax.broadcasted_iota(jnp.int32, (16, 256), 1)
    device = held_at // 64
    owner = jnp.where(device == 0, order[0], jnp.where(device == 1, order[1], jnp.where(device == 2, order[2], order[3])))
    right = jnp.where(orbital == owner * 4 + held_at % 4, 1.0, 0.0).astype(F32)
    exact = functools.partial(jnp.dot, precision=lax.Precision.HIGHEST, preferred_element_type=F32)
    mixing = exact(exact(left, inverse), right)
    at_row = lax.broadcasted_iota(jnp.int32, (64, 256), 0)
    at_column = lax.broadcasted_iota(jnp.int32, (64, 256), 1)
    mixing = jnp.where(at_row // 4 == at_column % 64 // 4, mixing, 0.0)
    mix_high, mix_low = split(mixing)
    for x in range(CX):
        field = jnp.concatenate([ref[x * 64 : x * 64 + 64, :] for ref in (a0, a1, a2, a3)], axis=0)
        high, low = split(field)
        flat[x * 64 : x * 64 + 64, :] = mm(mix_high, high) + mm(mix_high, low) + mm(mix_low, high)
    for o in range(ORB):
        for x in range(CX):
            for h in range(2):
                out_ref[o, x, 8 * h : 8 * h + 8, :] = flat[pl.ds(x * 64 + 4 * h + o, 8, stride=8), :]


def kernel_call(body, outs, ins, scratch=(), name=None):
    return pl.pallas_call(
        body,
        out_shape=[jax.ShapeDtypeStruct(shape, dtype) for shape, dtype in outs],
        in_specs=ins,
        out_specs=[VMEM] * len(outs),
        scratch_shapes=list(scratch),
        compiler_params=pltpu.CompilerParams(vmem_limit_bytes=LIMIT),
        name=name,
    )


def blocks(count, columns=128, dtype=F32):
    return (count * 8, columns), dtype


def beside(low_value, high_value, axis):
    count = lax.axis_size(axis)
    up = [(i, i + 1) for i in range(count - 1)]
    down = [(i + 1, i) for i in range(count - 1)]
    return lax.ppermute(low_value, axis, up), lax.ppermute(high_value, axis, down)


def fold(z, from_left, from_right, tile):
    block = pl.BlockSpec((24, 128), lambda i: (tile // 3, 0))
    whole = lambda rows: pl.BlockSpec((rows, 128), lambda i: (0, 0))
    return pl.pallas_call(
        fold_kernel,
        grid=(1,),
        out_shape=[jax.ShapeDtypeStruct((rows, 128), F32) for rows in (48, 32, 32)],
        in_specs=[whole(48), block, block],
        out_specs=[whole(48), whole(32), whole(32)],
        name="fold_coeffs",
    )(z, from_left, from_right)


def shards(orbitals, potential, kinetic_mu, projectors, strengths, box_offsets, block_counts):
    dz = jnp.asarray(derivative_table())
    groups = jnp.asarray(group_table())
    y, t, meta, xr, xl, yh, yl = kernel_call(
        prep_kernel,
        [blocks(TILES), blocks(64), blocks(1), blocks(FIRST_X), blocks(FIRST_X), blocks(FIRST_Y), blocks(FIRST_Y)],
        [SMEM, SMEM, SMEM, VMEM, VMEM, VMEM],
        name="prepare",
    )(box_offsets, strengths, block_counts, orbitals, kinetic_mu, projectors)
    from_left, from_right = beside(xr, xl, "gx")
    from_lo, from_hi = beside(yh, yl, "gy")
    t2, metas, hi2, lo2 = kernel_call(
        widen_kernel, [blocks(64), blocks(2), blocks(34), blocks(34)], [VMEM] * 4, name="widen"
    )(t, meta, from_left, from_right)
    from_lo2, from_hi2 = beside(hi2, lo2, "gy")
    (coefs,) = kernel_call(
        coef_kernel,
        [blocks(5 * TILES)],
        [VMEM] * 7,
        [pltpu.VMEM(((TILES + 2 * XH) * 8, 128), F32), pltpu.VMEM((CX * 20 * 8, 128), F32)],
        name="coefficients",
    )(kinetic_mu, potential, from_left, from_right, from_lo, from_hi, dz)
    q, s, w, z, zr, zl = kernel_call(
        build_kernel,
        [
            blocks(6 * 8 * 16, 256),
            ((4 * 128, 256), BF16),
            blocks(6),
            blocks(6),
            blocks(3),
            blocks(3),
        ],
        [VMEM] * 6,
        [pltpu.VMEM((32 * 8, 128), F32), pltpu.VMEM((48, 1024), F32)],
        name="build",
    )(t2, metas, from_lo2, from_hi2, y, groups)
    z_left, z_right = beside(zr, zl, "gx")
    z, z_hi, z_lo = fold(z, z_left, z_right, 0)
    c_lo, c_hi = beside(z_hi, z_lo, "gy")

    previous = y
    for step in range(1, STEPS + 1):
        last = step == STEPS
        outs = [blocks(TILES)]
        if not last:
            outs += [blocks(XH + 3), blocks(XH + 3), blocks(YH), blocks(YH), blocks(6)]
        result = kernel_call(
            functools.partial(step_kernel, step),
            outs,
            [VMEM] * 7 + [ANY] + [VMEM] * 7,
            [
                pltpu.VMEM((6 * 8 * 16 * 8, 256), F32),
                pltpu.VMEM(((TILES + 2 * XH) * 8, 128), F32),
                pltpu.VMEM((CX * 20 * 8, 128), F32),
                pltpu.VMEM((TILES * 8, 256), F32),
                pltpu.VMEM((48, 1024), F32),
                pltpu.VMEM((48, 1024), F32),
                pltpu.SemaphoreType.DMA,
            ],
            name="step",
        )(y, previous, from_left, from_right, from_lo, from_hi, coefs, q, s, w, z, c_lo, c_hi, dz, groups)
        previous = y
        if last:
            (y,) = result
        else:
            y, xr, xl, yh, yl, z = result
            from_left, from_right = beside(xr, xl, "gx")
            from_lo, from_hi = beside(yh, yl, "gy")
            z, z_hi, z_lo = fold(z, from_left, from_right, XH)
            c_lo, c_hi = beside(z_hi, z_lo, "gy")

    count = lax.axis_size("orb")
    me = lax.axis_index("orb")
    up = [(i, (i + 1) % count) for i in range(count)]
    down = [(i, (i - 1) % count) for i in range(count)]
    below = lax.ppermute(y, "orb", up)
    above = lax.ppermute(y, "orb", down)
    half = TILES * 4
    across_a = lax.ppermute(below[:half], "orb", up)
    across_b = lax.ppermute(above[half:], "orb", down)
    across = jnp.concatenate([across_a, across_b], axis=0)
    order = jnp.stack([me, (me + count - 1) % count, (me + 1) % count, (me + 2) % count]).astype(jnp.int32)
    (corr,) = kernel_call(
        gram_kernel,
        [((16, 128), F32)],
        [SMEM] + [VMEM] * 4,
        [pltpu.VMEM((4, TILES * 8, 128), F32)],
        name="gram",
    )(order, y, below, above, across)
    for axis in ("gx", "gy"):
        size = lax.axis_size(axis)
        stride = 1
        while stride < size:
            corr = corr + lax.ppermute(corr, axis, [(i, i ^ stride) for i in range(size)])
            stride *= 2
    cells = CX * CY * NZ * lax.axis_size("gx") * lax.axis_size("gy")
    (result,) = kernel_call(
        functools.partial(rotate_kernel, cells),
        [((ORB, CX, CY, NZ), F32)],
        [SMEM] + [VMEM] * 5,
        [pltpu.VMEM((TILES * 8, 128), F32)],
        name="rotate",
    )(order, corr, y, below, above, across)
    return result


def solution(mesh):
    in_specs = (
        P("orb", "gx", "gy", None),
        P("gx", "gy", None),
        P("gx", "gy", None),
        P(("gx", "gy"), None, None),
        P(("gx", "gy"), None),
        P(("gx", "gy"), None),
        P(("gx", "gy")),
    )
    out_specs = P("orb", "gx", "gy", None)
    return jax.shard_map(shards, mesh=mesh, in_specs=in_specs, out_specs=out_specs, check_vma=False)
```

time: 1190 us -> 253 us (0.21)
  the two profiles are of different devices: /device:TPU:448 before, /device:TPU:62 now
where the time goes in v1:
time: 253 us; the launch traced here: 251 us
  starting transfers between devices  110 us (43%)
  waiting for transfers between devices  82.2 us (32%)
  Pallas kernels  37.4 us (15%)
  local copies, waits for them, and re-layouts  20 us (8%)
    ppermute x11, starting transfers between devices, beside(): lax.ppermute(low_value, axis, up)  56.9 us
    ppermute x11, waiting for transfers between devices, beside(): lax.ppermute(high_value, axis, down)  37.8 us
    ppermute x7, waiting for transfers between devices, shards(): lax.ppermute(corr, axis, [(i, i ^ stride) for i in range(size)])  28.5 us
    ppermute x11, starting transfers between devices, beside(): lax.ppermute(high_value, axis, down)  22.6 us
    unnamed x58, local copies, waits for them, and re-layouts  19.9 us
    ppermute x7, starting transfers between devices, shards(): lax.ppermute(corr, axis, [(i, i ^ stride) for i in range(size)])  19 us
    pallas_call x3, Pallas kernels, shards(): kernel_call(functools.partial(step_kernel, step), outs, [VMEM] * 7 + [ANY...  17.5 us
    ppermute x1, waiting for transfers between devices, shards(): below = lax.ppermute(y, 'orb', up)  6.17 us
  transfers between devices with their start and end apart: 33, of which 18 were waited for; matrix products, arithmetic and copies ran while one was open for 0% of the time, Pallas kernels for 4%

profile of v1, /device:TPU:62, one launch (start us, length us, event | category | flops | bytes accessed | tf_op | source)
XLA Modules:
  0.0 250.9 jit_solution(5638444742684168849)
XLA Ops:
  6.3 1.8 collective-permute-start
  9.3 10.1 %collective-permute-start.2 = (f32[384,128]{1,0:T(8,128)S(1)}, f32[384,128]{1,0:T(8,128)S(1)}, u32[]{:S(2)}, u32[]{:S(2)}) collective-permute-start(f32[384,128]{1,0:T(8,128)S(1)} %get-tuple-element.46), channel_id=1, source_target_pairs={{0,4},{4,8},{8,12},{12,16},{16,20},{20,24},{24,28},{28,32},{32,36}... | collective-permute-start | bytes 589832 | tf_op jit(solution)/shard_map/ppermute | solution.py:537
  19.5 1.9 collective-permute-start.3
  21.5 9.9 %collective-permute-start.4 = (f32[272,128]{1,0:T(8,128)S(1)}, f32[272,128]{1,0:T(8,128)S(1)}, u32[]{:S(2)}, u32[]{:S(2)}) collective-permute-start(f32[272,128]{1,0:T(8,128)S(1)} %get-tuple-element.52), channel_id=1, source_target_pairs={{0,4},{4,8},{8,12},{12,16},{16,20},{20,24},{24,28},{28,32},{32,36}... | collective-permute-start | bytes 417800 | tf_op jit(solution)/shard_map/ppermute | solution.py:537
  31.5 1.9 collective-permute-start.5
  34.7 12.7 %collective-permute-done.5.hi_ref = f32[272,128]{1,0:T(8,128)S(1)} collective-permute-done((f32[272,128]{1,0:T(8,128)S(1)}, f32[272,128]{1,0:T(8,128)S(1)}, u32[]{:S(2)}, u32[]{:S(2)}) %collective-permute-start.5) | collective-permute-done | bytes 139296 | tf_op jit(solution)/shard_map/ppermute | solution.py:537
  48.4 4.8 %build.1 = (f32[6144,256]{1,0:T(8,128)}, bf16[512,256]{1,0:T(8,128)(2,1)S(1)}, f32[48,128]{1,0:T(8,128)S(1)}, f32[48,128]{1,0:T(8,128)S(1)}, f32[24,128]{1,0:T(8,128)S(1)}, /*index=5*/f32[24,128]{1,0:T(8,128)S(1)}) custom-call(f32[512,128]{1,0:T(8,128)S(1)} %get-tuple-element.50.t2_ref, f32[16,128]{1,0:T(8,128)S(1)} %get-tuple-element.51.m_ref, ...), custom_call_target="tpu_custom_call" | custom-call | tf_op jit(solution)/shard_map/build/pallas_call | solution.py:575
  53.8 3.0 %collective-permute-start.6 = (f32[24,128]{1,0:T(8,128)S(1)}, f32[24,128]{1,0:T(8,128)S(1)}, u32[]{:S(2)}, u32[]{:S(2)}) collective-permute-start(f32[24,128]{1,0:T(8,128)S(1)} %get-tuple-element.58), channel_id=1, source_target_pairs={{0,64},{64,128},{128,192},{192,256},{256,320},{320,384},{384,448},... | collective-permute-start | bytes 36872 | tf_op jit(solution)/shard_map/ppermute | solution.py:537
  58.1 2.3 collective-permute-done.7.fr_ref
  62.4 1.9 collective-permute-start.8
  64.3 3.9 %collective-permute-start.9 = (f32[32,128]{1,0:T(8,128)}, f32[32,128]{1,0:T(8,128)S(1)}, u32[]{:S(2)}, u32[]{:S(2)}) collective-permute-start(f32[32,128]{1,0:T(8,128)} %get-tuple-element.62), channel_id=1, source_target_pairs={{4,0},{8,4},{12,8},{16,12},{20,16},{24,20},{28,24},{32,28},{36,32}... | collective-permute-start | bytes 49160 | tf_op jit(solution)/shard_map/ppermute | solution.py:537
  73.3 2.9 %collective-permute-done.9.chi_ref = f32[32,128]{1,0:T(8,128)S(1)} collective-permute-done((f32[32,128]{1,0:T(8,128)}, f32[32,128]{1,0:T(8,128)S(1)}, u32[]{:S(2)}, u32[]{:S(2)}) %collective-permute-start.9) | collective-permute-done | bytes 16416 | tf_op jit(solution)/shard_map/ppermute | solution.py:537
  77.9 6.1 %step.3 = (f32[768,128]{1,0:T(8,128)S(1)}, f32[408,128]{1,0:T(8,128)S(1)}, f32[408,128]{1,0:T(8,128)S(1)}, f32[288,128]{1,0:T(8,128)S(1)}, f32[288,128]{1,0:T(8,128)S(1)}, /*index=5*/f32[48,128]{1,0:T(8,128)S(1)}) custom-call(f32[768,128]{1,0:T(8,128)S(1)} %get-tuple-element.43.y_ref.prev_ref, f32[768,128]{1,0:T(8,128)S(1)} %get-tuple-element.43.y_ref.prev_ref, ...), custom_call_target="tpu_custom_call" | custom-call | tf_op jit(solution)/shard_map/step/pallas_call | solution.py:599
  84.6 3.2 %collective-permute-start.10 = (f32[408,128]{1,0:T(8,128)S(1)}, f32[408,128]{1,0:T(8,128)S(1)}, u32[]{:S(2)}, u32[]{:S(2)}) collective-permute-start(f32[408,128]{1,0:T(8,128)S(1)} %get-tuple-element.64), channel_id=1, source_target_pairs={{0,64},{64,128},{128,192},{192,256},{256,320},{320,384},{384,448},... | collective-permute-start | bytes 626696 | tf_op jit(solution)/shard_map/ppermute | solution.py:537
  89.1 5.9 %collective-permute-start.12 = (f32[288,128]{1,0:T(8,128)S(1)}, f32[288,128]{1,0:T(8,128)S(1)}, u32[]{:S(2)}, u32[]{:S(2)}) collective-permute-start(f32[288,128]{1,0:T(8,128)S(1)} %get-tuple-element.66), channel_id=1, source_target_pairs={{0,4},{4,8},{8,12},{12,16},{16,20},{20,24},{24,28},{28,32},{32,36}... | collective-permute-start | bytes 442376 | tf_op jit(solution)/shard_map/ppermute | solution.py:537
  95.0 1.9 collective-permute-start.13
  99.1 9.9 %collective-permute-start.14 = (f32[32,128]{1,0:T(8,128)}, f32[32,128]{1,0:T(8,128)S(1)}, u32[]{:S(2)}, u32[]{:S(2)}) collective-permute-start(f32[32,128]{1,0:T(8,128)} %get-tuple-element.70), channel_id=1, source_target_pairs={{0,4},{4,8},{8,12},{12,16},{16,20},{20,24},{24,28},{28,32},{32,36}... | collective-permute-start | bytes 49160 | tf_op jit(solution)/shard_map/ppermute | solution.py:537
  109.0 1.9 collective-permute-start.15
  112.6 8.3 %collective-permute-done.15.chi_ref = f32[32,128]{1,0:T(8,128)S(1)} collective-permute-done((f32[32,128]{1,0:T(8,128)}, f32[32,128]{1,0:T(8,128)S(1)}, u32[]{:S(2)}, u32[]{:S(2)}) %collective-permute-start.15) | collective-permute-done | bytes 16416 | tf_op jit(solution)/shard_map/ppermute | solution.py:537
  123.5 6.1 %step.4 = (f32[768,128]{1,0:T(8,128)S(1)}, f32[408,128]{1,0:T(8,128)S(1)}, f32[408,128]{1,0:T(8,128)S(1)}, f32[288,128]{1,0:T(8,128)S(1)}, f32[288,128]{1,0:T(8,128)S(1)}, /*index=5*/f32[48,128]{1,0:T(8,128)S(1)}) custom-call(f32[768,128]{1,0:T(8,128)S(1)} %get-tuple-element.63.y_ref.prev_ref, f32[768,128]{1,0:T(8,128)S(1)} %get-tuple-element.43.y_ref.prev_ref, ...), custom_call_target="tpu_custom_call" | custom-call | tf_op jit(solution)/shard_map/step/pallas_call | solution.py:599
  132.8 1.9 collective-permute-start.18
  134.7 3.9 %collective-permute-start.19 = (f32[288,128]{1,0:T(8,128)S(1)}, f32[288,128]{1,0:T(8,128)S(1)}, u32[]{:S(2)}, u32[]{:S(2)}) collective-permute-start(f32[288,128]{1,0:T(8,128)S(1)} %get-tuple-element.76), channel_id=1, source_target_pairs={{4,0},{8,4},{12,8},{16,12},{20,16},{24,20},{28,24},{32,28},{36,32}... | collective-permute-start | bytes 442376 | tf_op jit(solution)/shard_map/ppermute | solution.py:537
  140.8 7.9 %collective-permute-start.20 = (f32[32,128]{1,0:T(8,128)}, f32[32,128]{1,0:T(8,128)S(1)}, u32[]{:S(2)}, u32[]{:S(2)}) collective-permute-start(f32[32,128]{1,0:T(8,128)} %get-tuple-element.79), channel_id=1, source_target_pairs={{0,4},{4,8},{8,12},{12,16},{16,20},{20,24},{24,28},{28,32},{32,36}... | collective-permute-start | bytes 49160 | tf_op jit(solution)/shard_map/ppermute | solution.py:537
  148.7 1.9 collective-permute-start.21
  150.7 9.9 %collective-permute-done.21.chi_ref = f32[32,128]{1,0:T(8,128)S(1)} collective-permute-done((f32[32,128]{1,0:T(8,128)}, f32[32,128]{1,0:T(8,128)S(1)}, u32[]{:S(2)}, u32[]{:S(2)}) %collective-permute-start.21) | collective-permute-done | bytes 16416 | tf_op jit(solution)/shard_map/ppermute | solution.py:537
  163.2 5.3 %step.5.a0 = f32[768,128]{1,0:T(8,128)S(1)} custom-call(f32[768,128]{1,0:T(8,128)S(1)} %get-tuple-element.72.y_ref, f32[768,128]{1,0:T(8,128)S(1)} %get-tuple-element.63.y_ref.prev_ref, f32[408,128]{1,0:T(8,128)S(1)} %copy-done.7, f32[408,128]{1,0:T(8,128)S(1)} %copy-done.11, f32[288,128]{1,0:T(8,128)S(1)} %collective-permute-done.18.plo_ref, ...), custom_call_target="tpu_custom_call" | custom-call | tf_op jit(solution)/shard_map/step/pallas_call | solution.py:599
  168.5 2.4 collective-permute-start.22
  170.9 3.5 %collective-permute-start.23 = (f32[768,128]{1,0:T(8,128)S(1)}, f32[768,128]{1,0:T(8,128)S(1)}, u32[]{:S(2)}, u32[]{:S(2)}) collective-permute-start(f32[768,128]{1,0:T(8,128)S(1)} %step.5.a0), channel_id=1, source_target_pairs={{0,3},{1,0},{2,1},{3,2},{4,7},{5,4},{6,5},{7,6},{8,11},{9,8},{10,9... | collective-permute-start | bytes 1179656 | tf_op jit(solution)/shard_map/ppermute | solution.py:629
  174.4 6.2 %collective-permute-done.22.a1 = f32[768,128]{1,0:T(8,128)S(1)} collective-permute-done((f32[768,128]{1,0:T(8,128)S(1)}, f32[768,128]{1,0:T(8,128)S(1)}, u32[]{:S(2)}, u32[]{:S(2)}) %collective-permute-start.22) | collective-permute-done | bytes 393248 | tf_op jit(solution)/shard_map/ppermute | solution.py:628
  180.6 3.6 %collective-permute-start.24 = (f32[384,128]{1,0:T(8,128)S(1)}, f32[384,128]{1,0:T(8,128)S(1)}, u32[]{:S(2)}, u32[]{:S(2)}) collective-permute-start(f32[384,128]{1,0:T(8,128)S(1)} %slice.8), channel_id=1, source_target_pairs={{0,1},{1,2},{2,3},{3,0},{4,5},{5,6},{6,7},{7,4},{8,9},{9,10},{10,1... | collective-permute-start | bytes 589832 | tf_op jit(solution)/shard_map/ppermute | solution.py:631
  184.5 2.2 collective-permute-start.25
  186.8 2.4 collective-permute-done.24
  189.3 5.7 %collective-permute-done.25 = f32[384,128]{1,0:T(8,128)S(1)} collective-permute-done((f32[384,128]{1,0:T(8,128)S(1)}, f32[384,128]{1,0:T(8,128)S(1)}, u32[]{:S(2)}, u32[]{:S(2)}) %collective-permute-start.25) | collective-permute-done | bytes 196640 | tf_op jit(solution)/shard_map/ppermute | solution.py:632
  195.0 4.3 %gram.1 = f32[16,128]{1,0:T(8,128)S(1)} custom-call(s32[4]{0:T(128)S(1)} %pad_add_fusion.order, f32[768,128]{1,0:T(8,128)S(1)} %step.5.a0, f32[768,128]{1,0:T(8,128)S(1)} %collective-permute-done.22.a1, f32[768,128]{1,0:T(8,128)S(1)} %collective-permute-done.23.a2, f32[768,128]{1,0:T(8,128)S(1)} %constant_dynamic-update-slice_fusion.a3), custom_call_target="tpu_custom_call" | custom-call | tf_op jit(solution)/shard_map/gram/pallas_call | solution.py:635
  199.4 2.1 collective-permute-start.26
  202.4 5.5 %collective-permute-start.27 = (f32[16,128]{1,0:T(8,128)S(1)}, f32[16,128]{1,0:T(8,128)S(1)}, u32[]{:S(2)}, u32[]{:S(2)}) collective-permute-start(f32[16,128]{1,0:T(8,128)S(1)} %add.46), channel_id=1, source_target_pairs={{0,128},{64,192},{128,0},{192,64},{256,384},{320,448},{384,256},{4... | collective-permute-start | bytes 24584 | tf_op jit(solution)/shard_map/ppermute | solution.py:646
  208.0 1.6 collective-permute-done.27
  209.6 3.7 %collective-permute-start.28 = (f32[16,128]{1,0:T(8,128)S(1)}, f32[16,128]{1,0:T(8,128)S(1)}, u32[]{:S(2)}, u32[]{:S(2)}) collective-permute-start(f32[16,128]{1,0:T(8,128)S(1)} %add.47), channel_id=1, source_target_pairs={{0,256},{64,320},{128,384},{192,448},{256,0},{320,64},{384,128},{4... | collective-permute-start | bytes 24584 | tf_op jit(solution)/shard_map/ppermute | solution.py:646
  213.3 2.7 %collective-permute-done.28 = f32[16,128]{1,0:T(8,128)S(1)} collective-permute-done((f32[16,128]{1,0:T(8,128)S(1)}, f32[16,128]{1,0:T(8,128)S(1)}, u32[]{:S(2)}, u32[]{:S(2)}) %collective-permute-start.28) | collective-permute-done | bytes 8224 | tf_op jit(solution)/shard_map/ppermute | solution.py:646
  216.0 1.9 collective-permute-start.29
  217.9 3.6 %collective-permute-done.29 = f32[16,128]{1,0:T(8,128)S(1)} collective-permute-done((f32[16,128]{1,0:T(8,128)S(1)}, f32[16,128]{1,0:T(8,128)S(1)}, u32[]{:S(2)}, u32[]{:S(2)}) %collective-permute-start.29) | collective-permute-done | bytes 8224 | tf_op jit(solution)/shard_map/ppermute | solution.py:646
  221.5 1.9 collective-permute-start.30
  223.5 4.5 %collective-permute-done.30 = f32[16,128]{1,0:T(8,128)S(1)} collective-permute-done((f32[16,128]{1,0:T(8,128)S(1)}, f32[16,128]{1,0:T(8,128)S(1)}, u32[]{:S(2)}, u32[]{:S(2)}) %collective-permute-start.30) | collective-permute-done | bytes 8224 | tf_op jit(solution)/shard_map/ppermute | solution.py:646
  228.0 1.9 collective-permute-start.31
  229.9 7.5 %collective-permute-done.31 = f32[16,128]{1,0:T(8,128)S(1)} collective-permute-done((f32[16,128]{1,0:T(8,128)S(1)}, f32[16,128]{1,0:T(8,128)S(1)}, u32[]{:S(2)}, u32[]{:S(2)}) %collective-permute-start.31) | collective-permute-done | bytes 8224 | tf_op jit(solution)/shard_map/ppermute | solution.py:646
  237.4 1.9 collective-permute-start.32
  239.3 7.5 %collective-permute-done.32 = f32[16,128]{1,0:T(8,128)S(1)} collective-permute-done((f32[16,128]{1,0:T(8,128)S(1)}, f32[16,128]{1,0:T(8,128)S(1)}, u32[]{:S(2)}, u32[]{:S(2)}) %collective-permute-start.32) | collective-permute-done | bytes 8224 | tf_op jit(solution)/shard_map/ppermute | solution.py:646
  246.9 4.1 %rotate.1 = f32[4,12,16,128]{3,2,1,0:T(8,128)} custom-call(s32[4]{0:T(128)S(1)} %pad_add_fusion.order, f32[16,128]{1,0:T(8,128)S(1)} %add.52.corr_ref, f32[768,128]{1,0:T(8,128)S(1)} %step.5.a0, f32[768,128]{1,0:T(8,128)S(1)} %collective-permute-done.22.a1, f32[768,128]{1,0:T(8,128)S(1)} %collective-permute-done.23.a2, ...), custom_call_target="tpu_custom_call" | custom-call | tf_op jit(solution)/shard_map/rotate/pallas_call | solution.py:649
  (99 shorter events, 37.4 us)
Async XLA Ops:
  0.0 76.3 %copy-start.2 = (bf16[1024,128]{1,0:T(8,128)(2,1)S(1)}, bf16[1024,128]{1,0:T(8,128)(2,1)}, u32[]{:S(2)}) copy-start(bf16[1024,128]{1,0:T(8,128)(2,1)} %constant.36.clone.g_ref) | copy-start | bytes 786436
  1.5 0.9 copy-start.14
  2.3 1.0 copy-start.16
  3.3 0.9 copy-start.17
  6.3 15.1 %collective-permute-start = (f32[616,128]{1,0:T(8,128)S(1)}, f32[616,128]{1,0:T(8,128)S(1)}, u32[]{:S(2)}, u32[]{:S(2)}) collective-permute-start(f32[616,128]{1,0:T(8,128)S(1)} %get-tuple-element.44), channel_id=1, source_target_pairs={{0,64},{64,128},{128,192},{192,256},{256,320},{320,384},{384,448},... | collective-permute-start | bytes 946184 | tf_op jit(solution)/shard_map/ppermute | solution.py:537
  8.0 13.4 %collective-permute-start.1 = (f32[616,128]{1,0:T(8,128)S(1)}, f32[616,128]{1,0:T(8,128)S(1)}, u32[]{:S(2)}, u32[]{:S(2)}) collective-permute-start(f32[616,128]{1,0:T(8,128)S(1)} %get-tuple-element.45), channel_id=1, source_target_pairs={{64,0},{128,64},{192,128},{256,192},{320,256},{384,320},{448,384},... | collective-permute-start | bytes 946184 | tf_op jit(solution)/shard_map/ppermute | solution.py:537
  9.3 58.9 %collective-permute-start.2 = (f32[384,128]{1,0:T(8,128)S(1)}, f32[384,128]{1,0:T(8,128)S(1)}, u32[]{:S(2)}, u32[]{:S(2)}) collective-permute-start(f32[384,128]{1,0:T(8,128)S(1)} %get-tuple-element.46), channel_id=1, source_target_pairs={{0,4},{4,8},{8,12},{12,16},{16,20},{20,24},{24,28},{28,32},{32,36}... | collective-permute-start | bytes 589832 | tf_op jit(solution)/shard_map/ppermute | solution.py:537
  19.5 48.8 %collective-permute-start.3 = (f32[384,128]{1,0:T(8,128)S(1)}, f32[384,128]{1,0:T(8,128)S(1)}, u32[]{:S(2)}, u32[]{:S(2)}) collective-permute-start(f32[384,128]{1,0:T(8,128)S(1)} %get-tuple-element.47), channel_id=1, source_target_pairs={{4,0},{8,4},{12,8},{16,12},{20,16},{24,20},{28,24},{32,28},{36,32}... | collective-permute-start | bytes 589832 | tf_op jit(solution)/shard_map/ppermute | solution.py:537
  21.5 13.2 %collective-permute-start.4 = (f32[272,128]{1,0:T(8,128)S(1)}, f32[272,128]{1,0:T(8,128)S(1)}, u32[]{:S(2)}, u32[]{:S(2)}) collective-permute-start(f32[272,128]{1,0:T(8,128)S(1)} %get-tuple-element.52), channel_id=1, source_target_pairs={{0,4},{4,8},{8,12},{12,16},{16,20},{20,24},{24,28},{28,32},{32,36}... | collective-permute-start | bytes 417800 | tf_op jit(solution)/shard_map/ppermute | solution.py:537
  31.5 16.0 %collective-permute-start.5 = (f32[272,128]{1,0:T(8,128)S(1)}, f32[272,128]{1,0:T(8,128)S(1)}, u32[]{:S(2)}, u32[]{:S(2)}) collective-permute-start(f32[272,128]{1,0:T(8,128)S(1)} %get-tuple-element.53), channel_id=1, source_target_pairs={{4,0},{8,4},{12,8},{16,12},{20,16},{24,20},{28,24},{32,28},{36,32}... | collective-permute-start | bytes 417800 | tf_op jit(solution)/shard_map/ppermute | solution.py:537
  47.5 1.0 copy-start.1
  53.8 4.3 %collective-permute-start.6 = (f32[24,128]{1,0:T(8,128)S(1)}, f32[24,128]{1,0:T(8,128)S(1)}, u32[]{:S(2)}, u32[]{:S(2)}) collective-permute-start(f32[24,128]{1,0:T(8,128)S(1)} %get-tuple-element.58), channel_id=1, source_target_pairs={{0,64},{64,128},{128,192},{192,256},{256,320},{320,384},{384,448},... | collective-permute-start | bytes 36872 | tf_op jit(solution)/shard_map/ppermute | solution.py:537
  56.8 3.6 %collective-permute-start.7 = (f32[24,128]{1,0:T(8,128)S(1)}, f32[24,128]{1,0:T(8,128)S(1)}, u32[]{:S(2)}, u32[]{:S(2)}) collective-permute-start(f32[24,128]{1,0:T(8,128)S(1)} %get-tuple-element.59), channel_id=1, source_target_pairs={{64,0},{128,64},{192,128},{256,192},{320,256},{384,320},{448,384},... | collective-permute-start | bytes 36872 | tf_op jit(solution)/shard_map/ppermute | solution.py:537
  58.1 2.3 copy-start.26
  62.4 11.0 %collective-permute-start.8 = (f32[32,128]{1,0:T(8,128)}, f32[32,128]{1,0:T(8,128)S(1)}, u32[]{:S(2)}, u32[]{:S(2)}) collective-permute-start(f32[32,128]{1,0:T(8,128)} %get-tuple-element.61), channel_id=1, source_target_pairs={{0,4},{4,8},{8,12},{12,16},{16,20},{20,24},{24,28},{28,32},{32,36}... | collective-permute-start | bytes 49160 | tf_op jit(solution)/shard_map/ppermute | solution.py:537
  64.3 12.0 %collective-permute-start.9 = (f32[32,128]{1,0:T(8,128)}, f32[32,128]{1,0:T(8,128)S(1)}, u32[]{:S(2)}, u32[]{:S(2)}) collective-permute-start(f32[32,128]{1,0:T(8,128)} %get-tuple-element.62), channel_id=1, source_target_pairs={{4,0},{8,4},{12,8},{16,12},{20,16},{24,20},{28,24},{32,28},{36,32}... | collective-permute-start | bytes 49160 | tf_op jit(solution)/shard_map/ppermute | solution.py:537
  68.2 0.9 copy-start.3
  69.2 0.9 copy-start.15
  70.9 50.0 %copy-start.5 = (bf16[256,256]{1,0:T(8,128)(2,1)S(1)}, bf16[256,256]{1,0:T(8,128)(2,1)}, u32[]{:S(2)}) copy-start(bf16[256,256]{1,0:T(8,128)(2,1)} %constant.35.clone.dz_ref) | copy-start | bytes 393220
  72.0 1.3 copy-start
  76.3 0.9 copy-start.4
  84.6 12.3 %collective-permute-start.10 = (f32[408,128]{1,0:T(8,128)S(1)}, f32[408,128]{1,0:T(8,128)S(1)}, u32[]{:S(2)}, u32[]{:S(2)}) collective-permute-start(f32[408,128]{1,0:T(8,128)S(1)} %get-tuple-element.64), channel_id=1, source_target_pairs={{0,64},{64,128},{128,192},{192,256},{256,320},{320,384},{384,448},... | collective-permute-start | bytes 626696 | tf_op jit(solution)/shard_map/ppermute | solution.py:537
  87.8 9.1 %collective-permute-start.11 = (f32[408,128]{1,0:T(8,128)S(1)}, f32[408,128]{1,0:T(8,128)S(1)}, u32[]{:S(2)}, u32[]{:S(2)}) collective-permute-start(f32[408,128]{1,0:T(8,128)S(1)} %get-tuple-element.65), channel_id=1, source_target_pairs={{64,0},{128,64},{192,128},{256,192},{320,256},{384,320},{448,384},... | collective-permute-start | bytes 626696 | tf_op jit(solution)/shard_map/ppermute | solution.py:537
  89.1 21.8 %collective-permute-start.12 = (f32[288,128]{1,0:T(8,128)S(1)}, f32[288,128]{1,0:T(8,128)S(1)}, u32[]{:S(2)}, u32[]{:S(2)}) collective-permute-start(f32[288,128]{1,0:T(8,128)S(1)} %get-tuple-element.66), channel_id=1, source_target_pairs={{0,4},{4,8},{8,12},{12,16},{16,20},{20,24},{24,28},{28,32},{32,36}... | collective-permute-start | bytes 442376 | tf_op jit(solution)/shard_map/ppermute | solution.py:537
  95.0 17.5 %collective-permute-start.13 = (f32[288,128]{1,0:T(8,128)S(1)}, f32[288,128]{1,0:T(8,128)S(1)}, u32[]{:S(2)}, u32[]{:S(2)}) collective-permute-start(f32[288,128]{1,0:T(8,128)S(1)} %get-tuple-element.67), channel_id=1, source_target_pairs={{4,0},{8,4},{12,8},{16,12},{20,16},{24,20},{28,24},{32,28},{36,32}... | collective-permute-start | bytes 442376 | tf_op jit(solution)/shard_map/ppermute | solution.py:537
  99.1 13.5 %collective-permute-start.14 = (f32[32,128]{1,0:T(8,128)}, f32[32,128]{1,0:T(8,128)S(1)}, u32[]{:S(2)}, u32[]{:S(2)}) collective-permute-start(f32[32,128]{1,0:T(8,128)} %get-tuple-element.70), channel_id=1, source_target_pairs={{0,4},{4,8},{8,12},{12,16},{16,20},{20,24},{24,28},{28,32},{32,36}... | collective-permute-start | bytes 49160 | tf_op jit(solution)/shard_map/ppermute | solution.py:537
  109.0 11.9 %collective-permute-start.15 = (f32[32,128]{1,0:T(8,128)}, f32[32,128]{1,0:T(8,128)S(1)}, u32[]{:S(2)}, u32[]{:S(2)}) collective-permute-start(f32[32,128]{1,0:T(8,128)} %get-tuple-element.71), channel_id=1, source_target_pairs={{4,0},{8,4},{12,8},{16,12},{20,16},{24,20},{28,24},{32,28},{36,32}... | collective-permute-start | bytes 49160 | tf_op jit(solution)/shard_map/ppermute | solution.py:537
  120.9 0.9 copy-start.9
  121.8 0.9 copy-start.13
  130.2 8.5 %collective-permute-start.16 = (f32[408,128]{1,0:T(8,128)S(1)}, f32[408,128]{1,0:T(8,128)S(1)}, u32[]{:S(2)}, u32[]{:S(2)}) collective-permute-start(f32[408,128]{1,0:T(8,128)S(1)} %get-tuple-element.73), channel_id=1, source_target_pairs={{0,64},{64,128},{128,192},{192,256},{256,320},{320,384},{384,448},... | collective-permute-start | bytes 626696 | tf_op jit(solution)/shard_map/ppermute | solution.py:537
  131.5 7.2 %collective-permute-start.17 = (f32[408,128]{1,0:T(8,128)S(1)}, f32[408,128]{1,0:T(8,128)S(1)}, u32[]{:S(2)}, u32[]{:S(2)}) collective-permute-start(f32[408,128]{1,0:T(8,128)S(1)} %get-tuple-element.74), channel_id=1, source_target_pairs={{64,0},{128,64},{192,128},{256,192},{320,256},{384,320},{448,384},... | collective-permute-start | bytes 626696 | tf_op jit(solution)/shard_map/ppermute | solution.py:537
  132.8 17.9 %collective-permute-start.18 = (f32[288,128]{1,0:T(8,128)S(1)}, f32[288,128]{1,0:T(8,128)S(1)}, u32[]{:S(2)}, u32[]{:S(2)}) collective-permute-start(f32[288,128]{1,0:T(8,128)S(1)} %get-tuple-element.75), channel_id=1, source_target_pairs={{0,4},{4,8},{8,12},{12,16},{16,20},{20,24},{24,28},{28,32},{32,36}... | collective-permute-start | bytes 442376 | tf_op jit(solution)/shard_map/ppermute | solution.py:537
  134.7 15.9 %collective-permute-start.19 = (f32[288,128]{1,0:T(8,128)S(1)}, f32[288,128]{1,0:T(8,128)S(1)}, u32[]{:S(2)}, u32[]{:S(2)}) collective-permute-start(f32[288,128]{1,0:T(8,128)S(1)} %get-tuple-element.76), channel_id=1, source_target_pairs={{4,0},{8,4},{12,8},{16,12},{20,16},{24,20},{28,24},{32,28},{36,32}... | collective-permute-start | bytes 442376 | tf_op jit(solution)/shard_map/ppermute | solution.py:537
  140.8 9.9 %collective-permute-start.20 = (f32[32,128]{1,0:T(8,128)}, f32[32,128]{1,0:T(8,128)S(1)}, u32[]{:S(2)}, u32[]{:S(2)}) collective-permute-start(f32[32,128]{1,0:T(8,128)} %get-tuple-element.79), channel_id=1, source_target_pairs={{0,4},{4,8},{8,12},{12,16},{16,20},{20,24},{24,28},{28,32},{32,36}... | collective-permute-start | bytes 49160 | tf_op jit(solution)/shard_map/ppermute | solution.py:537
  148.7 11.9 %collective-permute-start.21 = (f32[32,128]{1,0:T(8,128)}, f32[32,128]{1,0:T(8,128)S(1)}, u32[]{:S(2)}, u32[]{:S(2)}) collective-permute-start(f32[32,128]{1,0:T(8,128)} %get-tuple-element.80), channel_id=1, source_target_pairs={{4,0},{8,4},{12,8},{16,12},{20,16},{24,20},{28,24},{32,28},{36,32}... | collective-permute-start | bytes 49160 | tf_op jit(solution)/shard_map/ppermute | solution.py:537
  160.6 0.9 copy-start.7
  161.5 0.9 copy-start.11
  168.5 12.0 %collective-permute-start.22 = (f32[768,128]{1,0:T(8,128)S(1)}, f32[768,128]{1,0:T(8,128)S(1)}, u32[]{:S(2)}, u32[]{:S(2)}) collective-permute-start(f32[768,128]{1,0:T(8,128)S(1)} %step.5.a0), channel_id=1, source_target_pairs={{0,1},{1,2},{2,3},{3,0},{4,5},{5,6},{6,7},{7,4},{8,9},{9,10},{10,1... | collective-permute-start | bytes 1179656 | tf_op jit(solution)/shard_map/ppermute | solution.py:628
  170.9 13.5 %collective-permute-start.23 = (f32[768,128]{1,0:T(8,128)S(1)}, f32[768,128]{1,0:T(8,128)S(1)}, u32[]{:S(2)}, u32[]{:S(2)}) collective-permute-start(f32[768,128]{1,0:T(8,128)S(1)} %step.5.a0), channel_id=1, source_target_pairs={{0,3},{1,0},{2,1},{3,2},{4,7},{5,4},{6,5},{7,6},{8,11},{9,8},{10,9... | collective-permute-start | bytes 1179656 | tf_op jit(solution)/shard_map/ppermute | solution.py:629
  180.6 8.7 %collective-permute-start.24 = (f32[384,128]{1,0:T(8,128)S(1)}, f32[384,128]{1,0:T(8,128)S(1)}, u32[]{:S(2)}, u32[]{:S(2)}) collective-permute-start(f32[384,128]{1,0:T(8,128)S(1)} %slice.8), channel_id=1, source_target_pairs={{0,1},{1,2},{2,3},{3,0},{4,5},{5,6},{6,7},{7,4},{8,9},{9,10},{10,1... | collective-permute-start | bytes 589832 | tf_op jit(solution)/shard_map/ppermute | solution.py:631
  184.5 10.5 %collective-permute-start.25 = (f32[384,128]{1,0:T(8,128)S(1)}, f32[384,128]{1,0:T(8,128)S(1)}, u32[]{:S(2)}, u32[]{:S(2)}) collective-permute-start(f32[384,128]{1,0:T(8,128)S(1)} %slice.9), channel_id=1, source_target_pairs={{0,3},{1,0},{2,1},{3,2},{4,7},{5,4},{6,5},{7,6},{8,11},{9,8},{10,9... | collective-permute-start | bytes 589832 | tf_op jit(solution)/shard_map/ppermute | solution.py:632
  199.4 3.1 %collective-permute-start.26 = (f32[16,128]{1,0:T(8,128)S(1)}, f32[16,128]{1,0:T(8,128)S(1)}, u32[]{:S(2)}, u32[]{:S(2)}) collective-permute-start(f32[16,128]{1,0:T(8,128)S(1)} %gram.1), channel_id=1, source_target_pairs={{0,64},{64,0},{128,192},{192,128},{256,320},{320,256},{384,448},{4... | collective-permute-start | bytes 24584 | tf_op jit(solution)/shard_map/ppermute | solution.py:646
  202.4 7.1 %collective-permute-start.27 = (f32[16,128]{1,0:T(8,128)S(1)}, f32[16,128]{1,0:T(8,128)S(1)}, u32[]{:S(2)}, u32[]{:S(2)}) collective-permute-start(f32[16,128]{1,0:T(8,128)S(1)} %add.46), channel_id=1, source_target_pairs={{0,128},{64,192},{128,0},{192,64},{256,384},{320,448},{384,256},{4... | collective-permute-start | bytes 24584 | tf_op jit(solution)/shard_map/ppermute | solution.py:646
  209.6 6.4 %collective-permute-start.28 = (f32[16,128]{1,0:T(8,128)S(1)}, f32[16,128]{1,0:T(8,128)S(1)}, u32[]{:S(2)}, u32[]{:S(2)}) collective-permute-start(f32[16,128]{1,0:T(8,128)S(1)} %add.47), channel_id=1, source_target_pairs={{0,256},{64,320},{128,384},{192,448},{256,0},{320,64},{384,128},{4... | collective-permute-start | bytes 24584 | tf_op jit(solution)/shard_map/ppermute | solution.py:646
  216.0 5.5 %collective-permute-start.29 = (f32[16,128]{1,0:T(8,128)S(1)}, f32[16,128]{1,0:T(8,128)S(1)}, u32[]{:S(2)}, u32[]{:S(2)}) collective-permute-start(f32[16,128]{1,0:T(8,128)S(1)} %add.48), channel_id=1, source_target_pairs={{0,4},{4,0},{8,12},{12,8},{16,20},{20,16},{24,28},{28,24},{32,36},... | collective-permute-start | bytes 24584 | tf_op jit(solution)/shard_map/ppermute | solution.py:646
  221.5 6.4 %collective-permute-start.30 = (f32[16,128]{1,0:T(8,128)S(1)}, f32[16,128]{1,0:T(8,128)S(1)}, u32[]{:S(2)}, u32[]{:S(2)}) collective-permute-start(f32[16,128]{1,0:T(8,128)S(1)} %add.49), channel_id=1, source_target_pairs={{0,8},{4,12},{8,0},{12,4},{16,24},{20,28},{24,16},{28,20},{32,40},... | collective-permute-start | bytes 24584 | tf_op jit(solution)/shard_map/ppermute | solution.py:646
  228.0 9.4 %collective-permute-start.31 = (f32[16,128]{1,0:T(8,128)S(1)}, f32[16,128]{1,0:T(8,128)S(1)}, u32[]{:S(2)}, u32[]{:S(2)}) collective-permute-start(f32[16,128]{1,0:T(8,128)S(1)} %add.50), channel_id=1, source_target_pairs={{0,16},{4,20},{8,24},{12,28},{16,0},{20,4},{24,8},{28,12},{32,48},... | collective-permute-start | bytes 24584 | tf_op jit(solution)/shard_map/ppermute | solution.py:646
  237.4 9.4 %collective-permute-start.32 = (f32[16,128]{1,0:T(8,128)S(1)}, f32[16,128]{1,0:T(8,128)S(1)}, u32[]{:S(2)}, u32[]{:S(2)}) collective-permute-start(f32[16,128]{1,0:T(8,128)S(1)} %add.51), channel_id=1, source_target_pairs={{0,32},{4,36},{8,40},{12,44},{16,48},{20,52},{24,56},{28,60},{32,0... | collective-permute-start | bytes 24584 | tf_op jit(solution)/shard_map/ppermute | solution.py:646
  (13 other events, 9.0 us)

commit v2 on v1

--- a/solution.py
+++ b/solution.py
@@ -25,8 +25,7 @@
 F32, BF16 = jnp.float32, jnp.bfloat16
 VMEM = pl.BlockSpec(memory_space=pltpu.VMEM)
 SMEM = pl.BlockSpec(memory_space=pltpu.SMEM)
-ANY = pl.BlockSpec(memory_space=pl.ANY)
-LIMIT = 50 * 1024 * 1024
+LIMIT = 24 * 1024 * 1024
 
 
 def derivative_table():
@@ -346,14 +345,14 @@
     send_coeffs(z_ref, xr_ref, xl_ref, 0)
 
 
-def fold_kernel(z_ref, fl_ref, fr_ref, out_ref, hi_ref, lo_ref):
+def fold_kernel(base, z_ref, fl_ref, fr_ref, out_ref, hi_ref, lo_ref):
     _, lane = iotas()
     left_half = lane < 64
     tiles = []
     for side in range(2):
         near, far = (fl_ref, fr_ref) if side == 0 else (fr_ref, fl_ref)
         for t in range(3):
-            tiles.append(get(z_ref, side * 3 + t) + get(near, t) + jnp.where(left_half, get(far, t), 0.0))
+            tiles.append(get(z_ref, side * 3 + t) + get(near, base + t) + jnp.where(left_half, get(far, base + t), 0.0))
     for t in range(6):
         put(out_ref, t, tiles[t])
     for side in range(2):
@@ -364,16 +363,14 @@
 
 
 def step_kernel(
-    step, y_ref, prev_ref, fl_ref, fr_ref, plo_ref, phi_ref, coef_ref, q_hbm, s_ref, w_ref, z_ref, clo_ref, chi_ref,
+    step, y_ref, prev_ref, fl_ref, fr_ref, plo_ref, phi_ref, coef_ref, q_ref, s_ref, w_ref, z_ref, clo_ref, chi_ref,
     dz_ref, g_ref, *rest
 ):
     last = step == STEPS
     if last:
-        new_ref, q_ref, ex, ey, zd, acc, wp, sem = rest
+        new_ref, ex, ey, zd, acc, wp = rest
     else:
-        new_ref, xr_ref, xl_ref, yh_ref, yl_ref, zn_ref, q_ref, ex, ey, zd, acc, wp, sem = rest
-    copy = pltpu.make_async_copy(q_hbm, q_ref, sem)
-    copy.start()
+        new_ref, xr_ref, xl_ref, yh_ref, yl_ref, zn_ref, ex, ey, zd, acc, wp = rest
     sub, _ = iotas()
     low = sub < 4
     scale = 1.0 if step == 1 else 2.0
@@ -425,7 +422,6 @@
     weights = jnp.concatenate(tiles, axis=0) * w_ref[...] * scale
     wp[...] = pick_t(weights, g_ref[...])
 
-    copy.wait()
     for xt in range(3):
         for yq in range(2):
             b = xt * 2 + yq
@@ -452,17 +448,12 @@
         send_coeffs(zn_ref, xr_ref, xl_ref, XH)
 
 
-def gram_kernel(order, a0, a1, a2, a3, out_ref, held):
-    for n, ref in enumerate((a0, a1, a2, a3)):
-        held[order[n]] = ref[...]
-
-    def body(x, total):
-        at = pl.ds(pl.multiple_of(x * 64, 64), 64)
-        field = jnp.concatenate([held[d, at, :] for d in range(4)], axis=0)
+def gram_kernel(parts_ref, out_ref):
+    total = jnp.zeros((256, 256), F32)
+    for x in range(CX // 4):
+        field = jnp.concatenate([parts_ref[d, x * 64 : x * 64 + 64, :] for d in range(4)], axis=0)
         high, low = split(field)
-        return total + (mm_t(high, high) + mm_t(high, low) + mm_t(low, high))
-
-    total = lax.fori_loop(0, CX, body, jnp.zeros((256, 256), F32))
+        total = total + (mm_t(high, high) + mm_t(high, low) + mm_t(low, high))
     rows = lax.broadcasted_iota(jnp.int32, (256, 256), 0)
     columns = lax.broadcasted_iota(jnp.int32, (256, 256), 1)
     total = jnp.where((rows % 64) // 4 == (columns % 64) // 4, total, 0.0)
@@ -473,14 +464,17 @@
     small = lax.dot_general(
         first, hot, (((1,), (1,)), ((), ())), precision=lax.Precision.HIGHEST, preferred_element_type=F32
     )
-    out_ref[...] = jnp.zeros((16, 128), F32)
-    out_ref[:, 0:16] = small
+    out_ref[...] = jnp.zeros((8, 128), F32)
+    out_ref[:, 0:16] = small[0:8]
+    out_ref[:, 16:32] = small[8:16]
 
 
 def rotate_kernel(cells, order, corr_ref, a0, a1, a2, a3, out_ref, flat):
     lane = lax.broadcasted_iota(jnp.int32, (16, 128), 1)
     rows = lax.broadcasted_iota(jnp.int32, (16, 128), 0)
-    work = jnp.where(lane < 16, corr_ref[...] * (1.0 / cells), jnp.where(lane == rows + 16, 1.0, 0.0))
+    packed = corr_ref[...]
+    whole = jnp.concatenate([packed, pltpu.roll(packed, 112, 1)], axis=0)
+    work = jnp.where(lane < 16, whole * (1.0 / cells), jnp.where(lane == rows + 16, 1.0, 0.0))
     pivots = jnp.ones((16, 128), F32)
     for k in range(16):
         pivot_row = jnp.broadcast_to(work[k : k + 1, :], (16, 128))
@@ -538,15 +532,8 @@
 
 
 def fold(z, from_left, from_right, tile):
-    block = pl.BlockSpec((24, 128), lambda i: (tile // 3, 0))
-    whole = lambda rows: pl.BlockSpec((rows, 128), lambda i: (0, 0))
-    return pl.pallas_call(
-        fold_kernel,
-        grid=(1,),
-        out_shape=[jax.ShapeDtypeStruct((rows, 128), F32) for rows in (48, 32, 32)],
-        in_specs=[whole(48), block, block],
-        out_specs=[whole(48), whole(32), whole(32)],
-        name="fold_coeffs",
+    return kernel_call(
+        functools.partial(fold_kernel, tile), [blocks(6), blocks(4), blocks(4)], [VMEM] * 3, name="fold_coeffs"
     )(z, from_left, from_right)
 
 
@@ -599,15 +586,13 @@
         result = kernel_call(
             functools.partial(step_kernel, step),
             outs,
-            [VMEM] * 7 + [ANY] + [VMEM] * 7,
+            [VMEM] * 15,
             [
-                pltpu.VMEM((6 * 8 * 16 * 8, 256), F32),
                 pltpu.VMEM(((TILES + 2 * XH) * 8, 128), F32),
                 pltpu.VMEM((CX * 20 * 8, 128), F32),
                 pltpu.VMEM((TILES * 8, 256), F32),
                 pltpu.VMEM((48, 1024), F32),
                 pltpu.VMEM((48, 1024), F32),
-                pltpu.SemaphoreType.DMA,
             ],
             name="step",
         )(y, previous, from_left, from_right, from_lo, from_hi, coefs, q, s, w, z, c_lo, c_hi, dz, groups)
@@ -625,6 +610,9 @@
     me = lax.axis_index("orb")
     up = [(i, (i + 1) % count) for i in range(count)]
     down = [(i, (i - 1) % count) for i in range(count)]
+    parts = lax.all_to_all(y.reshape(count, -1, NZ), "orb", 0, 0, tiled=True)
+    y, parts = lax.optimization_barrier((y, parts))
+    (corr,) = kernel_call(gram_kernel, [blocks(1)], [VMEM], name="gram")(parts)
     below = lax.ppermute(y, "orb", up)
     above = lax.ppermute(y, "orb", down)
     half = TILES * 4
@@ -632,19 +620,10 @@
     across_b = lax.ppermute(above[half:], "orb", down)
     across = jnp.concatenate([across_a, across_b], axis=0)
     order = jnp.stack([me, (me + count - 1) % count, (me + 1) % count, (me + 2) % count]).astype(jnp.int32)
-    (corr,) = kernel_call(
-        gram_kernel,
-        [((16, 128), F32)],
-        [SMEM] + [VMEM] * 4,
-        [pltpu.VMEM((4, TILES * 8, 128), F32)],
-        name="gram",
-    )(order, y, below, above, across)
-    for axis in ("gx", "gy"):
+    for axis in ("orb", "gx", "gy"):
         size = lax.axis_size(axis)
-        stride = 1
-        while stride < size:
-            corr = corr + lax.ppermute(corr, axis, [(i, i ^ stride) for i in range(size)])
-            stride *= 2
+        copies = jnp.broadcast_to(corr[None], (size, 8, 128))
+        corr = jnp.sum(lax.all_to_all(copies, axis, 0, 0, tiled=True), axis=0)
     cells = CX * CY * NZ * lax.axis_size("gx") * lax.axis_size("gy")
     (result,) = kernel_call(
         functools.partial(rotate_kernel, cells),

time: 253 us -> 218 us (0.86)
  the two profiles are of different devices: /device:TPU:62 before, /device:TPU:8 now
where the time goes in v2:
time: 218 us; the launch traced here: 216 us
  starting transfers between devices  114 us (52%)
  waiting for transfers between devices  43.5 us (20%)
  blocking collectives  29 us (13%)
  Pallas kernels  20.3 us (9%)
  local copies, waits for them, and re-layouts  8.59 us (4%)
    ppermute x11, starting transfers between devices, beside(): lax.ppermute(low_value, axis, up)  44.3 us
    all_to_all x1, starting transfers between devices, shards(): corr = jnp.sum(lax.all_to_all(copies, axis, 0, 0, tiled=True), axis=0)  31.5 us
    ppermute x11, starting transfers between devices, beside(): lax.ppermute(high_value, axis, down)  23.8 us
    ppermute x11, waiting for transfers between devices, beside(): lax.ppermute(high_value, axis, down)  21.8 us
    all_to_all x2, blocking collectives, shards(): corr = jnp.sum(lax.all_to_all(copies, axis, 0, 0, tiled=True), axis=0)  16.6 us
    all_to_all x1, blocking collectives, shards(): parts = lax.all_to_all(y.reshape(count, -1, NZ), 'orb', 0, 0, tiled=True)  12.5 us
    all_to_all x1, waiting for transfers between devices, shards(): corr = jnp.sum(lax.all_to_all(copies, axis, 0, 0, tiled=True), axis=0)  11.4 us
    pallas_call x3, Pallas kernels, shards(): kernel_call(functools.partial(step_kernel, step), outs, [VMEM] * 15, [plt...  10.2 us
  transfers between devices with their start and end apart: 27, of which 9 were waited for; matrix products, arithmetic and copies ran while one was open for 0% of the time, Pallas kernels for 2%

profile of v2, /device:TPU:8, one launch (start us, length us, event | category | flops | bytes accessed | tf_op | source)
XLA Modules:
  0.0 216.4 jit_solution(14037025121966141524)
XLA Ops:
  2.4 1.0 copy-done.6
  3.3 0.9 copy-done.7
  4.9 1.3 prepare.1
  6.3 1.8 collective-permute-start
  8.0 1.3 collective-permute-start.1
  9.3 3.5 %collective-permute-start.2 = (f32[384,128]{1,0:T(8,128)S(1)}, f32[384,128]{1,0:T(8,128)S(1)}, u32[]{:S(2)}, u32[]{:S(2)}) collective-permute-start(f32[384,128]{1,0:T(8,128)S(1)} %get-tuple-element.48), channel_id=1, source_target_pairs={{0,4},{4,8},{8,12},{12,16},{16,20},{20,24},{24,28},{28,32},{32,36}... | collective-permute-start | bytes 589832 | tf_op jit(solution)/shard_map/ppermute | solution.py:531
  12.8 5.1 %collective-permute-start.3 = (f32[384,128]{1,0:T(8,128)S(1)}, f32[384,128]{1,0:T(8,128)S(1)}, u32[]{:S(2)}, u32[]{:S(2)}) collective-permute-start(f32[384,128]{1,0:T(8,128)S(1)} %get-tuple-element.49), channel_id=1, source_target_pairs={{4,0},{8,4},{12,8},{16,12},{20,16},{24,20},{28,24},{32,28},{36,32}... | collective-permute-start | bytes 589832 | tf_op jit(solution)/shard_map/ppermute | solution.py:531
  18.1 1.9 collective-permute-start.4
  20.0 3.9 %collective-permute-start.5 = (f32[272,128]{1,0:T(8,128)S(1)}, f32[272,128]{1,0:T(8,128)S(1)}, u32[]{:S(2)}, u32[]{:S(2)}) collective-permute-start(f32[272,128]{1,0:T(8,128)S(1)} %get-tuple-element.55), channel_id=1, source_target_pairs={{4,0},{8,4},{12,8},{16,12},{20,16},{24,20},{28,24},{32,28},{36,32}... | collective-permute-start | bytes 417800 | tf_op jit(solution)/shard_map/ppermute | solution.py:531
  23.9 2.3 %collective-permute-done.4.lo_ref = f32[272,128]{1,0:T(8,128)S(1)} collective-permute-done((f32[272,128]{1,0:T(8,128)S(1)}, f32[272,128]{1,0:T(8,128)S(1)}, u32[]{:S(2)}, u32[]{:S(2)}) %collective-permute-start.4) | collective-permute-done | bytes 139296 | tf_op jit(solution)/shard_map/ppermute | solution.py:531
  26.2 1.7 collective-permute-done.5.hi_ref
  28.0 0.9 copy-done
  28.9 2.4 %build.1 = (f32[6144,256]{1,0:T(8,128)S(1)}, bf16[512,256]{1,0:T(8,128)(2,1)S(1)}, f32[48,128]{1,0:T(8,128)S(1)}, f32[48,128]{1,0:T(8,128)S(1)}, f32[24,128]{1,0:T(8,128)S(1)}, /*index=5*/f32[24,128]{1,0:T(8,128)S(1)}) custom-call(f32[512,128]{1,0:T(8,128)S(1)} %get-tuple-element.52.t2_ref, f32[16,128]{1,0:T(8,128)S(1)} %get-tuple-element.53.m_ref, ...), custom_call_target="tpu_custom_call" | custom-call | tf_op jit(solution)/shard_map/build/pallas_call | solution.py:562
  31.3 2.3 %collective-permute-start.6 = (f32[24,128]{1,0:T(8,128)S(1)}, f32[24,128]{1,0:T(8,128)S(1)}, u32[]{:S(2)}, u32[]{:S(2)}) collective-permute-start(f32[24,128]{1,0:T(8,128)S(1)} %get-tuple-element.60), channel_id=1, source_target_pairs={{0,64},{64,128},{128,192},{192,256},{256,320},{320,384},{384,448},... | collective-permute-start | bytes 36872 | tf_op jit(solution)/shard_map/ppermute | solution.py:531
  33.6 1.3 collective-permute-start.7
  34.9 5.4 %collective-permute-done.7.fr_ref = f32[24,128]{1,0:T(8,128)S(1)} collective-permute-done((f32[24,128]{1,0:T(8,128)S(1)}, f32[24,128]{1,0:T(8,128)S(1)}, u32[]{:S(2)}, u32[]{:S(2)}) %collective-permute-start.7) | collective-permute-done | bytes 12320 | tf_op jit(solution)/shard_map/ppermute | solution.py:531
  40.4 4.5 %collective-permute-start.8 = (f32[32,128]{1,0:T(8,128)S(1)}, f32[32,128]{1,0:T(8,128)S(1)}, u32[]{:S(2)}, u32[]{:S(2)}) collective-permute-start(f32[32,128]{1,0:T(8,128)S(1)} %get-tuple-element.63), channel_id=1, source_target_pairs={{0,4},{4,8},{8,12},{12,16},{16,20},{20,24},{24,28},{28,32},{32,36}... | collective-permute-start | bytes 49160 | tf_op jit(solution)/shard_map/ppermute | solution.py:531
  44.9 1.9 collective-permute-start.9
  49.6 1.1 coefficients.1.coef_ref
  51.5 3.6 %step.3 = (f32[768,128]{1,0:T(8,128)S(1)}, f32[408,128]{1,0:T(8,128)S(1)}, f32[408,128]{1,0:T(8,128)S(1)}, f32[288,128]{1,0:T(8,128)S(1)}, f32[288,128]{1,0:T(8,128)S(1)}, /*index=5*/f32[48,128]{1,0:T(8,128)S(1)}) custom-call(f32[768,128]{1,0:T(8,128)S(1)} %get-tuple-element.45.y_ref.prev_ref, f32[768,128]{1,0:T(8,128)S(1)} %get-tuple-element.45.y_ref.prev_ref, ...), custom_call_target="tpu_custom_call" | custom-call | tf_op jit(solution)/shard_map/step/pallas_call | solution.py:586
  55.1 3.3 %collective-permute-start.10 = (f32[408,128]{1,0:T(8,128)S(1)}, f32[408,128]{1,0:T(8,128)S(1)}, u32[]{:S(2)}, u32[]{:S(2)}) collective-permute-start(f32[408,128]{1,0:T(8,128)S(1)} %get-tuple-element.66), channel_id=1, source_target_pairs={{0,64},{64,128},{128,192},{192,256},{256,320},{320,384},{384,448},... | collective-permute-start | bytes 626696 | tf_op jit(solution)/shard_map/ppermute | solution.py:531
  58.4 1.3 collective-permute-start.11
  59.7 4.9 %collective-permute-start.12 = (f32[288,128]{1,0:T(8,128)S(1)}, f32[288,128]{1,0:T(8,128)S(1)}, u32[]{:S(2)}, u32[]{:S(2)}) collective-permute-start(f32[288,128]{1,0:T(8,128)S(1)} %get-tuple-element.68), channel_id=1, source_target_pairs={{0,4},{4,8},{8,12},{12,16},{16,20},{20,24},{24,28},{28,32},{32,36}... | collective-permute-start | bytes 442376 | tf_op jit(solution)/shard_map/ppermute | solution.py:531
  64.6 1.9 collective-permute-start.13
  66.5 3.9 %collective-permute-start.14 = (f32[32,128]{1,0:T(8,128)S(1)}, f32[32,128]{1,0:T(8,128)S(1)}, u32[]{:S(2)}, u32[]{:S(2)}) collective-permute-start(f32[32,128]{1,0:T(8,128)S(1)} %get-tuple-element.72), channel_id=1, source_target_pairs={{0,4},{4,8},{8,12},{12,16},{16,20},{20,24},{24,28},{28,32},{32,36}... | collective-permute-start | bytes 49160 | tf_op jit(solution)/shard_map/ppermute | solution.py:531
  70.5 1.9 collective-permute-start.15
  73.2 6.3 %collective-permute-done.15.chi_ref = f32[32,128]{1,0:T(8,128)S(1)} collective-permute-done((f32[32,128]{1,0:T(8,128)S(1)}, f32[32,128]{1,0:T(8,128)S(1)}, u32[]{:S(2)}, u32[]{:S(2)}) %collective-permute-start.15) | collective-permute-done | bytes 16416 | tf_op jit(solution)/shard_map/ppermute | solution.py:531
  79.4 3.7 %step.4 = (f32[768,128]{1,0:T(8,128)S(1)}, f32[408,128]{1,0:T(8,128)S(1)}, f32[408,128]{1,0:T(8,128)S(1)}, f32[288,128]{1,0:T(8,128)S(1)}, f32[288,128]{1,0:T(8,128)S(1)}, /*index=5*/f32[48,128]{1,0:T(8,128)S(1)}) custom-call(f32[768,128]{1,0:T(8,128)S(1)} %get-tuple-element.65.y_ref.prev_ref, f32[768,128]{1,0:T(8,128)S(1)} %get-tuple-element.45.y_ref.prev_ref, ...), custom_call_target="tpu_custom_call" | custom-call | tf_op jit(solution)/shard_map/step/pallas_call | solution.py:586
  83.1 2.3 %collective-permute-start.16 = (f32[408,128]{1,0:T(8,128)S(1)}, f32[408,128]{1,0:T(8,128)S(1)}, u32[]{:S(2)}, u32[]{:S(2)}) collective-permute-start(f32[408,128]{1,0:T(8,128)S(1)} %get-tuple-element.75), channel_id=1, source_target_pairs={{0,64},{64,128},{128,192},{192,256},{256,320},{320,384},{384,448},... | collective-permute-start | bytes 626696 | tf_op jit(solution)/shard_map/ppermute | solution.py:531
  85.4 1.3 collective-permute-start.17
  86.7 11.1 %collective-permute-start.18 = (f32[288,128]{1,0:T(8,128)S(1)}, f32[288,128]{1,0:T(8,128)S(1)}, u32[]{:S(2)}, u32[]{:S(2)}) collective-permute-start(f32[288,128]{1,0:T(8,128)S(1)} %get-tuple-element.77), channel_id=1, source_target_pairs={{0,4},{4,8},{8,12},{12,16},{16,20},{20,24},{24,28},{28,32},{32,36}... | collective-permute-start | bytes 442376 | tf_op jit(solution)/shard_map/ppermute | solution.py:531
  97.8 1.9 collective-permute-start.19
  99.8 4.9 %collective-permute-start.20 = (f32[32,128]{1,0:T(8,128)S(1)}, f32[32,128]{1,0:T(8,128)S(1)}, u32[]{:S(2)}, u32[]{:S(2)}) collective-permute-start(f32[32,128]{1,0:T(8,128)S(1)} %get-tuple-element.81), channel_id=1, source_target_pairs={{0,4},{4,8},{8,12},{12,16},{16,20},{20,24},{24,28},{28,32},{32,36}... | collective-permute-start | bytes 49160 | tf_op jit(solution)/shard_map/ppermute | solution.py:531
  104.6 1.9 collective-permute-start.21
  106.6 6.8 %collective-permute-done.21.chi_ref = f32[32,128]{1,0:T(8,128)S(1)} collective-permute-done((f32[32,128]{1,0:T(8,128)S(1)}, f32[32,128]{1,0:T(8,128)S(1)}, u32[]{:S(2)}, u32[]{:S(2)}) %collective-permute-start.21) | collective-permute-done | bytes 16416 | tf_op jit(solution)/shard_map/ppermute | solution.py:531
  113.4 2.9 %step.5.a0 = f32[768,128]{1,0:T(8,128)S(1)} custom-call(f32[768,128]{1,0:T(8,128)S(1)} %get-tuple-element.74.y_ref, f32[768,128]{1,0:T(8,128)S(1)} %get-tuple-element.65.y_ref.prev_ref, f32[408,128]{1,0:T(8,128)S(1)} %collective-permute-done.16.fl_ref, f32[408,128]{1,0:T(8,128)S(1)} %collective-permute-done.17.fr_ref, ...), custom_call_target="tpu_custom_call" | custom-call | tf_op jit(solution)/shard_map/step/pallas_call | solution.py:586
  116.3 12.5 %all_to_all.20.parts_ref = f32[4,192,128]{2,1,0:T(8,128)S(1)} all-to-all(f32[4,192,128]{2,1,0:T(8,128)S(1)} %bitcast.5), channel_id=1, replica_groups=mesh['gx'=8,'gy'=16,'orb'=4] {'orb'}, dimensions={0} | all-to-all | bytes 786432 | tf_op jit(solution)/shard_map/all_to_all | solution.py:613
  128.8 2.5 %collective-permute-start.22 = (f32[768,128]{1,0:T(8,128)S(1)}, f32[768,128]{1,0:T(8,128)S(1)}, u32[]{:S(2)}, u32[]{:S(2)}) collective-permute-start(f32[768,128]{1,0:T(8,128)S(1)} %step.5.a0), channel_id=1, source_target_pairs={{0,1},{1,2},{2,3},{3,0},{4,5},{5,6},{6,7},{7,4},{8,9},{9,10},{10,1... | collective-permute-start | bytes 1179656 | tf_op jit(solution)/shard_map/ppermute | solution.py:616
  131.2 4.6 %collective-permute-start.23 = (f32[768,128]{1,0:T(8,128)S(1)}, f32[768,128]{1,0:T(8,128)S(1)}, u32[]{:S(2)}, u32[]{:S(2)}) collective-permute-start(f32[768,128]{1,0:T(8,128)S(1)} %step.5.a0), channel_id=1, source_target_pairs={{0,3},{1,0},{2,1},{3,2},{4,7},{5,4},{6,5},{7,6},{8,11},{9,8},{10,9... | collective-permute-start | bytes 1179656 | tf_op jit(solution)/shard_map/ppermute | solution.py:617
  135.8 8.0 %collective-permute-done.22.a1 = f32[768,128]{1,0:T(8,128)S(1)} collective-permute-done((f32[768,128]{1,0:T(8,128)S(1)}, f32[768,128]{1,0:T(8,128)S(1)}, u32[]{:S(2)}, u32[]{:S(2)}) %collective-permute-start.22) | collective-permute-done | bytes 393248 | tf_op jit(solution)/shard_map/ppermute | solution.py:616
  143.8 1.9 collective-permute-start.24
  145.8 5.1 %collective-permute-start.25 = (f32[384,128]{1,0:T(8,128)S(1)}, f32[384,128]{1,0:T(8,128)S(1)}, u32[]{:S(2)}, u32[]{:S(2)}) collective-permute-start(f32[384,128]{1,0:T(8,128)S(1)} %slice.9), channel_id=1, source_target_pairs={{0,3},{1,0},{2,1},{3,2},{4,7},{5,4},{6,5},{7,6},{8,11},{9,8},{10,9... | collective-permute-start | bytes 589832 | tf_op jit(solution)/shard_map/ppermute | solution.py:620
  150.9 1.1 gram.1
  152.0 7.7 %all_to_all.21 = f32[4,8,128]{2,1,0:T(8,128)S(1)} all-to-all(f32[4,8,128]{2,1,0:T(8,128)S(1)} %broadcast_in_dim.6), channel_id=1, replica_groups=mesh['gx'=8,'gy'=16,'orb'=4] {'orb'}, dimensions={0} | all-to-all | bytes 32768 | tf_op jit(solution)/shard_map/all_to_all | solution.py:626
  159.7 8.8 %all_to_all.22 = f32[8,8,128]{2,1,0:T(8,128)S(1)} all-to-all(f32[8,8,128]{2,1,0:T(8,128)S(1)} %broadcast_in_dim.7), channel_id=1, replica_groups=mesh['gx'=8,'gy'=16,'orb'=4] {'gx'}, dimensions={0} | all-to-all | bytes 65536 | tf_op jit(solution)/shard_map/all_to_all | solution.py:626
  169.2 31.5 %all-to-all-start.3 = ((f32[16,8,128]{2,1,0:T(8,128)}), f32[16,8,128]{2,1,0:T(8,128)S(1)}, u32[]{:S(2)}, u32[]{:S(2)}) async-start(f32[16,8,128]{2,1,0:T(8,128)} %broadcast_in_dim.8), calls=%async_computation.3 | async-start | bytes 131072 | tf_op jit(solution)/shard_map/all_to_all | solution.py:626
  200.8 11.4 %all-to-all-done.3 = f32[16,8,128]{2,1,0:T(8,128)S(1)} async-done(((f32[16,8,128]{2,1,0:T(8,128)}), f32[16,8,128]{2,1,0:T(8,128)S(1)}, u32[]{:S(2)}, u32[]{:S(2)}) %all-to-all-start.3) | async-done | bytes 65568 | tf_op jit(solution)/shard_map/all_to_all | solution.py:626
  212.3 4.1 %rotate.1 = f32[4,12,16,128]{3,2,1,0:T(8,128)} custom-call(s32[4]{0:T(128)S(1)} %pad_add_fusion.order, f32[8,128]{1,0:T(8,128)S(1)} %reduce_sum.29.corr_ref, f32[768,128]{1,0:T(8,128)S(1)} %step.5.a0, f32[768,128]{1,0:T(8,128)S(1)} %collective-permute-done.22.a1, f32[768,128]{1,0:T(8,128)S(1)} %collective-permute-done.23.a2, f32[768,128]{1,0:T(8,128)S(1)} %pad_maximum_fusion.a3), custom_call_target="tpu_custom_call" | custom-call | tf_op jit(solution)/shard_map/rotate/pallas_call | solution.py:628
  (52 shorter events, 7.7 us)
Async XLA Ops:
  0.0 51.5 %copy-start.1 = (bf16[1024,128]{1,0:T(8,128)(2,1)S(1)}, bf16[1024,128]{1,0:T(8,128)(2,1)}, u32[]{:S(2)}) copy-start(bf16[1024,128]{1,0:T(8,128)(2,1)} %constant.38.clone.g_ref) | copy-start | bytes 786436
  1.5 0.9 copy-start.4
  2.3 1.0 copy-start.6
  3.3 0.9 copy-start.7
  4.3 0.7 copy-start.9
  6.3 11.7 %collective-permute-start = (f32[616,128]{1,0:T(8,128)S(1)}, f32[616,128]{1,0:T(8,128)S(1)}, u32[]{:S(2)}, u32[]{:S(2)}) collective-permute-start(f32[616,128]{1,0:T(8,128)S(1)} %get-tuple-element.46), channel_id=1, source_target_pairs={{0,64},{64,128},{128,192},{192,256},{256,320},{320,384},{384,448},... | collective-permute-start | bytes 946184 | tf_op jit(solution)/shard_map/ppermute | solution.py:531
  8.0 9.9 %collective-permute-start.1 = (f32[616,128]{1,0:T(8,128)S(1)}, f32[616,128]{1,0:T(8,128)S(1)}, u32[]{:S(2)}, u32[]{:S(2)}) collective-permute-start(f32[616,128]{1,0:T(8,128)S(1)} %get-tuple-element.47), channel_id=1, source_target_pairs={{64,0},{128,64},{192,128},{256,192},{320,256},{384,320},{448,384},... | collective-permute-start | bytes 946184 | tf_op jit(solution)/shard_map/ppermute | solution.py:531
  9.3 37.5 %collective-permute-start.2 = (f32[384,128]{1,0:T(8,128)S(1)}, f32[384,128]{1,0:T(8,128)S(1)}, u32[]{:S(2)}, u32[]{:S(2)}) collective-permute-start(f32[384,128]{1,0:T(8,128)S(1)} %get-tuple-element.48), channel_id=1, source_target_pairs={{0,4},{4,8},{8,12},{12,16},{16,20},{20,24},{24,28},{28,32},{32,36}... | collective-permute-start | bytes 589832 | tf_op jit(solution)/shard_map/ppermute | solution.py:531
  12.8 34.0 %collective-permute-start.3 = (f32[384,128]{1,0:T(8,128)S(1)}, f32[384,128]{1,0:T(8,128)S(1)}, u32[]{:S(2)}, u32[]{:S(2)}) collective-permute-start(f32[384,128]{1,0:T(8,128)S(1)} %get-tuple-element.49), channel_id=1, source_target_pairs={{4,0},{8,4},{12,8},{16,12},{20,16},{24,20},{28,24},{32,28},{36,32}... | collective-permute-start | bytes 589832 | tf_op jit(solution)/shard_map/ppermute | solution.py:531
  18.1 8.1 %collective-permute-start.4 = (f32[272,128]{1,0:T(8,128)S(1)}, f32[272,128]{1,0:T(8,128)S(1)}, u32[]{:S(2)}, u32[]{:S(2)}) collective-permute-start(f32[272,128]{1,0:T(8,128)S(1)} %get-tuple-element.54), channel_id=1, source_target_pairs={{0,4},{4,8},{8,12},{12,16},{16,20},{20,24},{24,28},{28,32},{32,36}... | collective-permute-start | bytes 417800 | tf_op jit(solution)/shard_map/ppermute | solution.py:531
  20.0 8.0 %collective-permute-start.5 = (f32[272,128]{1,0:T(8,128)S(1)}, f32[272,128]{1,0:T(8,128)S(1)}, u32[]{:S(2)}, u32[]{:S(2)}) collective-permute-start(f32[272,128]{1,0:T(8,128)S(1)} %get-tuple-element.55), channel_id=1, source_target_pairs={{4,0},{8,4},{12,8},{16,12},{20,16},{24,20},{28,24},{32,28},{36,32}... | collective-permute-start | bytes 417800 | tf_op jit(solution)/shard_map/ppermute | solution.py:531
  28.0 0.9 copy-start
  31.3 3.6 %collective-permute-start.6 = (f32[24,128]{1,0:T(8,128)S(1)}, f32[24,128]{1,0:T(8,128)S(1)}, u32[]{:S(2)}, u32[]{:S(2)}) collective-permute-start(f32[24,128]{1,0:T(8,128)S(1)} %get-tuple-element.60), channel_id=1, source_target_pairs={{0,64},{64,128},{128,192},{192,256},{256,320},{320,384},{384,448},... | collective-permute-start | bytes 36872 | tf_op jit(solution)/shard_map/ppermute | solution.py:531
  33.6 6.7 %collective-permute-start.7 = (f32[24,128]{1,0:T(8,128)S(1)}, f32[24,128]{1,0:T(8,128)S(1)}, u32[]{:S(2)}, u32[]{:S(2)}) collective-permute-start(f32[24,128]{1,0:T(8,128)S(1)} %get-tuple-element.61), channel_id=1, source_target_pairs={{64,0},{128,64},{192,128},{256,192},{320,256},{384,320},{448,384},... | collective-permute-start | bytes 36872 | tf_op jit(solution)/shard_map/ppermute | solution.py:531
  40.4 10.3 %collective-permute-start.8 = (f32[32,128]{1,0:T(8,128)S(1)}, f32[32,128]{1,0:T(8,128)S(1)}, u32[]{:S(2)}, u32[]{:S(2)}) collective-permute-start(f32[32,128]{1,0:T(8,128)S(1)} %get-tuple-element.63), channel_id=1, source_target_pairs={{0,4},{4,8},{8,12},{12,16},{16,20},{20,24},{24,28},{28,32},{32,36}... | collective-permute-start | bytes 49160 | tf_op jit(solution)/shard_map/ppermute | solution.py:531
  44.9 6.6 %collective-permute-start.9 = (f32[32,128]{1,0:T(8,128)S(1)}, f32[32,128]{1,0:T(8,128)S(1)}, u32[]{:S(2)}, u32[]{:S(2)}) collective-permute-start(f32[32,128]{1,0:T(8,128)S(1)} %get-tuple-element.64), channel_id=1, source_target_pairs={{4,0},{8,4},{12,8},{16,12},{20,16},{24,20},{28,24},{32,28},{36,32}... | collective-permute-start | bytes 49160 | tf_op jit(solution)/shard_map/ppermute | solution.py:531
  46.9 0.9 copy-start.2
  47.8 0.9 copy-start.5
  48.7 0.9 copy-start.8
  50.6 28.8 %copy-start.3 = (bf16[256,256]{1,0:T(8,128)(2,1)S(1)}, bf16[256,256]{1,0:T(8,128)(2,1)}, u32[]{:S(2)}) copy-start(bf16[256,256]{1,0:T(8,128)(2,1)} %constant.37.clone.dz_ref) | copy-start | bytes 393220
  55.1 11.4 %collective-permute-start.10 = (f32[408,128]{1,0:T(8,128)S(1)}, f32[408,128]{1,0:T(8,128)S(1)}, u32[]{:S(2)}, u32[]{:S(2)}) collective-permute-start(f32[408,128]{1,0:T(8,128)S(1)} %get-tuple-element.66), channel_id=1, source_target_pairs={{0,64},{64,128},{128,192},{192,256},{256,320},{320,384},{384,448},... | collective-permute-start | bytes 626696 | tf_op jit(solution)/shard_map/ppermute | solution.py:531
  58.4 8.1 %collective-permute-start.11 = (f32[408,128]{1,0:T(8,128)S(1)}, f32[408,128]{1,0:T(8,128)S(1)}, u32[]{:S(2)}, u32[]{:S(2)}) collective-permute-start(f32[408,128]{1,0:T(8,128)S(1)} %get-tuple-element.67), channel_id=1, source_target_pairs={{64,0},{128,64},{192,128},{256,192},{320,256},{384,320},{448,384},... | collective-permute-start | bytes 626696 | tf_op jit(solution)/shard_map/ppermute | solution.py:531
  59.7 12.7 %collective-permute-start.12 = (f32[288,128]{1,0:T(8,128)S(1)}, f32[288,128]{1,0:T(8,128)S(1)}, u32[]{:S(2)}, u32[]{:S(2)}) collective-permute-start(f32[288,128]{1,0:T(8,128)S(1)} %get-tuple-element.68), channel_id=1, source_target_pairs={{0,4},{4,8},{8,12},{12,16},{16,20},{20,24},{24,28},{28,32},{32,36}... | collective-permute-start | bytes 442376 | tf_op jit(solution)/shard_map/ppermute | solution.py:531
  64.6 8.6 %collective-permute-start.13 = (f32[288,128]{1,0:T(8,128)S(1)}, f32[288,128]{1,0:T(8,128)S(1)}, u32[]{:S(2)}, u32[]{:S(2)}) collective-permute-start(f32[288,128]{1,0:T(8,128)S(1)} %get-tuple-element.69), channel_id=1, source_target_pairs={{4,0},{8,4},{12,8},{16,12},{20,16},{24,20},{28,24},{32,28},{36,32}... | collective-permute-start | bytes 442376 | tf_op jit(solution)/shard_map/ppermute | solution.py:531
  66.5 6.6 %collective-permute-start.14 = (f32[32,128]{1,0:T(8,128)S(1)}, f32[32,128]{1,0:T(8,128)S(1)}, u32[]{:S(2)}, u32[]{:S(2)}) collective-permute-start(f32[32,128]{1,0:T(8,128)S(1)} %get-tuple-element.72), channel_id=1, source_target_pairs={{0,4},{4,8},{8,12},{12,16},{16,20},{20,24},{24,28},{28,32},{32,36}... | collective-permute-start | bytes 49160 | tf_op jit(solution)/shard_map/ppermute | solution.py:531
  70.5 9.0 %collective-permute-start.15 = (f32[32,128]{1,0:T(8,128)S(1)}, f32[32,128]{1,0:T(8,128)S(1)}, u32[]{:S(2)}, u32[]{:S(2)}) collective-permute-start(f32[32,128]{1,0:T(8,128)S(1)} %get-tuple-element.73), channel_id=1, source_target_pairs={{4,0},{8,4},{12,8},{16,12},{20,16},{24,20},{28,24},{32,28},{36,32}... | collective-permute-start | bytes 49160 | tf_op jit(solution)/shard_map/ppermute | solution.py:531
  83.1 16.6 %collective-permute-start.16 = (f32[408,128]{1,0:T(8,128)S(1)}, f32[408,128]{1,0:T(8,128)S(1)}, u32[]{:S(2)}, u32[]{:S(2)}) collective-permute-start(f32[408,128]{1,0:T(8,128)S(1)} %get-tuple-element.75), channel_id=1, source_target_pairs={{0,64},{64,128},{128,192},{192,256},{256,320},{320,384},{384,448},... | collective-permute-start | bytes 626696 | tf_op jit(solution)/shard_map/ppermute | solution.py:531
  85.4 14.4 %collective-permute-start.17 = (f32[408,128]{1,0:T(8,128)S(1)}, f32[408,128]{1,0:T(8,128)S(1)}, u32[]{:S(2)}, u32[]{:S(2)}) collective-permute-start(f32[408,128]{1,0:T(8,128)S(1)} %get-tuple-element.76), channel_id=1, source_target_pairs={{64,0},{128,64},{192,128},{256,192},{320,256},{384,320},{448,384},... | collective-permute-start | bytes 626696 | tf_op jit(solution)/shard_map/ppermute | solution.py:531
  86.7 19.9 %collective-permute-start.18 = (f32[288,128]{1,0:T(8,128)S(1)}, f32[288,128]{1,0:T(8,128)S(1)}, u32[]{:S(2)}, u32[]{:S(2)}) collective-permute-start(f32[288,128]{1,0:T(8,128)S(1)} %get-tuple-element.77), channel_id=1, source_target_pairs={{0,4},{4,8},{8,12},{12,16},{16,20},{20,24},{24,28},{28,32},{32,36}... | collective-permute-start | bytes 442376 | tf_op jit(solution)/shard_map/ppermute | solution.py:531
  97.8 8.8 %collective-permute-start.19 = (f32[288,128]{1,0:T(8,128)S(1)}, f32[288,128]{1,0:T(8,128)S(1)}, u32[]{:S(2)}, u32[]{:S(2)}) collective-permute-start(f32[288,128]{1,0:T(8,128)S(1)} %get-tuple-element.78), channel_id=1, source_target_pairs={{4,0},{8,4},{12,8},{16,12},{20,16},{24,20},{28,24},{32,28},{36,32}... | collective-permute-start | bytes 442376 | tf_op jit(solution)/shard_map/ppermute | solution.py:531
  99.8 6.8 %collective-permute-start.20 = (f32[32,128]{1,0:T(8,128)S(1)}, f32[32,128]{1,0:T(8,128)S(1)}, u32[]{:S(2)}, u32[]{:S(2)}) collective-permute-start(f32[32,128]{1,0:T(8,128)S(1)} %get-tuple-element.81), channel_id=1, source_target_pairs={{0,4},{4,8},{8,12},{12,16},{16,20},{20,24},{24,28},{28,32},{32,36}... | collective-permute-start | bytes 49160 | tf_op jit(solution)/shard_map/ppermute | solution.py:531
  104.6 8.7 %collective-permute-start.21 = (f32[32,128]{1,0:T(8,128)S(1)}, f32[32,128]{1,0:T(8,128)S(1)}, u32[]{:S(2)}, u32[]{:S(2)}) collective-permute-start(f32[32,128]{1,0:T(8,128)S(1)} %get-tuple-element.82), channel_id=1, source_target_pairs={{4,0},{8,4},{12,8},{16,12},{20,16},{24,20},{28,24},{32,28},{36,32}... | collective-permute-start | bytes 49160 | tf_op jit(solution)/shard_map/ppermute | solution.py:531
  128.8 15.0 %collective-permute-start.22 = (f32[768,128]{1,0:T(8,128)S(1)}, f32[768,128]{1,0:T(8,128)S(1)}, u32[]{:S(2)}, u32[]{:S(2)}) collective-permute-start(f32[768,128]{1,0:T(8,128)S(1)} %step.5.a0), channel_id=1, source_target_pairs={{0,1},{1,2},{2,3},{3,0},{4,5},{5,6},{6,7},{7,4},{8,9},{9,10},{10,1... | collective-permute-start | bytes 1179656 | tf_op jit(solution)/shard_map/ppermute | solution.py:616
  131.2 14.5 %collective-permute-start.23 = (f32[768,128]{1,0:T(8,128)S(1)}, f32[768,128]{1,0:T(8,128)S(1)}, u32[]{:S(2)}, u32[]{:S(2)}) collective-permute-start(f32[768,128]{1,0:T(8,128)S(1)} %step.5.a0), channel_id=1, source_target_pairs={{0,3},{1,0},{2,1},{3,2},{4,7},{5,4},{6,5},{7,6},{8,11},{9,8},{10,9... | collective-permute-start | bytes 1179656 | tf_op jit(solution)/shard_map/ppermute | solution.py:617
  143.8 68.5 %collective-permute-start.24 = (f32[384,128]{1,0:T(8,128)S(1)}, f32[384,128]{1,0:T(8,128)S(1)}, u32[]{:S(2)}, u32[]{:S(2)}) collective-permute-start(f32[384,128]{1,0:T(8,128)S(1)} %slice.8), channel_id=1, source_target_pairs={{0,1},{1,2},{2,3},{3,0},{4,5},{5,6},{6,7},{7,4},{8,9},{9,10},{10,1... | collective-permute-start | bytes 589832 | tf_op jit(solution)/shard_map/ppermute | solution.py:619
  145.8 66.5 %collective-permute-start.25 = (f32[384,128]{1,0:T(8,128)S(1)}, f32[384,128]{1,0:T(8,128)S(1)}, u32[]{:S(2)}, u32[]{:S(2)}) collective-permute-start(f32[384,128]{1,0:T(8,128)S(1)} %slice.9), channel_id=1, source_target_pairs={{0,3},{1,0},{2,1},{3,2},{4,7},{5,4},{6,5},{7,6},{8,11},{9,8},{10,9... | collective-permute-start | bytes 589832 | tf_op jit(solution)/shard_map/ppermute | solution.py:620
  169.2 43.0 %all-to-all-start.3 = ((f32[16,8,128]{2,1,0:T(8,128)}), f32[16,8,128]{2,1,0:T(8,128)S(1)}, u32[]{:S(2)}, u32[]{:S(2)}) async-start(f32[16,8,128]{2,1,0:T(8,128)} %broadcast_in_dim.8), calls=%async_computation.3 | async-start | bytes 131072 | tf_op jit(solution)/shard_map/all_to_all | solution.py:626

commit v3 on v2

--- a/solution.py
+++ b/solution.py
@@ -44,15 +44,6 @@
     return np.concatenate([high, low], axis=0)
 
 
-def group_table():
-    table = np.zeros((8 * 128, 128), np.float32)
-    for p in range(8):
-        for slot in range(16):
-            for k in range(8):
-                table[p * 128 + slot * 8 + k, slot * 8 + p] = 1.0
-    return table.astype(ml_dtypes.bfloat16)
-
-
 def split(a):
     high = a.astype(BF16)
     return high, (a - high.astype(F32)).astype(BF16)
@@ -106,8 +97,27 @@
             put(lo_ref, x * 3 + m, jnp.where(low, get(y_ref, x * 8 + m), pltpu.roll(get(y_ref, x * 8 + 3 + m), 4, 0)))
 
 
-def prep_kernel(offs, strg, cnt, orb, mu, proj, y_ref, t_ref, meta_ref, xr_ref, xl_ref, yh_ref, yl_ref):
+def put_seam(refs, count, tile, value):
+    half = count // 2
+    put(refs[tile // half], tile % half, value)
+
+
+def get_seam(refs, count, tile):
+    half = count // 2
+    return get(refs[tile // half], tile % half)
+
+
+def prep_kernel(
+    flags, offs, strg, cnt, orb, mu, proj,
+    y_ref, t_ref, meta_ref, xr_ref, xl_ref, yh_ref, yl_ref, sa_ref, sb_ref, mu_out, g_ref
+):
+    mu_out[...] = mu[...]
+    at_row = lax.broadcasted_iota(jnp.int32, (1024, 128), 0)
+    at_column = lax.broadcasted_iota(jnp.int32, (1024, 128), 1)
+    same = (at_row % 128 // 8 == at_column // 8) & (at_row // 128 == at_column % 8)
+    g_ref[...] = jnp.where(same, 1.0, 0.0).astype(BF16)
     sub, lane = iotas()
+    above_seam = flags[0] == 1
     low = sub < 4
     left_half = lane < 64
     for x in range(CX):
@@ -115,17 +125,15 @@
             for h in range(2):
                 y_ref[pl.ds(x * 64 + 4 * h + o, 8, stride=8), :] = orb[o, x, 8 * h : 8 * h + 8, :]
     group = lane // 8
-    place = lane % 8
     meta = jnp.zeros((8, 128), F32)
     for s in range(8):
         for column in range(3):
-            value = offs[s, column].astype(F32)
+            value = offs[column, s].astype(F32)
             meta = jnp.where((group == s) & (sub == column), value, meta)
         alive = jnp.where(s < cnt[0], 1.0, 0.0).astype(F32)
         for p in range(8):
             weight = strg[s, p] * alive * (1.0 / (512.0 * filter_half))
             meta = jnp.where((lane == s * 8 + p) & (sub == 3), weight, meta)
-    del place
     meta_ref[...] = meta
     for i in range(8):
         for j in range(8):
@@ -157,13 +165,19 @@
     for x in range(CX):
         put(yh_ref, YH + x, mu[x, 8:16, :])
         put(yl_ref, YH + x, mu[x, 0:8, :])
+    pick_seam(yh_ref, yl_ref, (sa_ref, sb_ref), FIRST_Y, above_seam)
+
+
+def pick_seam(hi_ref, lo_ref, seams, count, above_seam):
+    for t in range(count):
+        put_seam(seams, count, t, jnp.where(above_seam, get(lo_ref, t), get(hi_ref, t)))
 
 
 FIRST_X = XH + 2 * HALO + 17
 FIRST_Y = YH + CX
 
 
-def widen_kernel(t_ref, meta_ref, fl_ref, fr_ref, t2_ref, m_ref, hi_ref, lo_ref):
+def widen_kernel(flags, t_ref, meta_ref, fl_ref, fr_ref, t2_ref, m_ref, hi_ref, lo_ref, sa_ref, sb_ref):
     _, lane = iotas()
     left_half = lane < 64
     base = XH + 2 * HALO
@@ -187,9 +201,10 @@
         put(m_ref, side, both)
         put(hi_ref, 32 + side, both)
         put(lo_ref, 32 + side, both)
-
-
-def coef_kernel(mu, pot, fl_ref, fr_ref, flo_ref, fhi_ref, dz_ref, out_ref, ex, ey):
+    pick_seam(hi_ref, lo_ref, (sa_ref, sb_ref), 34, flags[0] == 1)
+
+
+def coef_kernel(flags, mu, pot, fl_ref, fr_ref, flo_ref, fhi_ref, sa_ref, sb_ref, dz_ref, out_ref, ex, ey):
     sub, _ = iotas()
     low = sub < 4
 
@@ -206,7 +221,10 @@
         for yl in range(8):
             put(ex, x * 8 + yl, two(a, yl, b, yl))
     for x in range(CX):
-        parts = [get(flo_ref, YH + x), mu[x, 0:8, :], mu[x, 8:16, :], get(fhi_ref, YH + x)]
+        rim = get_seam((sa_ref, sb_ref), FIRST_Y, YH + x)
+        lo_rim = jnp.where(flags[0] == 1, rim, get(flo_ref, YH + x))
+        hi_rim = jnp.where(flags[1] == 1, rim, get(fhi_ref, YH + x))
+        parts = [lo_rim, mu[x, 0:8, :], mu[x, 8:16, :], hi_rim]
         for n in range(20):
             y = n - HALO
             put(ey, x * 20 + n, two(parts[(y + 8) // 8], y % 8, parts[(y + 16) // 8], y % 8))
@@ -287,7 +305,14 @@
         put(xl_ref, base + t, pltpu.roll(get(z_ref, t), 64, 1))
 
 
-def build_kernel(t2_ref, m_ref, lo_ref, hi_ref, y_ref, g_ref, q_ref, s_ref, w_ref, z_ref, xr_ref, xl_ref, tx, acc):
+def build_kernel(
+    flags, t2_ref, m_ref, lo_in, hi_in, sa_ref, sb_ref, y_ref, g_ref,
+    q_ref, s_ref, w_ref, z_ref, xr_ref, xl_ref, tx, acc, lo_ref, hi_ref
+):
+    for t in range(34):
+        seam = get_seam((sa_ref, sb_ref), 34, t)
+        put(lo_ref, t, jnp.where(flags[0] == 1, seam, get(lo_in, t)))
+        put(hi_ref, t, jnp.where(flags[1] == 1, seam, get(hi_in, t)))
     sub, lane = iotas()
     low = sub < 4
     right_half = lane >= 64
@@ -363,14 +388,14 @@
 
 
 def step_kernel(
-    step, y_ref, prev_ref, fl_ref, fr_ref, plo_ref, phi_ref, coef_ref, q_ref, s_ref, w_ref, z_ref, clo_ref, chi_ref,
+    step, seam_count, flags, y_ref, prev_ref, fl_ref, fr_ref, plo_ref, phi_ref, sa_ref, sb_ref, coef_ref, q_ref, s_ref, w_ref, z_ref, clo_ref, chi_ref,
     dz_ref, g_ref, *rest
 ):
     last = step == STEPS
     if last:
         new_ref, ex, ey, zd, acc, wp = rest
     else:
-        new_ref, xr_ref, xl_ref, yh_ref, yl_ref, zn_ref, ex, ey, zd, acc, wp = rest
+        new_ref, xr_ref, xl_ref, yh_ref, yl_ref, na_ref, nb_ref, zn_ref, ex, ey, zd, acc, wp = rest
     sub, _ = iotas()
     low = sub < 4
     scale = 1.0 if step == 1 else 2.0
@@ -384,10 +409,15 @@
     for x in range(CX):
         for yl in range(8):
             put(ey, x * 20 + HALO + yl, get(y_ref, x * 8 + yl))
+        lo_rims, hi_rims = [], []
+        for m in range(3):
+            seam = get_seam((sa_ref, sb_ref), seam_count, x * 3 + m)
+            lo_rims.append(jnp.where(flags[0] == 1, seam, get(plo_ref, x * 3 + m)))
+            hi_rims.append(jnp.where(flags[1] == 1, seam, get(phi_ref, x * 3 + m)))
         for m in range(HALO):
-            rim = get(plo_ref, x * 3 + m) if m < 3 else pltpu.roll(get(plo_ref, x * 3 + m - 3), 4, 0)
+            rim = lo_rims[m] if m < 3 else pltpu.roll(lo_rims[m - 3], 4, 0)
             put(ey, x * 20 + m, jnp.where(low, rim, pltpu.roll(get(y_ref, x * 8 + 2 + m), 4, 0)))
-            rim = pltpu.roll(get(phi_ref, x * 3 + m), 4, 0) if m < 3 else get(phi_ref, x * 3 + m - 3)
+            rim = pltpu.roll(hi_rims[m], 4, 0) if m < 3 else hi_rims[m - 3]
             put(ey, x * 20 + HALO + 8 + m, jnp.where(low, pltpu.roll(get(y_ref, x * 8 + m), 4, 0), rim))
 
     def body(x, carry):
@@ -444,6 +474,7 @@
             put(xr_ref, q, get(new_ref, XH + q))
             put(xl_ref, q, get(new_ref, q))
         pack_rims(new_ref, yh_ref, yl_ref, low)
+        pick_seam(yh_ref, yl_ref, (na_ref, nb_ref), YH, flags[0] == 1)
         partial_coeffs(new_ref, q_ref, s_ref, g_ref, zn_ref, acc)
         send_coeffs(zn_ref, xr_ref, xl_ref, XH)
 
@@ -531,6 +562,38 @@
     return lax.ppermute(low_value, axis, up), lax.ppermute(high_value, axis, down)
 
 
+def across_seam(part_a, part_b):
+    size, depth = lax.axis_size("gy"), lax.axis_size("gx") // 2
+    half = size // 2
+
+    def index(z, core, y):
+        z = z % (2 * depth)
+        return (z % depth * 2 + core) * size + z // depth * half + y
+
+    first, second = [], []
+    for z in range(2 * depth):
+        for core in range(2):
+            own, other = (half - 1, 0) if z < depth else (0, half - 1)
+            stop = index(z - depth // 2, core, own)
+            first.append((index(z, core, own), stop))
+            second.append((stop, index(z + depth, core, other)))
+    stopped = lax.ppermute(part_b, ("gx", "gy"), first)
+    straight = lax.ppermute(part_a, "gy", [(half - 1, half), (half, half - 1)])
+    return straight, lax.ppermute(stopped, ("gx", "gy"), second)
+
+
+def beside_in_half(low_value, high_value, axis):
+    count = lax.axis_size(axis)
+    steps = [i for i in range(count - 1) if i != count // 2 - 1]
+    up, down = [(i, i + 1) for i in steps], [(i + 1, i) for i in steps]
+    return lax.ppermute(low_value, axis, up), lax.ppermute(high_value, axis, down)
+
+
+def spread_sum(value, axis):
+    copies = jnp.broadcast_to(value[None], (lax.axis_size(axis),) + value.shape)
+    return jnp.sum(lax.all_to_all(copies, axis, 0, 0, tiled=True), axis=0)
+
+
 def fold(z, from_left, from_right, tile):
     return kernel_call(
         functools.partial(fold_kernel, tile), [blocks(6), blocks(4), blocks(4)], [VMEM] * 3, name="fold_coeffs"
@@ -539,40 +602,45 @@
 
 def shards(orbitals, potential, kinetic_mu, projectors, strengths, box_offsets, block_counts):
     dz = jnp.asarray(derivative_table())
-    groups = jnp.asarray(group_table())
-    y, t, meta, xr, xl, yh, yl = kernel_call(
+    row_at, rows = lax.axis_index("gy"), lax.axis_size("gy")
+    flags = jnp.stack([row_at == rows // 2, row_at == rows // 2 - 1]).astype(jnp.int32)
+    y, t, meta, xr, xl, yh, yl, sa, sb, mu, groups = kernel_call(
         prep_kernel,
-        [blocks(TILES), blocks(64), blocks(1), blocks(FIRST_X), blocks(FIRST_X), blocks(FIRST_Y), blocks(FIRST_Y)],
-        [SMEM, SMEM, SMEM, VMEM, VMEM, VMEM],
+        [blocks(TILES), blocks(64), blocks(1), blocks(FIRST_X), blocks(FIRST_X), blocks(FIRST_Y), blocks(FIRST_Y)]
+        + [blocks(FIRST_Y // 2), blocks(FIRST_Y // 2), ((CX, CY, NZ), F32), ((1024, 128), BF16)],
+        [SMEM] * 4 + [VMEM] * 3,
         name="prepare",
-    )(box_offsets, strengths, block_counts, orbitals, kinetic_mu, projectors)
+    )(flags, box_offsets.T, strengths, block_counts, orbitals, kinetic_mu, projectors)
+    seam_a, seam_b = across_seam(sa, sb)
     from_left, from_right = beside(xr, xl, "gx")
-    from_lo, from_hi = beside(yh, yl, "gy")
-    t2, metas, hi2, lo2 = kernel_call(
-        widen_kernel, [blocks(64), blocks(2), blocks(34), blocks(34)], [VMEM] * 4, name="widen"
-    )(t, meta, from_left, from_right)
-    from_lo2, from_hi2 = beside(hi2, lo2, "gy")
+    from_lo, from_hi = beside_in_half(yh, yl, "gy")
+    t2, metas, hi2, lo2, sa2, sb2 = kernel_call(
+        widen_kernel,
+        [blocks(64), blocks(2), blocks(34), blocks(34), blocks(17), blocks(17)],
+        [SMEM] + [VMEM] * 4,
+        name="widen",
+    )(flags, t, meta, from_left, from_right)
+    seam_a2, seam_b2 = across_seam(sa2, sb2)
+    from_lo2, from_hi2 = beside_in_half(hi2, lo2, "gy")
     (coefs,) = kernel_call(
         coef_kernel,
         [blocks(5 * TILES)],
-        [VMEM] * 7,
+        [SMEM] + [VMEM] * 9,
         [pltpu.VMEM(((TILES + 2 * XH) * 8, 128), F32), pltpu.VMEM((CX * 20 * 8, 128), F32)],
         name="coefficients",
-    )(kinetic_mu, potential, from_left, from_right, from_lo, from_hi, dz)
+    )(flags, mu, potential, from_left, from_right, from_lo, from_hi, seam_a, seam_b, dz)
     q, s, w, z, zr, zl = kernel_call(
         build_kernel,
+        [blocks(6 * 8 * 16, 256), ((4 * 128, 256), BF16), blocks(6), blocks(6), blocks(3), blocks(3)],
+        [SMEM] + [VMEM] * 8,
         [
-            blocks(6 * 8 * 16, 256),
-            ((4 * 128, 256), BF16),
-            blocks(6),
-            blocks(6),
-            blocks(3),
-            blocks(3),
+            pltpu.VMEM((32 * 8, 128), F32),
+            pltpu.VMEM((48, 1024), F32),
+            pltpu.VMEM((34 * 8, 128), F32),
+            pltpu.VMEM((34 * 8, 128), F32),
         ],
-        [VMEM] * 6,
-        [pltpu.VMEM((32 * 8, 128), F32), pltpu.VMEM((48, 1024), F32)],
         name="build",
-    )(t2, metas, from_lo2, from_hi2, y, groups)
+    )(flags, t2, metas, from_lo2, from_hi2, seam_a2, seam_b2, y, groups)
     z_left, z_right = beside(zr, zl, "gx")
     z, z_hi, z_lo = fold(z, z_left, z_right, 0)
     c_lo, c_hi = beside(z_hi, z_lo, "gy")
@@ -582,11 +650,11 @@
         last = step == STEPS
         outs = [blocks(TILES)]
         if not last:
-            outs += [blocks(XH + 3), blocks(XH + 3), blocks(YH), blocks(YH), blocks(6)]
+            outs += [blocks(XH + 3), blocks(XH + 3), blocks(YH), blocks(YH), blocks(YH // 2), blocks(YH // 2), blocks(6)]
         result = kernel_call(
-            functools.partial(step_kernel, step),
+            functools.partial(step_kernel, step, FIRST_Y if step == 1 else YH),
             outs,
-            [VMEM] * 15,
+            [SMEM] + [VMEM] * 17,
             [
                 pltpu.VMEM(((TILES + 2 * XH) * 8, 128), F32),
                 pltpu.VMEM((CX * 20 * 8, 128), F32),
@@ -595,14 +663,18 @@
                 pltpu.VMEM((48, 1024), F32),
             ],
             name="step",
-        )(y, previous, from_left, from_right, from_lo, from_hi, coefs, q, s, w, z, c_lo, c_hi, dz, groups)
+        )(
+            flags, y, previous, from_left, from_right, from_lo, from_hi, seam_a, seam_b,
+            coefs, q, s, w, z, c_lo, c_hi, dz, groups,
+        )
         previous = y
         if last:
             (y,) = result
         else:
-            y, xr, xl, yh, yl, z = result
+            y, xr, xl, yh, yl, sa, sb, z = result
+            seam_a, seam_b = across_seam(sa, sb)
             from_left, from_right = beside(xr, xl, "gx")
-            from_lo, from_hi = beside(yh, yl, "gy")
+            from_lo, from_hi = beside_in_half(yh, yl, "gy")
             z, z_hi, z_lo = fold(z, from_left, from_right, XH)
             c_lo, c_hi = beside(z_hi, z_lo, "gy")
 
@@ -611,19 +683,18 @@
     up = [(i, (i + 1) % count) for i in range(count)]
     down = [(i, (i - 1) % count) for i in range(count)]
     parts = lax.all_to_all(y.reshape(count, -1, NZ), "orb", 0, 0, tiled=True)
-    y, parts = lax.optimization_barrier((y, parts))
     (corr,) = kernel_call(gram_kernel, [blocks(1)], [VMEM], name="gram")(parts)
+    y, corr = lax.optimization_barrier((y, corr))
     below = lax.ppermute(y, "orb", up)
     above = lax.ppermute(y, "orb", down)
+    corr = spread_sum(corr, "gy")
+    below, above, corr = lax.optimization_barrier((below, above, corr))
     half = TILES * 4
     across_a = lax.ppermute(below[:half], "orb", up)
     across_b = lax.ppermute(above[half:], "orb", down)
+    corr = spread_sum(spread_sum(corr, "gx"), "orb")
     across = jnp.concatenate([across_a, across_b], axis=0)
     order = jnp.stack([me, (me + count - 1) % count, (me + 1) % count, (me + 2) % count]).astype(jnp.int32)
-    for axis in ("orb", "gx", "gy"):
-        size = lax.axis_size(axis)
-        copies = jnp.broadcast_to(corr[None], (size, 8, 128))
-        corr = jnp.sum(lax.all_to_all(copies, axis, 0, 0, tiled=True), axis=0)
     cells = CX * CY * NZ * lax.axis_size("gx") * lax.axis_size("gy")
     (result,) = kernel_call(
         functools.partial(rotate_kernel, cells),

time: 218 us -> 247 us (1.13)
  blocking collectives: 29 us -> 66 us
  starting transfers between devices: 114 us -> 107 us
  waiting for transfers between devices: 43.5 us -> 39.2 us
  Pallas kernels: 20.3 us -> 24.4 us
    ppermute x0 -> x20, starting transfers between devices: none -> 42.3 us  [the longest x4 26.2 us: beside_in_half(): lax.ppermute(low_value, axis, up)]
    all_to_all x2 -> x1, blocking collectives: 16.6 us -> 53.5 us  [spread_sum(): return jnp.sum(lax.all_to_all(copies, axis, 0, 0, tiled=True), axis=0)]
    all_to_all x1 -> x2, starting transfers between devices: 31.5 us -> 10.2 us  [spread_sum(): return jnp.sum(lax.all_to_all(copies, axis, 0, 0, tiled=True), axis=0)]
    ppermute x11 -> x7, starting transfers between devices: 44.3 us -> 29.4 us  [beside(): lax.ppermute(low_value, axis, up)]
    ppermute x11 -> x7, starting transfers between devices: 23.8 us -> 12.9 us  [beside(): lax.ppermute(high_value, axis, down)]
    ppermute x1, waiting for transfers between devices: 7.99 us -> 0.01 us  [shards(): below = lax.ppermute(y, 'orb', up)]
    ppermute x0 -> x20, waiting for transfers between devices: none -> 4.09 us  [the longest x4 4.05 us: beside_in_half(): lax.ppermute(high_value, axis, down)]
    pallas_call x5, Pallas kernels: 11.4 us -> 14.7 us  [the longest x3 12.4 us: shards(): kernel_call(functools.partial(step_kernel, step, FIRST_Y if step == 1 els...]
  transfers between devices with their start and end apart: 27 -> 40, of which waited for: 9 -> 10; matrix products, arithmetic and copies ran while one was open for 0% -> 1% of each run, Pallas kernels for 2% -> 2%
where the time goes in v3:
time: 247 us; the launch traced here: 245 us
  starting transfers between devices  107 us (43%)
  blocking collectives  66 us (27%)
  waiting for transfers between devices  39.2 us (16%)
  Pallas kernels  24.4 us (10%)
  local copies, waits for them, and re-layouts  7.22 us (3%)
    all_to_all x1, blocking collectives, spread_sum(): return jnp.sum(lax.all_to_all(copies, axis, 0, 0, tiled=True), axis=0)  53.5 us
    ppermute x7, starting transfers between devices, beside(): lax.ppermute(low_value, axis, up)  29.4 us
    ppermute x4, starting transfers between devices, beside_in_half(): lax.ppermute(low_value, axis, up)  26.2 us
    ppermute x7, waiting for transfers between devices, beside(): lax.ppermute(high_value, axis, down)  23.2 us
    ppermute x7, starting transfers between devices, beside(): lax.ppermute(high_value, axis, down)  12.9 us
    all_to_all x1, blocking collectives, shards(): parts = lax.all_to_all(y.reshape(count, -1, NZ), 'orb', 0, 0, tiled=True)  12.5 us
    pallas_call x3, Pallas kernels, shards(): kernel_call(functools.partial(step_kernel, step, FIRST_Y if step == 1 els...  12.4 us
    all_to_all x2, waiting for transfers between devices, spread_sum(): return jnp.sum(lax.all_to_all(copies, axis, 0, 0, tiled=True), axis=0)  11 us
  transfers between devices with their start and end apart: 40, of which 10 were waited for; matrix products, arithmetic and copies ran while one was open for 1% of the time, Pallas kernels for 2%

profile of v3, /device:TPU:8, one launch (start us, length us, event | category | flops | bytes accessed | tf_op | source)
XLA Modules:
  0.0 245.3 jit_solution(12161264171740764402)
XLA Ops:
  0.8 1.0 copy-done.2
  1.8 0.9 copy-done.3
  4.9 1.6 prepare.1
  6.5 1.8 collective-permute-start
  8.3 1.3 collective-permute-start.1
  10.2 3.7 %collective-permute-done.1.fr_ref = f32[616,128]{1,0:T(8,128)S(1)} collective-permute-done((f32[616,128]{1,0:T(8,128)S(1)}, f32[616,128]{1,0:T(8,128)S(1)}, u32[]{:S(2)}, u32[]{:S(2)}) %collective-permute-start.1) | collective-permute-done | bytes 315424 | tf_op jit(solution)/shard_map/ppermute | solution.py:562
  15.9 3.5 %collective-permute-start.7 = (f32[272,128]{1,0:T(8,128)S(1)}, f32[272,128]{1,0:T(8,128)S(1)}, u32[]{:S(2)}, u32[]{:S(2)}) collective-permute-start(f32[272,128]{1,0:T(8,128)S(1)} %get-tuple-element.70), channel_id=1, source_target_pairs={{0,4},{4,8},{8,12},{12,16},{16,20},{20,24},{24,28},{32,36},{36,40}... | collective-permute-start | bytes 417800 | tf_op jit(solution)/shard_map/ppermute | solution.py:589
  19.4 3.5 %collective-permute-start.2 = (f32[384,128]{1,0:T(8,128)S(1)}, f32[384,128]{1,0:T(8,128)S(1)}, u32[]{:S(2)}, u32[]{:S(2)}) collective-permute-start(f32[384,128]{1,0:T(8,128)S(1)} %get-tuple-element.61), channel_id=1, source_target_pairs={{0,4},{4,8},{8,12},{12,16},{16,20},{20,24},{24,28},{32,36},{36,40}... | collective-permute-start | bytes 589832 | tf_op jit(solution)/shard_map/ppermute | solution.py:589
  22.9 2.4 collective-permute-start.3
  26.0 1.9 collective-permute-start.8
  29.3 4.0 %collective-permute-done.8.hi_in = f32[272,128]{1,0:T(8,128)S(1)} collective-permute-done((f32[272,128]{1,0:T(8,128)S(1)}, f32[272,128]{1,0:T(8,128)S(1)}, u32[]{:S(2)}, u32[]{:S(2)}) %collective-permute-start.8) | collective-permute-done | bytes 139296 | tf_op jit(solution)/shard_map/ppermute | solution.py:589
  33.3 3.0 %build.1 = (f32[6144,256]{1,0:T(8,128)S(1)}, bf16[512,256]{1,0:T(8,128)(2,1)S(1)}, f32[48,128]{1,0:T(8,128)S(1)}, f32[48,128]{1,0:T(8,128)S(1)}, f32[24,128]{1,0:T(8,128)S(1)}, /*index=5*/f32[24,128]{1,0:T(8,128)S(1)}) custom-call(s32[2]{0:T(128)S(1)} %add_convert_fusion.flags, f32[512,128]{1,0:T(8,128)S(1)} %get-tuple-element.68.t2_ref, ...), custom_call_target="tpu_custom_call" | custom-call | tf_op jit(solution)/shard_map/build/pallas_call | solution.py:632
  36.3 5.7 %collective-permute-start.12 = (f32[24,128]{1,0:T(8,128)S(1)}, f32[24,128]{1,0:T(8,128)S(1)}, u32[]{:S(2)}, u32[]{:S(2)}) collective-permute-start(f32[24,128]{1,0:T(8,128)S(1)} %get-tuple-element.79), channel_id=1, source_target_pairs={{0,64},{64,128},{128,192},{192,256},{256,320},{320,384},{384,448},... | collective-permute-start | bytes 36872 | tf_op jit(solution)/shard_map/ppermute | solution.py:562
  42.8 1.3 collective-permute-start.13
  44.1 4.2 %collective-permute-done.13.fr_ref = f32[24,128]{1,0:T(8,128)S(1)} collective-permute-done((f32[24,128]{1,0:T(8,128)S(1)}, f32[24,128]{1,0:T(8,128)S(1)}, u32[]{:S(2)}, u32[]{:S(2)}) %collective-permute-start.13) | collective-permute-done | bytes 12320 | tf_op jit(solution)/shard_map/ppermute | solution.py:562
  48.2 4.2 %collective-permute-start.14 = (f32[32,128]{1,0:T(8,128)S(1)}, f32[32,128]{1,0:T(8,128)S(1)}, u32[]{:S(2)}, u32[]{:S(2)}) collective-permute-start(f32[32,128]{1,0:T(8,128)S(1)} %get-tuple-element.82), channel_id=1, source_target_pairs={{0,4},{4,8},{8,12},{12,16},{16,20},{20,24},{24,28},{28,32},{32,36}... | collective-permute-start | bytes 49160 | tf_op jit(solution)/shard_map/ppermute | solution.py:562
  52.5 1.9 collective-permute-start.15
  56.3 1.6 coefficients.1.coef_ref
  58.6 4.4 %step.3 = (f32[768,128]{1,0:T(8,128)S(1)}, f32[408,128]{1,0:T(8,128)S(1)}, f32[408,128]{1,0:T(8,128)S(1)}, f32[288,128]{1,0:T(8,128)S(1)}, f32[288,128]{1,0:T(8,...) custom-call(s32[2]{0:T(128)S(1)} %add_convert_fusion.flags, ...), custom_call_target="tpu_custom_call" | custom-call | tf_op jit(solution)/shard_map/step/pallas_call | solution.py:654
  63.0 4.0 %collective-permute-start.16 = (f32[408,128]{1,0:T(8,128)S(1)}, f32[408,128]{1,0:T(8,128)S(1)}, u32[]{:S(2)}, u32[]{:S(2)}) collective-permute-start(f32[408,128]{1,0:T(8,128)S(1)} %get-tuple-element.85), channel_id=1, source_target_pairs={{0,64},{64,128},{128,192},{192,256},{256,320},{320,384},{384,448},... | collective-permute-start | bytes 626696 | tf_op jit(solution)/shard_map/ppermute | solution.py:562
  67.0 1.3 collective-permute-start.17
  68.9 10.6 %collective-permute-start.18 = (f32[288,128]{1,0:T(8,128)S(1)}, f32[288,128]{1,0:T(8,128)S(1)}, u32[]{:S(2)}, u32[]{:S(2)}) collective-permute-start(f32[288,128]{1,0:T(8,128)S(1)} %get-tuple-element.87), channel_id=1, source_target_pairs={{0,4},{4,8},{8,12},{12,16},{16,20},{20,24},{24,28},{32,36},{36,40}... | collective-permute-start | bytes 442376 | tf_op jit(solution)/shard_map/ppermute | solution.py:589
  79.6 1.9 collective-permute-start.19
  82.9 4.2 %collective-permute-done.17.fr_ref = f32[408,128]{1,0:T(8,128)S(1)} collective-permute-done((f32[408,128]{1,0:T(8,128)S(1)}, f32[408,128]{1,0:T(8,128)S(1)}, u32[]{:S(2)}, u32[]{:S(2)}) %collective-permute-start.17) | collective-permute-done | bytes 208928 | tf_op jit(solution)/shard_map/ppermute | solution.py:562
  87.1 1.9 collective-permute-start.23
  89.0 3.9 %collective-permute-start.24 = (f32[32,128]{1,0:T(8,128)S(1)}, f32[32,128]{1,0:T(8,128)S(1)}, u32[]{:S(2)}, u32[]{:S(2)}) collective-permute-start(f32[32,128]{1,0:T(8,128)S(1)} %get-tuple-element.94), channel_id=1, source_target_pairs={{4,0},{8,4},{12,8},{16,12},{20,16},{24,20},{28,24},{32,28},{36,32}... | collective-permute-start | bytes 49160 | tf_op jit(solution)/shard_map/ppermute | solution.py:562
  93.0 1.9 collective-permute-done.24.chi_ref
  94.8 4.4 %step.4 = (f32[768,128]{1,0:T(8,128)S(1)}, f32[408,128]{1,0:T(8,128)S(1)}, f32[408,128]{1,0:T(8,128)S(1)}, f32[288,128]{1,0:T(8,128)S(1)}, f32[288,128]{1,0:T(8,...) custom-call(s32[2]{0:T(128)S(1)} %add_convert_fusion.flags, ...), custom_call_target="tpu_custom_call" | custom-call | tf_op jit(solution)/shard_map/step/pallas_call | solution.py:654
  99.2 7.0 %collective-permute-start.25 = (f32[408,128]{1,0:T(8,128)S(1)}, f32[408,128]{1,0:T(8,128)S(1)}, u32[]{:S(2)}, u32[]{:S(2)}) collective-permute-start(f32[408,128]{1,0:T(8,128)S(1)} %get-tuple-element.96), channel_id=1, source_target_pairs={{0,64},{64,128},{128,192},{192,256},{256,320},{320,384},{384,448},... | collective-permute-start | bytes 626696 | tf_op jit(solution)/shard_map/ppermute | solution.py:562
  106.2 1.3 collective-permute-start.26
  108.2 8.6 %collective-permute-start.27 = (f32[288,128]{1,0:T(8,128)S(1)}, f32[288,128]{1,0:T(8,128)S(1)}, u32[]{:S(2)}, u32[]{:S(2)}) collective-permute-start(f32[288,128]{1,0:T(8,128)S(1)} %get-tuple-element.98), channel_id=1, source_target_pairs={{0,4},{4,8},{8,12},{12,16},{16,20},{20,24},{24,28},{32,36},{36,40}... | collective-permute-start | bytes 442376 | tf_op jit(solution)/shard_map/ppermute | solution.py:589
  116.8 1.9 collective-permute-start.28
  120.1 4.9 %collective-permute-start.32 = (f32[32,128]{1,0:T(8,128)S(1)}, f32[32,128]{1,0:T(8,128)S(1)}, u32[]{:S(2)}, u32[]{:S(2)}) collective-permute-start(f32[32,128]{1,0:T(8,128)S(1)} %get-tuple-element.104), channel_id=1, source_target_pairs={{0,4},{4,8},{8,12},{12,16},{16,20},{20,24},{24,28},{28,32},{32,36}... | collective-permute-start | bytes 49160 | tf_op jit(solution)/shard_map/ppermute | solution.py:562
  125.0 1.9 collective-permute-start.33
  127.0 8.7 %collective-permute-done.33.chi_ref = f32[32,128]{1,0:T(8,128)S(1)} collective-permute-done((f32[32,128]{1,0:T(8,128)S(1)}, f32[32,128]{1,0:T(8,128)S(1)}, u32[]{:S(2)}, u32[]{:S(2)}) %collective-permute-start.33) | collective-permute-done | bytes 16416 | tf_op jit(solution)/shard_map/ppermute | solution.py:562
  135.6 3.6 %step.5.a0 = f32[768,128]{1,0:T(8,128)S(1)} custom-call(s32[2]{0:T(128)S(1)} %add_convert_fusion.flags, f32[768,128]{1,0:T(8,128)S(1)} %get-tuple-element.95.y_ref, f32[768,128]{1,0:T(8,128)S(1)} %get-tuple-element.84.y_ref.prev_ref, f32[408,128]{1,0:T(8,128)S(1)} %collective-permute-done.25.fl_ref, f32[408,128]{1,0:T(8,128)S(1)} %collective-permute-done.26.fr_ref, ...), custom_call_target="tpu_custom_call" | custom-call | tf_op jit(solution)/shard_map/step/pallas_call | solution.py:654
  139.3 12.5 %all_to_all.20.parts_ref = f32[4,192,128]{2,1,0:T(8,128)S(1)} all-to-all(f32[4,192,128]{2,1,0:T(8,128)S(1)} %bitcast.8), channel_id=1, replica_groups=mesh['gx'=8,'gy'=16,'orb'=4] {'orb'}, dimensions={0} | all-to-all | bytes 786432 | tf_op jit(solution)/shard_map/all_to_all | solution.py:685
  151.7 1.1 gram.1
  152.8 3.1 %collective-permute-start.35 = (f32[768,128]{1,0:T(8,128)S(1)}, f32[768,128]{1,0:T(8,128)S(1)}, u32[]{:S(2)}, u32[]{:S(2)}) collective-permute-start(f32[768,128]{1,0:T(8,128)S(1)} %step.5.a0), channel_id=1, source_target_pairs={{0,3},{1,0},{2,1},{3,2},{4,7},{5,4},{6,5},{7,6},{8,11},{9,8},{10,9... | collective-permute-start | bytes 1179656 | tf_op jit(solution)/shard_map/ppermute | solution.py:689
  155.9 2.8 %collective-permute-start.34 = (f32[768,128]{1,0:T(8,128)S(1)}, f32[768,128]{1,0:T(8,128)S(1)}, u32[]{:S(2)}, u32[]{:S(2)}) collective-permute-start(f32[768,128]{1,0:T(8,128)S(1)} %step.5.a0), channel_id=1, source_target_pairs={{0,1},{1,2},{2,3},{3,0},{4,5},{5,6},{6,7},{7,4},{8,9},{9,10},{10,1... | collective-permute-start | bytes 1179656 | tf_op jit(solution)/shard_map/ppermute | solution.py:688
  158.7 53.5 %all_to_all.21 = f32[16,8,128]{2,1,0:T(8,128)S(1)} all-to-all(f32[16,8,128]{2,1,0:T(8,128)S(1)} %broadcast_in_dim.6), channel_id=1, replica_groups=mesh['gx'=8,'gy'=16,'orb'=4] {'gy'}, dimensions={0} | all-to-all | bytes 131072 | tf_op jit(solution)/shard_map/all_to_all | solution.py:594
  212.3 4.3 %collective-permute-start.37 = (f32[384,128]{1,0:T(8,128)S(1)}, f32[384,128]{1,0:T(8,128)S(1)}, u32[]{:S(2)}, u32[]{:S(2)}) collective-permute-start(f32[384,128]{1,0:T(8,128)S(1)} %slice.7), channel_id=1, source_target_pairs={{0,3},{1,0},{2,1},{3,2},{4,7},{5,4},{6,5},{7,6},{8,11},{9,8},{10,9... | collective-permute-start | bytes 589832 | tf_op jit(solution)/shard_map/ppermute | solution.py:694
  216.6 1.9 collective-permute-start.36
  219.2 5.8 %all-to-all-start.2 = ((f32[8,8,128]{2,1,0:T(8,128)}), f32[8,8,128]{2,1,0:T(8,128)S(1)}, u32[]{:S(2)}, u32[]{:S(2)}) async-start(f32[8,8,128]{2,1,0:T(8,128)} %broadcast_in_dim.7), calls=%async_computation.2 | async-start | bytes 65536 | tf_op jit(solution)/shard_map/all_to_all | solution.py:594
  224.9 5.7 %all-to-all-done.2 = f32[8,8,128]{2,1,0:T(8,128)S(1)} async-done(((f32[8,8,128]{2,1,0:T(8,128)}), f32[8,8,128]{2,1,0:T(8,128)S(1)}, u32[]{:S(2)}, u32[]{:S(2)}) %all-to-all-start.2) | async-done | bytes 32800 | tf_op jit(solution)/shard_map/all_to_all | solution.py:594
  231.3 4.5 %all-to-all-start.3 = ((f32[4,8,128]{2,1,0:T(8,128)}), f32[4,8,128]{2,1,0:T(8,128)S(1)}, u32[]{:S(2)}, u32[]{:S(2)}) async-start(f32[4,8,128]{2,1,0:T(8,128)} %broadcast_in_dim.8), calls=%async_computation.3 | async-start | bytes 32768 | tf_op jit(solution)/shard_map/all_to_all | solution.py:594
  235.8 5.3 %all-to-all-done.3 = f32[4,8,128]{2,1,0:T(8,128)S(1)} async-done(((f32[4,8,128]{2,1,0:T(8,128)}), f32[4,8,128]{2,1,0:T(8,128)S(1)}, u32[]{:S(2)}, u32[]{:S(2)}) %all-to-all-start.3) | async-done | bytes 16416 | tf_op jit(solution)/shard_map/all_to_all | solution.py:594
  241.2 4.1 %rotate.1 = f32[4,12,16,128]{3,2,1,0:T(8,128)} custom-call(s32[4]{0:T(128)S(1)} %pad_add_fusion.order, f32[8,128]{1,0:T(8,128)S(1)} %reduce_sum.29.corr_ref, f32[768,128]{1,0:T(8,128)S(1)} %step.5.a0, f32[768,128]{1,0:T(8,128)S(1)} %collective-permute-done.34.a1, f32[768,128]{1,0:T(8,128)S(1)} %collective-permute-done.35.a2, f32[768,128]{1,0:T(8,128)S(1)} %pad_maximum_fusion.a3), custom_call_target="tpu_custom_call" | custom-call | tf_op jit(solution)/shard_map/rotate/pallas_call | solution.py:699
  (73 shorter events, 15.8 us)
Async XLA Ops:
  0.0 58.6 %copy-start.1 = (bf16[256,256]{1,0:T(8,128)(2,1)S(1)}, bf16[256,256]{1,0:T(8,128)(2,1)}, u32[]{:S(2)}) copy-start(bf16[256,256]{1,0:T(8,128)(2,1)} %constant.44.clone.dz_ref) | copy-start | bytes 393220
  0.8 1.0 copy-start.2
  1.8 0.9 copy-start.3
  2.7 0.9 copy-start.5
  3.6 0.7 copy-start.6
  4.2 0.7 copy-start.7
  6.5 3.7 %collective-permute-start = (f32[616,128]{1,0:T(8,128)S(1)}, f32[616,128]{1,0:T(8,128)S(1)}, u32[]{:S(2)}, u32[]{:S(2)}) collective-permute-start(f32[616,128]{1,0:T(8,128)S(1)} %get-tuple-element.59), channel_id=1, source_target_pairs={{0,64},{64,128},{128,192},{192,256},{256,320},{320,384},{384,448},... | collective-permute-start | bytes 946184 | tf_op jit(solution)/shard_map/ppermute | solution.py:562
  8.3 5.6 %collective-permute-start.1 = (f32[616,128]{1,0:T(8,128)S(1)}, f32[616,128]{1,0:T(8,128)S(1)}, u32[]{:S(2)}, u32[]{:S(2)}) collective-permute-start(f32[616,128]{1,0:T(8,128)S(1)} %get-tuple-element.60), channel_id=1, source_target_pairs={{64,0},{128,64},{192,128},{256,192},{320,256},{384,320},{448,384},... | collective-permute-start | bytes 946184 | tf_op jit(solution)/shard_map/ppermute | solution.py:562
  9.6 13.3 %collective-permute-start.5 = (f32[192,128]{1,0:T(8,128)S(1)}, f32[192,128]{1,0:T(8,128)S(1)}, u32[]{:S(2)}, u32[]{:S(2)}) collective-permute-start(f32[192,128]{1,0:T(8,128)S(1)} %get-tuple-element.64), channel_id=1, source_target_pairs={{28,316},{92,380},{156,444},{220,508},{284,28},{348,92},{412,156},... | collective-permute-start | bytes 294920 | tf_op jit(solution)/shard_map/ppermute | solution.py:580
  14.6 10.7 %collective-permute-start.10 = (f32[136,128]{1,0:T(8,128)S(1)}, f32[136,128]{1,0:T(8,128)S(1)}, u32[]{:S(2)}, u32[]{:S(2)}) collective-permute-start(f32[136,128]{1,0:T(8,128)S(1)} %get-tuple-element.73), channel_id=1, source_target_pairs={{28,316},{92,380},{156,444},{220,508},{284,28},{348,92},{412,156},... | collective-permute-start | bytes 208904 | tf_op jit(solution)/shard_map/ppermute | solution.py:580
  15.2 10.7 %collective-permute-start.9 = (f32[136,128]{1,0:T(8,128)S(1)}, f32[136,128]{1,0:T(8,128)S(1)}, u32[]{:S(2)}, u32[]{:S(2)}) collective-permute-start(f32[136,128]{1,0:T(8,128)S(1)} %get-tuple-element.72), channel_id=1, source_target_pairs={{28,32},{32,28},{29,33},{33,29},{30,34},{34,30},{31,35},{35,31},{9... | collective-permute-start | bytes 208904 | tf_op jit(solution)/shard_map/ppermute | solution.py:581
  15.9 12.7 %collective-permute-start.7 = (f32[272,128]{1,0:T(8,128)S(1)}, f32[272,128]{1,0:T(8,128)S(1)}, u32[]{:S(2)}, u32[]{:S(2)}) collective-permute-start(f32[272,128]{1,0:T(8,128)S(1)} %get-tuple-element.70), channel_id=1, source_target_pairs={{0,4},{4,8},{8,12},{12,16},{16,20},{20,24},{24,28},{32,36},{36,40}... | collective-permute-start | bytes 417800 | tf_op jit(solution)/shard_map/ppermute | solution.py:589
  19.4 35.0 %collective-permute-start.2 = (f32[384,128]{1,0:T(8,128)S(1)}, f32[384,128]{1,0:T(8,128)S(1)}, u32[]{:S(2)}, u32[]{:S(2)}) collective-permute-start(f32[384,128]{1,0:T(8,128)S(1)} %get-tuple-element.61), channel_id=1, source_target_pairs={{0,4},{4,8},{8,12},{12,16},{16,20},{20,24},{24,28},{32,36},{36,40}... | collective-permute-start | bytes 589832 | tf_op jit(solution)/shard_map/ppermute | solution.py:589
  22.9 31.5 %collective-permute-start.3 = (f32[384,128]{1,0:T(8,128)S(1)}, f32[384,128]{1,0:T(8,128)S(1)}, u32[]{:S(2)}, u32[]{:S(2)}) collective-permute-start(f32[384,128]{1,0:T(8,128)S(1)} %get-tuple-element.62), channel_id=1, source_target_pairs={{4,0},{8,4},{12,8},{16,12},{20,16},{24,20},{28,24},{36,32},{40,36}... | collective-permute-start | bytes 589832 | tf_op jit(solution)/shard_map/ppermute | solution.py:589
  25.3 2.6 %collective-permute-start.11 = (f32[136,128]{1,0:T(8,128)S(1)}, f32[136,128]{1,0:T(8,128)S(1)}, u32[]{:S(2)}, u32[]{:S(2)}) collective-permute-start(f32[136,128]{1,0:T(8,128)S(1)} %collective-permute-done.10), channel_id=1, source_target_pairs={{316,32},{380,96},{444,160},{508,224},{28,288},{92,352},{156,416},... | collective-permute-start | bytes 208904 | tf_op jit(solution)/shard_map/ppermute | solution.py:582
  26.0 7.3 %collective-permute-start.8 = (f32[272,128]{1,0:T(8,128)S(1)}, f32[272,128]{1,0:T(8,128)S(1)}, u32[]{:S(2)}, u32[]{:S(2)}) collective-permute-start(f32[272,128]{1,0:T(8,128)S(1)} %get-tuple-element.71), channel_id=1, source_target_pairs={{4,0},{8,4},{12,8},{16,12},{20,16},{24,20},{28,24},{36,32},{40,36}... | collective-permute-start | bytes 417800 | tf_op jit(solution)/shard_map/ppermute | solution.py:589
  27.9 24.6 %collective-permute-start.4 = (f32[192,128]{1,0:T(8,128)S(1)}, f32[192,128]{1,0:T(8,128)S(1)}, u32[]{:S(2)}, u32[]{:S(2)}) collective-permute-start(f32[192,128]{1,0:T(8,128)S(1)} %get-tuple-element.63), channel_id=1, source_target_pairs={{28,32},{32,28},{29,33},{33,29},{30,34},{34,30},{31,35},{35,31},{9... | collective-permute-start | bytes 294920 | tf_op jit(solution)/shard_map/ppermute | solution.py:581
  28.6 25.8 %collective-permute-start.6 = (f32[192,128]{1,0:T(8,128)S(1)}, f32[192,128]{1,0:T(8,128)S(1)}, u32[]{:S(2)}, u32[]{:S(2)}) collective-permute-start(f32[192,128]{1,0:T(8,128)S(1)} %collective-permute-done.5), channel_id=1, source_target_pairs={{316,32},{380,96},{444,160},{508,224},{28,288},{92,352},{156,416},... | collective-permute-start | bytes 294920 | tf_op jit(solution)/shard_map/ppermute | solution.py:582
  36.3 6.5 %collective-permute-start.12 = (f32[24,128]{1,0:T(8,128)S(1)}, f32[24,128]{1,0:T(8,128)S(1)}, u32[]{:S(2)}, u32[]{:S(2)}) collective-permute-start(f32[24,128]{1,0:T(8,128)S(1)} %get-tuple-element.79), channel_id=1, source_target_pairs={{0,64},{64,128},{128,192},{192,256},{256,320},{320,384},{384,448},... | collective-permute-start | bytes 36872 | tf_op jit(solution)/shard_map/ppermute | solution.py:562
  42.8 5.5 %collective-permute-start.13 = (f32[24,128]{1,0:T(8,128)S(1)}, f32[24,128]{1,0:T(8,128)S(1)}, u32[]{:S(2)}, u32[]{:S(2)}) collective-permute-start(f32[24,128]{1,0:T(8,128)S(1)} %get-tuple-element.80), channel_id=1, source_target_pairs={{64,0},{128,64},{192,128},{256,192},{320,256},{384,320},{448,384},... | collective-permute-start | bytes 36872 | tf_op jit(solution)/shard_map/ppermute | solution.py:562
  48.2 9.7 %collective-permute-start.14 = (f32[32,128]{1,0:T(8,128)S(1)}, f32[32,128]{1,0:T(8,128)S(1)}, u32[]{:S(2)}, u32[]{:S(2)}) collective-permute-start(f32[32,128]{1,0:T(8,128)S(1)} %get-tuple-element.82), channel_id=1, source_target_pairs={{0,4},{4,8},{8,12},{12,16},{16,20},{20,24},{24,28},{28,32},{32,36}... | collective-permute-start | bytes 49160 | tf_op jit(solution)/shard_map/ppermute | solution.py:562
  52.5 6.1 %collective-permute-start.15 = (f32[32,128]{1,0:T(8,128)S(1)}, f32[32,128]{1,0:T(8,128)S(1)}, u32[]{:S(2)}, u32[]{:S(2)}) collective-permute-start(f32[32,128]{1,0:T(8,128)S(1)} %get-tuple-element.83), channel_id=1, source_target_pairs={{4,0},{8,4},{12,8},{16,12},{20,16},{24,20},{28,24},{32,28},{36,32}... | collective-permute-start | bytes 49160 | tf_op jit(solution)/shard_map/ppermute | solution.py:562
  54.5 0.9 copy-start
  55.4 0.9 copy-start.4
  63.0 19.2 %collective-permute-start.16 = (f32[408,128]{1,0:T(8,128)S(1)}, f32[408,128]{1,0:T(8,128)S(1)}, u32[]{:S(2)}, u32[]{:S(2)}) collective-permute-start(f32[408,128]{1,0:T(8,128)S(1)} %get-tuple-element.85), channel_id=1, source_target_pairs={{0,64},{64,128},{128,192},{192,256},{256,320},{320,384},{384,448},... | collective-permute-start | bytes 626696 | tf_op jit(solution)/shard_map/ppermute | solution.py:562
  67.0 20.1 %collective-permute-start.17 = (f32[408,128]{1,0:T(8,128)S(1)}, f32[408,128]{1,0:T(8,128)S(1)}, u32[]{:S(2)}, u32[]{:S(2)}) collective-permute-start(f32[408,128]{1,0:T(8,128)S(1)} %get-tuple-element.86), channel_id=1, source_target_pairs={{64,0},{128,64},{192,128},{256,192},{320,256},{384,320},{448,384},... | collective-permute-start | bytes 626696 | tf_op jit(solution)/shard_map/ppermute | solution.py:562
  68.3 13.3 %collective-permute-start.21 = (f32[144,128]{1,0:T(8,128)S(1)}, f32[144,128]{1,0:T(8,128)S(1)}, u32[]{:S(2)}, u32[]{:S(2)}) collective-permute-start(f32[144,128]{1,0:T(8,128)S(1)} %get-tuple-element.90), channel_id=1, source_target_pairs={{28,316},{92,380},{156,444},{220,508},{284,28},{348,92},{412,156},... | collective-permute-start | bytes 221192 | tf_op jit(solution)/shard_map/ppermute | solution.py:580
  68.9 24.0 %collective-permute-start.18 = (f32[288,128]{1,0:T(8,128)S(1)}, f32[288,128]{1,0:T(8,128)S(1)}, u32[]{:S(2)}, u32[]{:S(2)}) collective-permute-start(f32[288,128]{1,0:T(8,128)S(1)} %get-tuple-element.87), channel_id=1, source_target_pairs={{0,4},{4,8},{8,12},{12,16},{16,20},{20,24},{24,28},{32,36},{36,40}... | collective-permute-start | bytes 442376 | tf_op jit(solution)/shard_map/ppermute | solution.py:589
  79.6 13.4 %collective-permute-start.19 = (f32[288,128]{1,0:T(8,128)S(1)}, f32[288,128]{1,0:T(8,128)S(1)}, u32[]{:S(2)}, u32[]{:S(2)}) collective-permute-start(f32[288,128]{1,0:T(8,128)S(1)} %get-tuple-element.88), channel_id=1, source_target_pairs={{4,0},{8,4},{12,8},{16,12},{20,16},{24,20},{28,24},{36,32},{40,36}... | collective-permute-start | bytes 442376 | tf_op jit(solution)/shard_map/ppermute | solution.py:589
  81.5 7.5 %collective-permute-start.20 = (f32[144,128]{1,0:T(8,128)S(1)}, f32[144,128]{1,0:T(8,128)S(1)}, u32[]{:S(2)}, u32[]{:S(2)}) collective-permute-start(f32[144,128]{1,0:T(8,128)S(1)} %get-tuple-element.89), channel_id=1, source_target_pairs={{28,32},{32,28},{29,33},{33,29},{30,34},{34,30},{31,35},{35,31},{9... | collective-permute-start | bytes 221192 | tf_op jit(solution)/shard_map/ppermute | solution.py:581
  82.2 10.7 %collective-permute-start.22 = (f32[144,128]{1,0:T(8,128)S(1)}, f32[144,128]{1,0:T(8,128)S(1)}, u32[]{:S(2)}, u32[]{:S(2)}) collective-permute-start(f32[144,128]{1,0:T(8,128)S(1)} %collective-permute-done.21), channel_id=1, source_target_pairs={{316,32},{380,96},{444,160},{508,224},{28,288},{92,352},{156,416},... | collective-permute-start | bytes 221192 | tf_op jit(solution)/shard_map/ppermute | solution.py:582
  87.1 5.9 %collective-permute-start.23 = (f32[32,128]{1,0:T(8,128)S(1)}, f32[32,128]{1,0:T(8,128)S(1)}, u32[]{:S(2)}, u32[]{:S(2)}) collective-permute-start(f32[32,128]{1,0:T(8,128)S(1)} %get-tuple-element.93), channel_id=1, source_target_pairs={{0,4},{4,8},{8,12},{12,16},{16,20},{20,24},{24,28},{28,32},{32,36}... | collective-permute-start | bytes 49160 | tf_op jit(solution)/shard_map/ppermute | solution.py:562
  89.0 5.8 %collective-permute-start.24 = (f32[32,128]{1,0:T(8,128)S(1)}, f32[32,128]{1,0:T(8,128)S(1)}, u32[]{:S(2)}, u32[]{:S(2)}) collective-permute-start(f32[32,128]{1,0:T(8,128)S(1)} %get-tuple-element.94), channel_id=1, source_target_pairs={{4,0},{8,4},{12,8},{16,12},{20,16},{24,20},{28,24},{32,28},{36,32}... | collective-permute-start | bytes 49160 | tf_op jit(solution)/shard_map/ppermute | solution.py:562
  99.2 20.2 %collective-permute-start.25 = (f32[408,128]{1,0:T(8,128)S(1)}, f32[408,128]{1,0:T(8,128)S(1)}, u32[]{:S(2)}, u32[]{:S(2)}) collective-permute-start(f32[408,128]{1,0:T(8,128)S(1)} %get-tuple-element.96), channel_id=1, source_target_pairs={{0,64},{64,128},{128,192},{192,256},{256,320},{320,384},{384,448},... | collective-permute-start | bytes 626696 | tf_op jit(solution)/shard_map/ppermute | solution.py:562
  106.2 13.9 %collective-permute-start.26 = (f32[408,128]{1,0:T(8,128)S(1)}, f32[408,128]{1,0:T(8,128)S(1)}, u32[]{:S(2)}, u32[]{:S(2)}) collective-permute-start(f32[408,128]{1,0:T(8,128)S(1)} %get-tuple-element.97), channel_id=1, source_target_pairs={{64,0},{128,64},{192,128},{256,192},{320,256},{384,320},{448,384},... | collective-permute-start | bytes 626696 | tf_op jit(solution)/shard_map/ppermute | solution.py:562
  107.5 11.2 %collective-permute-start.30 = (f32[144,128]{1,0:T(8,128)S(1)}, f32[144,128]{1,0:T(8,128)S(1)}, u32[]{:S(2)}, u32[]{:S(2)}) collective-permute-start(f32[144,128]{1,0:T(8,128)S(1)} %get-tuple-element.101), channel_id=1, source_target_pairs={{28,316},{92,380},{156,444},{220,508},{284,28},{348,92},{412,156},... | collective-permute-start | bytes 221192 | tf_op jit(solution)/shard_map/ppermute | solution.py:580
  108.2 18.8 %collective-permute-start.27 = (f32[288,128]{1,0:T(8,128)S(1)}, f32[288,128]{1,0:T(8,128)S(1)}, u32[]{:S(2)}, u32[]{:S(2)}) collective-permute-start(f32[288,128]{1,0:T(8,128)S(1)} %get-tuple-element.98), channel_id=1, source_target_pairs={{0,4},{4,8},{8,12},{12,16},{16,20},{20,24},{24,28},{32,36},{36,40}... | collective-permute-start | bytes 442376 | tf_op jit(solution)/shard_map/ppermute | solution.py:589
  116.8 10.2 %collective-permute-start.28 = (f32[288,128]{1,0:T(8,128)S(1)}, f32[288,128]{1,0:T(8,128)S(1)}, u32[]{:S(2)}, u32[]{:S(2)}) collective-permute-start(f32[288,128]{1,0:T(8,128)S(1)} %get-tuple-element.99), channel_id=1, source_target_pairs={{4,0},{8,4},{12,8},{16,12},{20,16},{24,20},{28,24},{36,32},{40,36}... | collective-permute-start | bytes 442376 | tf_op jit(solution)/shard_map/ppermute | solution.py:589
  118.7 6.3 %collective-permute-start.29 = (f32[144,128]{1,0:T(8,128)S(1)}, f32[144,128]{1,0:T(8,128)S(1)}, u32[]{:S(2)}, u32[]{:S(2)}) collective-permute-start(f32[144,128]{1,0:T(8,128)S(1)} %get-tuple-element.100), channel_id=1, source_target_pairs={{28,32},{32,28},{29,33},{33,29},{30,34},{34,30},{31,35},{35,31},{9... | collective-permute-start | bytes 221192 | tf_op jit(solution)/shard_map/ppermute | solution.py:581
  119.4 7.5 %collective-permute-start.31 = (f32[144,128]{1,0:T(8,128)S(1)}, f32[144,128]{1,0:T(8,128)S(1)}, u32[]{:S(2)}, u32[]{:S(2)}) collective-permute-start(f32[144,128]{1,0:T(8,128)S(1)} %collective-permute-done.30), channel_id=1, source_target_pairs={{316,32},{380,96},{444,160},{508,224},{28,288},{92,352},{156,416},... | collective-permute-start | bytes 221192 | tf_op jit(solution)/shard_map/ppermute | solution.py:582
  120.1 6.9 %collective-permute-start.32 = (f32[32,128]{1,0:T(8,128)S(1)}, f32[32,128]{1,0:T(8,128)S(1)}, u32[]{:S(2)}, u32[]{:S(2)}) collective-permute-start(f32[32,128]{1,0:T(8,128)S(1)} %get-tuple-element.104), channel_id=1, source_target_pairs={{0,4},{4,8},{8,12},{12,16},{16,20},{20,24},{24,28},{28,32},{32,36}... | collective-permute-start | bytes 49160 | tf_op jit(solution)/shard_map/ppermute | solution.py:562
  125.0 10.6 %collective-permute-start.33 = (f32[32,128]{1,0:T(8,128)S(1)}, f32[32,128]{1,0:T(8,128)S(1)}, u32[]{:S(2)}, u32[]{:S(2)}) collective-permute-start(f32[32,128]{1,0:T(8,128)S(1)} %get-tuple-element.105), channel_id=1, source_target_pairs={{4,0},{8,4},{12,8},{16,12},{20,16},{24,20},{28,24},{32,28},{36,32}... | collective-permute-start | bytes 49160 | tf_op jit(solution)/shard_map/ppermute | solution.py:562
  152.8 59.4 %collective-permute-start.35 = (f32[768,128]{1,0:T(8,128)S(1)}, f32[768,128]{1,0:T(8,128)S(1)}, u32[]{:S(2)}, u32[]{:S(2)}) collective-permute-start(f32[768,128]{1,0:T(8,128)S(1)} %step.5.a0), channel_id=1, source_target_pairs={{0,3},{1,0},{2,1},{3,2},{4,7},{5,4},{6,5},{7,6},{8,11},{9,8},{10,9... | collective-permute-start | bytes 1179656 | tf_op jit(solution)/shard_map/ppermute | solution.py:689
  155.9 56.3 %collective-permute-start.34 = (f32[768,128]{1,0:T(8,128)S(1)}, f32[768,128]{1,0:T(8,128)S(1)}, u32[]{:S(2)}, u32[]{:S(2)}) collective-permute-start(f32[768,128]{1,0:T(8,128)S(1)} %step.5.a0), channel_id=1, source_target_pairs={{0,1},{1,2},{2,3},{3,0},{4,5},{5,6},{6,7},{7,4},{8,9},{9,10},{10,1... | collective-permute-start | bytes 1179656 | tf_op jit(solution)/shard_map/ppermute | solution.py:688
  212.3 28.8 %collective-permute-start.37 = (f32[384,128]{1,0:T(8,128)S(1)}, f32[384,128]{1,0:T(8,128)S(1)}, u32[]{:S(2)}, u32[]{:S(2)}) collective-permute-start(f32[384,128]{1,0:T(8,128)S(1)} %slice.7), channel_id=1, source_target_pairs={{0,3},{1,0},{2,1},{3,2},{4,7},{5,4},{6,5},{7,6},{8,11},{9,8},{10,9... | collective-permute-start | bytes 589832 | tf_op jit(solution)/shard_map/ppermute | solution.py:694
  216.6 24.5 %collective-permute-start.36 = (f32[384,128]{1,0:T(8,128)S(1)}, f32[384,128]{1,0:T(8,128)S(1)}, u32[]{:S(2)}, u32[]{:S(2)}) collective-permute-start(f32[384,128]{1,0:T(8,128)S(1)} %slice.6), channel_id=1, source_target_pairs={{0,1},{1,2},{2,3},{3,0},{4,5},{5,6},{6,7},{7,4},{8,9},{9,10},{10,1... | collective-permute-start | bytes 589832 | tf_op jit(solution)/shard_map/ppermute | solution.py:693
  219.2 11.5 %all-to-all-start.2 = ((f32[8,8,128]{2,1,0:T(8,128)}), f32[8,8,128]{2,1,0:T(8,128)S(1)}, u32[]{:S(2)}, u32[]{:S(2)}) async-start(f32[8,8,128]{2,1,0:T(8,128)} %broadcast_in_dim.7), calls=%async_computation.2 | async-start | bytes 65536 | tf_op jit(solution)/shard_map/all_to_all | solution.py:594
  231.3 9.9 %all-to-all-start.3 = ((f32[4,8,128]{2,1,0:T(8,128)}), f32[4,8,128]{2,1,0:T(8,128)S(1)}, u32[]{:S(2)}, u32[]{:S(2)}) async-start(f32[4,8,128]{2,1,0:T(8,128)} %broadcast_in_dim.8), calls=%async_computation.3 | async-start | bytes 32768 | tf_op jit(solution)/shard_map/all_to_all | solution.py:594

commit v4 on v2

--- a/solution.py
+++ b/solution.py
@@ -44,15 +44,6 @@
     return np.concatenate([high, low], axis=0)
 
 
-def group_table():
-    table = np.zeros((8 * 128, 128), np.float32)
-    for p in range(8):
-        for slot in range(16):
-            for k in range(8):
-                table[p * 128 + slot * 8 + k, slot * 8 + p] = 1.0
-    return table.astype(ml_dtypes.bfloat16)
-
-
 def split(a):
     high = a.astype(BF16)
     return high, (a - high.astype(F32)).astype(BF16)
@@ -106,7 +97,42 @@
             put(lo_ref, x * 3 + m, jnp.where(low, get(y_ref, x * 8 + m), pltpu.roll(get(y_ref, x * 8 + 3 + m), 4, 0)))
 
 
-def prep_kernel(offs, strg, cnt, orb, mu, proj, y_ref, t_ref, meta_ref, xr_ref, xl_ref, yh_ref, yl_ref):
+def sides(odd, even_op, odd_op):
+    return jnp.where(odd, even_op, odd_op), jnp.where(odd, odd_op, even_op)
+
+
+def send(flag, below, above, even_ref, odd_ref, tiles, base=0):
+    even_from = jnp.where(flag == 1, 0, 1)
+    for t in range(tiles):
+        one, two = get(below, t), get(above, t)
+        put(even_ref, base + t, jnp.where(even_from == 0, one, two))
+        put(odd_ref, base + t, jnp.where(even_from == 0, two, one))
+
+
+def take(flag, even_ref, odd_ref, target, rows, low_at, high_at):
+    even_at = pl.multiple_of(jnp.where(flag == 1, low_at, high_at), 8)
+    odd_at = pl.multiple_of(jnp.where(flag == 1, high_at, low_at), 8)
+    target[pl.ds(even_at, rows), :] = even_ref[0:rows, :]
+    target[pl.ds(odd_at, rows), :] = odd_ref[0:rows, :]
+
+
+def give_ends(flag, y_ref, even_ref, odd_ref):
+    rows = XH * 8
+    even_at = pl.multiple_of(jnp.where(flag == 1, 0, rows), 8)
+    odd_at = pl.multiple_of(jnp.where(flag == 1, rows, 0), 8)
+    even_ref[0:rows, :] = y_ref[pl.ds(even_at, rows), :]
+    odd_ref[0:rows, :] = y_ref[pl.ds(odd_at, rows), :]
+
+
+def prep_kernel(
+    flags, offs, strg, cnt, orb, mu, proj,
+    y_ref, t_ref, meta_ref, xe_ref, xo_ref, ye_ref, yo_ref, mu_out, g_ref, xr_ref, xl_ref, yh_ref, yl_ref
+):
+    mu_out[...] = mu[...]
+    at_row = lax.broadcasted_iota(jnp.int32, (1024, 128), 0)
+    at_column = lax.broadcasted_iota(jnp.int32, (1024, 128), 1)
+    same = (at_row % 128 // 8 == at_column // 8) & (at_row // 128 == at_column % 8)
+    g_ref[...] = jnp.where(same, 1.0, 0.0).astype(BF16)
     sub, lane = iotas()
     low = sub < 4
     left_half = lane < 64
@@ -115,17 +141,15 @@
             for h in range(2):
                 y_ref[pl.ds(x * 64 + 4 * h + o, 8, stride=8), :] = orb[o, x, 8 * h : 8 * h + 8, :]
     group = lane // 8
-    place = lane % 8
     meta = jnp.zeros((8, 128), F32)
     for s in range(8):
         for column in range(3):
-            value = offs[s, column].astype(F32)
+            value = offs[column, s].astype(F32)
             meta = jnp.where((group == s) & (sub == column), value, meta)
         alive = jnp.where(s < cnt[0], 1.0, 0.0).astype(F32)
         for p in range(8):
             weight = strg[s, p] * alive * (1.0 / (512.0 * filter_half))
             meta = jnp.where((lane == s * 8 + p) & (sub == 3), weight, meta)
-    del place
     meta_ref[...] = meta
     for i in range(8):
         for j in range(8):
@@ -137,14 +161,12 @@
                 moved = pltpu.roll(source, shift, 1) if shift else source
                 total = jnp.where(group == s, moved, total)
             put(t_ref, i * 8 + j, total)
-    for q in range(XH):
-        put(xr_ref, q, get(y_ref, XH + q))
-        put(xl_ref, q, get(y_ref, q))
+    give_ends(flags[0], y_ref, xe_ref, xo_ref)
     for x in range(HALO):
         for h in range(2):
-            put(xr_ref, XH + 2 * x + h, mu[CX - HALO + x, 8 * h : 8 * h + 8, :])
-            put(xl_ref, XH + 2 * x + h, mu[x, 8 * h : 8 * h + 8, :])
-    base = XH + 2 * HALO
+            put(xr_ref, 2 * x + h, mu[CX - HALO + x, 8 * h : 8 * h + 8, :])
+            put(xl_ref, 2 * x + h, mu[x, 8 * h : 8 * h + 8, :])
+    base = 2 * HALO
     for i in range(2):
         for j in range(8):
             for ref, first in ((xr_ref, 4), (xl_ref, 0)):
@@ -157,16 +179,22 @@
     for x in range(CX):
         put(yh_ref, YH + x, mu[x, 8:16, :])
         put(yl_ref, YH + x, mu[x, 0:8, :])
+    send(flags[0], xl_ref, xr_ref, xe_ref, xo_ref, 2 * HALO + 17, XH)
+    send(flags[1], yl_ref, yh_ref, ye_ref, yo_ref, FIRST_Y)
 
 
 FIRST_X = XH + 2 * HALO + 17
 FIRST_Y = YH + CX
 
 
-def widen_kernel(t_ref, meta_ref, fl_ref, fr_ref, t2_ref, m_ref, hi_ref, lo_ref):
+def widen_kernel(flags, t_ref, meta_ref, xe_ref, xo_ref, t2_ref, m_ref, ye_ref, yo_ref, fl_ref, fr_ref, hi_ref, lo_ref):
     _, lane = iotas()
     left_half = lane < 64
-    base = XH + 2 * HALO
+    base = 0
+    for t in range(17):
+        left, right = sides(flags[0] == 1, get(xe_ref, XH + 2 * HALO + t), get(xo_ref, XH + 2 * HALO + t))
+        put(fl_ref, t, left)
+        put(fr_ref, t, right)
     for i in range(8):
         for j in range(8):
             if i >= 4:
@@ -187,26 +215,29 @@
         put(m_ref, side, both)
         put(hi_ref, 32 + side, both)
         put(lo_ref, 32 + side, both)
-
-
-def coef_kernel(mu, pot, fl_ref, fr_ref, flo_ref, fhi_ref, dz_ref, out_ref, ex, ey):
+    send(flags[1], lo_ref, hi_ref, ye_ref, yo_ref, 34)
+
+
+def coef_kernel(flags, mu, pot, xe_ref, xo_ref, ye_ref, yo_ref, dz_ref, out_ref, ex, ey):
     sub, _ = iotas()
     low = sub < 4
 
     def two(a, ia, b, ib):
         return jnp.where(low, row(a, ia), row(b, ib))
 
+    ends = [sides(flags[0] == 1, get(xe_ref, XH + t), get(xo_ref, XH + t)) for t in range(2 * HALO)]
     for x in range(CX + 2 * HALO):
         if x < HALO:
-            a, b = get(fl_ref, XH + 2 * x), get(fl_ref, XH + 2 * x + 1)
+            a, b = ends[2 * x][0], ends[2 * x + 1][0]
         elif x < HALO + CX:
             a, b = mu[x - HALO, 0:8, :], mu[x - HALO, 8:16, :]
         else:
-            a, b = get(fr_ref, XH + 2 * (x - HALO - CX)), get(fr_ref, XH + 2 * (x - HALO - CX) + 1)
+            a, b = ends[2 * (x - HALO - CX)][1], ends[2 * (x - HALO - CX) + 1][1]
         for yl in range(8):
             put(ex, x * 8 + yl, two(a, yl, b, yl))
     for x in range(CX):
-        parts = [get(flo_ref, YH + x), mu[x, 0:8, :], mu[x, 8:16, :], get(fhi_ref, YH + x)]
+        lo_rim, hi_rim = sides(flags[1] == 1, get(ye_ref, YH + x), get(yo_ref, YH + x))
+        parts = [lo_rim, mu[x, 0:8, :], mu[x, 8:16, :], hi_rim]
         for n in range(20):
             y = n - HALO
             put(ey, x * 20 + n, two(parts[(y + 8) // 8], y % 8, parts[(y + 16) // 8], y % 8))
@@ -281,13 +312,21 @@
     z_ref[...] = pick(acc[...], g_ref[...])
 
 
-def send_coeffs(z_ref, xr_ref, xl_ref, base):
+def send_coeffs(flag, z_ref, xe_ref, xo_ref, base):
     for t in range(3):
-        put(xr_ref, base + t, pltpu.roll(get(z_ref, 3 + t), 64, 1))
-        put(xl_ref, base + t, pltpu.roll(get(z_ref, t), 64, 1))
-
-
-def build_kernel(t2_ref, m_ref, lo_ref, hi_ref, y_ref, g_ref, q_ref, s_ref, w_ref, z_ref, xr_ref, xl_ref, tx, acc):
+        left, right = pltpu.roll(get(z_ref, t), 64, 1), pltpu.roll(get(z_ref, 3 + t), 64, 1)
+        put(xe_ref, base + t, jnp.where(flag == 1, left, right))
+        put(xo_ref, base + t, jnp.where(flag == 1, right, left))
+
+
+def build_kernel(
+    flags, t2_ref, m_ref, ye_ref, yo_ref, y_ref, g_ref,
+    q_ref, s_ref, w_ref, z_ref, xe_ref, xo_ref, tx, acc, lo_ref, hi_ref
+):
+    for t in range(34):
+        lo, hi = sides(flags[1] == 1, get(ye_ref, t), get(yo_ref, t))
+        put(lo_ref, t, lo)
+        put(hi_ref, t, hi)
     sub, lane = iotas()
     low = sub < 4
     right_half = lane >= 64
@@ -342,35 +381,36 @@
                             value = jnp.where(low, row(rows[0], p), row(rows[1], p))
                             q_ref[base : base + 8, col * 128 : col * 128 + 128] = value
     partial_coeffs(y_ref, q_ref, s_ref, g_ref, z_ref, acc)
-    send_coeffs(z_ref, xr_ref, xl_ref, 0)
-
-
-def fold_kernel(base, z_ref, fl_ref, fr_ref, out_ref, hi_ref, lo_ref):
+    send_coeffs(flags[0], z_ref, xe_ref, xo_ref, 0)
+
+
+def fold_kernel(base, flags, z_ref, xe_ref, xo_ref, out_ref, ye_ref, yo_ref):
     _, lane = iotas()
     left_half = lane < 64
+    from_x = [sides(flags[0] == 1, get(xe_ref, base + t), get(xo_ref, base + t)) for t in range(3)]
     tiles = []
     for side in range(2):
-        near, far = (fl_ref, fr_ref) if side == 0 else (fr_ref, fl_ref)
         for t in range(3):
-            tiles.append(get(z_ref, side * 3 + t) + get(near, base + t) + jnp.where(left_half, get(far, base + t), 0.0))
+            near, far = from_x[t][side], from_x[t][1 - side]
+            tiles.append(get(z_ref, side * 3 + t) + near + jnp.where(left_half, far, 0.0))
     for t in range(6):
         put(out_ref, t, tiles[t])
     for side in range(2):
-        put(hi_ref, side * 2, tiles[side * 3 + 2])
-        put(hi_ref, side * 2 + 1, tiles[side * 3])
-        put(lo_ref, side * 2, tiles[side * 3 + 1])
-        put(lo_ref, side * 2 + 1, tiles[side * 3])
+        for n, (above, below) in enumerate(((2, 1), (0, 0))):
+            above, below = tiles[side * 3 + above], tiles[side * 3 + below]
+            put(ye_ref, side * 2 + n, jnp.where(flags[1] == 1, below, above))
+            put(yo_ref, side * 2 + n, jnp.where(flags[1] == 1, above, below))
 
 
 def step_kernel(
-    step, y_ref, prev_ref, fl_ref, fr_ref, plo_ref, phi_ref, coef_ref, q_ref, s_ref, w_ref, z_ref, clo_ref, chi_ref,
+    step, flags, y_ref, prev_ref, xe_ref, xo_ref, ye_ref, yo_ref, coef_ref, q_ref, s_ref, w_ref, z_ref, ce_ref, co_ref,
     dz_ref, g_ref, *rest
 ):
     last = step == STEPS
     if last:
-        new_ref, ex, ey, zd, acc, wp = rest
+        new_ref, ex, ey, zd, acc, wp, rims = rest
     else:
-        new_ref, xr_ref, xl_ref, yh_ref, yl_ref, zn_ref, ex, ey, zd, acc, wp = rest
+        new_ref, nxe_ref, nxo_ref, nye_ref, nyo_ref, zn_ref, ex, ey, zd, acc, wp, rims = rest
     sub, _ = iotas()
     low = sub < 4
     scale = 1.0 if step == 1 else 2.0
@@ -378,16 +418,18 @@
     high, rest_part = split(y_ref[...])
     zd[...] = mm(high, dz_ref[0:NZ, :]) + mm(rest_part, dz_ref[0:NZ, :]) + mm(high, dz_ref[NZ : 2 * NZ, :])
 
-    ex[0 : XH * 8, :] = fl_ref[0 : XH * 8, :]
+    take(flags[0], xe_ref, xo_ref, ex, XH * 8, 0, (XH + TILES) * 8)
+    take(flags[1], ye_ref, yo_ref, rims, YH * 8, 0, YH * 8)
     ex[XH * 8 : (XH + TILES) * 8, :] = y_ref[...]
-    ex[(XH + TILES) * 8 : (2 * XH + TILES) * 8, :] = fr_ref[0 : XH * 8, :]
     for x in range(CX):
         for yl in range(8):
             put(ey, x * 20 + HALO + yl, get(y_ref, x * 8 + yl))
+        lo_rims = [get(rims, x * 3 + m) for m in range(3)]
+        hi_rims = [get(rims, YH + x * 3 + m) for m in range(3)]
         for m in range(HALO):
-            rim = get(plo_ref, x * 3 + m) if m < 3 else pltpu.roll(get(plo_ref, x * 3 + m - 3), 4, 0)
+            rim = lo_rims[m] if m < 3 else pltpu.roll(lo_rims[m - 3], 4, 0)
             put(ey, x * 20 + m, jnp.where(low, rim, pltpu.roll(get(y_ref, x * 8 + 2 + m), 4, 0)))
-            rim = pltpu.roll(get(phi_ref, x * 3 + m), 4, 0) if m < 3 else get(phi_ref, x * 3 + m - 3)
+            rim = pltpu.roll(hi_rims[m], 4, 0) if m < 3 else hi_rims[m - 3]
             put(ey, x * 20 + HALO + 8 + m, jnp.where(low, pltpu.roll(get(y_ref, x * 8 + m), 4, 0), rim))
 
     def body(x, carry):
@@ -416,9 +458,10 @@
     tiles = []
     for side in range(2):
         own, lo, hi = (get(z_ref, side * 3 + t) for t in range(3))
-        tiles.append(own + get(clo_ref, side * 2) + get(chi_ref, side * 2))
-        tiles.append(lo + get(clo_ref, side * 2 + 1))
-        tiles.append(hi + get(chi_ref, side * 2 + 1))
+        tiles.append(own + get(ce_ref, side * 2) + get(co_ref, side * 2))
+        from_lo, from_hi = sides(flags[1] == 1, get(ce_ref, side * 2 + 1), get(co_ref, side * 2 + 1))
+        tiles.append(lo + from_lo)
+        tiles.append(hi + from_hi)
     weights = jnp.concatenate(tiles, axis=0) * w_ref[...] * scale
     wp[...] = pick_t(weights, g_ref[...])
 
@@ -440,20 +483,28 @@
                 new_ref[t * 8 : t * 8 + 32, :] += spread[a * 32 : a * 32 + 32, :]
 
     if not last:
-        for q in range(XH):
-            put(xr_ref, q, get(new_ref, XH + q))
-            put(xl_ref, q, get(new_ref, q))
-        pack_rims(new_ref, yh_ref, yl_ref, low)
+        give_ends(flags[0], new_ref, nxe_ref, nxo_ref)
+        pack_rims(new_ref, rims.at[pl.ds(YH * 8, YH * 8)], rims.at[pl.ds(0, YH * 8)], low)
+        rows = YH * 8
+        nye_ref[...] = rims[pl.ds(pl.multiple_of(jnp.where(flags[1] == 1, 0, rows), 8), rows), :]
+        nyo_ref[...] = rims[pl.ds(pl.multiple_of(jnp.where(flags[1] == 1, rows, 0), 8), rows), :]
         partial_coeffs(new_ref, q_ref, s_ref, g_ref, zn_ref, acc)
-        send_coeffs(zn_ref, xr_ref, xl_ref, XH)
-
-
-def gram_kernel(parts_ref, out_ref):
-    total = jnp.zeros((256, 256), F32)
-    for x in range(CX // 4):
-        field = jnp.concatenate([parts_ref[d, x * 64 : x * 64 + 64, :] for d in range(4)], axis=0)
+        send_coeffs(flags[0], zn_ref, nxe_ref, nxo_ref, XH)
+
+
+def gram_kernel(order, a0, a1, a2, a3, out_ref, held):
+    for n, ref in enumerate((a0, a1, a2, a3)):
+        held[order[n]] = ref[...]
+
+    def body(x, totals):
+        at = pl.ds(pl.multiple_of(x * 64, 64), 64)
+        field = jnp.concatenate([held[d, at, :] for d in range(4)], axis=0)
         high, low = split(field)
-        total = total + (mm_t(high, high) + mm_t(high, low) + mm_t(low, high))
+        return totals[0] + mm_t(high, high), totals[1] + mm_t(high, low)
+
+    zero = jnp.zeros((256, 256), F32)
+    total, mixed = lax.fori_loop(0, CX, body, (zero, zero))
+    total = total + mixed + mixed.T
     rows = lax.broadcasted_iota(jnp.int32, (256, 256), 0)
     columns = lax.broadcasted_iota(jnp.int32, (256, 256), 1)
     total = jnp.where((rows % 64) // 4 == (columns % 64) // 4, total, 0.0)
@@ -524,58 +575,75 @@
     return (count * 8, columns), dtype
 
 
-def beside(low_value, high_value, axis):
+def exchange(even_value, odd_value, axis):
     count = lax.axis_size(axis)
-    up = [(i, i + 1) for i in range(count - 1)]
-    down = [(i + 1, i) for i in range(count - 1)]
-    return lax.ppermute(low_value, axis, up), lax.ppermute(high_value, axis, down)
-
-
-def fold(z, from_left, from_right, tile):
+    results = []
+    for first, value in ((1, odd_value), (0, even_value)):
+        pairs = [p for i in range(first, count - 1, 2) for p in ((i, i + 1), (i + 1, i))]
+        results.append(lax.ppermute(value, axis, pairs))
+    return results[1], results[0]
+
+
+def spread_sum(value, axis):
+    copies = jnp.broadcast_to(value[None], (lax.axis_size(axis),) + value.shape)
+    return jnp.sum(lax.all_to_all(copies, axis, 0, 0, tiled=True), axis=0)
+
+
+def fold(flags, z, even, odd, tile):
     return kernel_call(
-        functools.partial(fold_kernel, tile), [blocks(6), blocks(4), blocks(4)], [VMEM] * 3, name="fold_coeffs"
-    )(z, from_left, from_right)
+        functools.partial(fold_kernel, tile), [blocks(6), blocks(4), blocks(4)], [SMEM] + [VMEM] * 3, name="fold_coeffs"
+    )(flags, z, even, odd)
 
 
 def shards(orbitals, potential, kinetic_mu, projectors, strengths, box_offsets, block_counts):
     dz = jnp.asarray(derivative_table())
-    groups = jnp.asarray(group_table())
-    y, t, meta, xr, xl, yh, yl = kernel_call(
+    flags = jnp.stack([lax.axis_index("gx") % 2, lax.axis_index("gy") % 2]).astype(jnp.int32)
+    mu_blocks = 2 * HALO + 17
+    y, t, meta, xe, xo, ye, yo, mu, groups = kernel_call(
         prep_kernel,
-        [blocks(TILES), blocks(64), blocks(1), blocks(FIRST_X), blocks(FIRST_X), blocks(FIRST_Y), blocks(FIRST_Y)],
-        [SMEM, SMEM, SMEM, VMEM, VMEM, VMEM],
+        [blocks(TILES), blocks(64), blocks(1), blocks(FIRST_X), blocks(FIRST_X), blocks(FIRST_Y), blocks(FIRST_Y)]
+        + [((CX, CY, NZ), F32), ((1024, 128), BF16)],
+        [SMEM] * 4 + [VMEM] * 3,
+        [
+            pltpu.VMEM((mu_blocks * 8, 128), F32),
+            pltpu.VMEM((mu_blocks * 8, 128), F32),
+            pltpu.VMEM((FIRST_Y * 8, 128), F32),
+            pltpu.VMEM((FIRST_Y * 8, 128), F32),
+        ],
         name="prepare",
-    )(box_offsets, strengths, block_counts, orbitals, kinetic_mu, projectors)
-    from_left, from_right = beside(xr, xl, "gx")
-    from_lo, from_hi = beside(yh, yl, "gy")
-    t2, metas, hi2, lo2 = kernel_call(
-        widen_kernel, [blocks(64), blocks(2), blocks(34), blocks(34)], [VMEM] * 4, name="widen"
-    )(t, meta, from_left, from_right)
-    from_lo2, from_hi2 = beside(hi2, lo2, "gy")
+    )(flags, box_offsets.T, strengths, block_counts, orbitals, kinetic_mu, projectors)
+    xe, xo = exchange(xe, xo, "gx")
+    t2, metas, ye2, yo2 = kernel_call(
+        widen_kernel,
+        [blocks(64), blocks(2), blocks(34), blocks(34)],
+        [SMEM] + [VMEM] * 4,
+        [pltpu.VMEM((17 * 8, 128), F32)] * 2 + [pltpu.VMEM((34 * 8, 128), F32)] * 2,
+        name="widen",
+    )(flags, t, meta, xe, xo)
+    ye, yo = exchange(ye, yo, "gy")
+    ye2, yo2 = exchange(ye2, yo2, "gy")
     (coefs,) = kernel_call(
         coef_kernel,
         [blocks(5 * TILES)],
-        [VMEM] * 7,
+        [SMEM] + [VMEM] * 7,
         [pltpu.VMEM(((TILES + 2 * XH) * 8, 128), F32), pltpu.VMEM((CX * 20 * 8, 128), F32)],
         name="coefficients",
-    )(kinetic_mu, potential, from_left, from_right, from_lo, from_hi, dz)
-    q, s, w, z, zr, zl = kernel_call(
+    )(flags, mu, potential, xe, xo, ye, yo, dz)
+    q, s, w, z, ce, co = kernel_call(
         build_kernel,
+        [blocks(6 * 8 * 16, 256), ((4 * 128, 256), BF16), blocks(6), blocks(6), blocks(3), blocks(3)],
+        [SMEM] + [VMEM] * 6,
         [
-            blocks(6 * 8 * 16, 256),
-            ((4 * 128, 256), BF16),
-            blocks(6),
-            blocks(6),
-            blocks(3),
-            blocks(3),
+            pltpu.VMEM((32 * 8, 128), F32),
+            pltpu.VMEM((48, 1024), F32),
+            pltpu.VMEM((34 * 8, 128), F32),
+            pltpu.VMEM((34 * 8, 128), F32),
         ],
-        [VMEM] * 6,
-        [pltpu.VMEM((32 * 8, 128), F32), pltpu.VMEM((48, 1024), F32)],
         name="build",
-    )(t2, metas, from_lo2, from_hi2, y, groups)
-    z_left, z_right = beside(zr, zl, "gx")
-    z, z_hi, z_lo = fold(z, z_left, z_right, 0)
-    c_lo, c_hi = beside(z_hi, z_lo, "gy")
+    )(flags, t2, metas, ye2, yo2, y, groups)
+    ce, co = exchange(ce, co, "gx")
+    z, ce, co = fold(flags, z, ce, co, 0)
+    ce, co = exchange(ce, co, "gy")
 
     previous = y
     for step in range(1, STEPS + 1):
@@ -586,44 +654,47 @@
         result = kernel_call(
             functools.partial(step_kernel, step),
             outs,
-            [VMEM] * 15,
+            [SMEM] + [VMEM] * 15,
             [
                 pltpu.VMEM(((TILES + 2 * XH) * 8, 128), F32),
                 pltpu.VMEM((CX * 20 * 8, 128), F32),
                 pltpu.VMEM((TILES * 8, 256), F32),
                 pltpu.VMEM((48, 1024), F32),
                 pltpu.VMEM((48, 1024), F32),
+                pltpu.VMEM((2 * YH * 8, 128), F32),
             ],
             name="step",
-        )(y, previous, from_left, from_right, from_lo, from_hi, coefs, q, s, w, z, c_lo, c_hi, dz, groups)
+        )(flags, y, previous, xe, xo, ye, yo, coefs, q, s, w, z, ce, co, dz, groups)
         previous = y
         if last:
             (y,) = result
         else:
-            y, xr, xl, yh, yl, z = result
-            from_left, from_right = beside(xr, xl, "gx")
-            from_lo, from_hi = beside(yh, yl, "gy")
-            z, z_hi, z_lo = fold(z, from_left, from_right, XH)
-            c_lo, c_hi = beside(z_hi, z_lo, "gy")
+            y, xe, xo, ye, yo, z = result
+            ye, yo = exchange(ye, yo, "gy")
+            xe, xo = exchange(xe, xo, "gx")
+            z, ce, co = fold(flags, z, xe, xo, XH)
+            ce, co = exchange(ce, co, "gy")
 
     count = lax.axis_size("orb")
     me = lax.axis_index("orb")
-    up = [(i, (i + 1) % count) for i in range(count)]
-    down = [(i, (i - 1) % count) for i in range(count)]
-    parts = lax.all_to_all(y.reshape(count, -1, NZ), "orb", 0, 0, tiled=True)
-    y, parts = lax.optimization_barrier((y, parts))
-    (corr,) = kernel_call(gram_kernel, [blocks(1)], [VMEM], name="gram")(parts)
-    below = lax.ppermute(y, "orb", up)
-    above = lax.ppermute(y, "orb", down)
+    even = [(i, i ^ 1) for i in range(count)]
+    odd = [(i, count - 1 - i) for i in range(count)]
+    one = lax.ppermute(y, "orb", even)
+    other = lax.ppermute(y, "orb", odd)
     half = TILES * 4
-    across_a = lax.ppermute(below[:half], "orb", up)
-    across_b = lax.ppermute(above[half:], "orb", down)
+    across_a = lax.ppermute(one[:half], "orb", odd)
+    across_b = lax.ppermute(other[half:], "orb", even)
     across = jnp.concatenate([across_a, across_b], axis=0)
-    order = jnp.stack([me, (me + count - 1) % count, (me + 1) % count, (me + 2) % count]).astype(jnp.int32)
-    for axis in ("orb", "gx", "gy"):
-        size = lax.axis_size(axis)
-        copies = jnp.broadcast_to(corr[None], (size, 8, 128))
-        corr = jnp.sum(lax.all_to_all(copies, axis, 0, 0, tiled=True), axis=0)
+    order = jnp.stack([me, me ^ 1, count - 1 - me, (me + 2) % count]).astype(jnp.int32)
+    (corr,) = kernel_call(
+        gram_kernel,
+        [blocks(1)],
+        [SMEM] + [VMEM] * 4,
+        [pltpu.VMEM((4, TILES * 8, 128), F32)],
+        name="gram",
+    )(order, y, one, other, across)
+    for axis in ("gx", "gy"):
+        corr = spread_sum(corr, axis)
     cells = CX * CY * NZ * lax.axis_size("gx") * lax.axis_size("gy")
     (result,) = kernel_call(
         functools.partial(rotate_kernel, cells),
@@ -631,7 +702,7 @@
         [SMEM] + [VMEM] * 5,
         [pltpu.VMEM((TILES * 8, 128), F32)],
         name="rotate",
-    )(order, corr, y, below, above, across)
+    )(order, corr, y, one, other, across)
     return result
 
 

time: 218 us -> 195 us (0.89)
  waiting for transfers between devices: 43.5 us -> 19.3 us
  starting transfers between devices: 114 us -> 98.1 us
  blocking collectives: 29 us -> 39.4 us
  Pallas kernels: 20.3 us -> 29.6 us
  local copies, waits for them, and re-layouts: 8.59 us -> 6.03 us
    all_to_all x1 -> x0, starting transfers between devices: 31.5 us -> none  [shards(): corr = jnp.sum(lax.all_to_all(copies, axis, 0, 0, tiled=True), axis=0)]
    ppermute x26, starting transfers between devices: 82.2 us -> 98.1 us  [the longest x22 83.8 us: exchange(): results.append(lax.ppermute(value, axis, pairs))]
    ppermute x26, waiting for transfers between devices: 32.1 us -> 19.3 us  [the longest x22 6.55 us: exchange(): results.append(lax.ppermute(value, axis, pairs))]
    all_to_all x1 -> x0, waiting for transfers between devices: 11.4 us -> none  [shards(): corr = jnp.sum(lax.all_to_all(copies, axis, 0, 0, tiled=True), axis=0)]
    all_to_all x3 -> x2, blocking collectives: 29 us -> 39.4 us  [spread_sum(): return jnp.sum(lax.all_to_all(copies, axis, 0, 0, tiled=True), axis=0)]
    pallas_call x5, Pallas kernels: 12.4 us -> 18.7 us  [the longest x3 12.6 us: shards(): kernel_call(functools.partial(step_kernel, step), outs, [SMEM] + [VMEM] *...]
    unnamed x21 -> x17, local copies, waits for them, and re-layouts: 7.92 us -> 5.97 us
  transfers between devices with their start and end apart: 27 -> 26, of which waited for: 9 -> 8; matrix products, arithmetic and copies ran while one was open for 0% -> 0% of each run, Pallas kernels for 2% -> 4%
where the time goes in v4:
time: 195 us; the launch traced here: 194 us
  starting transfers between devices  98.1 us (50%)
  blocking collectives  39.4 us (20%)
  Pallas kernels  29.6 us (15%)
  waiting for transfers between devices  19.3 us (10%)
  local copies, waits for them, and re-layouts  6.03 us (3%)
    ppermute x22, starting transfers between devices, exchange(): results.append(lax.ppermute(value, axis, pairs))  83.8 us
    all_to_all x2, blocking collectives, spread_sum(): return jnp.sum(lax.all_to_all(copies, axis, 0, 0, tiled=True), axis=0)  39.4 us
    pallas_call x3, Pallas kernels, shards(): kernel_call(functools.partial(step_kernel, step), outs, [SMEM] + [VMEM] *...  12.6 us
    ppermute x22, waiting for transfers between devices, exchange(): results.append(lax.ppermute(value, axis, pairs))  6.55 us
    ppermute x1, waiting for transfers between devices, shards(): one = lax.ppermute(y, 'orb', even)  6.43 us
    unnamed x17, local copies, waits for them, and re-layouts  5.97 us
    ppermute x1, starting transfers between devices, shards(): across_a = lax.ppermute(one[:half], 'orb', odd)  4.69 us
    pallas_call x1, Pallas kernels, shards(): kernel_call(gram_kernel, [blocks(1)], [SMEM] + [VMEM] * 4, [pltpu.VMEM((4...  4.49 us
  transfers between devices with their start and end apart: 26, of which 8 were waited for; matrix products, arithmetic and copies ran while one was open for 0% of the time, Pallas kernels for 4%

profile of v4, /device:TPU:8, one launch (start us, length us, event | category | flops | bytes accessed | tf_op | source)
XLA Modules:
  0.0 193.7 jit_solution(17254160449605928195)
XLA Ops:
  0.8 1.0 copy-done.2
  1.8 0.9 copy-done.3
  2.7 0.9 copy-done.5
  3.6 0.7 copy-done.6
  4.3 0.7 copy-done.7
  4.9 1.6 prepare.1
  6.5 1.9 collective-permute-start
  8.4 0.7 collective-permute-start.1
  9.1 7.7 %collective-permute-start.2 = (f32[384,128]{1,0:T(8,128)S(1)}, f32[384,128]{1,0:T(8,128)S(1)}, u32[]{:S(2)}, u32[]{:S(2)}) collective-permute-start(f32[384,128]{1,0:T(8,128)S(1)} %get-tuple-element.48), channel_id=1, source_target_pairs={{0,4},{4,0},{8,12},{12,8},{16,20},{20,16},{24,28},{28,24},{32,36},... | collective-permute-start | bytes 589832 | tf_op jit(solution)/shard_map/ppermute | solution.py:583
  16.9 1.9 collective-permute-start.3
  19.5 1.9 collective-permute-start.4
  21.4 3.9 %collective-permute-start.5 = (f32[272,128]{1,0:T(8,128)S(1)}, f32[272,128]{1,0:T(8,128)S(1)}, u32[]{:S(2)}, u32[]{:S(2)}) collective-permute-start(f32[272,128]{1,0:T(8,128)S(1)} %get-tuple-element.56), channel_id=1, source_target_pairs={{4,8},{8,4},{12,16},{16,12},{20,24},{24,20},{28,32},{32,28},{36,40... | collective-permute-start | bytes 417800 | tf_op jit(solution)/shard_map/ppermute | solution.py:583
  25.3 1.1 collective-permute-done.4.ye_ref
  26.4 1.9 collective-permute-done.5.yo_ref
  28.4 3.0 %build.1 = (f32[6144,256]{1,0:T(8,128)S(1)}, bf16[512,256]{1,0:T(8,128)(2,1)S(1)}, f32[48,128]{1,0:T(8,128)S(1)}, f32[48,128]{1,0:T(8,128)S(1)}, f32[24,128]{1,0:T(8,128)S(1)}, /*index=5*/f32[24,128]{1,0:T(8,128)S(1)}) custom-call(s32[2]{0:T(128)S(1)} %pad_add_fusion.1.flags, f32[512,128]{1,0:T(8,128)S(1)} %get-tuple-element.53.t2_ref, ...), custom_call_target="tpu_custom_call" | custom-call | tf_op jit(solution)/shard_map/build/pallas_call | solution.py:632
  31.3 5.0 %collective-permute-start.6 = (f32[24,128]{1,0:T(8,128)S(1)}, f32[24,128]{1,0:T(8,128)S(1)}, u32[]{:S(2)}, u32[]{:S(2)}) collective-permute-start(f32[24,128]{1,0:T(8,128)S(1)} %get-tuple-element.62), channel_id=1, source_target_pairs={{0,64},{64,0},{128,192},{192,128},{256,320},{320,256},{384,448},{4... | collective-permute-start | bytes 36872 | tf_op jit(solution)/shard_map/ppermute | solution.py:583
  37.7 1.9 collective-permute-start.8
  39.6 5.8 %collective-permute-start.9 = (f32[32,128]{1,0:T(8,128)S(1)}, f32[32,128]{1,0:T(8,128)S(1)}, u32[]{:S(2)}, u32[]{:S(2)}) collective-permute-start(f32[32,128]{1,0:T(8,128)S(1)} %get-tuple-element.66), channel_id=1, source_target_pairs={{4,8},{8,4},{12,16},{16,12},{20,24},{24,20},{28,32},{32,28},{36,40... | collective-permute-start | bytes 49160 | tf_op jit(solution)/shard_map/ppermute | solution.py:583
  45.5 0.9 copy-done
  46.4 0.9 copy-done.4
  47.3 1.6 coefficients.1.coef_ref
  49.0 4.4 %step.3 = (f32[768,128]{1,0:T(8,128)S(1)}, f32[408,128]{1,0:T(8,128)S(1)}, f32[408,128]{1,0:T(8,128)S(1)}, f32[288,128]{1,0:T(8,128)S(1)}, f32[288,128]{1,0:T(8,128)S(1)}, /*index=5*/f32[48,128]{1,0:T(8,128)S(1)}) custom-call(s32[2]{0:T(128)S(1)} %pad_add_fusion.1.flags, f32[768,128]{1,0:T(8,128)S(1)} %get-tuple-element.45.y_ref.prev_ref, ...), custom_call_target="tpu_custom_call" | custom-call | tf_op jit(solution)/shard_map/step/pallas_call | solution.py:654
  53.4 5.7 %collective-permute-start.10 = (f32[408,128]{1,0:T(8,128)S(1)}, f32[408,128]{1,0:T(8,128)S(1)}, u32[]{:S(2)}, u32[]{:S(2)}) collective-permute-start(f32[408,128]{1,0:T(8,128)S(1)} %get-tuple-element.68), channel_id=1, source_target_pairs={{0,64},{64,0},{128,192},{192,128},{256,320},{320,256},{384,448},{4... | collective-permute-start | bytes 626696 | tf_op jit(solution)/shard_map/ppermute | solution.py:583
  59.1 0.7 collective-permute-start.11
  59.8 1.9 collective-permute-start.12
  61.7 7.3 %collective-permute-start.13 = (f32[288,128]{1,0:T(8,128)S(1)}, f32[288,128]{1,0:T(8,128)S(1)}, u32[]{:S(2)}, u32[]{:S(2)}) collective-permute-start(f32[288,128]{1,0:T(8,128)S(1)} %get-tuple-element.71), channel_id=1, source_target_pairs={{4,8},{8,4},{12,16},{16,12},{20,24},{24,20},{28,32},{32,28},{36,40... | collective-permute-start | bytes 442376 | tf_op jit(solution)/shard_map/ppermute | solution.py:583
  69.6 1.9 collective-permute-start.14
  71.5 11.9 %collective-permute-start.15 = (f32[32,128]{1,0:T(8,128)S(1)}, f32[32,128]{1,0:T(8,128)S(1)}, u32[]{:S(2)}, u32[]{:S(2)}) collective-permute-start(f32[32,128]{1,0:T(8,128)S(1)} %get-tuple-element.75), channel_id=1, source_target_pairs={{4,8},{8,4},{12,16},{16,12},{20,24},{24,20},{28,32},{32,28},{36,40... | collective-permute-start | bytes 49160 | tf_op jit(solution)/shard_map/ppermute | solution.py:583
  83.5 1.7 collective-permute-done.15.co_ref
  85.1 4.5 %step.4 = (f32[768,128]{1,0:T(8,128)S(1)}, f32[408,128]{1,0:T(8,128)S(1)}, f32[408,128]{1,0:T(8,128)S(1)}, f32[288,128]{1,0:T(8,128)S(1)}, f32[288,128]{1,0:T(8,128)S(1)}, /*index=5*/f32[48,128]{1,0:T(8,128)S(1)}) custom-call(s32[2]{0:T(128)S(1)} %pad_add_fusion.1.flags, f32[768,128]{1,0:T(8,128)S(1)} %get-tuple-element.67.y_ref.prev_ref, ...), custom_call_target="tpu_custom_call" | custom-call | tf_op jit(solution)/shard_map/step/pallas_call | solution.py:654
  89.6 3.7 %collective-permute-start.16 = (f32[408,128]{1,0:T(8,128)S(1)}, f32[408,128]{1,0:T(8,128)S(1)}, u32[]{:S(2)}, u32[]{:S(2)}) collective-permute-start(f32[408,128]{1,0:T(8,128)S(1)} %get-tuple-element.77), channel_id=1, source_target_pairs={{0,64},{64,0},{128,192},{192,128},{256,320},{320,256},{384,448},{4... | collective-permute-start | bytes 626696 | tf_op jit(solution)/shard_map/ppermute | solution.py:583
  94.1 1.9 collective-permute-start.18
  96.0 8.1 %collective-permute-start.19 = (f32[288,128]{1,0:T(8,128)S(1)}, f32[288,128]{1,0:T(8,128)S(1)}, u32[]{:S(2)}, u32[]{:S(2)}) collective-permute-start(f32[288,128]{1,0:T(8,128)S(1)} %get-tuple-element.80), channel_id=1, source_target_pairs={{4,8},{8,4},{12,16},{16,12},{20,24},{24,20},{28,32},{32,28},{36,40... | collective-permute-start | bytes 442376 | tf_op jit(solution)/shard_map/ppermute | solution.py:583
  104.7 1.9 collective-permute-start.20
  106.6 6.6 %collective-permute-start.21 = (f32[32,128]{1,0:T(8,128)S(1)}, f32[32,128]{1,0:T(8,128)S(1)}, u32[]{:S(2)}, u32[]{:S(2)}) collective-permute-start(f32[32,128]{1,0:T(8,128)S(1)} %get-tuple-element.84), channel_id=1, source_target_pairs={{4,8},{8,4},{12,16},{16,12},{20,24},{24,20},{28,32},{32,28},{36,40... | collective-permute-start | bytes 49160 | tf_op jit(solution)/shard_map/ppermute | solution.py:583
  113.3 1.7 collective-permute-done.21.co_ref
  114.9 3.6 %step.5.a0 = f32[768,128]{1,0:T(8,128)S(1)} custom-call(s32[2]{0:T(128)S(1)} %pad_add_fusion.1.flags, f32[768,128]{1,0:T(8,128)S(1)} %get-tuple-element.76.y_ref, f32[768,128]{1,0:T(8,128)S(1)} %get-tuple-element.67.y_ref.prev_ref, f32[408,128]{1,0:T(8,128)S(1)} %collective-permute-done.16.xe_ref, f32[408,128]{1,0:T(8,128)S(1)} %collective-permute-done.17.xo_ref, ...), custom_call_target="tpu_custom_call" | custom-call | tf_op jit(solution)/shard_map/step/pallas_call | solution.py:654
  118.5 3.4 %collective-permute-start.22 = (f32[768,128]{1,0:T(8,128)S(1)}, f32[768,128]{1,0:T(8,128)S(1)}, u32[]{:S(2)}, u32[]{:S(2)}) collective-permute-start(f32[768,128]{1,0:T(8,128)S(1)} %step.5.a0), channel_id=1, source_target_pairs={{0,1},{1,0},{2,3},{3,2},{4,5},{5,4},{6,7},{7,6},{8,9},{9,8},{10,11... | collective-permute-start | bytes 1179656 | tf_op jit(solution)/shard_map/ppermute | solution.py:682
  122.0 4.0 %collective-permute-start.23 = (f32[768,128]{1,0:T(8,128)S(1)}, f32[768,128]{1,0:T(8,128)S(1)}, u32[]{:S(2)}, u32[]{:S(2)}) collective-permute-start(f32[768,128]{1,0:T(8,128)S(1)} %step.5.a0), channel_id=1, source_target_pairs={{0,3},{1,2},{2,1},{3,0},{4,7},{5,6},{6,5},{7,4},{8,11},{9,10},{10,... | collective-permute-start | bytes 1179656 | tf_op jit(solution)/shard_map/ppermute | solution.py:683
  126.0 6.4 %collective-permute-done.22.a1 = f32[768,128]{1,0:T(8,128)S(1)} collective-permute-done((f32[768,128]{1,0:T(8,128)S(1)}, f32[768,128]{1,0:T(8,128)S(1)}, u32[]{:S(2)}, u32[]{:S(2)}) %collective-permute-start.22) | collective-permute-done | bytes 393248 | tf_op jit(solution)/shard_map/ppermute | solution.py:682
  132.4 4.7 %collective-permute-start.24 = (f32[384,128]{1,0:T(8,128)S(1)}, f32[384,128]{1,0:T(8,128)S(1)}, u32[]{:S(2)}, u32[]{:S(2)}) collective-permute-start(f32[384,128]{1,0:T(8,128)S(1)} %slice.8), channel_id=1, source_target_pairs={{0,3},{1,2},{2,1},{3,0},{4,7},{5,6},{6,5},{7,4},{8,11},{9,10},{10,... | collective-permute-start | bytes 589832 | tf_op jit(solution)/shard_map/ppermute | solution.py:685
  137.2 2.1 %collective-permute-start.25 = (f32[384,128]{1,0:T(8,128)S(1)}, f32[384,128]{1,0:T(8,128)S(1)}, u32[]{:S(2)}, u32[]{:S(2)}) collective-permute-start(f32[384,128]{1,0:T(8,128)S(1)} %slice.9), channel_id=1, source_target_pairs={{0,1},{1,0},{2,3},{3,2},{4,5},{5,4},{6,7},{7,6},{8,9},{9,8},{10,11... | collective-permute-start | bytes 589832 | tf_op jit(solution)/shard_map/ppermute | solution.py:686
  139.4 3.1 %collective-permute-done.24 = f32[384,128]{1,0:T(8,128)S(1)} collective-permute-done((f32[384,128]{1,0:T(8,128)S(1)}, f32[384,128]{1,0:T(8,128)S(1)}, u32[]{:S(2)}, u32[]{:S(2)}) %collective-permute-start.24) | collective-permute-done | bytes 196640 | tf_op jit(solution)/shard_map/ppermute | solution.py:685
  142.5 3.2 %collective-permute-done.25 = f32[384,128]{1,0:T(8,128)S(1)} collective-permute-done((f32[384,128]{1,0:T(8,128)S(1)}, f32[384,128]{1,0:T(8,128)S(1)}, u32[]{:S(2)}, u32[]{:S(2)}) %collective-permute-start.25) | collective-permute-done | bytes 196640 | tf_op jit(solution)/shard_map/ppermute | solution.py:686
  145.7 4.5 %gram.1 = f32[8,128]{1,0:T(8,128)S(1)} custom-call(s32[4]{0:T(128)S(1)} %pad_add_fusion.order, f32[768,128]{1,0:T(8,128)S(1)} %step.5.a0, f32[768,128]{1,0:T(8,128)S(1)} %collective-permute-done.22.a1, f32[768,128]{1,0:T(8,128)S(1)} %collective-permute-done.23.a2, f32[768,128]{1,0:T(8,128)S(1)} %constant_dynamic-update-slice_fusion.a3), custom_call_target="tpu_custom_call" | custom-call | tf_op jit(solution)/shard_map/gram/pallas_call | solution.py:689
  150.2 9.3 %all_to_all.10 = f32[8,8,128]{2,1,0:T(8,128)S(1)} all-to-all(f32[8,8,128]{2,1,0:T(8,128)S(1)} %broadcast_in_dim.4), channel_id=1, replica_groups=mesh['gx'=8,'gy'=16,'orb'=4] {'gx'}, dimensions={0} | all-to-all | bytes 65536 | tf_op jit(solution)/shard_map/all_to_all | solution.py:589
  159.6 30.0 %all_to_all.11 = f32[16,8,128]{2,1,0:T(8,128)S(1)} all-to-all(f32[16,8,128]{2,1,0:T(8,128)S(1)} %broadcast_in_dim.5), channel_id=1, replica_groups=mesh['gx'=8,'gy'=16,'orb'=4] {'gy'}, dimensions={0} | all-to-all | bytes 131072 | tf_op jit(solution)/shard_map/all_to_all | solution.py:589
  189.6 4.1 %rotate.1 = f32[4,12,16,128]{3,2,1,0:T(8,128)} custom-call(s32[4]{0:T(128)S(1)} %pad_add_fusion.order, f32[8,128]{1,0:T(8,128)S(1)} %reduce_sum.19.corr_ref, f32[768,128]{1,0:T(8,128)S(1)} %step.5.a0, f32[768,128]{1,0:T(8,128)S(1)} %collective-permute-done.22.a1, f32[768,128]{1,0:T(8,128)S(1)} %collective-permute-done.23.a2, ...), custom_call_target="tpu_custom_call" | custom-call | tf_op jit(solution)/shard_map/rotate/pallas_call | solution.py:699
  (44 shorter events, 4.1 us)
Async XLA Ops:
  0.0 48.9 %copy-start.1 = (bf16[256,256]{1,0:T(8,128)(2,1)S(1)}, bf16[256,256]{1,0:T(8,128)(2,1)}, u32[]{:S(2)}) copy-start(bf16[256,256]{1,0:T(8,128)(2,1)} %constant.48.clone.dz_ref) | copy-start | bytes 393220
  0.8 1.0 copy-start.2
  1.8 0.9 copy-start.3
  2.7 0.9 copy-start.5
  3.6 0.7 copy-start.6
  4.3 0.7 copy-start.7
  6.5 12.3 %collective-permute-start = (f32[616,128]{1,0:T(8,128)S(1)}, f32[616,128]{1,0:T(8,128)S(1)}, u32[]{:S(2)}, u32[]{:S(2)}) collective-permute-start(f32[616,128]{1,0:T(8,128)S(1)} %get-tuple-element.46), channel_id=1, source_target_pairs={{0,64},{64,0},{128,192},{192,128},{256,320},{320,256},{384,448},{4... | collective-permute-start | bytes 946184 | tf_op jit(solution)/shard_map/ppermute | solution.py:583
  8.4 10.4 %collective-permute-start.1 = (f32[616,128]{1,0:T(8,128)S(1)}, f32[616,128]{1,0:T(8,128)S(1)}, u32[]{:S(2)}, u32[]{:S(2)}) collective-permute-start(f32[616,128]{1,0:T(8,128)S(1)} %get-tuple-element.47), channel_id=1, source_target_pairs={{64,128},{128,64},{192,256},{256,192},{320,384},{384,320},{65,129}... | collective-permute-start | bytes 946184 | tf_op jit(solution)/shard_map/ppermute | solution.py:583
  9.1 36.3 %collective-permute-start.2 = (f32[384,128]{1,0:T(8,128)S(1)}, f32[384,128]{1,0:T(8,128)S(1)}, u32[]{:S(2)}, u32[]{:S(2)}) collective-permute-start(f32[384,128]{1,0:T(8,128)S(1)} %get-tuple-element.48), channel_id=1, source_target_pairs={{0,4},{4,0},{8,12},{12,8},{16,20},{20,16},{24,28},{28,24},{32,36},... | collective-permute-start | bytes 589832 | tf_op jit(solution)/shard_map/ppermute | solution.py:583
  16.9 28.6 %collective-permute-start.3 = (f32[384,128]{1,0:T(8,128)S(1)}, f32[384,128]{1,0:T(8,128)S(1)}, u32[]{:S(2)}, u32[]{:S(2)}) collective-permute-start(f32[384,128]{1,0:T(8,128)S(1)} %get-tuple-element.49), channel_id=1, source_target_pairs={{4,8},{8,4},{12,16},{16,12},{20,24},{24,20},{28,32},{32,28},{36,40... | collective-permute-start | bytes 589832 | tf_op jit(solution)/shard_map/ppermute | solution.py:583
  19.5 6.9 %collective-permute-start.4 = (f32[272,128]{1,0:T(8,128)S(1)}, f32[272,128]{1,0:T(8,128)S(1)}, u32[]{:S(2)}, u32[]{:S(2)}) collective-permute-start(f32[272,128]{1,0:T(8,128)S(1)} %get-tuple-element.55), channel_id=1, source_target_pairs={{0,4},{4,0},{8,12},{12,8},{16,20},{20,16},{24,28},{28,24},{32,36},... | collective-permute-start | bytes 417800 | tf_op jit(solution)/shard_map/ppermute | solution.py:583
  21.4 6.9 %collective-permute-start.5 = (f32[272,128]{1,0:T(8,128)S(1)}, f32[272,128]{1,0:T(8,128)S(1)}, u32[]{:S(2)}, u32[]{:S(2)}) collective-permute-start(f32[272,128]{1,0:T(8,128)S(1)} %get-tuple-element.56), channel_id=1, source_target_pairs={{4,8},{8,4},{12,16},{16,12},{20,24},{24,20},{28,32},{32,28},{36,40... | collective-permute-start | bytes 417800 | tf_op jit(solution)/shard_map/ppermute | solution.py:583
  31.3 5.8 %collective-permute-start.6 = (f32[24,128]{1,0:T(8,128)S(1)}, f32[24,128]{1,0:T(8,128)S(1)}, u32[]{:S(2)}, u32[]{:S(2)}) collective-permute-start(f32[24,128]{1,0:T(8,128)S(1)} %get-tuple-element.62), channel_id=1, source_target_pairs={{0,64},{64,0},{128,192},{192,128},{256,320},{320,256},{384,448},{4... | collective-permute-start | bytes 36872 | tf_op jit(solution)/shard_map/ppermute | solution.py:583
  36.3 0.8 collective-permute-start.7
  37.7 11.2 %collective-permute-start.8 = (f32[32,128]{1,0:T(8,128)S(1)}, f32[32,128]{1,0:T(8,128)S(1)}, u32[]{:S(2)}, u32[]{:S(2)}) collective-permute-start(f32[32,128]{1,0:T(8,128)S(1)} %get-tuple-element.65), channel_id=1, source_target_pairs={{0,4},{4,0},{8,12},{12,8},{16,20},{20,16},{24,28},{28,24},{32,36},... | collective-permute-start | bytes 49160 | tf_op jit(solution)/shard_map/ppermute | solution.py:583
  39.6 9.3 %collective-permute-start.9 = (f32[32,128]{1,0:T(8,128)S(1)}, f32[32,128]{1,0:T(8,128)S(1)}, u32[]{:S(2)}, u32[]{:S(2)}) collective-permute-start(f32[32,128]{1,0:T(8,128)S(1)} %get-tuple-element.66), channel_id=1, source_target_pairs={{4,8},{8,4},{12,16},{16,12},{20,24},{24,20},{28,32},{32,28},{36,40... | collective-permute-start | bytes 49160 | tf_op jit(solution)/shard_map/ppermute | solution.py:583
  45.5 0.9 copy-start
  46.4 0.9 copy-start.4
  53.4 15.6 %collective-permute-start.10 = (f32[408,128]{1,0:T(8,128)S(1)}, f32[408,128]{1,0:T(8,128)S(1)}, u32[]{:S(2)}, u32[]{:S(2)}) collective-permute-start(f32[408,128]{1,0:T(8,128)S(1)} %get-tuple-element.68), channel_id=1, source_target_pairs={{0,64},{64,0},{128,192},{192,128},{256,320},{320,256},{384,448},{4... | collective-permute-start | bytes 626696 | tf_op jit(solution)/shard_map/ppermute | solution.py:583
  59.1 9.9 %collective-permute-start.11 = (f32[408,128]{1,0:T(8,128)S(1)}, f32[408,128]{1,0:T(8,128)S(1)}, u32[]{:S(2)}, u32[]{:S(2)}) collective-permute-start(f32[408,128]{1,0:T(8,128)S(1)} %get-tuple-element.69), channel_id=1, source_target_pairs={{64,128},{128,64},{192,256},{256,192},{320,384},{384,320},{65,129}... | collective-permute-start | bytes 626696 | tf_op jit(solution)/shard_map/ppermute | solution.py:583
  59.8 23.6 %collective-permute-start.12 = (f32[288,128]{1,0:T(8,128)S(1)}, f32[288,128]{1,0:T(8,128)S(1)}, u32[]{:S(2)}, u32[]{:S(2)}) collective-permute-start(f32[288,128]{1,0:T(8,128)S(1)} %get-tuple-element.70), channel_id=1, source_target_pairs={{0,4},{4,0},{8,12},{12,8},{16,20},{20,16},{24,28},{28,24},{32,36},... | collective-permute-start | bytes 442376 | tf_op jit(solution)/shard_map/ppermute | solution.py:583
  61.7 21.7 %collective-permute-start.13 = (f32[288,128]{1,0:T(8,128)S(1)}, f32[288,128]{1,0:T(8,128)S(1)}, u32[]{:S(2)}, u32[]{:S(2)}) collective-permute-start(f32[288,128]{1,0:T(8,128)S(1)} %get-tuple-element.71), channel_id=1, source_target_pairs={{4,8},{8,4},{12,16},{16,12},{20,24},{24,20},{28,32},{32,28},{36,40... | collective-permute-start | bytes 442376 | tf_op jit(solution)/shard_map/ppermute | solution.py:583
  69.6 13.8 %collective-permute-start.14 = (f32[32,128]{1,0:T(8,128)S(1)}, f32[32,128]{1,0:T(8,128)S(1)}, u32[]{:S(2)}, u32[]{:S(2)}) collective-permute-start(f32[32,128]{1,0:T(8,128)S(1)} %get-tuple-element.74), channel_id=1, source_target_pairs={{0,4},{4,0},{8,12},{12,8},{16,20},{20,16},{24,28},{28,24},{32,36},... | collective-permute-start | bytes 49160 | tf_op jit(solution)/shard_map/ppermute | solution.py:583
  71.5 13.6 %collective-permute-start.15 = (f32[32,128]{1,0:T(8,128)S(1)}, f32[32,128]{1,0:T(8,128)S(1)}, u32[]{:S(2)}, u32[]{:S(2)}) collective-permute-start(f32[32,128]{1,0:T(8,128)S(1)} %get-tuple-element.75), channel_id=1, source_target_pairs={{4,8},{8,4},{12,16},{16,12},{20,24},{24,20},{28,32},{32,28},{36,40... | collective-permute-start | bytes 49160 | tf_op jit(solution)/shard_map/ppermute | solution.py:583
  89.6 14.5 %collective-permute-start.16 = (f32[408,128]{1,0:T(8,128)S(1)}, f32[408,128]{1,0:T(8,128)S(1)}, u32[]{:S(2)}, u32[]{:S(2)}) collective-permute-start(f32[408,128]{1,0:T(8,128)S(1)} %get-tuple-element.77), channel_id=1, source_target_pairs={{0,64},{64,0},{128,192},{192,128},{256,320},{320,256},{384,448},{4... | collective-permute-start | bytes 626696 | tf_op jit(solution)/shard_map/ppermute | solution.py:583
  93.4 10.8 %collective-permute-start.17 = (f32[408,128]{1,0:T(8,128)S(1)}, f32[408,128]{1,0:T(8,128)S(1)}, u32[]{:S(2)}, u32[]{:S(2)}) collective-permute-start(f32[408,128]{1,0:T(8,128)S(1)} %get-tuple-element.78), channel_id=1, source_target_pairs={{64,128},{128,64},{192,256},{256,192},{320,384},{384,320},{65,129}... | collective-permute-start | bytes 626696 | tf_op jit(solution)/shard_map/ppermute | solution.py:583
  94.1 19.2 %collective-permute-start.18 = (f32[288,128]{1,0:T(8,128)S(1)}, f32[288,128]{1,0:T(8,128)S(1)}, u32[]{:S(2)}, u32[]{:S(2)}) collective-permute-start(f32[288,128]{1,0:T(8,128)S(1)} %get-tuple-element.79), channel_id=1, source_target_pairs={{0,4},{4,0},{8,12},{12,8},{16,20},{20,16},{24,28},{28,24},{32,36},... | collective-permute-start | bytes 442376 | tf_op jit(solution)/shard_map/ppermute | solution.py:583
  96.0 17.3 %collective-permute-start.19 = (f32[288,128]{1,0:T(8,128)S(1)}, f32[288,128]{1,0:T(8,128)S(1)}, u32[]{:S(2)}, u32[]{:S(2)}) collective-permute-start(f32[288,128]{1,0:T(8,128)S(1)} %get-tuple-element.80), channel_id=1, source_target_pairs={{4,8},{8,4},{12,16},{16,12},{20,24},{24,20},{28,32},{32,28},{36,40... | collective-permute-start | bytes 442376 | tf_op jit(solution)/shard_map/ppermute | solution.py:583
  104.7 8.5 %collective-permute-start.20 = (f32[32,128]{1,0:T(8,128)S(1)}, f32[32,128]{1,0:T(8,128)S(1)}, u32[]{:S(2)}, u32[]{:S(2)}) collective-permute-start(f32[32,128]{1,0:T(8,128)S(1)} %get-tuple-element.83), channel_id=1, source_target_pairs={{0,4},{4,0},{8,12},{12,8},{16,20},{20,16},{24,28},{28,24},{32,36},... | collective-permute-start | bytes 49160 | tf_op jit(solution)/shard_map/ppermute | solution.py:583
  106.6 8.3 %collective-permute-start.21 = (f32[32,128]{1,0:T(8,128)S(1)}, f32[32,128]{1,0:T(8,128)S(1)}, u32[]{:S(2)}, u32[]{:S(2)}) collective-permute-start(f32[32,128]{1,0:T(8,128)S(1)} %get-tuple-element.84), channel_id=1, source_target_pairs={{4,8},{8,4},{12,16},{16,12},{20,24},{24,20},{28,32},{32,28},{36,40... | collective-permute-start | bytes 49160 | tf_op jit(solution)/shard_map/ppermute | solution.py:583
  118.5 13.9 %collective-permute-start.22 = (f32[768,128]{1,0:T(8,128)S(1)}, f32[768,128]{1,0:T(8,128)S(1)}, u32[]{:S(2)}, u32[]{:S(2)}) collective-permute-start(f32[768,128]{1,0:T(8,128)S(1)} %step.5.a0), channel_id=1, source_target_pairs={{0,1},{1,0},{2,3},{3,2},{4,5},{5,4},{6,7},{7,6},{8,9},{9,8},{10,11... | collective-permute-start | bytes 1179656 | tf_op jit(solution)/shard_map/ppermute | solution.py:682
  122.0 15.2 %collective-permute-start.23 = (f32[768,128]{1,0:T(8,128)S(1)}, f32[768,128]{1,0:T(8,128)S(1)}, u32[]{:S(2)}, u32[]{:S(2)}) collective-permute-start(f32[768,128]{1,0:T(8,128)S(1)} %step.5.a0), channel_id=1, source_target_pairs={{0,3},{1,2},{2,1},{3,0},{4,7},{5,6},{6,5},{7,4},{8,11},{9,10},{10,... | collective-permute-start | bytes 1179656 | tf_op jit(solution)/shard_map/ppermute | solution.py:683
  132.4 10.0 %collective-permute-start.24 = (f32[384,128]{1,0:T(8,128)S(1)}, f32[384,128]{1,0:T(8,128)S(1)}, u32[]{:S(2)}, u32[]{:S(2)}) collective-permute-start(f32[384,128]{1,0:T(8,128)S(1)} %slice.8), channel_id=1, source_target_pairs={{0,3},{1,2},{2,1},{3,0},{4,7},{5,6},{6,5},{7,4},{8,11},{9,10},{10,... | collective-permute-start | bytes 589832 | tf_op jit(solution)/shard_map/ppermute | solution.py:685
  137.2 8.5 %collective-permute-start.25 = (f32[384,128]{1,0:T(8,128)S(1)}, f32[384,128]{1,0:T(8,128)S(1)}, u32[]{:S(2)}, u32[]{:S(2)}) collective-permute-start(f32[384,128]{1,0:T(8,128)S(1)} %slice.9), channel_id=1, source_target_pairs={{0,1},{1,0},{2,3},{3,2},{4,5},{5,4},{6,7},{7,6},{8,9},{9,8},{10,11... | collective-permute-start | bytes 589832 | tf_op jit(solution)/shard_map/ppermute | solution.py:686

commit v5 on v4

--- a/solution.py
+++ b/solution.py
@@ -124,22 +124,13 @@
     odd_ref[0:rows, :] = y_ref[pl.ds(odd_at, rows), :]
 
 
-def prep_kernel(
-    flags, offs, strg, cnt, orb, mu, proj,
-    y_ref, t_ref, meta_ref, xe_ref, xo_ref, ye_ref, yo_ref, mu_out, g_ref, xr_ref, xl_ref, yh_ref, yl_ref
-):
-    mu_out[...] = mu[...]
+def prep_slots_kernel(flags, offs, strg, cnt, proj, t_ref, meta_ref, xe_ref, xo_ref, g_ref, xr_ref, xl_ref):
     at_row = lax.broadcasted_iota(jnp.int32, (1024, 128), 0)
     at_column = lax.broadcasted_iota(jnp.int32, (1024, 128), 1)
     same = (at_row % 128 // 8 == at_column // 8) & (at_row // 128 == at_column % 8)
     g_ref[...] = jnp.where(same, 1.0, 0.0).astype(BF16)
     sub, lane = iotas()
-    low = sub < 4
     left_half = lane < 64
-    for x in range(CX):
-        for o in range(ORB):
-            for h in range(2):
-                y_ref[pl.ds(x * 64 + 4 * h + o, 8, stride=8), :] = orb[o, x, 8 * h : 8 * h + 8, :]
     group = lane // 8
     meta = jnp.zeros((8, 128), F32)
     for s in range(8):
@@ -161,30 +152,37 @@
                 moved = pltpu.roll(source, shift, 1) if shift else source
                 total = jnp.where(group == s, moved, total)
             put(t_ref, i * 8 + j, total)
-    give_ends(flags[0], y_ref, xe_ref, xo_ref)
-    for x in range(HALO):
-        for h in range(2):
-            put(xr_ref, 2 * x + h, mu[CX - HALO + x, 8 * h : 8 * h + 8, :])
-            put(xl_ref, 2 * x + h, mu[x, 8 * h : 8 * h + 8, :])
-    base = 2 * HALO
     for i in range(2):
         for j in range(8):
             for ref, first in ((xr_ref, 4), (xl_ref, 0)):
                 one = get(t_ref, (first + i) * 8 + j)
                 two = pltpu.roll(get(t_ref, (first + 2 + i) * 8 + j), 64, 1)
-                put(ref, base + i * 8 + j, jnp.where(left_half, one, two))
-    put(xr_ref, base + 16, meta)
-    put(xl_ref, base + 16, meta)
-    pack_rims(y_ref, yh_ref, yl_ref, low)
+                put(ref, i * 8 + j, jnp.where(left_half, one, two))
+    put(xr_ref, 16, meta)
+    put(xl_ref, 16, meta)
+    send(flags[0], xl_ref, xr_ref, xe_ref, xo_ref, 17)
+
+
+def prep_fields_kernel(orb, mu, pot, y_ref, mu_out, pot_out):
+    mu_out[...] = mu[...]
+    pot_out[...] = pot[...]
     for x in range(CX):
-        put(yh_ref, YH + x, mu[x, 8:16, :])
-        put(yl_ref, YH + x, mu[x, 0:8, :])
-    send(flags[0], xl_ref, xr_ref, xe_ref, xo_ref, 2 * HALO + 17, XH)
-    send(flags[1], yl_ref, yh_ref, ye_ref, yo_ref, FIRST_Y)
-
-
-FIRST_X = XH + 2 * HALO + 17
-FIRST_Y = YH + CX
+        for o in range(ORB):
+            for h in range(2):
+                y_ref[pl.ds(x * 64 + 4 * h + o, 8, stride=8), :] = orb[o, x, 8 * h : 8 * h + 8, :]
+
+
+X_SUMS, Y_SUMS = XH, YH
+X_MU, Y_MU = XH + 3, YH + 4
+X_ALL, Y_ALL = X_MU + 2 * HALO, Y_MU + CX
+
+
+def send_rims(flag, y_ref, rims, ye_ref, yo_ref):
+    low = iotas()[0] < 4
+    rows = YH * 8
+    pack_rims(y_ref, rims.at[pl.ds(rows, rows)], rims.at[pl.ds(0, rows)], low)
+    ye_ref[0:rows, :] = rims[pl.ds(pl.multiple_of(jnp.where(flag == 1, 0, rows), 8), rows), :]
+    yo_ref[0:rows, :] = rims[pl.ds(pl.multiple_of(jnp.where(flag == 1, rows, 0), 8), rows), :]
 
 
 def widen_kernel(flags, t_ref, meta_ref, xe_ref, xo_ref, t2_ref, m_ref, ye_ref, yo_ref, fl_ref, fr_ref, hi_ref, lo_ref):
@@ -192,7 +190,7 @@
     left_half = lane < 64
     base = 0
     for t in range(17):
-        left, right = sides(flags[0] == 1, get(xe_ref, XH + 2 * HALO + t), get(xo_ref, XH + 2 * HALO + t))
+        left, right = sides(flags[0] == 1, get(xe_ref, t), get(xo_ref, t))
         put(fl_ref, t, left)
         put(fr_ref, t, right)
     for i in range(8):
@@ -225,7 +223,7 @@
     def two(a, ia, b, ib):
         return jnp.where(low, row(a, ia), row(b, ib))
 
-    ends = [sides(flags[0] == 1, get(xe_ref, XH + t), get(xo_ref, XH + t)) for t in range(2 * HALO)]
+    ends = [sides(flags[0] == 1, get(xe_ref, X_MU + t), get(xo_ref, X_MU + t)) for t in range(2 * HALO)]
     for x in range(CX + 2 * HALO):
         if x < HALO:
             a, b = ends[2 * x][0], ends[2 * x + 1][0]
@@ -236,7 +234,7 @@
         for yl in range(8):
             put(ex, x * 8 + yl, two(a, yl, b, yl))
     for x in range(CX):
-        lo_rim, hi_rim = sides(flags[1] == 1, get(ye_ref, YH + x), get(yo_ref, YH + x))
+        lo_rim, hi_rim = sides(flags[1] == 1, get(ye_ref, Y_MU + x), get(yo_ref, Y_MU + x))
         parts = [lo_rim, mu[x, 0:8, :], mu[x, 8:16, :], hi_rim]
         for n in range(20):
             y = n - HALO
@@ -312,16 +310,17 @@
     z_ref[...] = pick(acc[...], g_ref[...])
 
 
-def send_coeffs(flag, z_ref, xe_ref, xo_ref, base):
-    for t in range(3):
-        left, right = pltpu.roll(get(z_ref, t), 64, 1), pltpu.roll(get(z_ref, 3 + t), 64, 1)
-        put(xe_ref, base + t, jnp.where(flag == 1, left, right))
-        put(xo_ref, base + t, jnp.where(flag == 1, right, left))
+def send_coeffs(flag, z_ref, ye_ref, yo_ref, base):
+    for side in range(2):
+        for n, (above, below) in enumerate(((2, 1), (0, 0))):
+            above, below = get(z_ref, side * 3 + above), get(z_ref, side * 3 + below)
+            put(ye_ref, base + side * 2 + n, jnp.where(flag == 1, below, above))
+            put(yo_ref, base + side * 2 + n, jnp.where(flag == 1, above, below))
 
 
 def build_kernel(
-    flags, t2_ref, m_ref, ye_ref, yo_ref, y_ref, g_ref,
-    q_ref, s_ref, w_ref, z_ref, xe_ref, xo_ref, tx, acc, lo_ref, hi_ref
+    flags, t2_ref, m_ref, ye_ref, yo_ref, y_ref, mu, g_ref,
+    q_ref, s_ref, w_ref, z_ref, nye_ref, nyo_ref, tx, acc, lo_ref, hi_ref, rims
 ):
     for t in range(34):
         lo, hi = sides(flags[1] == 1, get(ye_ref, t), get(yo_ref, t))
@@ -381,37 +380,48 @@
                             value = jnp.where(low, row(rows[0], p), row(rows[1], p))
                             q_ref[base : base + 8, col * 128 : col * 128 + 128] = value
     partial_coeffs(y_ref, q_ref, s_ref, g_ref, z_ref, acc)
-    send_coeffs(flags[0], z_ref, xe_ref, xo_ref, 0)
-
-
-def fold_kernel(base, flags, z_ref, xe_ref, xo_ref, out_ref, ye_ref, yo_ref):
-    _, lane = iotas()
-    left_half = lane < 64
-    from_x = [sides(flags[0] == 1, get(xe_ref, base + t), get(xo_ref, base + t)) for t in range(3)]
-    tiles = []
+    send_coeffs(flags[1], z_ref, nye_ref, nyo_ref, Y_SUMS)
+    send_rims(flags[1], y_ref, rims, nye_ref, nyo_ref)
+    for x in range(CX):
+        below, above = mu[x, 0:8, :], mu[x, 8:16, :]
+        put(nye_ref, Y_MU + x, jnp.where(flags[1] == 1, below, above))
+        put(nyo_ref, Y_MU + x, jnp.where(flags[1] == 1, above, below))
+
+
+def fold_kernel(flags, z_ref, y_ref, ye_ref, yo_ref, *rest):
+    out_ref, xe_ref, xo_ref = rest[-3:]
+    give_ends(flags[0], y_ref, xe_ref, xo_ref)
+    if len(rest) == 4:
+        mu = rest[0]
+        for x in range(HALO):
+            for h in range(2):
+                left, right = mu[x, 8 * h : 8 * h + 8, :], mu[CX - HALO + x, 8 * h : 8 * h + 8, :]
+                put(xe_ref, X_MU + 2 * x + h, jnp.where(flags[0] == 1, left, right))
+                put(xo_ref, X_MU + 2 * x + h, jnp.where(flags[0] == 1, right, left))
+    base = Y_SUMS
     for side in range(2):
-        for t in range(3):
-            near, far = from_x[t][side], from_x[t][1 - side]
-            tiles.append(get(z_ref, side * 3 + t) + near + jnp.where(left_half, far, 0.0))
-    for t in range(6):
-        put(out_ref, t, tiles[t])
-    for side in range(2):
-        for n, (above, below) in enumerate(((2, 1), (0, 0))):
-            above, below = tiles[side * 3 + above], tiles[side * 3 + below]
-            put(ye_ref, side * 2 + n, jnp.where(flags[1] == 1, below, above))
-            put(yo_ref, side * 2 + n, jnp.where(flags[1] == 1, above, below))
+        own, lo, hi = (get(z_ref, side * 3 + t) for t in range(3))
+        across = [(get(ye_ref, base + side * 2 + n), get(yo_ref, base + side * 2 + n)) for n in range(2)]
+        from_lo, from_hi = sides(flags[1] == 1, *across[1])
+        put(out_ref, side * 3, own + across[0][0] + across[0][1])
+        put(out_ref, side * 3 + 1, lo + from_lo)
+        put(out_ref, side * 3 + 2, hi + from_hi)
+    for t in range(3):
+        left, right = pltpu.roll(get(out_ref, t), 64, 1), pltpu.roll(get(out_ref, 3 + t), 64, 1)
+        put(xe_ref, X_SUMS + t, jnp.where(flags[0] == 1, left, right))
+        put(xo_ref, X_SUMS + t, jnp.where(flags[0] == 1, right, left))
 
 
 def step_kernel(
-    step, flags, y_ref, prev_ref, xe_ref, xo_ref, ye_ref, yo_ref, coef_ref, q_ref, s_ref, w_ref, z_ref, ce_ref, co_ref,
+    step, flags, y_ref, prev_ref, xe_ref, xo_ref, ye_ref, yo_ref, coef_ref, q_ref, s_ref, w_ref, z_ref,
     dz_ref, g_ref, *rest
 ):
     last = step == STEPS
     if last:
-        new_ref, ex, ey, zd, acc, wp, rims = rest
+        first_ref, second_ref, ex, ey, zd, wp, rims, new_ref = rest
     else:
-        new_ref, nxe_ref, nxo_ref, nye_ref, nyo_ref, zn_ref, ex, ey, zd, acc, wp, rims = rest
-    sub, _ = iotas()
+        new_ref, nye_ref, nyo_ref, zn_ref, ex, ey, zd, wp, rims, acc = rest
+    sub, lane = iotas()
     low = sub < 4
     scale = 1.0 if step == 1 else 2.0
 
@@ -455,13 +465,13 @@
 
     lax.fori_loop(0, CX, body, 0)
 
+    left_half = lane < 64
+    from_x = [sides(flags[0] == 1, get(xe_ref, X_SUMS + t), get(xo_ref, X_SUMS + t)) for t in range(3)]
     tiles = []
     for side in range(2):
-        own, lo, hi = (get(z_ref, side * 3 + t) for t in range(3))
-        tiles.append(own + get(ce_ref, side * 2) + get(co_ref, side * 2))
-        from_lo, from_hi = sides(flags[1] == 1, get(ce_ref, side * 2 + 1), get(co_ref, side * 2 + 1))
-        tiles.append(lo + from_lo)
-        tiles.append(hi + from_hi)
+        for t in range(3):
+            near, far = from_x[t][side], from_x[t][1 - side]
+            tiles.append(get(z_ref, side * 3 + t) + near + jnp.where(left_half, far, 0.0))
     weights = jnp.concatenate(tiles, axis=0) * w_ref[...] * scale
     wp[...] = pick_t(weights, g_ref[...])
 
@@ -482,19 +492,21 @@
             for a, t in enumerate(block_tiles(xt, yq)):
                 new_ref[t * 8 : t * 8 + 32, :] += spread[a * 32 : a * 32 + 32, :]
 
-    if not last:
-        give_ends(flags[0], new_ref, nxe_ref, nxo_ref)
-        pack_rims(new_ref, rims.at[pl.ds(YH * 8, YH * 8)], rims.at[pl.ds(0, YH * 8)], low)
-        rows = YH * 8
-        nye_ref[...] = rims[pl.ds(pl.multiple_of(jnp.where(flags[1] == 1, 0, rows), 8), rows), :]
-        nyo_ref[...] = rims[pl.ds(pl.multiple_of(jnp.where(flags[1] == 1, rows, 0), 8), rows), :]
+    if last:
+        half = TILES * 4
+        first_ref[...] = new_ref[0:half, :]
+        second_ref[...] = new_ref[half : 2 * half, :]
+    else:
+        send_rims(flags[1], new_ref, rims, nye_ref, nyo_ref)
         partial_coeffs(new_ref, q_ref, s_ref, g_ref, zn_ref, acc)
-        send_coeffs(flags[0], zn_ref, nxe_ref, nxo_ref, XH)
-
-
-def gram_kernel(order, a0, a1, a2, a3, out_ref, held):
-    for n, ref in enumerate((a0, a1, a2, a3)):
-        held[order[n]] = ref[...]
+        send_coeffs(flags[1], zn_ref, nye_ref, nyo_ref, Y_SUMS)
+
+
+def gram_kernel(order, *refs):
+    out_ref, held = refs[8:]
+    for n in range(4):
+        for h in range(2):
+            held[order[n], h * TILES * 4 : (h + 1) * TILES * 4, :] = refs[2 * n + h][...]
 
     def body(x, totals):
         at = pl.ds(pl.multiple_of(x * 64, 64), 64)
@@ -520,7 +532,8 @@
     out_ref[:, 16:32] = small[8:16]
 
 
-def rotate_kernel(cells, order, corr_ref, a0, a1, a2, a3, out_ref, flat):
+def rotate_kernel(cells, order, corr_ref, *refs):
+    out_ref, flat = refs[8:]
     lane = lax.broadcasted_iota(jnp.int32, (16, 128), 1)
     rows = lax.broadcasted_iota(jnp.int32, (16, 128), 0)
     packed = corr_ref[...]
@@ -550,7 +563,8 @@
     mixing = jnp.where(at_row // 4 == at_column % 64 // 4, mixing, 0.0)
     mix_high, mix_low = split(mixing)
     for x in range(CX):
-        field = jnp.concatenate([ref[x * 64 : x * 64 + 64, :] for ref in (a0, a1, a2, a3)], axis=0)
+        at = x % (CX // 2) * 64
+        field = jnp.concatenate([refs[2 * n + x // (CX // 2)][at : at + 64, :] for n in range(4)], axis=0)
         high, low = split(field)
         flat[x * 64 : x * 64 + 64, :] = mm(mix_high, high) + mm(mix_high, low) + mm(mix_low, high)
     for o in range(ORB):
@@ -589,120 +603,118 @@
     return jnp.sum(lax.all_to_all(copies, axis, 0, 0, tiled=True), axis=0)
 
 
-def fold(flags, z, even, odd, tile):
+def fold(flags, z, y, even, odd, *mu):
+    count = X_ALL if mu else X_MU
     return kernel_call(
-        functools.partial(fold_kernel, tile), [blocks(6), blocks(4), blocks(4)], [SMEM] + [VMEM] * 3, name="fold_coeffs"
-    )(flags, z, even, odd)
+        fold_kernel, [blocks(6), blocks(count), blocks(count)], [SMEM] + [VMEM] * (4 + len(mu)), name="fold_coeffs"
+    )(flags, z, y, even, odd, *mu)
 
 
 def shards(orbitals, potential, kinetic_mu, projectors, strengths, box_offsets, block_counts):
     dz = jnp.asarray(derivative_table())
     flags = jnp.stack([lax.axis_index("gx") % 2, lax.axis_index("gy") % 2]).astype(jnp.int32)
-    mu_blocks = 2 * HALO + 17
-    y, t, meta, xe, xo, ye, yo, mu, groups = kernel_call(
-        prep_kernel,
-        [blocks(TILES), blocks(64), blocks(1), blocks(FIRST_X), blocks(FIRST_X), blocks(FIRST_Y), blocks(FIRST_Y)]
-        + [((CX, CY, NZ), F32), ((1024, 128), BF16)],
-        [SMEM] * 4 + [VMEM] * 3,
-        [
-            pltpu.VMEM((mu_blocks * 8, 128), F32),
-            pltpu.VMEM((mu_blocks * 8, 128), F32),
-            pltpu.VMEM((FIRST_Y * 8, 128), F32),
-            pltpu.VMEM((FIRST_Y * 8, 128), F32),
-        ],
-        name="prepare",
-    )(flags, box_offsets.T, strengths, block_counts, orbitals, kinetic_mu, projectors)
-    xe, xo = exchange(xe, xo, "gx")
+    t, meta, xte, xto, groups = kernel_call(
+        prep_slots_kernel,
+        [blocks(64), blocks(1), blocks(17), blocks(17), ((1024, 128), BF16)],
+        [SMEM] * 4 + [VMEM],
+        [pltpu.VMEM((17 * 8, 128), F32)] * 2,
+        name="prepare_slots",
+    )(flags, box_offsets.T, strengths, block_counts, projectors)
+    orbitals, xte, xto = lax.optimization_barrier((orbitals, xte, xto))
+    xte, xto = exchange(xte, xto, "gx")
+    y, mu, pot = kernel_call(
+        prep_fields_kernel,
+        [blocks(TILES), ((CX, CY, NZ), F32), ((CX, CY, NZ), F32)],
+        [VMEM] * 3,
+        name="prepare_fields",
+    )(orbitals, kinetic_mu, potential)
     t2, metas, ye2, yo2 = kernel_call(
         widen_kernel,
         [blocks(64), blocks(2), blocks(34), blocks(34)],
         [SMEM] + [VMEM] * 4,
         [pltpu.VMEM((17 * 8, 128), F32)] * 2 + [pltpu.VMEM((34 * 8, 128), F32)] * 2,
         name="widen",
-    )(flags, t, meta, xe, xo)
+    )(flags, t, meta, xte, xto)
+    ye2, yo2 = exchange(ye2, yo2, "gy")
+    q, s, w, z, ye, yo = kernel_call(
+        build_kernel,
+        [blocks(6 * 8 * 16, 256), ((4 * 128, 256), BF16), blocks(6), blocks(6), blocks(Y_ALL), blocks(Y_ALL)],
+        [SMEM] + [VMEM] * 7,
+        [
+            pltpu.VMEM((32 * 8, 128), F32),
+            pltpu.VMEM((48, 1024), F32),
+            pltpu.VMEM((34 * 8, 128), F32),
+            pltpu.VMEM((34 * 8, 128), F32),
+            pltpu.VMEM((2 * YH * 8, 128), F32),
+        ],
+        name="build",
+    )(flags, t2, metas, ye2, yo2, y, mu, groups)
     ye, yo = exchange(ye, yo, "gy")
-    ye2, yo2 = exchange(ye2, yo2, "gy")
+    z, xe, xo = fold(flags, z, y, ye, yo, mu)
+    xe, xo = exchange(xe, xo, "gx")
     (coefs,) = kernel_call(
         coef_kernel,
         [blocks(5 * TILES)],
         [SMEM] + [VMEM] * 7,
         [pltpu.VMEM(((TILES + 2 * XH) * 8, 128), F32), pltpu.VMEM((CX * 20 * 8, 128), F32)],
         name="coefficients",
-    )(flags, mu, potential, xe, xo, ye, yo, dz)
-    q, s, w, z, ce, co = kernel_call(
-        build_kernel,
-        [blocks(6 * 8 * 16, 256), ((4 * 128, 256), BF16), blocks(6), blocks(6), blocks(3), blocks(3)],
-        [SMEM] + [VMEM] * 6,
-        [
-            pltpu.VMEM((32 * 8, 128), F32),
-            pltpu.VMEM((48, 1024), F32),
-            pltpu.VMEM((34 * 8, 128), F32),
-            pltpu.VMEM((34 * 8, 128), F32),
-        ],
-        name="build",
-    )(flags, t2, metas, ye2, yo2, y, groups)
-    ce, co = exchange(ce, co, "gx")
-    z, ce, co = fold(flags, z, ce, co, 0)
-    ce, co = exchange(ce, co, "gy")
+    )(flags, mu, pot, xe, xo, ye, yo, dz)
 
     previous = y
     for step in range(1, STEPS + 1):
         last = step == STEPS
-        outs = [blocks(TILES)]
-        if not last:
-            outs += [blocks(XH + 3), blocks(XH + 3), blocks(YH), blocks(YH), blocks(6)]
+        if last:
+            outs = [blocks(TILES // 2), blocks(TILES // 2)]
+        else:
+            outs = [blocks(TILES), blocks(Y_MU), blocks(Y_MU), blocks(6)]
         result = kernel_call(
             functools.partial(step_kernel, step),
             outs,
-            [SMEM] + [VMEM] * 15,
+            [SMEM] + [VMEM] * 13,
             [
                 pltpu.VMEM(((TILES + 2 * XH) * 8, 128), F32),
                 pltpu.VMEM((CX * 20 * 8, 128), F32),
                 pltpu.VMEM((TILES * 8, 256), F32),
                 pltpu.VMEM((48, 1024), F32),
-                pltpu.VMEM((48, 1024), F32),
                 pltpu.VMEM((2 * YH * 8, 128), F32),
+                pltpu.VMEM((TILES * 8, 128) if last else (48, 1024), F32),
             ],
             name="step",
-        )(flags, y, previous, xe, xo, ye, yo, coefs, q, s, w, z, ce, co, dz, groups)
+        )(flags, y, previous, xe, xo, ye, yo, coefs, q, s, w, z, dz, groups)
         previous = y
-        if last:
-            (y,) = result
-        else:
-            y, xe, xo, ye, yo, z = result
+        if not last:
+            y, ye, yo, z = result
             ye, yo = exchange(ye, yo, "gy")
+            z, xe, xo = fold(flags, z, y, ye, yo)
             xe, xo = exchange(xe, xo, "gx")
-            z, ce, co = fold(flags, z, xe, xo, XH)
-            ce, co = exchange(ce, co, "gy")
 
     count = lax.axis_size("orb")
     me = lax.axis_index("orb")
     even = [(i, i ^ 1) for i in range(count)]
     odd = [(i, count - 1 - i) for i in range(count)]
-    one = lax.ppermute(y, "orb", even)
-    other = lax.ppermute(y, "orb", odd)
-    half = TILES * 4
-    across_a = lax.ppermute(one[:half], "orb", odd)
-    across_b = lax.ppermute(other[half:], "orb", even)
-    across = jnp.concatenate([across_a, across_b], axis=0)
+    parts = result
+    one_a, other_b = lax.ppermute(parts[0], "orb", even), lax.ppermute(parts[1], "orb", odd)
+    one_b, other_a = lax.ppermute(parts[1], "orb", even), lax.ppermute(parts[0], "orb", odd)
+    across_a, across_b = lax.ppermute(one_a, "orb", odd), lax.ppermute(other_b, "orb", even)
+    gathered = (parts[0], parts[1], one_a, one_b, other_a, other_b, across_a, across_b)
     order = jnp.stack([me, me ^ 1, count - 1 - me, (me + 2) % count]).astype(jnp.int32)
     (corr,) = kernel_call(
         gram_kernel,
         [blocks(1)],
-        [SMEM] + [VMEM] * 4,
+        [SMEM] + [VMEM] * 8,
         [pltpu.VMEM((4, TILES * 8, 128), F32)],
         name="gram",
-    )(order, y, one, other, across)
+    )(order, *gathered)
     for axis in ("gx", "gy"):
         corr = spread_sum(corr, axis)
     cells = CX * CY * NZ * lax.axis_size("gx") * lax.axis_size("gy")
     (result,) = kernel_call(
         functools.partial(rotate_kernel, cells),
         [((ORB, CX, CY, NZ), F32)],
-        [SMEM] + [VMEM] * 5,
+        [SMEM] + [VMEM] * 9,
         [pltpu.VMEM((TILES * 8, 128), F32)],
         name="rotate",
-    )(order, corr, y, one, other, across)
+    )(order, corr, *gathered)
     return result
 
 

time: 195 us -> 196 us (level)
  starting transfers between devices: 98.1 us -> 78.8 us
  blocking collectives: 39.4 us -> 57.7 us
  waiting for transfers between devices: 19.3 us -> 21.9 us
    ppermute x22 -> x16, starting transfers between devices: 83.8 us -> 59.1 us  [exchange(): results.append(lax.ppermute(value, axis, pairs))]
    all_to_all x2, blocking collectives: 39.4 us -> 57.7 us  [spread_sum(): return jnp.sum(lax.all_to_all(copies, axis, 0, 0, tiled=True), axis=0)]
    ppermute x22 -> x16, waiting for transfers between devices: 6.55 us -> 16.3 us  [exchange(): results.append(lax.ppermute(value, axis, pairs))]
    ppermute x4 -> x6, waiting for transfers between devices: 12.7 us -> 5.58 us  [the longest x1 3.49 us: shards(): lax.ppermute(other_b, 'orb', even)]
    ppermute x4 -> x6, starting transfers between devices: 14.2 us -> 19.7 us  [the longest x1 4.01 us: shards(): lax.ppermute(parts[1], 'orb', odd)]
    pallas_call x5 -> x6, Pallas kernels: 7.72 us -> 7.89 us  [the longest x1 4.49 us: shards(): kernel_call(gram_kernel, [blocks(1)], [SMEM] + [VMEM] * 8, [pltpu.VMEM((4...]
    unnamed x17 -> x16, local copies, waits for them, and re-layouts: 5.97 us -> 5.96 us
  transfers between devices with their start and end apart: 26 -> 22, of which waited for: 8 -> 11; matrix products, arithmetic and copies ran while one was open for 0% -> 0% of each run, Pallas kernels for 4% -> 0%
where the time goes in v5:
time: 196 us; the launch traced here: 195 us
  starting transfers between devices  78.8 us (40%)
  blocking collectives  57.7 us (29%)
  Pallas kernels  29.1 us (15%)
  waiting for transfers between devices  21.9 us (11%)
  local copies, waits for them, and re-layouts  5.97 us (3%)
    ppermute x16, starting transfers between devices, exchange(): results.append(lax.ppermute(value, axis, pairs))  59.1 us
    all_to_all x2, blocking collectives, spread_sum(): return jnp.sum(lax.all_to_all(copies, axis, 0, 0, tiled=True), axis=0)  57.7 us
    ppermute x16, waiting for transfers between devices, exchange(): results.append(lax.ppermute(value, axis, pairs))  16.3 us
    pallas_call x3, Pallas kernels, shards(): kernel_call(functools.partial(step_kernel, step), outs, [SMEM] + [VMEM] *...  11.9 us
    unnamed x16, local copies, waits for them, and re-layouts  5.96 us
    pallas_call x1, Pallas kernels, shards(): kernel_call(gram_kernel, [blocks(1)], [SMEM] + [VMEM] * 8, [pltpu.VMEM((4...  4.49 us
    pallas_call x1, Pallas kernels, shards(): kernel_call(functools.partial(rotate_kernel, cells), [((ORB, CX, CY, NZ),...  4.1 us
    ppermute x1, starting transfers between devices, shards(): lax.ppermute(parts[1], 'orb', odd)  4.01 us
  transfers between devices with their start and end apart: 22, of which 11 were waited for; matrix products, arithmetic and copies ran while one was open for 0% of the time, Pallas kernels for 0%

profile of v5, /device:TPU:8, one launch (start us, length us, event | category | flops | bytes accessed | tf_op | source)
XLA Modules:
  0.0 194.5 jit_solution(2037521398800412462)
XLA Ops:
  0.7 0.9 copy-done.3
  1.6 0.7 copy-done.6
  2.3 0.7 copy-done.7
  3.0 1.5 prepare_slots.1
  4.5 1.9 collective-permute-start
  6.4 0.7 collective-permute-start.1
  7.7 0.6 widen.1
  8.3 7.7 %collective-permute-start.2 = (f32[272,128]{1,0:T(8,128)S(1)}, f32[272,128]{1,0:T(8,128)S(1)}, u32[]{:S(2)}, u32[]{:S(2)}) collective-permute-start(f32[272,128]{1,0:T(8,128)S(1)} %get-tuple-element.55), channel_id=1, source_target_pairs={{0,4},{4,0},{8,12},{12,8},{16,20},{20,16},{24,28},{28,24},{32,36},... | collective-permute-start | bytes 417800 | tf_op jit(solution)/shard_map/ppermute | solution.py:597
  16.0 1.9 collective-permute-start.3
  18.0 1.0 copy-done.2
  19.0 0.9 copy-done.4
  19.9 0.9 copy-done.5
  20.8 2.1 %collective-permute-done.3.yo_ref = f32[272,128]{1,0:T(8,128)S(1)} collective-permute-done((f32[272,128]{1,0:T(8,128)S(1)}, f32[272,128]{1,0:T(8,128)S(1)}, u32[]{:S(2)}, u32[]{:S(2)}) %collective-permute-start.3) | collective-permute-done | bytes 139296 | tf_op jit(solution)/shard_map/ppermute | solution.py:597
  23.0 2.9 %build.1 = (f32[6144,256]{1,0:T(8,128)S(1)}, bf16[512,256]{1,0:T(8,128)(2,1)S(1)}, f32[48,128]{1,0:T(8,128)S(1)}, f32[48,128]{1,0:T(8,128)S(1)}, f32[416,128]{1,0:T(8,128)S(1)}, /*index=5*/f32[416,128]{1,0:T(8,128)S(1)}) custom-call(s32[2]{0:T(128)S(1)} %pad_add_fusion.1.flags, f32[512,128]{1,0:T(8,128)S(1)} %get-tuple-element.53.t2_ref, ...), custom_call_target="tpu_custom_call" | custom-call | tf_op jit(solution)/shard_map/build/pallas_call | solution.py:639
  25.9 1.9 collective-permute-start.4
  27.8 1.9 collective-permute-start.5
  29.8 3.9 %collective-permute-done.4.ye_ref = f32[416,128]{1,0:T(8,128)S(1)} collective-permute-done((f32[416,128]{1,0:T(8,128)S(1)}, f32[416,128]{1,0:T(8,128)S(1)}, u32[]{:S(2)}, u32[]{:S(2)}) %collective-permute-start.4) | collective-permute-done | bytes 213024 | tf_op jit(solution)/shard_map/ppermute | solution.py:597
  33.6 1.9 collective-permute-done.5.yo_ref
  35.6 0.6 fold_coeffs.3
  36.2 4.2 %collective-permute-start.6 = (f32[504,128]{1,0:T(8,128)S(1)}, f32[504,128]{1,0:T(8,128)S(1)}, u32[]{:S(2)}, u32[]{:S(2)}) collective-permute-start(f32[504,128]{1,0:T(8,128)S(1)} %get-tuple-element.62), channel_id=1, source_target_pairs={{0,64},{64,0},{128,192},{192,128},{256,320},{320,256},{384,448},{4... | collective-permute-start | bytes 774152 | tf_op jit(solution)/shard_map/ppermute | solution.py:597
  40.4 0.7 collective-permute-start.7
  41.6 0.9 copy-done
  42.5 1.6 coefficients.1.coef_ref
  44.1 4.2 %step.3 = (f32[768,128]{1,0:T(8,128)S(1)}, f32[320,128]{1,0:T(8,128)S(1)}, f32[320,128]{1,0:T(8,128)S(1)}, f32[48,128]{1,0:T(8,128)S(1)}) custom-call(s32[2]{0:T(128)S(1)} %pad_add_fusion.1.flags, f32[768,128]{1,0:T(8,128)S(1)} %get-tuple-element.48.y_ref.prev_ref, f32[768,128]{1,0:T(8,128)S(1)} %get-tuple-element.48.y_ref.prev_ref, ...), custom_call_target="tpu_custom_call" | custom-call | tf_op jit(solution)/shard_map/step/pallas_call | solution.py:670
  48.3 1.9 collective-permute-start.8
  50.2 5.6 %collective-permute-start.9 = (f32[320,128]{1,0:T(8,128)S(1)}, f32[320,128]{1,0:T(8,128)S(1)}, u32[]{:S(2)}, u32[]{:S(2)}) collective-permute-start(f32[320,128]{1,0:T(8,128)S(1)} %get-tuple-element.72), channel_id=1, source_target_pairs={{4,8},{8,4},{12,16},{16,12},{20,24},{24,20},{28,32},{32,28},{36,40... | collective-permute-start | bytes 491528 | tf_op jit(solution)/shard_map/ppermute | solution.py:597
  55.8 3.3 %collective-permute-done.9.yo_ref = f32[320,128]{1,0:T(8,128)S(1)} collective-permute-done((f32[320,128]{1,0:T(8,128)S(1)}, f32[320,128]{1,0:T(8,128)S(1)}, u32[]{:S(2)}, u32[]{:S(2)}) %collective-permute-start.9) | collective-permute-done | bytes 163872 | tf_op jit(solution)/shard_map/ppermute | solution.py:597
  59.7 8.8 %collective-permute-start.10 = (f32[408,128]{1,0:T(8,128)S(1)}, f32[408,128]{1,0:T(8,128)S(1)}, u32[]{:S(2)}, u32[]{:S(2)}) collective-permute-start(f32[408,128]{1,0:T(8,128)S(1)} %get-tuple-element.73), channel_id=1, source_target_pairs={{0,64},{64,0},{128,192},{192,128},{256,320},{320,256},{384,448},{4... | collective-permute-start | bytes 626696 | tf_op jit(solution)/shard_map/ppermute | solution.py:597
  68.5 0.7 collective-permute-start.11
  69.6 4.2 %step.4 = (f32[768,128]{1,0:T(8,128)S(1)}, f32[320,128]{1,0:T(8,128)S(1)}, f32[320,128]{1,0:T(8,128)S(1)}, f32[48,128]{1,0:T(8,128)S(1)}) custom-call(s32[2]{0:T(128)S(1)} %pad_add_fusion.1.flags, f32[768,128]{1,0:T(8,128)S(1)} %get-tuple-element.69.y_ref.prev_ref, f32[768,128]{1,0:T(8,128)S(1)} %get-tuple-element.48.y_ref.prev_ref, ...), custom_call_target="tpu_custom_call" | custom-call | tf_op jit(solution)/shard_map/step/pallas_call | solution.py:670
  73.8 1.9 collective-permute-start.12
  75.7 9.1 %collective-permute-start.13 = (f32[320,128]{1,0:T(8,128)S(1)}, f32[320,128]{1,0:T(8,128)S(1)}, u32[]{:S(2)}, u32[]{:S(2)}) collective-permute-start(f32[320,128]{1,0:T(8,128)S(1)} %get-tuple-element.79), channel_id=1, source_target_pairs={{4,8},{8,4},{12,16},{16,12},{20,24},{24,20},{28,32},{32,28},{36,40... | collective-permute-start | bytes 491528 | tf_op jit(solution)/shard_map/ppermute | solution.py:597
  84.8 3.3 %collective-permute-done.13.yo_ref = f32[320,128]{1,0:T(8,128)S(1)} collective-permute-done((f32[320,128]{1,0:T(8,128)S(1)}, f32[320,128]{1,0:T(8,128)S(1)}, u32[]{:S(2)}, u32[]{:S(2)}) %collective-permute-start.13) | collective-permute-done | bytes 163872 | tf_op jit(solution)/shard_map/ppermute | solution.py:597
  88.7 9.5 %collective-permute-start.14 = (f32[408,128]{1,0:T(8,128)S(1)}, f32[408,128]{1,0:T(8,128)S(1)}, u32[]{:S(2)}, u32[]{:S(2)}) collective-permute-start(f32[408,128]{1,0:T(8,128)S(1)} %get-tuple-element.80), channel_id=1, source_target_pairs={{0,64},{64,0},{128,192},{192,128},{256,320},{320,256},{384,448},{4... | collective-permute-start | bytes 626696 | tf_op jit(solution)/shard_map/ppermute | solution.py:597
  98.2 0.7 collective-permute-start.15
  99.3 3.5 %step.5 = (f32[384,128]{1,0:T(8,128)S(1)}, f32[384,128]{1,0:T(8,128)S(1)}) custom-call(s32[2]{0:T(128)S(1)} %pad_add_fusion.1.flags, f32[768,128]{1,0:T(8,128)S(1)} %get-tuple-element.76.y_ref, f32[768,128]{1,0:T(8,128)S(1)} %get-tuple-element.69.y_ref.prev_ref, f32[408,128]{1,0:T(8,128)S(1)} %collective-permute-done.14.xe_ref, ...), custom_call_target="tpu_custom_call" | custom-call | tf_op jit(solution)/shard_map/step/pallas_call | solution.py:670
  102.8 3.4 %collective-permute-start.16 = (f32[384,128]{1,0:T(8,128)S(1)}, f32[384,128]{1,0:T(8,128)S(1)}, u32[]{:S(2)}, u32[]{:S(2)}) collective-permute-start(f32[384,128]{1,0:T(8,128)S(1)} %get-tuple-element.83.refs_0_), channel_id=1, source_target_pairs={{0,1},{1,0},{2,3},{3,2},{4,5},{5,4},{6,7},{7,6},{8,9},{9,8},{10,11... | collective-permute-start | bytes 589832 | tf_op jit(solution)/shard_map/ppermute | solution.py:696
  106.2 4.0 %collective-permute-start.19 = (f32[384,128]{1,0:T(8,128)S(1)}, f32[384,128]{1,0:T(8,128)S(1)}, u32[]{:S(2)}, u32[]{:S(2)}) collective-permute-start(f32[384,128]{1,0:T(8,128)S(1)} %get-tuple-element.84.refs_1_), channel_id=1, source_target_pairs={{0,3},{1,2},{2,1},{3,0},{4,7},{5,6},{6,5},{7,4},{8,11},{9,10},{10,... | collective-permute-start | bytes 589832 | tf_op jit(solution)/shard_map/ppermute | solution.py:696
  110.2 3.0 %collective-permute-start.18 = (f32[384,128]{1,0:T(8,128)S(1)}, f32[384,128]{1,0:T(8,128)S(1)}, u32[]{:S(2)}, u32[]{:S(2)}) collective-permute-start(f32[384,128]{1,0:T(8,128)S(1)} %get-tuple-element.83.refs_0_), channel_id=1, source_target_pairs={{0,3},{1,2},{2,1},{3,0},{4,7},{5,6},{6,5},{7,4},{8,11},{9,10},{10,... | collective-permute-start | bytes 589832 | tf_op jit(solution)/shard_map/ppermute | solution.py:697
  113.3 1.9 collective-permute-start.17
  115.2 4.0 %collective-permute-start.20 = (f32[384,128]{1,0:T(8,128)S(1)}, f32[384,128]{1,0:T(8,128)S(1)}, u32[]{:S(2)}, u32[]{:S(2)}) collective-permute-start(f32[384,128]{1,0:T(8,128)S(1)} %collective-permute-done.16.refs_2_), channel_id=1, source_target_pairs={{0,3},{1,2},{2,1},{3,0},{4,7},{5,6},{6,5},{7,4},{8,11},{9,10},{10,... | collective-permute-start | bytes 589832 | tf_op jit(solution)/shard_map/ppermute | solution.py:698
  119.2 3.3 %collective-permute-start.21 = (f32[384,128]{1,0:T(8,128)S(1)}, f32[384,128]{1,0:T(8,128)S(1)}, u32[]{:S(2)}, u32[]{:S(2)}) collective-permute-start(f32[384,128]{1,0:T(8,128)S(1)} %collective-permute-done.19.refs_5_), channel_id=1, source_target_pairs={{0,1},{1,0},{2,3},{3,2},{4,5},{5,4},{6,7},{7,6},{8,9},{9,8},{10,11... | collective-permute-start | bytes 589832 | tf_op jit(solution)/shard_map/ppermute | solution.py:698
  122.7 2.1 %collective-permute-done.20.refs_6_ = f32[384,128]{1,0:T(8,128)S(1)} collective-permute-done((f32[384,128]{1,0:T(8,128)S(1)}, f32[384,128]{1,0:T(8,128)S(1)}, u32[]{:S(2)}, u32[]{:S(2)}) %collective-permute-start.20) | collective-permute-done | bytes 196640 | tf_op jit(solution)/shard_map/ppermute | solution.py:698
  124.7 3.5 %collective-permute-done.21.refs_7_ = f32[384,128]{1,0:T(8,128)S(1)} collective-permute-done((f32[384,128]{1,0:T(8,128)S(1)}, f32[384,128]{1,0:T(8,128)S(1)}, u32[]{:S(2)}, u32[]{:S(2)}) %collective-permute-start.21) | collective-permute-done | bytes 196640 | tf_op jit(solution)/shard_map/ppermute | solution.py:698
  128.2 4.5 %gram.1 = f32[8,128]{1,0:T(8,128)S(1)} custom-call(s32[4]{0:T(128)S(1)} %pad_add_fusion.order, f32[384,128]{1,0:T(8,128)S(1)} %get-tuple-element.83.refs_0_, f32[384,128]{1,0:T(8,128)S(1)} %get-tuple-element.84.refs_1_, f32[384,128]{1,0:T(8,128)S(1)} %collective-permute-done.16.refs_2_, f32[384,128]{1,0:T(8,128)S(1)} %collective-permute-done.17.refs_3_, ...), custom_call_target="tpu_custom_call" | custom-call | tf_op jit(solution)/shard_map/gram/pallas_call | solution.py:701
  132.7 17.6 %all_to_all.10 = f32[8,8,128]{2,1,0:T(8,128)S(1)} all-to-all(f32[8,8,128]{2,1,0:T(8,128)S(1)} %broadcast_in_dim.4), channel_id=1, replica_groups=mesh['gx'=8,'gy'=16,'orb'=4] {'gx'}, dimensions={0} | all-to-all | bytes 65536 | tf_op jit(solution)/shard_map/all_to_all | solution.py:603
  150.3 40.1 %all_to_all.11 = f32[16,8,128]{2,1,0:T(8,128)S(1)} all-to-all(f32[16,8,128]{2,1,0:T(8,128)S(1)} %broadcast_in_dim.5), channel_id=1, replica_groups=mesh['gx'=8,'gy'=16,'orb'=4] {'gy'}, dimensions={0} | all-to-all | bytes 131072 | tf_op jit(solution)/shard_map/all_to_all | solution.py:603
  190.4 4.1 %rotate.1 = f32[4,12,16,128]{3,2,1,0:T(8,128)} custom-call(s32[4]{0:T(128)S(1)} %pad_add_fusion.order, f32[8,128]{1,0:T(8,128)S(1)} %reduce_sum.19.corr_ref, f32[384,128]{1,0:T(8,128)S(1)} %get-tuple-element.83.refs_0_, f32[384,128]{1,0:T(8,128)S(1)} %get-tuple-element.84.refs_1_, f32[384,128]{1,0:T(8,128)S(1)} %collective-permute-done.16.refs_2_, ...), custom_call_target="tpu_custom_call" | custom-call | tf_op jit(solution)/shard_map/rotate/pallas_call | solution.py:711
  (33 shorter events, 3.3 us)
Async XLA Ops:
  0.7 0.9 copy-start.3
  1.6 0.7 copy-start.6
  2.3 0.7 copy-start.7
  4.5 3.2 %collective-permute-start = (f32[136,128]{1,0:T(8,128)S(1)}, f32[136,128]{1,0:T(8,128)S(1)}, u32[]{:S(2)}, u32[]{:S(2)}) collective-permute-start(f32[136,128]{1,0:T(8,128)S(1)} %get-tuple-element.51), channel_id=1, source_target_pairs={{0,64},{64,0},{128,192},{192,128},{256,320},{320,256},{384,448},{4... | collective-permute-start | bytes 208904 | tf_op jit(solution)/shard_map/ppermute | solution.py:597
  6.4 1.2 collective-permute-start.1
  8.3 12.5 %collective-permute-start.2 = (f32[272,128]{1,0:T(8,128)S(1)}, f32[272,128]{1,0:T(8,128)S(1)}, u32[]{:S(2)}, u32[]{:S(2)}) collective-permute-start(f32[272,128]{1,0:T(8,128)S(1)} %get-tuple-element.55), channel_id=1, source_target_pairs={{0,4},{4,0},{8,12},{12,8},{16,20},{20,16},{24,28},{28,24},{32,36},... | collective-permute-start | bytes 417800 | tf_op jit(solution)/shard_map/ppermute | solution.py:597
  16.0 6.9 %collective-permute-start.3 = (f32[272,128]{1,0:T(8,128)S(1)}, f32[272,128]{1,0:T(8,128)S(1)}, u32[]{:S(2)}, u32[]{:S(2)}) collective-permute-start(f32[272,128]{1,0:T(8,128)S(1)} %get-tuple-element.56), channel_id=1, source_target_pairs={{4,8},{8,4},{12,16},{16,12},{20,24},{24,20},{28,32},{32,28},{36,40... | collective-permute-start | bytes 417800 | tf_op jit(solution)/shard_map/ppermute | solution.py:597
  18.0 1.0 copy-start.2
  19.0 0.9 copy-start.4
  19.9 0.9 copy-start.5
  25.9 7.7 %collective-permute-start.4 = (f32[416,128]{1,0:T(8,128)S(1)}, f32[416,128]{1,0:T(8,128)S(1)}, u32[]{:S(2)}, u32[]{:S(2)}) collective-permute-start(f32[416,128]{1,0:T(8,128)S(1)} %get-tuple-element.60), channel_id=1, source_target_pairs={{0,4},{4,0},{8,12},{12,8},{16,20},{20,16},{24,28},{28,24},{32,36},... | collective-permute-start | bytes 638984 | tf_op jit(solution)/shard_map/ppermute | solution.py:597
  27.8 7.7 %collective-permute-start.5 = (f32[416,128]{1,0:T(8,128)S(1)}, f32[416,128]{1,0:T(8,128)S(1)}, u32[]{:S(2)}, u32[]{:S(2)}) collective-permute-start(f32[416,128]{1,0:T(8,128)S(1)} %get-tuple-element.61), channel_id=1, source_target_pairs={{4,8},{8,4},{12,16},{16,12},{20,24},{24,20},{28,32},{32,28},{36,40... | collective-permute-start | bytes 638984 | tf_op jit(solution)/shard_map/ppermute | solution.py:597
  36.2 5.4 %collective-permute-start.6 = (f32[504,128]{1,0:T(8,128)S(1)}, f32[504,128]{1,0:T(8,128)S(1)}, u32[]{:S(2)}, u32[]{:S(2)}) collective-permute-start(f32[504,128]{1,0:T(8,128)S(1)} %get-tuple-element.62), channel_id=1, source_target_pairs={{0,64},{64,0},{128,192},{192,128},{256,320},{320,256},{384,448},{4... | collective-permute-start | bytes 774152 | tf_op jit(solution)/shard_map/ppermute | solution.py:597
  40.4 1.1 collective-permute-start.7
  41.6 0.9 copy-start
  44.1 25.5 %copy-start.1 = (bf16[256,256]{1,0:T(8,128)(2,1)S(1)}, bf16[256,256]{1,0:T(8,128)(2,1)}, u32[]{:S(2)}) copy-start(bf16[256,256]{1,0:T(8,128)(2,1)} %constant.48.clone.dz_ref) | copy-start | bytes 393220
  48.3 7.5 %collective-permute-start.8 = (f32[320,128]{1,0:T(8,128)S(1)}, f32[320,128]{1,0:T(8,128)S(1)}, u32[]{:S(2)}, u32[]{:S(2)}) collective-permute-start(f32[320,128]{1,0:T(8,128)S(1)} %get-tuple-element.71), channel_id=1, source_target_pairs={{0,4},{4,0},{8,12},{12,8},{16,20},{20,16},{24,28},{28,24},{32,36},... | collective-permute-start | bytes 491528 | tf_op jit(solution)/shard_map/ppermute | solution.py:597
  50.2 8.9 %collective-permute-start.9 = (f32[320,128]{1,0:T(8,128)S(1)}, f32[320,128]{1,0:T(8,128)S(1)}, u32[]{:S(2)}, u32[]{:S(2)}) collective-permute-start(f32[320,128]{1,0:T(8,128)S(1)} %get-tuple-element.72), channel_id=1, source_target_pairs={{4,8},{8,4},{12,16},{16,12},{20,24},{24,20},{28,32},{32,28},{36,40... | collective-permute-start | bytes 491528 | tf_op jit(solution)/shard_map/ppermute | solution.py:597
  59.7 9.8 %collective-permute-start.10 = (f32[408,128]{1,0:T(8,128)S(1)}, f32[408,128]{1,0:T(8,128)S(1)}, u32[]{:S(2)}, u32[]{:S(2)}) collective-permute-start(f32[408,128]{1,0:T(8,128)S(1)} %get-tuple-element.73), channel_id=1, source_target_pairs={{0,64},{64,0},{128,192},{192,128},{256,320},{320,256},{384,448},{4... | collective-permute-start | bytes 626696 | tf_op jit(solution)/shard_map/ppermute | solution.py:597
  68.5 1.1 collective-permute-start.11
  73.8 11.0 %collective-permute-start.12 = (f32[320,128]{1,0:T(8,128)S(1)}, f32[320,128]{1,0:T(8,128)S(1)}, u32[]{:S(2)}, u32[]{:S(2)}) collective-permute-start(f32[320,128]{1,0:T(8,128)S(1)} %get-tuple-element.78), channel_id=1, source_target_pairs={{0,4},{4,0},{8,12},{12,8},{16,20},{20,16},{24,28},{28,24},{32,36},... | collective-permute-start | bytes 491528 | tf_op jit(solution)/shard_map/ppermute | solution.py:597
  75.7 12.4 %collective-permute-start.13 = (f32[320,128]{1,0:T(8,128)S(1)}, f32[320,128]{1,0:T(8,128)S(1)}, u32[]{:S(2)}, u32[]{:S(2)}) collective-permute-start(f32[320,128]{1,0:T(8,128)S(1)} %get-tuple-element.79), channel_id=1, source_target_pairs={{4,8},{8,4},{12,16},{16,12},{20,24},{24,20},{28,32},{32,28},{36,40... | collective-permute-start | bytes 491528 | tf_op jit(solution)/shard_map/ppermute | solution.py:597
  88.7 10.6 %collective-permute-start.14 = (f32[408,128]{1,0:T(8,128)S(1)}, f32[408,128]{1,0:T(8,128)S(1)}, u32[]{:S(2)}, u32[]{:S(2)}) collective-permute-start(f32[408,128]{1,0:T(8,128)S(1)} %get-tuple-element.80), channel_id=1, source_target_pairs={{0,64},{64,0},{128,192},{192,128},{256,320},{320,256},{384,448},{4... | collective-permute-start | bytes 626696 | tf_op jit(solution)/shard_map/ppermute | solution.py:597
  98.2 1.1 collective-permute-start.15
  102.8 12.4 %collective-permute-start.16 = (f32[384,128]{1,0:T(8,128)S(1)}, f32[384,128]{1,0:T(8,128)S(1)}, u32[]{:S(2)}, u32[]{:S(2)}) collective-permute-start(f32[384,128]{1,0:T(8,128)S(1)} %get-tuple-element.83.refs_0_), channel_id=1, source_target_pairs={{0,1},{1,0},{2,3},{3,2},{4,5},{5,4},{6,7},{7,6},{8,9},{9,8},{10,11... | collective-permute-start | bytes 589832 | tf_op jit(solution)/shard_map/ppermute | solution.py:696
  106.2 13.0 %collective-permute-start.19 = (f32[384,128]{1,0:T(8,128)S(1)}, f32[384,128]{1,0:T(8,128)S(1)}, u32[]{:S(2)}, u32[]{:S(2)}) collective-permute-start(f32[384,128]{1,0:T(8,128)S(1)} %get-tuple-element.84.refs_1_), channel_id=1, source_target_pairs={{0,3},{1,2},{2,1},{3,0},{4,7},{5,6},{6,5},{7,4},{8,11},{9,10},{10,... | collective-permute-start | bytes 589832 | tf_op jit(solution)/shard_map/ppermute | solution.py:696
  110.2 12.4 %collective-permute-start.18 = (f32[384,128]{1,0:T(8,128)S(1)}, f32[384,128]{1,0:T(8,128)S(1)}, u32[]{:S(2)}, u32[]{:S(2)}) collective-permute-start(f32[384,128]{1,0:T(8,128)S(1)} %get-tuple-element.83.refs_0_), channel_id=1, source_target_pairs={{0,3},{1,2},{2,1},{3,0},{4,7},{5,6},{6,5},{7,4},{8,11},{9,10},{10,... | collective-permute-start | bytes 589832 | tf_op jit(solution)/shard_map/ppermute | solution.py:697
  113.3 9.4 %collective-permute-start.17 = (f32[384,128]{1,0:T(8,128)S(1)}, f32[384,128]{1,0:T(8,128)S(1)}, u32[]{:S(2)}, u32[]{:S(2)}) collective-permute-start(f32[384,128]{1,0:T(8,128)S(1)} %get-tuple-element.84.refs_1_), channel_id=1, source_target_pairs={{0,1},{1,0},{2,3},{3,2},{4,5},{5,4},{6,7},{7,6},{8,9},{9,8},{10,11... | collective-permute-start | bytes 589832 | tf_op jit(solution)/shard_map/ppermute | solution.py:697
  115.2 9.5 %collective-permute-start.20 = (f32[384,128]{1,0:T(8,128)S(1)}, f32[384,128]{1,0:T(8,128)S(1)}, u32[]{:S(2)}, u32[]{:S(2)}) collective-permute-start(f32[384,128]{1,0:T(8,128)S(1)} %collective-permute-done.16.refs_2_), channel_id=1, source_target_pairs={{0,3},{1,2},{2,1},{3,0},{4,7},{5,6},{6,5},{7,4},{8,11},{9,10},{10,... | collective-permute-start | bytes 589832 | tf_op jit(solution)/shard_map/ppermute | solution.py:698
  119.2 9.0 %collective-permute-start.21 = (f32[384,128]{1,0:T(8,128)S(1)}, f32[384,128]{1,0:T(8,128)S(1)}, u32[]{:S(2)}, u32[]{:S(2)}) collective-permute-start(f32[384,128]{1,0:T(8,128)S(1)} %collective-permute-done.19.refs_5_), channel_id=1, source_target_pairs={{0,1},{1,0},{2,3},{3,2},{4,5},{5,4},{6,7},{7,6},{8,9},{9,8},{10,11... | collective-permute-start | bytes 589832 | tf_op jit(solution)/shard_map/ppermute | solution.py:698

commit v6 on v5

--- a/solution.py
+++ b/solution.py
@@ -124,7 +124,8 @@
     odd_ref[0:rows, :] = y_ref[pl.ds(odd_at, rows), :]
 
 
-def prep_slots_kernel(flags, offs, strg, cnt, proj, t_ref, meta_ref, xe_ref, xo_ref, g_ref, xr_ref, xl_ref):
+def prep_slots_kernel(flags, offs, strg, cnt, proj, mu, t_ref, meta_ref, xe_ref, xo_ref, g_ref, mu_out, xr_ref, xl_ref):
+    mu_out[...] = mu[...]
     at_row = lax.broadcasted_iota(jnp.int32, (1024, 128), 0)
     at_column = lax.broadcasted_iota(jnp.int32, (1024, 128), 1)
     same = (at_row % 128 // 8 == at_column // 8) & (at_row // 128 == at_column % 8)
@@ -161,10 +162,14 @@
     put(xr_ref, 16, meta)
     put(xl_ref, 16, meta)
     send(flags[0], xl_ref, xr_ref, xe_ref, xo_ref, 17)
-
-
-def prep_fields_kernel(orb, mu, pot, y_ref, mu_out, pot_out):
-    mu_out[...] = mu[...]
+    for x in range(HALO):
+        for h in range(2):
+            left, right = mu[x, 8 * h : 8 * h + 8, :], mu[CX - HALO + x, 8 * h : 8 * h + 8, :]
+            put(xe_ref, 17 + 2 * x + h, jnp.where(flags[0] == 1, left, right))
+            put(xo_ref, 17 + 2 * x + h, jnp.where(flags[0] == 1, right, left))
+
+
+def prep_fields_kernel(orb, pot, y_ref, pot_out):
     pot_out[...] = pot[...]
     for x in range(CX):
         for o in range(ORB):
@@ -173,8 +178,8 @@
 
 
 X_SUMS, Y_SUMS = XH, YH
-X_MU, Y_MU = XH + 3, YH + 4
-X_ALL, Y_ALL = X_MU + 2 * HALO, Y_MU + CX
+X_ALL, Y_MU = XH + 3, YH + 4
+Y_ALL = Y_MU + CX
 
 
 def send_rims(flag, y_ref, rims, ye_ref, yo_ref):
@@ -223,7 +228,7 @@
     def two(a, ia, b, ib):
         return jnp.where(low, row(a, ia), row(b, ib))
 
-    ends = [sides(flags[0] == 1, get(xe_ref, X_MU + t), get(xo_ref, X_MU + t)) for t in range(2 * HALO)]
+    ends = [sides(flags[0] == 1, get(xe_ref, 17 + t), get(xo_ref, 17 + t)) for t in range(2 * HALO)]
     for x in range(CX + 2 * HALO):
         if x < HALO:
             a, b = ends[2 * x][0], ends[2 * x + 1][0]
@@ -388,16 +393,8 @@
         put(nyo_ref, Y_MU + x, jnp.where(flags[1] == 1, above, below))
 
 
-def fold_kernel(flags, z_ref, y_ref, ye_ref, yo_ref, *rest):
-    out_ref, xe_ref, xo_ref = rest[-3:]
+def fold_kernel(flags, z_ref, y_ref, ye_ref, yo_ref, out_ref, xe_ref, xo_ref):
     give_ends(flags[0], y_ref, xe_ref, xo_ref)
-    if len(rest) == 4:
-        mu = rest[0]
-        for x in range(HALO):
-            for h in range(2):
-                left, right = mu[x, 8 * h : 8 * h + 8, :], mu[CX - HALO + x, 8 * h : 8 * h + 8, :]
-                put(xe_ref, X_MU + 2 * x + h, jnp.where(flags[0] == 1, left, right))
-                put(xo_ref, X_MU + 2 * x + h, jnp.where(flags[0] == 1, right, left))
     base = Y_SUMS
     for side in range(2):
         own, lo, hi = (get(z_ref, side * 3 + t) for t in range(3))
@@ -502,27 +499,32 @@
         send_coeffs(flags[1], zn_ref, nye_ref, nyo_ref, Y_SUMS)
 
 
+def two_layers(refs, x):
+    half, at = x // (CX // 2), x % (CX // 2) * 64
+    sides = [[refs[2 * n + half][a : a + 64, :] for n in range(4)] for a in (at, at + 64)]
+    return jnp.concatenate([jnp.concatenate(side, axis=0) for side in sides], axis=1)
+
+
+def ring_orbitals(order):
+    orbital = lax.broadcasted_iota(jnp.int32, (16, 256), 0)
+    held_at = lax.broadcasted_iota(jnp.int32, (16, 256), 1)
+    device = held_at // 64
+    owner = jnp.where(device == 0, order[0], jnp.where(device == 1, order[1], jnp.where(device == 2, order[2], order[3])))
+    return jnp.where(orbital == owner * 4 + held_at % 4, 1.0, 0.0).astype(F32)
+
+
 def gram_kernel(order, *refs):
-    out_ref, held = refs[8:]
-    for n in range(4):
-        for h in range(2):
-            held[order[n], h * TILES * 4 : (h + 1) * TILES * 4, :] = refs[2 * n + h][...]
-
-    def body(x, totals):
-        at = pl.ds(pl.multiple_of(x * 64, 64), 64)
-        field = jnp.concatenate([held[d, at, :] for d in range(4)], axis=0)
-        high, low = split(field)
-        return totals[0] + mm_t(high, high), totals[1] + mm_t(high, low)
-
-    zero = jnp.zeros((256, 256), F32)
-    total, mixed = lax.fori_loop(0, CX, body, (zero, zero))
+    out_ref = refs[8]
+    total = mixed = None
+    for x in range(0, CX, 2):
+        high, low = split(two_layers(refs, x))
+        one, two = mm_t(high, high), mm_t(high, low)
+        total, mixed = (one, two) if x == 0 else (total + one, mixed + two)
     total = total + mixed + mixed.T
     rows = lax.broadcasted_iota(jnp.int32, (256, 256), 0)
     columns = lax.broadcasted_iota(jnp.int32, (256, 256), 1)
     total = jnp.where((rows % 64) // 4 == (columns % 64) // 4, total, 0.0)
-    orbital = lax.broadcasted_iota(jnp.int32, (16, 256), 0)
-    held_at = lax.broadcasted_iota(jnp.int32, (16, 256), 1)
-    hot = jnp.where(orbital == held_at // 64 * 4 + held_at % 4, 1.0, 0.0).astype(F32)
+    hot = ring_orbitals(order)
     first = jnp.dot(hot, total, precision=lax.Precision.HIGHEST, preferred_element_type=F32)
     small = lax.dot_general(
         first, hot, (((1,), (1,)), ((), ())), precision=lax.Precision.HIGHEST, preferred_element_type=F32
@@ -551,22 +553,18 @@
     own_row = lax.broadcasted_iota(jnp.int32, (64, 16), 0)
     orbital = lax.broadcasted_iota(jnp.int32, (64, 16), 1)
     left = jnp.where(orbital == me * 4 + own_row % 4, 1.0, 0.0).astype(F32)
-    orbital = lax.broadcasted_iota(jnp.int32, (16, 256), 0)
-    held_at = lax.broadcasted_iota(jnp.int32, (16, 256), 1)
-    device = held_at // 64
-    owner = jnp.where(device == 0, order[0], jnp.where(device == 1, order[1], jnp.where(device == 2, order[2], order[3])))
-    right = jnp.where(orbital == owner * 4 + held_at % 4, 1.0, 0.0).astype(F32)
+    right = ring_orbitals(order)
     exact = functools.partial(jnp.dot, precision=lax.Precision.HIGHEST, preferred_element_type=F32)
     mixing = exact(exact(left, inverse), right)
     at_row = lax.broadcasted_iota(jnp.int32, (64, 256), 0)
     at_column = lax.broadcasted_iota(jnp.int32, (64, 256), 1)
     mixing = jnp.where(at_row // 4 == at_column % 64 // 4, mixing, 0.0)
     mix_high, mix_low = split(mixing)
-    for x in range(CX):
-        at = x % (CX // 2) * 64
-        field = jnp.concatenate([refs[2 * n + x // (CX // 2)][at : at + 64, :] for n in range(4)], axis=0)
-        high, low = split(field)
-        flat[x * 64 : x * 64 + 64, :] = mm(mix_high, high) + mm(mix_high, low) + mm(mix_low, high)
+    for x in range(0, CX, 2):
+        high, low = split(two_layers(refs, x))
+        both = mm(mix_high, high) + mm(mix_high, low) + mm(mix_low, high)
+        flat[x * 64 : x * 64 + 64, :] = both[:, :NZ]
+        flat[x * 64 + 64 : x * 64 + 128, :] = both[:, NZ:]
     for o in range(ORB):
         for x in range(CX):
             for h in range(2):
@@ -603,31 +601,31 @@
     return jnp.sum(lax.all_to_all(copies, axis, 0, 0, tiled=True), axis=0)
 
 
-def fold(flags, z, y, even, odd, *mu):
-    count = X_ALL if mu else X_MU
+def fold(flags, z, y, even, odd):
     return kernel_call(
-        fold_kernel, [blocks(6), blocks(count), blocks(count)], [SMEM] + [VMEM] * (4 + len(mu)), name="fold_coeffs"
-    )(flags, z, y, even, odd, *mu)
+        fold_kernel, [blocks(6), blocks(X_ALL), blocks(X_ALL)], [SMEM] + [VMEM] * 4, name="fold_coeffs"
+    )(flags, z, y, even, odd)
 
 
 def shards(orbitals, potential, kinetic_mu, projectors, strengths, box_offsets, block_counts):
     dz = jnp.asarray(derivative_table())
     flags = jnp.stack([lax.axis_index("gx") % 2, lax.axis_index("gy") % 2]).astype(jnp.int32)
-    t, meta, xte, xto, groups = kernel_call(
+    t, meta, xte, xto, groups, mu = kernel_call(
         prep_slots_kernel,
-        [blocks(64), blocks(1), blocks(17), blocks(17), ((1024, 128), BF16)],
-        [SMEM] * 4 + [VMEM],
+        [blocks(64), blocks(1), blocks(17 + 2 * HALO), blocks(17 + 2 * HALO)]
+        + [((1024, 128), BF16), ((CX, CY, NZ), F32)],
+        [SMEM] * 4 + [VMEM] * 2,
         [pltpu.VMEM((17 * 8, 128), F32)] * 2,
         name="prepare_slots",
-    )(flags, box_offsets.T, strengths, block_counts, projectors)
+    )(flags, box_offsets.T, strengths, block_counts, projectors, kinetic_mu)
     orbitals, xte, xto = lax.optimization_barrier((orbitals, xte, xto))
     xte, xto = exchange(xte, xto, "gx")
-    y, mu, pot = kernel_call(
+    y, pot = kernel_call(
         prep_fields_kernel,
-        [blocks(TILES), ((CX, CY, NZ), F32), ((CX, CY, NZ), F32)],
-        [VMEM] * 3,
+        [blocks(TILES), ((CX, CY, NZ), F32)],
+        [VMEM] * 2,
         name="prepare_fields",
-    )(orbitals, kinetic_mu, potential)
+    )(orbitals, potential)
     t2, metas, ye2, yo2 = kernel_call(
         widen_kernel,
         [blocks(64), blocks(2), blocks(34), blocks(34)],
@@ -650,7 +648,7 @@
         name="build",
     )(flags, t2, metas, ye2, yo2, y, mu, groups)
     ye, yo = exchange(ye, yo, "gy")
-    z, xe, xo = fold(flags, z, y, ye, yo, mu)
+    z, xe, xo = fold(flags, z, y, ye, yo)
     xe, xo = exchange(xe, xo, "gx")
     (coefs,) = kernel_call(
         coef_kernel,
@@ -658,7 +656,7 @@
         [SMEM] + [VMEM] * 7,
         [pltpu.VMEM(((TILES + 2 * XH) * 8, 128), F32), pltpu.VMEM((CX * 20 * 8, 128), F32)],
         name="coefficients",
-    )(flags, mu, pot, xe, xo, ye, yo, dz)
+    )(flags, mu, pot, xte, xto, ye, yo, dz)
 
     previous = y
     for step in range(1, STEPS + 1):
@@ -702,7 +700,6 @@
         gram_kernel,
         [blocks(1)],
         [SMEM] + [VMEM] * 8,
-        [pltpu.VMEM((4, TILES * 8, 128), F32)],
         name="gram",
     )(order, *gathered)
     for axis in ("gx", "gy"):

time: 196 us -> 191 us (0.974)
  Pallas kernels: 29.1 us -> 26.4 us
  starting transfers between devices: 78.8 us -> 76.6 us
    pallas_call x6, Pallas kernels: 7.89 us -> 5.17 us  [the longest x3 1.85 us: fold(): kernel_call(fold_kernel, [blocks(6), blocks(X_ALL), blocks(X_ALL)], [SMEM...]
    ppermute x16, starting transfers between devices: 59.1 us -> 56.9 us  [exchange(): results.append(lax.ppermute(value, axis, pairs))]
  transfers between devices with their start and end apart: 22 -> 22, of which waited for: 11 -> 11; matrix products, arithmetic and copies ran while one was open for 0% -> 0% of each run, Pallas kernels for 0% -> 1%
where the time goes in v6:
time: 191 us; the launch traced here: 190 us
  starting transfers between devices  76.6 us (40%)
  blocking collectives  57.8 us (30%)
  Pallas kernels  26.4 us (14%)
  waiting for transfers between devices  22.4 us (12%)
  local copies, waits for them, and re-layouts  5.97 us (3%)
    all_to_all x2, blocking collectives, spread_sum(): return jnp.sum(lax.all_to_all(copies, axis, 0, 0, tiled=True), axis=0)  57.8 us
    ppermute x16, starting transfers between devices, exchange(): results.append(lax.ppermute(value, axis, pairs))  56.9 us
    ppermute x16, waiting for transfers between devices, exchange(): results.append(lax.ppermute(value, axis, pairs))  16.8 us
    pallas_call x3, Pallas kernels, shards(): kernel_call(functools.partial(step_kernel, step), outs, [SMEM] + [VMEM] *...  11.9 us
    unnamed x16, local copies, waits for them, and re-layouts  5.95 us
    pallas_call x1, Pallas kernels, shards(): kernel_call(functools.partial(rotate_kernel, cells), [((ORB, CX, CY, NZ),...  4.11 us
    ppermute x1, starting transfers between devices, shards(): lax.ppermute(parts[1], 'orb', odd)  4 us
    ppermute x1, starting transfers between devices, shards(): lax.ppermute(one_a, 'orb', odd)  4 us
  transfers between devices with their start and end apart: 22, of which 11 were waited for; matrix products, arithmetic and copies ran while one was open for 0% of the time, Pallas kernels for 1%

profile of v6, /device:TPU:8, one launch (start us, length us, event | category | flops | bytes accessed | tf_op | source)
XLA Modules:
  0.0 190.3 jit_solution(7392094755967416602)
XLA Ops:
  0.7 0.9 copy-done.3
  1.6 0.9 copy-done.4
  2.5 0.7 copy-done.6
  3.2 0.7 copy-done.7
  3.9 1.5 prepare_slots.1
  5.4 1.9 %collective-permute-start = (f32[232,128]{1,0:T(8,128)S(1)}, f32[232,128]{1,0:T(8,128)S(1)}, u32[]{:S(2)}, u32[]{:S(2)}) collective-permute-start(f32[232,128]{1,0:T(8,128)S(1)} %get-tuple-element.51), channel_id=1, source_target_pairs={{0,64},{64,0},{128,192},{192,128},{256,320},{320,256},{384,448},{4... | collective-permute-start | bytes 356360 | tf_op jit(solution)/shard_map/ppermute | solution.py:595
  7.3 0.7 collective-permute-start.1
  8.0 0.6 collective-permute-done.xe_ref
  8.6 0.6 widen.1
  9.3 7.7 %collective-permute-start.2 = (f32[272,128]{1,0:T(8,128)S(1)}, f32[272,128]{1,0:T(8,128)S(1)}, u32[]{:S(2)}, u32[]{:S(2)}) collective-permute-start(f32[272,128]{1,0:T(8,128)S(1)} %get-tuple-element.55), channel_id=1, source_target_pairs={{0,4},{4,0},{8,12},{12,8},{16,20},{20,16},{24,28},{28,24},{32,36},... | collective-permute-start | bytes 417800 | tf_op jit(solution)/shard_map/ppermute | solution.py:595
  17.0 1.9 %collective-permute-start.3 = (f32[272,128]{1,0:T(8,128)S(1)}, f32[272,128]{1,0:T(8,128)S(1)}, u32[]{:S(2)}, u32[]{:S(2)}) collective-permute-start(f32[272,128]{1,0:T(8,128)S(1)} %get-tuple-element.56), channel_id=1, source_target_pairs={{4,8},{8,4},{12,16},{16,12},{20,24},{24,20},{28,32},{32,28},{36,40... | collective-permute-start | bytes 417800 | tf_op jit(solution)/shard_map/ppermute | solution.py:595
  19.0 1.0 copy-done.2
  19.9 0.9 copy-done.5
  20.9 3.0 %collective-permute-done.3.yo_ref = f32[272,128]{1,0:T(8,128)S(1)} collective-permute-done((f32[272,128]{1,0:T(8,128)S(1)}, f32[272,128]{1,0:T(8,128)S(1)}, u32[]{:S(2)}, u32[]{:S(2)}) %collective-permute-start.3) | collective-permute-done | bytes 139296 | tf_op jit(solution)/shard_map/ppermute | solution.py:595
  24.0 2.9 %build.1 = (f32[6144,256]{1,0:T(8,128)S(1)}, bf16[512,256]{1,0:T(8,128)(2,1)S(1)}, f32[48,128]{1,0:T(8,128)S(1)}, f32[48,128]{1,0:T(8,128)S(1)}, f32[416,128]{1,0:T(8,128)S(1)}, /*index=5*/f32[416,128]{1,0:T(8,128)S(1)}) custom-call(s32[2]{0:T(128)S(1)} %pad_add_fusion.1.flags, f32[512,128]{1,0:T(8,128)S(1)} %get-tuple-element.53.t2_ref, ...), custom_call_target="tpu_custom_call" | custom-call | tf_op jit(solution)/shard_map/build/pallas_call | solution.py:637
  26.9 1.9 %collective-permute-start.4 = (f32[416,128]{1,0:T(8,128)S(1)}, f32[416,128]{1,0:T(8,128)S(1)}, u32[]{:S(2)}, u32[]{:S(2)}) collective-permute-start(f32[416,128]{1,0:T(8,128)S(1)} %get-tuple-element.60), channel_id=1, source_target_pairs={{0,4},{4,0},{8,12},{12,8},{16,20},{20,16},{24,28},{28,24},{32,36},... | collective-permute-start | bytes 638984 | tf_op jit(solution)/shard_map/ppermute | solution.py:595
  28.8 1.9 %collective-permute-start.5 = (f32[416,128]{1,0:T(8,128)S(1)}, f32[416,128]{1,0:T(8,128)S(1)}, u32[]{:S(2)}, u32[]{:S(2)}) collective-permute-start(f32[416,128]{1,0:T(8,128)S(1)} %get-tuple-element.61), channel_id=1, source_target_pairs={{4,8},{8,4},{12,16},{16,12},{20,24},{24,20},{28,32},{32,28},{36,40... | collective-permute-start | bytes 638984 | tf_op jit(solution)/shard_map/ppermute | solution.py:595
  30.7 3.9 %collective-permute-done.4.ye_ref = f32[416,128]{1,0:T(8,128)S(1)} collective-permute-done((f32[416,128]{1,0:T(8,128)S(1)}, f32[416,128]{1,0:T(8,128)S(1)}, u32[]{:S(2)}, u32[]{:S(2)}) %collective-permute-start.4) | collective-permute-done | bytes 213024 | tf_op jit(solution)/shard_map/ppermute | solution.py:595
  34.6 1.9 %collective-permute-done.5.yo_ref = f32[416,128]{1,0:T(8,128)S(1)} collective-permute-done((f32[416,128]{1,0:T(8,128)S(1)}, f32[416,128]{1,0:T(8,128)S(1)}, u32[]{:S(2)}, u32[]{:S(2)}) %collective-permute-start.5) | collective-permute-done | bytes 213024 | tf_op jit(solution)/shard_map/ppermute | solution.py:595
  37.1 4.7 %collective-permute-start.6 = (f32[408,128]{1,0:T(8,128)S(1)}, f32[408,128]{1,0:T(8,128)S(1)}, u32[]{:S(2)}, u32[]{:S(2)}) collective-permute-start(f32[408,128]{1,0:T(8,128)S(1)} %get-tuple-element.62), channel_id=1, source_target_pairs={{0,64},{64,0},{128,192},{192,128},{256,320},{320,256},{384,448},{4... | collective-permute-start | bytes 626696 | tf_op jit(solution)/shard_map/ppermute | solution.py:595
  41.8 0.7 collective-permute-start.7
  42.5 0.9 copy-done
  43.4 1.6 coefficients.1.coef_ref
  45.1 4.2 %step.3 = (f32[768,128]{1,0:T(8,128)S(1)}, f32[320,128]{1,0:T(8,128)S(1)}, f32[320,128]{1,0:T(8,128)S(1)}, f32[48,128]{1,0:T(8,128)S(1)}) custom-call(s32[2]{0:T(128)S(1)} %pad_add_fusion.1.flags, f32[768,128]{1,0:T(8,128)S(1)} %get-tuple-element.48.y_ref.prev_ref, f32[768,128]{1,0:T(8,128)S(1)} %get-tuple-element.48.y_ref.prev_ref, ...), custom_call_target="tpu_custom_call" | custom-call | tf_op jit(solution)/shard_map/step/pallas_call | solution.py:668
  49.3 1.9 %collective-permute-start.8 = (f32[320,128]{1,0:T(8,128)S(1)}, f32[320,128]{1,0:T(8,128)S(1)}, u32[]{:S(2)}, u32[]{:S(2)}) collective-permute-start(f32[320,128]{1,0:T(8,128)S(1)} %get-tuple-element.71), channel_id=1, source_target_pairs={{0,4},{4,0},{8,12},{12,8},{16,20},{20,16},{24,28},{28,24},{32,36},... | collective-permute-start | bytes 491528 | tf_op jit(solution)/shard_map/ppermute | solution.py:595
  51.2 5.1 %collective-permute-start.9 = (f32[320,128]{1,0:T(8,128)S(1)}, f32[320,128]{1,0:T(8,128)S(1)}, u32[]{:S(2)}, u32[]{:S(2)}) collective-permute-start(f32[320,128]{1,0:T(8,128)S(1)} %get-tuple-element.72), channel_id=1, source_target_pairs={{4,8},{8,4},{12,16},{16,12},{20,24},{24,20},{28,32},{32,28},{36,40... | collective-permute-start | bytes 491528 | tf_op jit(solution)/shard_map/ppermute | solution.py:595
  56.5 3.1 %collective-permute-done.9.yo_ref = f32[320,128]{1,0:T(8,128)S(1)} collective-permute-done((f32[320,128]{1,0:T(8,128)S(1)}, f32[320,128]{1,0:T(8,128)S(1)}, u32[]{:S(2)}, u32[]{:S(2)}) %collective-permute-start.9) | collective-permute-done | bytes 163872 | tf_op jit(solution)/shard_map/ppermute | solution.py:595
  60.3 6.6 %collective-permute-start.10 = (f32[408,128]{1,0:T(8,128)S(1)}, f32[408,128]{1,0:T(8,128)S(1)}, u32[]{:S(2)}, u32[]{:S(2)}) collective-permute-start(f32[408,128]{1,0:T(8,128)S(1)} %get-tuple-element.73), channel_id=1, source_target_pairs={{0,64},{64,0},{128,192},{192,128},{256,320},{320,256},{384,448},{4... | collective-permute-start | bytes 626696 | tf_op jit(solution)/shard_map/ppermute | solution.py:595
  66.8 0.7 collective-permute-start.11
  67.9 4.2 %step.4 = (f32[768,128]{1,0:T(8,128)S(1)}, f32[320,128]{1,0:T(8,128)S(1)}, f32[320,128]{1,0:T(8,128)S(1)}, f32[48,128]{1,0:T(8,128)S(1)}) custom-call(s32[2]{0:T(128)S(1)} %pad_add_fusion.1.flags, f32[768,128]{1,0:T(8,128)S(1)} %get-tuple-element.69.y_ref.prev_ref, f32[768,128]{1,0:T(8,128)S(1)} %get-tuple-element.48.y_ref.prev_ref, ...), custom_call_target="tpu_custom_call" | custom-call | tf_op jit(solution)/shard_map/step/pallas_call | solution.py:668
  72.1 1.9 %collective-permute-start.12 = (f32[320,128]{1,0:T(8,128)S(1)}, f32[320,128]{1,0:T(8,128)S(1)}, u32[]{:S(2)}, u32[]{:S(2)}) collective-permute-start(f32[320,128]{1,0:T(8,128)S(1)} %get-tuple-element.78), channel_id=1, source_target_pairs={{0,4},{4,0},{8,12},{12,8},{16,20},{20,16},{24,28},{28,24},{32,36},... | collective-permute-start | bytes 491528 | tf_op jit(solution)/shard_map/ppermute | solution.py:595
  74.1 9.0 %collective-permute-start.13 = (f32[320,128]{1,0:T(8,128)S(1)}, f32[320,128]{1,0:T(8,128)S(1)}, u32[]{:S(2)}, u32[]{:S(2)}) collective-permute-start(f32[320,128]{1,0:T(8,128)S(1)} %get-tuple-element.79), channel_id=1, source_target_pairs={{4,8},{8,4},{12,16},{16,12},{20,24},{24,20},{28,32},{32,28},{36,40... | collective-permute-start | bytes 491528 | tf_op jit(solution)/shard_map/ppermute | solution.py:595
  83.1 3.3 %collective-permute-done.13.yo_ref = f32[320,128]{1,0:T(8,128)S(1)} collective-permute-done((f32[320,128]{1,0:T(8,128)S(1)}, f32[320,128]{1,0:T(8,128)S(1)}, u32[]{:S(2)}, u32[]{:S(2)}) %collective-permute-start.13) | collective-permute-done | bytes 163872 | tf_op jit(solution)/shard_map/ppermute | solution.py:595
  87.0 9.6 %collective-permute-start.14 = (f32[408,128]{1,0:T(8,128)S(1)}, f32[408,128]{1,0:T(8,128)S(1)}, u32[]{:S(2)}, u32[]{:S(2)}) collective-permute-start(f32[408,128]{1,0:T(8,128)S(1)} %get-tuple-element.80), channel_id=1, source_target_pairs={{0,64},{64,0},{128,192},{192,128},{256,320},{320,256},{384,448},{4... | collective-permute-start | bytes 626696 | tf_op jit(solution)/shard_map/ppermute | solution.py:595
  96.6 0.7 collective-permute-start.15
  97.6 3.5 %step.5 = (f32[384,128]{1,0:T(8,128)S(1)}, f32[384,128]{1,0:T(8,128)S(1)}) custom-call(s32[2]{0:T(128)S(1)} %pad_add_fusion.1.flags, f32[768,128]{1,0:T(8,128)S(1)} %get-tuple-element.76.y_ref, f32[768,128]{1,0:T(8,128)S(1)} %get-tuple-element.69.y_ref.prev_ref, f32[408,128]{1,0:T(8,128)S(1)} %collective-permute-done.14.xe_ref, ...), custom_call_target="tpu_custom_call" | custom-call | tf_op jit(solution)/shard_map/step/pallas_call | solution.py:668
  101.2 3.4 %collective-permute-start.16 = (f32[384,128]{1,0:T(8,128)S(1)}, f32[384,128]{1,0:T(8,128)S(1)}, u32[]{:S(2)}, u32[]{:S(2)}) collective-permute-start(f32[384,128]{1,0:T(8,128)S(1)} %get-tuple-element.83.refs_0_), channel_id=1, source_target_pairs={{0,1},{1,0},{2,3},{3,2},{4,5},{5,4},{6,7},{7,6},{8,9},{9,8},{10,11... | collective-permute-start | bytes 589832 | tf_op jit(solution)/shard_map/ppermute | solution.py:694
  104.6 4.0 %collective-permute-start.19 = (f32[384,128]{1,0:T(8,128)S(1)}, f32[384,128]{1,0:T(8,128)S(1)}, u32[]{:S(2)}, u32[]{:S(2)}) collective-permute-start(f32[384,128]{1,0:T(8,128)S(1)} %get-tuple-element.84.refs_1_), channel_id=1, source_target_pairs={{0,3},{1,2},{2,1},{3,0},{4,7},{5,6},{6,5},{7,4},{8,11},{9,10},{10,... | collective-permute-start | bytes 589832 | tf_op jit(solution)/shard_map/ppermute | solution.py:694
  108.6 3.0 %collective-permute-start.18 = (f32[384,128]{1,0:T(8,128)S(1)}, f32[384,128]{1,0:T(8,128)S(1)}, u32[]{:S(2)}, u32[]{:S(2)}) collective-permute-start(f32[384,128]{1,0:T(8,128)S(1)} %get-tuple-element.83.refs_0_), channel_id=1, source_target_pairs={{0,3},{1,2},{2,1},{3,0},{4,7},{5,6},{6,5},{7,4},{8,11},{9,10},{10,... | collective-permute-start | bytes 589832 | tf_op jit(solution)/shard_map/ppermute | solution.py:695
  111.6 1.9 %collective-permute-start.17 = (f32[384,128]{1,0:T(8,128)S(1)}, f32[384,128]{1,0:T(8,128)S(1)}, u32[]{:S(2)}, u32[]{:S(2)}) collective-permute-start(f32[384,128]{1,0:T(8,128)S(1)} %get-tuple-element.84.refs_1_), channel_id=1, source_target_pairs={{0,1},{1,0},{2,3},{3,2},{4,5},{5,4},{6,7},{7,6},{8,9},{9,8},{10,11... | collective-permute-start | bytes 589832 | tf_op jit(solution)/shard_map/ppermute | solution.py:695
  113.6 4.0 %collective-permute-start.20 = (f32[384,128]{1,0:T(8,128)S(1)}, f32[384,128]{1,0:T(8,128)S(1)}, u32[]{:S(2)}, u32[]{:S(2)}) collective-permute-start(f32[384,128]{1,0:T(8,128)S(1)} %collective-permute-done.16.refs_2_), channel_id=1, source_target_pairs={{0,3},{1,2},{2,1},{3,0},{4,7},{5,6},{6,5},{7,4},{8,11},{9,10},{10,... | collective-permute-start | bytes 589832 | tf_op jit(solution)/shard_map/ppermute | solution.py:696
  117.6 3.3 %collective-permute-start.21 = (f32[384,128]{1,0:T(8,128)S(1)}, f32[384,128]{1,0:T(8,128)S(1)}, u32[]{:S(2)}, u32[]{:S(2)}) collective-permute-start(f32[384,128]{1,0:T(8,128)S(1)} %collective-permute-done.19.refs_5_), channel_id=1, source_target_pairs={{0,1},{1,0},{2,3},{3,2},{4,5},{5,4},{6,7},{7,6},{8,9},{9,8},{10,11... | collective-permute-start | bytes 589832 | tf_op jit(solution)/shard_map/ppermute | solution.py:696
  121.0 2.1 %collective-permute-done.20.refs_6_ = f32[384,128]{1,0:T(8,128)S(1)} collective-permute-done((f32[384,128]{1,0:T(8,128)S(1)}, f32[384,128]{1,0:T(8,128)S(1)}, u32[]{:S(2)}, u32[]{:S(2)}) %collective-permute-start.20) | collective-permute-done | bytes 196640 | tf_op jit(solution)/shard_map/ppermute | solution.py:696
  123.1 3.5 %collective-permute-done.21.refs_7_ = f32[384,128]{1,0:T(8,128)S(1)} collective-permute-done((f32[384,128]{1,0:T(8,128)S(1)}, f32[384,128]{1,0:T(8,128)S(1)}, u32[]{:S(2)}, u32[]{:S(2)}) %collective-permute-start.21) | collective-permute-done | bytes 196640 | tf_op jit(solution)/shard_map/ppermute | solution.py:696
  126.6 1.8 gram.1
  128.4 17.6 %all_to_all.10 = f32[8,8,128]{2,1,0:T(8,128)S(1)} all-to-all(f32[8,8,128]{2,1,0:T(8,128)S(1)} %broadcast_in_dim.4), channel_id=1, replica_groups=mesh['gx'=8,'gy'=16,'orb'=4] {'gx'}, dimensions={0} | all-to-all | bytes 65536 | tf_op jit(solution)/shard_map/all_to_all | solution.py:601
  146.0 40.2 %all_to_all.11 = f32[16,8,128]{2,1,0:T(8,128)S(1)} all-to-all(f32[16,8,128]{2,1,0:T(8,128)S(1)} %broadcast_in_dim.5), channel_id=1, replica_groups=mesh['gx'=8,'gy'=16,'orb'=4] {'gy'}, dimensions={0} | all-to-all | bytes 131072 | tf_op jit(solution)/shard_map/all_to_all | solution.py:601
  186.2 4.1 %rotate.1 = f32[4,12,16,128]{3,2,1,0:T(8,128)} custom-call(s32[4]{0:T(128)S(1)} %pad_add_fusion.order, f32[8,128]{1,0:T(8,128)S(1)} %reduce_sum.19.corr_ref, f32[384,128]{1,0:T(8,128)S(1)} %get-tuple-element.83.refs_0_, f32[384,128]{1,0:T(8,128)S(1)} %get-tuple-element.84.refs_1_, f32[384,128]{1,0:T(8,128)S(1)} %collective-permute-done.16.refs_2_, ...), custom_call_target="tpu_custom_call" | custom-call | tf_op jit(solution)/shard_map/rotate/pallas_call | solution.py:708
  (33 shorter events, 3.1 us)
Async XLA Ops:
  0.7 0.9 copy-start.3
  1.6 0.9 copy-start.4
  2.5 0.7 copy-start.6
  3.2 0.7 copy-start.7
  5.4 3.2 %collective-permute-start = (f32[232,128]{1,0:T(8,128)S(1)}, f32[232,128]{1,0:T(8,128)S(1)}, u32[]{:S(2)}, u32[]{:S(2)}) collective-permute-start(f32[232,128]{1,0:T(8,128)S(1)} %get-tuple-element.51), channel_id=1, source_target_pairs={{0,64},{64,0},{128,192},{192,128},{256,320},{320,256},{384,448},{4... | collective-permute-start | bytes 356360 | tf_op jit(solution)/shard_map/ppermute | solution.py:595
  7.3 1.3 collective-permute-start.1
  9.3 11.6 %collective-permute-start.2 = (f32[272,128]{1,0:T(8,128)S(1)}, f32[272,128]{1,0:T(8,128)S(1)}, u32[]{:S(2)}, u32[]{:S(2)}) collective-permute-start(f32[272,128]{1,0:T(8,128)S(1)} %get-tuple-element.55), channel_id=1, source_target_pairs={{0,4},{4,0},{8,12},{12,8},{16,20},{20,16},{24,28},{28,24},{32,36},... | collective-permute-start | bytes 417800 | tf_op jit(solution)/shard_map/ppermute | solution.py:595
  17.0 6.9 %collective-permute-start.3 = (f32[272,128]{1,0:T(8,128)S(1)}, f32[272,128]{1,0:T(8,128)S(1)}, u32[]{:S(2)}, u32[]{:S(2)}) collective-permute-start(f32[272,128]{1,0:T(8,128)S(1)} %get-tuple-element.56), channel_id=1, source_target_pairs={{4,8},{8,4},{12,16},{16,12},{20,24},{24,20},{28,32},{32,28},{36,40... | collective-permute-start | bytes 417800 | tf_op jit(solution)/shard_map/ppermute | solution.py:595
  18.9 1.0 copy-start.2
  19.9 0.9 copy-start.5
  26.9 7.7 %collective-permute-start.4 = (f32[416,128]{1,0:T(8,128)S(1)}, f32[416,128]{1,0:T(8,128)S(1)}, u32[]{:S(2)}, u32[]{:S(2)}) collective-permute-start(f32[416,128]{1,0:T(8,128)S(1)} %get-tuple-element.60), channel_id=1, source_target_pairs={{0,4},{4,0},{8,12},{12,8},{16,20},{20,16},{24,28},{28,24},{32,36},... | collective-permute-start | bytes 638984 | tf_op jit(solution)/shard_map/ppermute | solution.py:595
  28.8 7.7 %collective-permute-start.5 = (f32[416,128]{1,0:T(8,128)S(1)}, f32[416,128]{1,0:T(8,128)S(1)}, u32[]{:S(2)}, u32[]{:S(2)}) collective-permute-start(f32[416,128]{1,0:T(8,128)S(1)} %get-tuple-element.61), channel_id=1, source_target_pairs={{4,8},{8,4},{12,16},{16,12},{20,24},{24,20},{28,32},{32,28},{36,40... | collective-permute-start | bytes 638984 | tf_op jit(solution)/shard_map/ppermute | solution.py:595
  37.1 7.9 %collective-permute-start.6 = (f32[408,128]{1,0:T(8,128)S(1)}, f32[408,128]{1,0:T(8,128)S(1)}, u32[]{:S(2)}, u32[]{:S(2)}) collective-permute-start(f32[408,128]{1,0:T(8,128)S(1)} %get-tuple-element.62), channel_id=1, source_target_pairs={{0,64},{64,0},{128,192},{192,128},{256,320},{320,256},{384,448},{4... | collective-permute-start | bytes 626696 | tf_op jit(solution)/shard_map/ppermute | solution.py:595
  41.8 3.3 %collective-permute-start.7 = (f32[408,128]{1,0:T(8,128)S(1)}, f32[408,128]{1,0:T(8,128)S(1)}, u32[]{:S(2)}, u32[]{:S(2)}) collective-permute-start(f32[408,128]{1,0:T(8,128)S(1)} %get-tuple-element.63), channel_id=1, source_target_pairs={{64,128},{128,64},{192,256},{256,192},{320,384},{384,320},{65,129}... | collective-permute-start | bytes 626696 | tf_op jit(solution)/shard_map/ppermute | solution.py:595
  42.5 0.9 copy-start
  45.1 22.8 %copy-start.1 = (bf16[256,256]{1,0:T(8,128)(2,1)S(1)}, bf16[256,256]{1,0:T(8,128)(2,1)}, u32[]{:S(2)}) copy-start(bf16[256,256]{1,0:T(8,128)(2,1)} %constant.48.clone.dz_ref) | copy-start | bytes 393220
  49.3 7.2 %collective-permute-start.8 = (f32[320,128]{1,0:T(8,128)S(1)}, f32[320,128]{1,0:T(8,128)S(1)}, u32[]{:S(2)}, u32[]{:S(2)}) collective-permute-start(f32[320,128]{1,0:T(8,128)S(1)} %get-tuple-element.71), channel_id=1, source_target_pairs={{0,4},{4,0},{8,12},{12,8},{16,20},{20,16},{24,28},{28,24},{32,36},... | collective-permute-start | bytes 491528 | tf_op jit(solution)/shard_map/ppermute | solution.py:595
  51.2 8.4 %collective-permute-start.9 = (f32[320,128]{1,0:T(8,128)S(1)}, f32[320,128]{1,0:T(8,128)S(1)}, u32[]{:S(2)}, u32[]{:S(2)}) collective-permute-start(f32[320,128]{1,0:T(8,128)S(1)} %get-tuple-element.72), channel_id=1, source_target_pairs={{4,8},{8,4},{12,16},{16,12},{20,24},{24,20},{28,32},{32,28},{36,40... | collective-permute-start | bytes 491528 | tf_op jit(solution)/shard_map/ppermute | solution.py:595
  60.3 7.6 %collective-permute-start.10 = (f32[408,128]{1,0:T(8,128)S(1)}, f32[408,128]{1,0:T(8,128)S(1)}, u32[]{:S(2)}, u32[]{:S(2)}) collective-permute-start(f32[408,128]{1,0:T(8,128)S(1)} %get-tuple-element.73), channel_id=1, source_target_pairs={{0,64},{64,0},{128,192},{192,128},{256,320},{320,256},{384,448},{4... | collective-permute-start | bytes 626696 | tf_op jit(solution)/shard_map/ppermute | solution.py:595
  66.8 1.1 collective-permute-start.11
  72.1 11.0 %collective-permute-start.12 = (f32[320,128]{1,0:T(8,128)S(1)}, f32[320,128]{1,0:T(8,128)S(1)}, u32[]{:S(2)}, u32[]{:S(2)}) collective-permute-start(f32[320,128]{1,0:T(8,128)S(1)} %get-tuple-element.78), channel_id=1, source_target_pairs={{0,4},{4,0},{8,12},{12,8},{16,20},{20,16},{24,28},{28,24},{32,36},... | collective-permute-start | bytes 491528 | tf_op jit(solution)/shard_map/ppermute | solution.py:595
  74.1 12.3 %collective-permute-start.13 = (f32[320,128]{1,0:T(8,128)S(1)}, f32[320,128]{1,0:T(8,128)S(1)}, u32[]{:S(2)}, u32[]{:S(2)}) collective-permute-start(f32[320,128]{1,0:T(8,128)S(1)} %get-tuple-element.79), channel_id=1, source_target_pairs={{4,8},{8,4},{12,16},{16,12},{20,24},{24,20},{28,32},{32,28},{36,40... | collective-permute-start | bytes 491528 | tf_op jit(solution)/shard_map/ppermute | solution.py:595
  87.0 10.6 %collective-permute-start.14 = (f32[408,128]{1,0:T(8,128)S(1)}, f32[408,128]{1,0:T(8,128)S(1)}, u32[]{:S(2)}, u32[]{:S(2)}) collective-permute-start(f32[408,128]{1,0:T(8,128)S(1)} %get-tuple-element.80), channel_id=1, source_target_pairs={{0,64},{64,0},{128,192},{192,128},{256,320},{320,256},{384,448},{4... | collective-permute-start | bytes 626696 | tf_op jit(solution)/shard_map/ppermute | solution.py:595
  96.6 1.1 collective-permute-start.15
  101.2 12.4 %collective-permute-start.16 = (f32[384,128]{1,0:T(8,128)S(1)}, f32[384,128]{1,0:T(8,128)S(1)}, u32[]{:S(2)}, u32[]{:S(2)}) collective-permute-start(f32[384,128]{1,0:T(8,128)S(1)} %get-tuple-element.83.refs_0_), channel_id=1, source_target_pairs={{0,1},{1,0},{2,3},{3,2},{4,5},{5,4},{6,7},{7,6},{8,9},{9,8},{10,11... | collective-permute-start | bytes 589832 | tf_op jit(solution)/shard_map/ppermute | solution.py:694
  104.6 13.0 %collective-permute-start.19 = (f32[384,128]{1,0:T(8,128)S(1)}, f32[384,128]{1,0:T(8,128)S(1)}, u32[]{:S(2)}, u32[]{:S(2)}) collective-permute-start(f32[384,128]{1,0:T(8,128)S(1)} %get-tuple-element.84.refs_1_), channel_id=1, source_target_pairs={{0,3},{1,2},{2,1},{3,0},{4,7},{5,6},{6,5},{7,4},{8,11},{9,10},{10,... | collective-permute-start | bytes 589832 | tf_op jit(solution)/shard_map/ppermute | solution.py:694
  108.6 12.4 %collective-permute-start.18 = (f32[384,128]{1,0:T(8,128)S(1)}, f32[384,128]{1,0:T(8,128)S(1)}, u32[]{:S(2)}, u32[]{:S(2)}) collective-permute-start(f32[384,128]{1,0:T(8,128)S(1)} %get-tuple-element.83.refs_0_), channel_id=1, source_target_pairs={{0,3},{1,2},{2,1},{3,0},{4,7},{5,6},{6,5},{7,4},{8,11},{9,10},{10,... | collective-permute-start | bytes 589832 | tf_op jit(solution)/shard_map/ppermute | solution.py:695
  111.6 9.4 %collective-permute-start.17 = (f32[384,128]{1,0:T(8,128)S(1)}, f32[384,128]{1,0:T(8,128)S(1)}, u32[]{:S(2)}, u32[]{:S(2)}) collective-permute-start(f32[384,128]{1,0:T(8,128)S(1)} %get-tuple-element.84.refs_1_), channel_id=1, source_target_pairs={{0,1},{1,0},{2,3},{3,2},{4,5},{5,4},{6,7},{7,6},{8,9},{9,8},{10,11... | collective-permute-start | bytes 589832 | tf_op jit(solution)/shard_map/ppermute | solution.py:695
  113.6 9.5 %collective-permute-start.20 = (f32[384,128]{1,0:T(8,128)S(1)}, f32[384,128]{1,0:T(8,128)S(1)}, u32[]{:S(2)}, u32[]{:S(2)}) collective-permute-start(f32[384,128]{1,0:T(8,128)S(1)} %collective-permute-done.16.refs_2_), channel_id=1, source_target_pairs={{0,3},{1,2},{2,1},{3,0},{4,7},{5,6},{6,5},{7,4},{8,11},{9,10},{10,... | collective-permute-start | bytes 589832 | tf_op jit(solution)/shard_map/ppermute | solution.py:696
  117.6 9.0 %collective-permute-start.21 = (f32[384,128]{1,0:T(8,128)S(1)}, f32[384,128]{1,0:T(8,128)S(1)}, u32[]{:S(2)}, u32[]{:S(2)}) collective-permute-start(f32[384,128]{1,0:T(8,128)S(1)} %collective-permute-done.19.refs_5_), channel_id=1, source_target_pairs={{0,1},{1,0},{2,3},{3,2},{4,5},{5,4},{6,7},{7,6},{8,9},{9,8},{10,11... | collective-permute-start | bytes 589832 | tf_op jit(solution)/shard_map/ppermute | solution.py:696

commit v7 on v6

--- a/solution.py
+++ b/solution.py
@@ -190,7 +190,7 @@
     yo_ref[0:rows, :] = rims[pl.ds(pl.multiple_of(jnp.where(flag == 1, rows, 0), 8), rows), :]
 
 
-def widen_kernel(flags, t_ref, meta_ref, xe_ref, xo_ref, t2_ref, m_ref, ye_ref, yo_ref, fl_ref, fr_ref, hi_ref, lo_ref):
+def widen_kernel(flags, t_ref, meta_ref, xo_ref, xe_ref, t2_ref, m_ref, ye_ref, yo_ref, fl_ref, fr_ref, hi_ref, lo_ref):
     _, lane = iotas()
     left_half = lane < 64
     base = 0
@@ -324,7 +324,7 @@
 
 
 def build_kernel(
-    flags, t2_ref, m_ref, ye_ref, yo_ref, y_ref, mu, g_ref,
+    flags, t2_ref, m_ref, yo_ref, ye_ref, y_ref, mu, g_ref,
     q_ref, s_ref, w_ref, z_ref, nye_ref, nyo_ref, tx, acc, lo_ref, hi_ref, rims
 ):
     for t in range(34):
@@ -393,7 +393,7 @@
         put(nyo_ref, Y_MU + x, jnp.where(flags[1] == 1, above, below))
 
 
-def fold_kernel(flags, z_ref, y_ref, ye_ref, yo_ref, out_ref, xe_ref, xo_ref):
+def fold_kernel(flags, z_ref, y_ref, yo_ref, ye_ref, out_ref, xe_ref, xo_ref):
     give_ends(flags[0], y_ref, xe_ref, xo_ref)
     base = Y_SUMS
     for side in range(2):
@@ -410,7 +410,7 @@
 
 
 def step_kernel(
-    step, flags, y_ref, prev_ref, xe_ref, xo_ref, ye_ref, yo_ref, coef_ref, q_ref, s_ref, w_ref, z_ref,
+    step, flags, y_ref, prev_ref, xo_ref, xe_ref, yo_ref, ye_ref, coef_ref, q_ref, s_ref, w_ref, z_ref,
     dz_ref, g_ref, *rest
 ):
     last = step == STEPS
@@ -544,8 +544,8 @@
     pivots = jnp.ones((16, 128), F32)
     for k in range(16):
         pivot_row = jnp.broadcast_to(work[k : k + 1, :], (16, 128))
-        pivot = jnp.broadcast_to(pivot_row[:, k : k + 1], (16, 128))
         column = jnp.broadcast_to(work[:, k : k + 1], (16, 128))
+        pivot = jnp.broadcast_to(column[k : k + 1, :], (16, 128))
         pivots = jnp.where(rows == k, pivot, pivots)
         work = jnp.where(rows > k, work - column / pivot * pivot_row, work)
     inverse = (work / jnp.sqrt(pivots))[:, 16:32]
@@ -604,7 +604,7 @@
 def fold(flags, z, y, even, odd):
     return kernel_call(
         fold_kernel, [blocks(6), blocks(X_ALL), blocks(X_ALL)], [SMEM] + [VMEM] * 4, name="fold_coeffs"
-    )(flags, z, y, even, odd)
+    )(flags, z, y, odd, even)
 
 
 def shards(orbitals, potential, kinetic_mu, projectors, strengths, box_offsets, block_counts):
@@ -632,7 +632,7 @@
         [SMEM] + [VMEM] * 4,
         [pltpu.VMEM((17 * 8, 128), F32)] * 2 + [pltpu.VMEM((34 * 8, 128), F32)] * 2,
         name="widen",
-    )(flags, t, meta, xte, xto)
+    )(flags, t, meta, xto, xte)
     ye2, yo2 = exchange(ye2, yo2, "gy")
     q, s, w, z, ye, yo = kernel_call(
         build_kernel,
@@ -646,7 +646,7 @@
             pltpu.VMEM((2 * YH * 8, 128), F32),
         ],
         name="build",
-    )(flags, t2, metas, ye2, yo2, y, mu, groups)
+    )(flags, t2, metas, yo2, ye2, y, mu, groups)
     ye, yo = exchange(ye, yo, "gy")
     z, xe, xo = fold(flags, z, y, ye, yo)
     xe, xo = exchange(xe, xo, "gx")
@@ -678,7 +678,7 @@
                 pltpu.VMEM((TILES * 8, 128) if last else (48, 1024), F32),
             ],
             name="step",
-        )(flags, y, previous, xe, xo, ye, yo, coefs, q, s, w, z, dz, groups)
+        )(flags, y, previous, xo, xe, yo, ye, coefs, q, s, w, z, dz, groups)
         previous = y
         if not last:
             y, ye, yo, z = result

time: 191 us -> 179 us (0.937)
  the two profiles are of different devices: /device:TPU:8 before, /device:TPU:2 now
where the time goes in v7:
time: 179 us; the launch traced here: 178 us
  starting transfers between devices  73.9 us (41%)
  blocking collectives  47.5 us (27%)
  Pallas kernels  26.4 us (15%)
  waiting for transfers between devices  22.9 us (13%)
  local copies, waits for them, and re-layouts  5.97 us (3%)
    ppermute x16, starting transfers between devices, exchange(): results.append(lax.ppermute(value, axis, pairs))  55 us
    all_to_all x2, blocking collectives, spread_sum(): return jnp.sum(lax.all_to_all(copies, axis, 0, 0, tiled=True), axis=0)  47.5 us
    ppermute x16, waiting for transfers between devices, exchange(): results.append(lax.ppermute(value, axis, pairs))  17.5 us
    pallas_call x3, Pallas kernels, shards(): kernel_call(functools.partial(step_kernel, step), outs, [SMEM] + [VMEM] *...  11.9 us
    unnamed x16, local copies, waits for them, and re-layouts  5.95 us
    ppermute x1, starting transfers between devices, shards(): lax.ppermute(parts[1], 'orb', even)  4.47 us
    pallas_call x1, Pallas kernels, shards(): kernel_call(functools.partial(rotate_kernel, cells), [((ORB, CX, CY, NZ),...  4.11 us
    ppermute x1, starting transfers between devices, shards(): lax.ppermute(parts[1], 'orb', odd)  4.07 us
  transfers between devices with their start and end apart: 22, of which 9 were waited for; matrix products, arithmetic and copies ran while one was open for 0% of the time, Pallas kernels for 1%

profile of v7, /device:TPU:2, one launch (start us, length us, event | category | flops | bytes accessed | tf_op | source)
XLA Modules:
  0.0 177.9 jit_solution(12297305449297715840)
XLA Ops:
  0.7 0.9 copy-done.3
  1.6 0.9 copy-done.4
  2.5 0.7 copy-done.6
  3.2 0.7 copy-done.7
  3.9 1.5 prepare_slots.1
  5.4 0.7 collective-permute-start
  6.1 5.6 %collective-permute-start.1 = (f32[232,128]{1,0:T(8,128)S(1)}, f32[232,128]{1,0:T(8,128)S(1)}, u32[]{:S(2)}, u32[]{:S(2)}) collective-permute-start(f32[232,128]{1,0:T(8,128)S(1)} %get-tuple-element.52), channel_id=1, source_target_pairs={{0,64},{64,0},{128,192},{192,128},{256,320},{320,256},{384,448},{4... | collective-permute-start | bytes 356360 | tf_op jit(solution)/shard_map/ppermute | solution.py:595
  11.7 0.9 collective-permute-done.1.xe_ref
  13.3 0.7 collective-permute-start.2
  14.0 6.3 %collective-permute-start.3 = (f32[272,128]{1,0:T(8,128)S(1)}, f32[272,128]{1,0:T(8,128)S(1)}, u32[]{:S(2)}, u32[]{:S(2)}) collective-permute-start(f32[272,128]{1,0:T(8,128)S(1)} %get-tuple-element.56), channel_id=1, source_target_pairs={{0,4},{4,0},{8,12},{12,8},{16,20},{20,16},{24,28},{28,24},{32,36},... | collective-permute-start | bytes 417800 | tf_op jit(solution)/shard_map/ppermute | solution.py:595
  20.3 1.0 copy-done.2
  21.3 0.9 copy-done.5
  22.3 1.9 %collective-permute-done.3.ye_ref = f32[272,128]{1,0:T(8,128)S(1)} collective-permute-done((f32[272,128]{1,0:T(8,128)S(1)}, f32[272,128]{1,0:T(8,128)S(1)}, u32[]{:S(2)}, u32[]{:S(2)}) %collective-permute-start.3) | collective-permute-done | bytes 139296 | tf_op jit(solution)/shard_map/ppermute | solution.py:595
  24.2 2.9 %build.1 = (f32[6144,256]{1,0:T(8,128)S(1)}, bf16[512,256]{1,0:T(8,128)(2,1)S(1)}, f32[48,128]{1,0:T(8,128)S(1)}, f32[48,128]{1,0:T(8,128)S(1)}, f32[416,128]{1,0:T(8,128)S(1)}, /*index=5*/f32[416,128]{1,0:T(8,128)S(1)}) custom-call(s32[2]{0:T(128)S(1)} %pad_add_fusion.1.flags, f32[512,128]{1,0:T(8,128)S(1)} %get-tuple-element.53.t2_ref, ...), custom_call_target="tpu_custom_call" | custom-call | tf_op jit(solution)/shard_map/build/pallas_call | solution.py:637
  27.1 0.7 collective-permute-start.4
  27.8 7.5 %collective-permute-start.5 = (f32[416,128]{1,0:T(8,128)S(1)}, f32[416,128]{1,0:T(8,128)S(1)}, u32[]{:S(2)}, u32[]{:S(2)}) collective-permute-start(f32[416,128]{1,0:T(8,128)S(1)} %get-tuple-element.61), channel_id=1, source_target_pairs={{0,4},{4,0},{8,12},{12,8},{16,20},{20,16},{24,28},{28,24},{32,36},... | collective-permute-start | bytes 638984 | tf_op jit(solution)/shard_map/ppermute | solution.py:595
  35.3 4.7 %collective-permute-done.5.ye_ref = f32[416,128]{1,0:T(8,128)S(1)} collective-permute-done((f32[416,128]{1,0:T(8,128)S(1)}, f32[416,128]{1,0:T(8,128)S(1)}, u32[]{:S(2)}, u32[]{:S(2)}) %collective-permute-start.5) | collective-permute-done | bytes 213024 | tf_op jit(solution)/shard_map/ppermute | solution.py:595
  40.6 0.7 collective-permute-start.6
  41.2 5.6 %collective-permute-start.7 = (f32[408,128]{1,0:T(8,128)S(1)}, f32[408,128]{1,0:T(8,128)S(1)}, u32[]{:S(2)}, u32[]{:S(2)}) collective-permute-start(f32[408,128]{1,0:T(8,128)S(1)} %get-tuple-element.63), channel_id=1, source_target_pairs={{0,64},{64,0},{128,192},{192,128},{256,320},{320,256},{384,448},{4... | collective-permute-start | bytes 626696 | tf_op jit(solution)/shard_map/ppermute | solution.py:595
  46.9 0.9 copy-done
  47.8 1.6 coefficients.1.coef_ref
  49.5 4.2 %step.3 = (f32[768,128]{1,0:T(8,128)S(1)}, f32[320,128]{1,0:T(8,128)S(1)}, f32[320,128]{1,0:T(8,128)S(1)}, f32[48,128]{1,0:T(8,128)S(1)}) custom-call(s32[2]{0:T(128)S(1)} %pad_add_fusion.1.flags, f32[768,128]{1,0:T(8,128)S(1)} %get-tuple-element.48.y_ref.prev_ref, f32[768,128]{1,0:T(8,128)S(1)} %get-tuple-element.48.y_ref.prev_ref, ...), custom_call_target="tpu_custom_call" | custom-call | tf_op jit(solution)/shard_map/step/pallas_call | solution.py:668
  53.7 0.7 collective-permute-start.8
  54.3 5.2 %collective-permute-start.9 = (f32[320,128]{1,0:T(8,128)S(1)}, f32[320,128]{1,0:T(8,128)S(1)}, u32[]{:S(2)}, u32[]{:S(2)}) collective-permute-start(f32[320,128]{1,0:T(8,128)S(1)} %get-tuple-element.72), channel_id=1, source_target_pairs={{0,4},{4,0},{8,12},{12,8},{16,20},{20,16},{24,28},{28,24},{32,36},... | collective-permute-start | bytes 491528 | tf_op jit(solution)/shard_map/ppermute | solution.py:595
  59.5 3.3 %collective-permute-done.9.ye_ref = f32[320,128]{1,0:T(8,128)S(1)} collective-permute-done((f32[320,128]{1,0:T(8,128)S(1)}, f32[320,128]{1,0:T(8,128)S(1)}, u32[]{:S(2)}, u32[]{:S(2)}) %collective-permute-start.9) | collective-permute-done | bytes 163872 | tf_op jit(solution)/shard_map/ppermute | solution.py:595
  63.4 0.7 collective-permute-start.10
  64.1 8.1 %collective-permute-start.11 = (f32[408,128]{1,0:T(8,128)S(1)}, f32[408,128]{1,0:T(8,128)S(1)}, u32[]{:S(2)}, u32[]{:S(2)}) collective-permute-start(f32[408,128]{1,0:T(8,128)S(1)} %get-tuple-element.74), channel_id=1, source_target_pairs={{0,64},{64,0},{128,192},{192,128},{256,320},{320,256},{384,448},{4... | collective-permute-start | bytes 626696 | tf_op jit(solution)/shard_map/ppermute | solution.py:595
  72.2 1.1 collective-permute-done.11.xe_ref
  73.3 4.2 %step.4 = (f32[768,128]{1,0:T(8,128)S(1)}, f32[320,128]{1,0:T(8,128)S(1)}, f32[320,128]{1,0:T(8,128)S(1)}, f32[48,128]{1,0:T(8,128)S(1)}) custom-call(s32[2]{0:T(128)S(1)} %pad_add_fusion.1.flags, f32[768,128]{1,0:T(8,128)S(1)} %get-tuple-element.69.y_ref.prev_ref, f32[768,128]{1,0:T(8,128)S(1)} %get-tuple-element.48.y_ref.prev_ref, ...), custom_call_target="tpu_custom_call" | custom-call | tf_op jit(solution)/shard_map/step/pallas_call | solution.py:668
  77.5 0.7 collective-permute-start.12
  78.2 7.0 %collective-permute-start.13 = (f32[320,128]{1,0:T(8,128)S(1)}, f32[320,128]{1,0:T(8,128)S(1)}, u32[]{:S(2)}, u32[]{:S(2)}) collective-permute-start(f32[320,128]{1,0:T(8,128)S(1)} %get-tuple-element.79), channel_id=1, source_target_pairs={{0,4},{4,0},{8,12},{12,8},{16,20},{20,16},{24,28},{28,24},{32,36},... | collective-permute-start | bytes 491528 | tf_op jit(solution)/shard_map/ppermute | solution.py:595
  85.2 4.6 %collective-permute-done.13.ye_ref = f32[320,128]{1,0:T(8,128)S(1)} collective-permute-done((f32[320,128]{1,0:T(8,128)S(1)}, f32[320,128]{1,0:T(8,128)S(1)}, u32[]{:S(2)}, u32[]{:S(2)}) %collective-permute-start.13) | collective-permute-done | bytes 163872 | tf_op jit(solution)/shard_map/ppermute | solution.py:595
  90.4 0.7 collective-permute-start.14
  91.1 4.3 %collective-permute-start.15 = (f32[408,128]{1,0:T(8,128)S(1)}, f32[408,128]{1,0:T(8,128)S(1)}, u32[]{:S(2)}, u32[]{:S(2)}) collective-permute-start(f32[408,128]{1,0:T(8,128)S(1)} %get-tuple-element.81), channel_id=1, source_target_pairs={{0,64},{64,0},{128,192},{192,128},{256,320},{320,256},{384,448},{4... | collective-permute-start | bytes 626696 | tf_op jit(solution)/shard_map/ppermute | solution.py:595
  95.4 1.1 collective-permute-done.15.xe_ref
  96.5 3.5 %step.5 = (f32[384,128]{1,0:T(8,128)S(1)}, f32[384,128]{1,0:T(8,128)S(1)}) custom-call(s32[2]{0:T(128)S(1)} %pad_add_fusion.1.flags, f32[768,128]{1,0:T(8,128)S(1)} %get-tuple-element.76.y_ref, f32[768,128]{1,0:T(8,128)S(1)} %get-tuple-element.69.y_ref.prev_ref, f32[408,128]{1,0:T(8,128)S(1)} %collective-permute-done.14.xo_ref, ...), custom_call_target="tpu_custom_call" | custom-call | tf_op jit(solution)/shard_map/step/pallas_call | solution.py:668
  100.0 2.4 %collective-permute-start.16 = (f32[384,128]{1,0:T(8,128)S(1)}, f32[384,128]{1,0:T(8,128)S(1)}, u32[]{:S(2)}, u32[]{:S(2)}) collective-permute-start(f32[384,128]{1,0:T(8,128)S(1)} %get-tuple-element.83.refs_0_), channel_id=1, source_target_pairs={{0,1},{1,0},{2,3},{3,2},{4,5},{5,4},{6,7},{7,6},{8,9},{9,8},{10,11... | collective-permute-start | bytes 589832 | tf_op jit(solution)/shard_map/ppermute | solution.py:694
  102.4 4.1 %collective-permute-start.19 = (f32[384,128]{1,0:T(8,128)S(1)}, f32[384,128]{1,0:T(8,128)S(1)}, u32[]{:S(2)}, u32[]{:S(2)}) collective-permute-start(f32[384,128]{1,0:T(8,128)S(1)} %get-tuple-element.84.refs_1_), channel_id=1, source_target_pairs={{0,3},{1,2},{2,1},{3,0},{4,7},{5,6},{6,5},{7,4},{8,11},{9,10},{10,... | collective-permute-start | bytes 589832 | tf_op jit(solution)/shard_map/ppermute | solution.py:694
  106.5 1.9 %collective-permute-start.18 = (f32[384,128]{1,0:T(8,128)S(1)}, f32[384,128]{1,0:T(8,128)S(1)}, u32[]{:S(2)}, u32[]{:S(2)}) collective-permute-start(f32[384,128]{1,0:T(8,128)S(1)} %get-tuple-element.83.refs_0_), channel_id=1, source_target_pairs={{0,3},{1,2},{2,1},{3,0},{4,7},{5,6},{6,5},{7,4},{8,11},{9,10},{10,... | collective-permute-start | bytes 589832 | tf_op jit(solution)/shard_map/ppermute | solution.py:695
  108.4 4.5 %collective-permute-start.17 = (f32[384,128]{1,0:T(8,128)S(1)}, f32[384,128]{1,0:T(8,128)S(1)}, u32[]{:S(2)}, u32[]{:S(2)}) collective-permute-start(f32[384,128]{1,0:T(8,128)S(1)} %get-tuple-element.84.refs_1_), channel_id=1, source_target_pairs={{0,1},{1,0},{2,3},{3,2},{4,5},{5,4},{6,7},{7,6},{8,9},{9,8},{10,11... | collective-permute-start | bytes 589832 | tf_op jit(solution)/shard_map/ppermute | solution.py:695
  112.9 3.4 %collective-permute-start.20 = (f32[384,128]{1,0:T(8,128)S(1)}, f32[384,128]{1,0:T(8,128)S(1)}, u32[]{:S(2)}, u32[]{:S(2)}) collective-permute-start(f32[384,128]{1,0:T(8,128)S(1)} %collective-permute-done.16.refs_2_), channel_id=1, source_target_pairs={{0,3},{1,2},{2,1},{3,0},{4,7},{5,6},{6,5},{7,4},{8,11},{9,10},{10,... | collective-permute-start | bytes 589832 | tf_op jit(solution)/shard_map/ppermute | solution.py:696
  116.3 2.5 %collective-permute-start.21 = (f32[384,128]{1,0:T(8,128)S(1)}, f32[384,128]{1,0:T(8,128)S(1)}, u32[]{:S(2)}, u32[]{:S(2)}) collective-permute-start(f32[384,128]{1,0:T(8,128)S(1)} %collective-permute-done.19.refs_5_), channel_id=1, source_target_pairs={{0,1},{1,0},{2,3},{3,2},{4,5},{5,4},{6,7},{7,6},{8,9},{9,8},{10,11... | collective-permute-start | bytes 589832 | tf_op jit(solution)/shard_map/ppermute | solution.py:696
  119.0 2.3 %collective-permute-done.20.refs_6_ = f32[384,128]{1,0:T(8,128)S(1)} collective-permute-done((f32[384,128]{1,0:T(8,128)S(1)}, f32[384,128]{1,0:T(8,128)S(1)}, u32[]{:S(2)}, u32[]{:S(2)}) %collective-permute-start.20) | collective-permute-done | bytes 196640 | tf_op jit(solution)/shard_map/ppermute | solution.py:696
  121.3 3.1 %collective-permute-done.21.refs_7_ = f32[384,128]{1,0:T(8,128)S(1)} collective-permute-done((f32[384,128]{1,0:T(8,128)S(1)}, f32[384,128]{1,0:T(8,128)S(1)}, u32[]{:S(2)}, u32[]{:S(2)}) %collective-permute-start.21) | collective-permute-done | bytes 196640 | tf_op jit(solution)/shard_map/ppermute | solution.py:696
  124.4 1.8 gram.1
  126.2 17.6 %all_to_all.10 = f32[8,8,128]{2,1,0:T(8,128)S(1)} all-to-all(f32[8,8,128]{2,1,0:T(8,128)S(1)} %broadcast_in_dim.4), channel_id=1, replica_groups=mesh['gx'=8,'gy'=16,'orb'=4] {'gx'}, dimensions={0} | all-to-all | bytes 65536 | tf_op jit(solution)/shard_map/all_to_all | solution.py:601
  143.8 30.0 %all_to_all.11 = f32[16,8,128]{2,1,0:T(8,128)S(1)} all-to-all(f32[16,8,128]{2,1,0:T(8,128)S(1)} %broadcast_in_dim.5), channel_id=1, replica_groups=mesh['gx'=8,'gy'=16,'orb'=4] {'gy'}, dimensions={0} | all-to-all | bytes 131072 | tf_op jit(solution)/shard_map/all_to_all | solution.py:601
  173.8 4.1 %rotate.1 = f32[4,12,16,128]{3,2,1,0:T(8,128)} custom-call(s32[4]{0:T(128)S(1)} %pad_add_fusion.order, f32[8,128]{1,0:T(8,128)S(1)} %reduce_sum.19.corr_ref, f32[384,128]{1,0:T(8,128)S(1)} %get-tuple-element.83.refs_0_, f32[384,128]{1,0:T(8,128)S(1)} %get-tuple-element.84.refs_1_, f32[384,128]{1,0:T(8,128)S(1)} %collective-permute-done.16.refs_2_, ...), custom_call_target="tpu_custom_call" | custom-call | tf_op jit(solution)/shard_map/rotate/pallas_call | solution.py:708
  (33 shorter events, 2.8 us)
Async XLA Ops:
  0.7 0.9 copy-start.3
  1.6 0.9 copy-start.4
  2.5 0.7 copy-start.6
  3.2 0.7 copy-start.7
  5.4 6.3 %collective-permute-start = (f32[232,128]{1,0:T(8,128)S(1)}, f32[232,128]{1,0:T(8,128)S(1)}, u32[]{:S(2)}, u32[]{:S(2)}) collective-permute-start(f32[232,128]{1,0:T(8,128)S(1)} %get-tuple-element.51), channel_id=1, source_target_pairs={{64,128},{128,64},{192,256},{256,192},{320,384},{384,320},{65,129}... | collective-permute-start | bytes 356360 | tf_op jit(solution)/shard_map/ppermute | solution.py:595
  6.1 6.6 %collective-permute-start.1 = (f32[232,128]{1,0:T(8,128)S(1)}, f32[232,128]{1,0:T(8,128)S(1)}, u32[]{:S(2)}, u32[]{:S(2)}) collective-permute-start(f32[232,128]{1,0:T(8,128)S(1)} %get-tuple-element.52), channel_id=1, source_target_pairs={{0,64},{64,0},{128,192},{192,128},{256,320},{320,256},{384,448},{4... | collective-permute-start | bytes 356360 | tf_op jit(solution)/shard_map/ppermute | solution.py:595
  13.3 9.0 %collective-permute-start.2 = (f32[272,128]{1,0:T(8,128)S(1)}, f32[272,128]{1,0:T(8,128)S(1)}, u32[]{:S(2)}, u32[]{:S(2)}) collective-permute-start(f32[272,128]{1,0:T(8,128)S(1)} %get-tuple-element.55), channel_id=1, source_target_pairs={{4,8},{8,4},{12,16},{16,12},{20,24},{24,20},{28,32},{32,28},{36,40... | collective-permute-start | bytes 417800 | tf_op jit(solution)/shard_map/ppermute | solution.py:595
  14.0 10.2 %collective-permute-start.3 = (f32[272,128]{1,0:T(8,128)S(1)}, f32[272,128]{1,0:T(8,128)S(1)}, u32[]{:S(2)}, u32[]{:S(2)}) collective-permute-start(f32[272,128]{1,0:T(8,128)S(1)} %get-tuple-element.56), channel_id=1, source_target_pairs={{0,4},{4,0},{8,12},{12,8},{16,20},{20,16},{24,28},{28,24},{32,36},... | collective-permute-start | bytes 417800 | tf_op jit(solution)/shard_map/ppermute | solution.py:595
  20.3 1.0 copy-start.2
  21.3 0.9 copy-start.5
  27.1 8.2 %collective-permute-start.4 = (f32[416,128]{1,0:T(8,128)S(1)}, f32[416,128]{1,0:T(8,128)S(1)}, u32[]{:S(2)}, u32[]{:S(2)}) collective-permute-start(f32[416,128]{1,0:T(8,128)S(1)} %get-tuple-element.60), channel_id=1, source_target_pairs={{4,8},{8,4},{12,16},{16,12},{20,24},{24,20},{28,32},{32,28},{36,40... | collective-permute-start | bytes 638984 | tf_op jit(solution)/shard_map/ppermute | solution.py:595
  27.8 12.2 %collective-permute-start.5 = (f32[416,128]{1,0:T(8,128)S(1)}, f32[416,128]{1,0:T(8,128)S(1)}, u32[]{:S(2)}, u32[]{:S(2)}) collective-permute-start(f32[416,128]{1,0:T(8,128)S(1)} %get-tuple-element.61), channel_id=1, source_target_pairs={{0,4},{4,0},{8,12},{12,8},{16,20},{20,16},{24,28},{28,24},{32,36},... | collective-permute-start | bytes 638984 | tf_op jit(solution)/shard_map/ppermute | solution.py:595
  40.6 8.9 %collective-permute-start.6 = (f32[408,128]{1,0:T(8,128)S(1)}, f32[408,128]{1,0:T(8,128)S(1)}, u32[]{:S(2)}, u32[]{:S(2)}) collective-permute-start(f32[408,128]{1,0:T(8,128)S(1)} %get-tuple-element.62), channel_id=1, source_target_pairs={{64,128},{128,64},{192,256},{256,192},{320,384},{384,320},{65,129}... | collective-permute-start | bytes 626696 | tf_op jit(solution)/shard_map/ppermute | solution.py:595
  41.2 8.2 %collective-permute-start.7 = (f32[408,128]{1,0:T(8,128)S(1)}, f32[408,128]{1,0:T(8,128)S(1)}, u32[]{:S(2)}, u32[]{:S(2)}) collective-permute-start(f32[408,128]{1,0:T(8,128)S(1)} %get-tuple-element.63), channel_id=1, source_target_pairs={{0,64},{64,0},{128,192},{192,128},{256,320},{320,256},{384,448},{4... | collective-permute-start | bytes 626696 | tf_op jit(solution)/shard_map/ppermute | solution.py:595
  46.9 0.9 copy-start
  49.4 23.8 %copy-start.1 = (bf16[256,256]{1,0:T(8,128)(2,1)S(1)}, bf16[256,256]{1,0:T(8,128)(2,1)}, u32[]{:S(2)}) copy-start(bf16[256,256]{1,0:T(8,128)(2,1)} %constant.48.clone.dz_ref) | copy-start | bytes 393220
  53.7 5.9 %collective-permute-start.8 = (f32[320,128]{1,0:T(8,128)S(1)}, f32[320,128]{1,0:T(8,128)S(1)}, u32[]{:S(2)}, u32[]{:S(2)}) collective-permute-start(f32[320,128]{1,0:T(8,128)S(1)} %get-tuple-element.71), channel_id=1, source_target_pairs={{4,8},{8,4},{12,16},{16,12},{20,24},{24,20},{28,32},{32,28},{36,40... | collective-permute-start | bytes 491528 | tf_op jit(solution)/shard_map/ppermute | solution.py:595
  54.3 8.5 %collective-permute-start.9 = (f32[320,128]{1,0:T(8,128)S(1)}, f32[320,128]{1,0:T(8,128)S(1)}, u32[]{:S(2)}, u32[]{:S(2)}) collective-permute-start(f32[320,128]{1,0:T(8,128)S(1)} %get-tuple-element.72), channel_id=1, source_target_pairs={{0,4},{4,0},{8,12},{12,8},{16,20},{20,16},{24,28},{28,24},{32,36},... | collective-permute-start | bytes 491528 | tf_op jit(solution)/shard_map/ppermute | solution.py:595
  63.4 8.8 %collective-permute-start.10 = (f32[408,128]{1,0:T(8,128)S(1)}, f32[408,128]{1,0:T(8,128)S(1)}, u32[]{:S(2)}, u32[]{:S(2)}) collective-permute-start(f32[408,128]{1,0:T(8,128)S(1)} %get-tuple-element.73), channel_id=1, source_target_pairs={{64,128},{128,64},{192,256},{256,192},{320,384},{384,320},{65,129}... | collective-permute-start | bytes 626696 | tf_op jit(solution)/shard_map/ppermute | solution.py:595
  64.1 9.2 %collective-permute-start.11 = (f32[408,128]{1,0:T(8,128)S(1)}, f32[408,128]{1,0:T(8,128)S(1)}, u32[]{:S(2)}, u32[]{:S(2)}) collective-permute-start(f32[408,128]{1,0:T(8,128)S(1)} %get-tuple-element.74), channel_id=1, source_target_pairs={{0,64},{64,0},{128,192},{192,128},{256,320},{320,256},{384,448},{4... | collective-permute-start | bytes 626696 | tf_op jit(solution)/shard_map/ppermute | solution.py:595
  77.5 7.7 %collective-permute-start.12 = (f32[320,128]{1,0:T(8,128)S(1)}, f32[320,128]{1,0:T(8,128)S(1)}, u32[]{:S(2)}, u32[]{:S(2)}) collective-permute-start(f32[320,128]{1,0:T(8,128)S(1)} %get-tuple-element.78), channel_id=1, source_target_pairs={{4,8},{8,4},{12,16},{16,12},{20,24},{24,20},{28,32},{32,28},{36,40... | collective-permute-start | bytes 491528 | tf_op jit(solution)/shard_map/ppermute | solution.py:595
  78.2 11.6 %collective-permute-start.13 = (f32[320,128]{1,0:T(8,128)S(1)}, f32[320,128]{1,0:T(8,128)S(1)}, u32[]{:S(2)}, u32[]{:S(2)}) collective-permute-start(f32[320,128]{1,0:T(8,128)S(1)} %get-tuple-element.79), channel_id=1, source_target_pairs={{0,4},{4,0},{8,12},{12,8},{16,20},{20,16},{24,28},{28,24},{32,36},... | collective-permute-start | bytes 491528 | tf_op jit(solution)/shard_map/ppermute | solution.py:595
  90.4 5.0 %collective-permute-start.14 = (f32[408,128]{1,0:T(8,128)S(1)}, f32[408,128]{1,0:T(8,128)S(1)}, u32[]{:S(2)}, u32[]{:S(2)}) collective-permute-start(f32[408,128]{1,0:T(8,128)S(1)} %get-tuple-element.80), channel_id=1, source_target_pairs={{64,128},{128,64},{192,256},{256,192},{320,384},{384,320},{65,129}... | collective-permute-start | bytes 626696 | tf_op jit(solution)/shard_map/ppermute | solution.py:595
  91.1 5.4 %collective-permute-start.15 = (f32[408,128]{1,0:T(8,128)S(1)}, f32[408,128]{1,0:T(8,128)S(1)}, u32[]{:S(2)}, u32[]{:S(2)}) collective-permute-start(f32[408,128]{1,0:T(8,128)S(1)} %get-tuple-element.81), channel_id=1, source_target_pairs={{0,64},{64,0},{128,192},{192,128},{256,320},{320,256},{384,448},{4... | collective-permute-start | bytes 626696 | tf_op jit(solution)/shard_map/ppermute | solution.py:595
  100.0 12.9 %collective-permute-start.16 = (f32[384,128]{1,0:T(8,128)S(1)}, f32[384,128]{1,0:T(8,128)S(1)}, u32[]{:S(2)}, u32[]{:S(2)}) collective-permute-start(f32[384,128]{1,0:T(8,128)S(1)} %get-tuple-element.83.refs_0_), channel_id=1, source_target_pairs={{0,1},{1,0},{2,3},{3,2},{4,5},{5,4},{6,7},{7,6},{8,9},{9,8},{10,11... | collective-permute-start | bytes 589832 | tf_op jit(solution)/shard_map/ppermute | solution.py:694
  102.4 13.9 %collective-permute-start.19 = (f32[384,128]{1,0:T(8,128)S(1)}, f32[384,128]{1,0:T(8,128)S(1)}, u32[]{:S(2)}, u32[]{:S(2)}) collective-permute-start(f32[384,128]{1,0:T(8,128)S(1)} %get-tuple-element.84.refs_1_), channel_id=1, source_target_pairs={{0,3},{1,2},{2,1},{3,0},{4,7},{5,6},{6,5},{7,4},{8,11},{9,10},{10,... | collective-permute-start | bytes 589832 | tf_op jit(solution)/shard_map/ppermute | solution.py:694
  106.5 12.5 %collective-permute-start.18 = (f32[384,128]{1,0:T(8,128)S(1)}, f32[384,128]{1,0:T(8,128)S(1)}, u32[]{:S(2)}, u32[]{:S(2)}) collective-permute-start(f32[384,128]{1,0:T(8,128)S(1)} %get-tuple-element.83.refs_0_), channel_id=1, source_target_pairs={{0,3},{1,2},{2,1},{3,0},{4,7},{5,6},{6,5},{7,4},{8,11},{9,10},{10,... | collective-permute-start | bytes 589832 | tf_op jit(solution)/shard_map/ppermute | solution.py:695
  108.4 10.5 %collective-permute-start.17 = (f32[384,128]{1,0:T(8,128)S(1)}, f32[384,128]{1,0:T(8,128)S(1)}, u32[]{:S(2)}, u32[]{:S(2)}) collective-permute-start(f32[384,128]{1,0:T(8,128)S(1)} %get-tuple-element.84.refs_1_), channel_id=1, source_target_pairs={{0,1},{1,0},{2,3},{3,2},{4,5},{5,4},{6,7},{7,6},{8,9},{9,8},{10,11... | collective-permute-start | bytes 589832 | tf_op jit(solution)/shard_map/ppermute | solution.py:695
  112.9 8.3 %collective-permute-start.20 = (f32[384,128]{1,0:T(8,128)S(1)}, f32[384,128]{1,0:T(8,128)S(1)}, u32[]{:S(2)}, u32[]{:S(2)}) collective-permute-start(f32[384,128]{1,0:T(8,128)S(1)} %collective-permute-done.16.refs_2_), channel_id=1, source_target_pairs={{0,3},{1,2},{2,1},{3,0},{4,7},{5,6},{6,5},{7,4},{8,11},{9,10},{10,... | collective-permute-start | bytes 589832 | tf_op jit(solution)/shard_map/ppermute | solution.py:696
  116.3 8.1 %collective-permute-start.21 = (f32[384,128]{1,0:T(8,128)S(1)}, f32[384,128]{1,0:T(8,128)S(1)}, u32[]{:S(2)}, u32[]{:S(2)}) collective-permute-start(f32[384,128]{1,0:T(8,128)S(1)} %collective-permute-done.19.refs_5_), channel_id=1, source_target_pairs={{0,1},{1,0},{2,3},{3,2},{4,5},{5,4},{6,7},{7,6},{8,9},{9,8},{10,11... | collective-permute-start | bytes 589832 | tf_op jit(solution)/shard_map/ppermute | solution.py:696
